TPU v7x, 32 devices: a whole 2x2x4 slice. The times are simulated.
32 devices in a mesh: dp: 8 (over y, x, core), tensor: 4 (over z).
Axes of the slice: x: 2, y: 2, z: 4, core: 2. Of those that a mesh axis runs over, the one named last changes fastest.
Arguments:
- tokens: bfloat16 [1024, 1152], P('dp', 'tensor'), may hold values from -6 to 6
- resets: int32 [1024], P('dp'), may hold values 0 or 1
- routes: int32 [1024, 1], P('dp'), may hold values from 0 to 7; in each aligned block of 128 rows (0 to 127, 128 to 255, ...) at most 32 rows name the same one
- norm_one: float32 [1152], replicated, may hold values from 0.5 to 1.5
- in_proj: bfloat16 [2, 1152, 2304], P(None, None, 'tensor'), may hold values from -0.1875 to 0.1875
- conv_weight: float32 [4, 2304], P(None, 'tensor'), may hold values from -3 to 3
- conv_bias: float32 [2304], P('tensor'), may hold values from -3 to 3
- x_proj: bfloat16 [2304, 104], P('tensor'), may hold values from -0.125 to 0.125
- dt_proj: bfloat16 [72, 2304], P(None, 'tensor'), may hold values from -0.75 to 0.75
- dt_bias: float32 [2304], P('tensor'), may hold values from -4 to -1
- decay_log: float32 [16, 2304], P(None, 'tensor'), may hold values from 0 to 2.77
- skip_gain: float32 [2304], P('tensor'), may hold values from 0.5 to 1.5
- out_proj: bfloat16 [2304, 1152], P('tensor'), may hold values from -0.5 to 0.5
- norm_two: float32 [1152], replicated, may hold values from 0.5 to 1.5
- expert_in: bfloat16 [8, 1152, 3072], P(None, 'dp', 'tensor'), may hold values from -0.1875 to 0.1875
- expert_out: bfloat16 [8, 1152, 3072], P(None, 'dp', 'tensor'), may hold values from -0.15625 to 0.15625
- cotangent: bfloat16 [1024, 1152], P('dp'), may hold values from -6 to 6
Outputs:
- result: bfloat16 [1024, 1152], P('dp', 'tensor')
- grad_tokens: float32 [1024, 1152], P('dp', 'tensor')
- grad_norm_one: float32 [1152], replicated
- grad_in_proj: float32 [2, 1152, 2304], P(None, None, 'tensor')
- grad_conv_weight: float32 [4, 2304], P(None, 'tensor')
- grad_conv_bias: float32 [2304], P('tensor')
- grad_x_proj: float32 [2304, 104], P('tensor')
- grad_dt_proj: float32 [72, 2304], P(None, 'tensor')
- grad_dt_bias: float32 [2304], P('tensor')
- grad_decay_log: float32 [16, 2304], P(None, 'tensor')
- grad_skip_gain: float32 [2304], P('tensor')
- grad_out_proj: float32 [2304, 1152], P('tensor')
- grad_norm_two: float32 [1152], replicated
- grad_expert_in: float32 [8, 1152, 3072], P(None, 'dp', 'tensor')
- grad_expert_out: float32 [8, 1152, 3072], P(None, 'dp', 'tensor')
Inputs may be any that keep to these rules, and one draw needn't show every extreme that they name: `routes`: in each aligned block of 128 rows no expert is named by more than 32 rows.
All inputs are finite; a program needn't handle non-finite values. No bound on the sum of `resets` on one device may be relied on, other than what follows from the above.
Results may differ from a plain program's by a relative error of at most 0.02.
Values may be sent and summed in bfloat16 or wider, within the bound.
No kernel may reach another device: no remote copies, remote signals or barrier semaphores. Data moves between devices by JAX's collectives and lax.ppermute only.
A program may use at most 128 MiB of HBM per device.

v0:
```python
import math

import jax
import jax.numpy as jnp
from jax import lax
from jax.sharding import PartitionSpec as P

EPSILON = 1e-05
PRECISE = lax.Precision.HIGHEST


def rms_scale(values, gain):
    return values * lax.rsqrt(jnp.mean(values * values, axis=-1, keepdims=True) + EPSILON) * gain


def conv_mix(values, weight, offset, segment):
    length = values.shape[0]
    tap_count = weight.shape[0]
    running_sum = offset + weight[tap_count - 1] * values
    for shift_by in range(1, tap_count):
        moved_rows = jnp.concatenate(
            [jnp.zeros((shift_by, values.shape[1]), values.dtype), values[: length - shift_by]],
            axis=0,
        )
        earlier = jnp.concatenate(
            [jnp.full((shift_by,), -1, jnp.int32), segment[: length - shift_by]], axis=0
        )
        same_doc = (earlier == segment).astype(values.dtype)
        running_sum = (
            running_sum + weight[tap_count - 1 - shift_by] * moved_rows * same_doc[:, None]
        )
    return running_sum


def scan_piece(
    activ_in, step_prod, step_bias, decay_in, skip_in, b_input, c_input, gate_in, keep_mask
):
    length, chans = activ_in.shape
    states = decay_in.shape[0]
    block_len = math.gcd(length, 16)
    block_num = length // block_len
    step_size = jax.nn.softplus(step_prod + step_bias)
    rate_flat = -jnp.exp(decay_in).reshape(1, states * chans)
    row_ids = jnp.arange(block_len, dtype=jnp.int32)
    lower = row_ids[:, None] >= row_ids[None, :]

    def block_fn(carried, pieces):
        step_b, activ_b, b_block, c_block, keep_b = pieces
        log_decay = rate_flat * jnp.tile(step_b, (1, states))
        cum = jnp.cumsum(log_decay, axis=0)
        reset_count = jnp.cumsum((keep_b == 0).astype(jnp.int32))
        allowed = jnp.logical_and(lower, reset_count[:, None] == reset_count[None, :])
        allowed_f = allowed.astype(activ_b.dtype)
        diff = cum[:, None, :] - cum[None, :, :]
        weights = jnp.exp(jnp.where(allowed[:, :, None], diff, 0.0)) * allowed_f[:, :, None]
        drive_in = (b_block[:, :, None] * (step_b * activ_b)[:, None, :]).reshape(
            block_len, states * chans
        )
        from_block = jnp.sum(weights * drive_in[None, :, :], axis=1)
        carry_keep = (reset_count == 0).astype(activ_b.dtype)
        new_states = from_block + jnp.exp(cum) * carry_keep[:, None] * carried[None, :]
        out_rows = jnp.einsum(
            "snc,sn->sc", new_states.reshape(block_len, states, chans), c_block, precision=PRECISE
        )
        return (new_states[-1], out_rows)

    pieces = (
        step_size.reshape(block_num, block_len, chans),
        activ_in.reshape(block_num, block_len, chans),
        b_input.reshape(block_num, block_len, states),
        c_input.reshape(block_num, block_len, states),
        keep_mask.reshape(block_num, block_len),
    )
    start_state = jnp.zeros((states * chans,), activ_in.dtype)
    last_state, out_blocks = lax.scan(jax.checkpoint(block_fn), start_state, pieces)
    y_rows = out_blocks.reshape(length, chans) + skip_in * activ_in
    return y_rows * jax.nn.silu(gate_in)


def contract_last(left, right):
    return lax.dot_general(
        left, right, (((1,), (1,)), ((), ())), preferred_element_type=jnp.float32
    )


def contract_first(left, right):
    return lax.dot_general(
        left, right, (((0,), (0,)), ((), ())), preferred_element_type=jnp.float32
    )


def share_total(values):
    return lax.psum_scatter(
        values.astype(jnp.bfloat16), "tensor", scatter_dimension=1, tiled=True
    ).astype(jnp.float32)


def grad_total(values):
    return lax.psum_scatter(
        values.astype(jnp.bfloat16), "tensor", scatter_dimension=1, tiled=True
    ).astype(jnp.float32)


def body(
    tokens,
    resets,
    routes,
    norm_one,
    in_proj,
    conv_weight,
    conv_bias,
    x_proj,
    dt_proj,
    dt_bias,
    decay_log,
    skip_gain,
    out_proj,
    norm_two,
    expert_in,
    expert_out,
    cotangent,
):
    groups = lax.axis_size("dp")
    tensor_count = lax.axis_size("tensor")
    my_tensor = lax.axis_index("tensor")
    length = tokens.shape[0]
    model_width = norm_one.shape[0]
    rank_dt = dt_proj.shape[0]
    states = decay_log.shape[0]
    experts = expert_in.shape[0]
    share_rows = expert_in.shape[1]
    col_count = model_width // tensor_count
    tile_count = groups // experts
    first_w, second_w = (
        lax.all_to_all(
            jnp.tile(expert_in, (tile_count, 1, 1)), "dp", split_axis=0, concat_axis=0, tiled=True
        ),
        lax.all_to_all(
            jnp.tile(expert_out, (tile_count, 1, 1)), "dp", split_axis=0, concat_axis=0, tiled=True
        ),
    )
    first_w = first_w.reshape(model_width, -1)
    second_w = second_w.reshape(model_width, -1)
    row_data = lax.all_gather(tokens, "tensor", axis=1, tiled=True).astype(jnp.float32)
    normed, norm_one_back = jax.vjp(rms_scale, row_data, norm_one)
    normed_low = normed.astype(jnp.bfloat16)
    inner_raw = jnp.dot(normed_low, in_proj[0], preferred_element_type=jnp.float32)
    gate_in = jnp.dot(normed_low, in_proj[1], preferred_element_type=jnp.float32)
    segment = jnp.cumsum(resets)
    keep_mask = (resets == 0).astype(jnp.float32)

    def conv_activ(values, weight, offset):
        return jax.nn.silu(conv_mix(values, weight, offset, segment))

    activ, conv_back = jax.vjp(conv_activ, inner_raw, conv_weight, conv_bias)
    activ_low = activ.astype(jnp.bfloat16)
    mixed_proj = lax.psum(
        jnp.dot(activ_low, x_proj, preferred_element_type=jnp.float32).astype(jnp.bfloat16),
        "tensor",
    ).astype(jnp.float32)
    dt_low = mixed_proj[:, :rank_dt].astype(jnp.bfloat16)
    b_input = mixed_proj[:, rank_dt : rank_dt + states]
    c_input = mixed_proj[:, rank_dt + states :]
    step_prod = jnp.dot(dt_low, dt_proj, preferred_element_type=jnp.float32)

    def mixer_core(values, product, step_bias, decay_in, skip_in, b_block, c_block, gate_block):
        return scan_piece(
            values, product, step_bias, decay_in, skip_in, b_block, c_block, gate_block, keep_mask
        )

    gated_out, core_back = jax.vjp(
        mixer_core,
        activ_low.astype(jnp.float32),
        step_prod,
        dt_bias,
        decay_log,
        skip_gain,
        b_input,
        c_input,
        gate_in,
    )
    gated_low = gated_out.astype(jnp.bfloat16)
    mixer_out = lax.psum(
        jnp.dot(gated_low, out_proj, preferred_element_type=jnp.float32).astype(jnp.bfloat16),
        "tensor",
    ).astype(jnp.float32)
    residual = row_data + mixer_out
    normed_two, norm_two_back = jax.vjp(rms_scale, residual, norm_two)
    send_rows = normed_two.astype(jnp.bfloat16)
    expert_ids = routes[:, 0]
    block_rows = length * experts // groups
    capacity = max(2, block_rows // 4)
    block_num = length // block_rows
    choose = (expert_ids[:, None] == jnp.arange(experts, dtype=jnp.int32)[None, :]).astype(
        jnp.int32
    )
    running = jnp.cumsum(choose.reshape(block_num, block_rows, experts), axis=1).reshape(
        length, experts
    )
    slot_rank = jnp.sum((running - 1) * choose, axis=1)
    position = jnp.arange(length, dtype=jnp.int32)
    slot_index = (expert_ids + experts * (position // block_rows)) * capacity + slot_rank
    source = jnp.full((groups * capacity,), length, jnp.int32).at[slot_index].set(position)
    padded = jnp.concatenate([send_rows, jnp.zeros((1, model_width), jnp.bfloat16)], axis=0)
    arrived = lax.all_to_all(
        padded[source].reshape(groups, capacity, model_width),
        "dp",
        split_axis=0,
        concat_axis=0,
        tiled=True,
    ).reshape(groups * capacity, model_width)
    pre_gelu = jnp.dot(arrived, first_w, preferred_element_type=jnp.float32)
    hidden, gelu_back = jax.vjp(jax.nn.gelu, pre_gelu)
    hidden_low = hidden.astype(jnp.bfloat16)
    partial_value = contract_last(hidden_low, second_w)
    returned = lax.all_to_all(
        partial_value.reshape(groups, capacity, -1).astype(jnp.bfloat16),
        "dp",
        split_axis=0,
        concat_axis=0,
        tiled=True,
    ).astype(jnp.float32)
    per_row = returned.reshape(groups * capacity, -1)[slot_index]
    moe_part = share_total(per_row)
    residual_cols = lax.dynamic_slice_in_dim(residual, my_tensor * col_count, col_count, 1)
    outcome = (residual_cols + moe_part).astype(jnp.bfloat16)
    grad_pad = jnp.concatenate([cotangent, jnp.zeros((1, model_width), jnp.bfloat16)], axis=0)
    grad_slots = lax.all_to_all(
        grad_pad[source].reshape(groups, capacity, model_width),
        "dp",
        split_axis=0,
        concat_axis=0,
        tiled=True,
    ).reshape(groups * capacity, model_width)
    d_hidden = jnp.dot(grad_slots, second_w, preferred_element_type=jnp.float32)
    grad_second = contract_first(grad_slots, hidden_low)
    d_pre = gelu_back(d_hidden)[0].astype(jnp.bfloat16)
    grad_first = contract_first(arrived, d_pre)
    d_slots = contract_last(d_pre, first_w)
    back_slots, back_first, back_second = (
        lax.all_to_all(
            d_slots.reshape(groups, capacity, -1).astype(jnp.bfloat16),
            "dp",
            split_axis=0,
            concat_axis=0,
            tiled=True,
        ).astype(jnp.float32),
        lax.all_to_all(
            grad_first.reshape(groups, share_rows, -1).astype(jnp.bfloat16),
            "dp",
            split_axis=0,
            concat_axis=0,
            tiled=True,
        ).astype(jnp.float32),
        lax.all_to_all(
            grad_second.reshape(groups, share_rows, -1).astype(jnp.bfloat16),
            "dp",
            split_axis=0,
            concat_axis=0,
            tiled=True,
        ).astype(jnp.float32),
    )
    grad_expert_in = jnp.sum(back_first.reshape(tile_count, experts, share_rows, -1), axis=0)
    grad_expert_out = jnp.sum(back_second.reshape(tile_count, experts, share_rows, -1), axis=0)
    slot_rows = back_slots.reshape(groups * capacity, -1)[slot_index]
    send_cols = grad_total(slot_rows)
    d_send = lax.all_gather(send_cols.astype(jnp.bfloat16), "tensor", axis=1, tiled=True).astype(
        send_cols.dtype
    )
    d_resid_norm, grad_norm_two = norm_two_back(d_send)
    d_residual = cotangent.astype(jnp.float32) + d_resid_norm
    d_mix = d_residual.astype(jnp.bfloat16)
    grad_out_proj = contract_first(gated_low, d_mix)
    d_gated = contract_last(d_mix, out_proj)
    d_act_scan, d_step, grad_dt_bias, grad_decay, grad_skip, d_b, d_c, d_gate = core_back(d_gated)
    d_step_low = d_step.astype(jnp.bfloat16)
    grad_dt_proj = contract_first(dt_low, d_step_low)
    d_dt_low = contract_last(d_step_low, dt_proj)
    d_mixed = lax.psum(jnp.concatenate([d_dt_low, d_b, d_c], axis=1).astype(jnp.bfloat16), "tensor")
    grad_x_proj = contract_first(activ_low, d_mixed)
    d_activ = d_act_scan + contract_last(d_mixed, x_proj)
    d_inner, grad_conv_weight, grad_conv_bias = conv_back(d_activ)
    d_inner_low = d_inner.astype(jnp.bfloat16)
    d_gate_low = d_gate.astype(jnp.bfloat16)
    grad_in_proj = jnp.stack(
        [contract_first(normed_low, d_inner_low), contract_first(normed_low, d_gate_low)]
    )
    d_normed = lax.psum(
        (contract_last(d_inner_low, in_proj[0]) + contract_last(d_gate_low, in_proj[1])).astype(
            jnp.bfloat16
        ),
        "tensor",
    ).astype(jnp.float32)
    d_rows_norm, grad_norm_one = norm_one_back(d_normed)
    grad_tokens = lax.dynamic_slice_in_dim(
        d_residual + d_rows_norm, my_tensor * col_count, col_count, 1
    )
    summed = lax.psum(
        (
            grad_norm_one,
            grad_in_proj,
            grad_conv_weight,
            grad_conv_bias,
            grad_x_proj,
            grad_dt_proj,
            grad_dt_bias,
            grad_decay,
            grad_skip,
            grad_out_proj,
            grad_norm_two,
        ),
        "dp",
    )
    return (
        outcome,
        grad_tokens,
        summed[0],
        summed[1],
        summed[2],
        summed[3],
        summed[4],
        summed[5],
        summed[6],
        summed[7],
        summed[8],
        summed[9],
        summed[10],
        grad_expert_in,
        grad_expert_out,
    )


def solution(mesh):
    placed = (
        P("dp", "tensor"),
        P("dp"),
        P("dp", None),
        P(),
        P(None, None, "tensor"),
        P(None, "tensor"),
        P("tensor"),
        P("tensor", None),
        P(None, "tensor"),
        P("tensor"),
        P(None, "tensor"),
        P("tensor"),
        P("tensor", None),
        P(),
        P(None, "dp", "tensor"),
        P(None, "dp", "tensor"),
        P("dp", None),
    )
    return jax.shard_map(
        body,
        mesh=mesh,
        in_specs=placed,
        out_specs=(
            P("dp", "tensor"),
            P("dp", "tensor"),
            P(),
            P(None, None, "tensor"),
            P(None, "tensor"),
            P("tensor"),
            P("tensor", None),
            P(None, "tensor"),
            P("tensor"),
            P(None, "tensor"),
            P("tensor"),
            P("tensor", None),
            P(),
            P(None, "dp", "tensor"),
            P(None, "dp", "tensor"),
        ),
        check_vma=False,
    )
```

profile of v0, /device:TPU:0, one launch (start us, length us, event | category | flops | bytes accessed | tf_op | source)
XLA Modules:
  0.0 837.4 jit_solution(1765879617625221497)
XLA Ops:
  11.6 15.8 %all_gather.6 = bf16[128,1152]{0,1:T(8,128)(2,1)S(1)} all-gather(bf16[128,288]{0,1:T(8,128)(2,1)} %param.21), channel_id=1, replica_groups=mesh['dp'=8,'tensor'=4] {'tensor'}, dimensions={1}, use_global_device_ids=true | all-gather | bytes 368640 | tf_op jit(solution)/shard_map/all_gather | solution.py:144
  33.8 19.8 %psum.105 = bf16[128,104]{0,1:T(8,128)(2,1)S(1)} all-reduce(bf16[128,104]{0,1:T(8,128)(2,1)S(1)} %convolution_convert_fusion.5), channel_id=1, replica_groups=mesh['dp'=8,'tensor'=4] {'tensor'}, use_global_device_ids=true, to_apply=%region_2.3 | all-reduce | flops 13312 | bytes 53248 | tf_op jit(solution)/shard_map/psum | solution.py:157
  58.5 152.2 %while.41 = (s32[]{:T(128)}, f32[9216]{0:T(1024)}, f32[8,16,576]{2,1,0:T(8,128)}, f32[8,9216]{1,0:T(8,128)}, f32[8,16]{1,0:T(8,128)}, /*index=5*/f32[1,9216]{1,0...) while((s32[]{:T(128)}, f32[9216]{0:T(1024)}, ...), condition=%wide.region_7.8_spmd.clone, body=%wide.region_3.7_spmd.clone.sunk | while | flops 16405810 | bytes 13506033 | solution.py:75
  223.2 26.9 %all-reduce.21.cloned.1.call-done = bf16[128,1152]{1,0:T(8,128)(2,1)} async-done(((bf16[128,1152]{1,0:T(8,128)(2,1)}), bf16[128,1152]{1,0:T(8,128)(2,1)}) %all-reduce.21.cloned.1.call-update) | async-done | bytes 294928 | tf_op jit(solution)/shard_map/psum | solution.py:183
  254.4 14.0 %all_to_all.40 = bf16[8,32,1152]{2,1,0:T(8,128)(2,1)} all-to-all(bf16[8,32,1152]{2,1,0:T(8,128)(2,1)S(1)} %bitcast.219), channel_id=1, replica_groups=mesh['dp'=8,'tensor'=4] {'dp'}, dimensions={0} | all-to-all | bytes 1179648 | tf_op jit(solution)/shard_map/all_to_all | solution.py:205
  268.4 26.8 %all_to_all.41 = bf16[8,144,768]{2,1,0:T(8,128)(2,1)S(1)} all-to-all(bf16[8,144,768]{2,1,0:T(8,128)(2,1)} %param.36), channel_id=1, replica_groups=mesh['dp'=8,'tensor'=4] {'dp'}, dimensions={0} | all-to-all | bytes 3538944 | tf_op jit(solution)/shard_map/all_to_all | solution.py:138
  302.1 20.5 %all-to-all-done.1 = bf16[8,144,768]{2,1,0:T(8,128)(2,1)} async-done(((bf16[8,144,768]{2,1,0:T(8,128)(2,1)}), bf16[8,144,768]{2,1,0:T(8,128)(2,1)}, u32[]{:S(2)}, u32[]{:S(2)}) %all-to-all-start.1) | async-done | bytes 1769504 | tf_op jit(solution)/shard_map/all_to_all | solution.py:135
  333.7 10.3 %all-to-all-done.5 = bf16[8,32,1152]{2,1,0:T(8,128)(2,1)S(1)} async-done(((bf16[8,32,1152]{2,1,0:T(8,128)(2,1)}), bf16[8,32,1152]{2,1,0:T(8,128)(2,1)S(1)}, u32[]{:S(2)}, u32[]{:S(2)}) %all-to-all-start.5) | async-done | bytes 589856 | tf_op jit(solution)/shard_map/all_to_all | solution.py:241
  352.6 10.3 %all-to-all-done.3 = bf16[8,32,1152]{2,1,0:T(8,128)(2,1)S(1)} async-done(((bf16[8,32,1152]{2,1,0:T(8,128)(2,1)}), bf16[8,32,1152]{2,1,0:T(8,128)(2,1)S(1)}, u32[]{:S(2)}, u32[]{:S(2)}) %all-to-all-start.3) | async-done | bytes 589856 | tf_op jit(solution)/shard_map/all_to_all | solution.py:216
  364.8 14.8 %all_gather.7 = bf16[128,1152]{0,1:T(8,128)(2,1)S(1)} all-gather(bf16[128,288]{0,1:T(8,128)(2,1)} %bitcast.235), channel_id=1, replica_groups=mesh['dp'=8,'tensor'=4] {'tensor'}, dimensions={1}, use_global_device_ids=true | all-gather | bytes 368640 | tf_op jit(solution)/shard_map/all_gather | solution.py:267
  390.0 215.6 %while.42 = (s32[]{:T(128)}, f32[1,9216]{1,0:T(1,128)}, f32[9216]{0:T(1024)}, f32[8,16,576]{2,1,0:T(8,128)}, f32[8,16,576]{2,1,0:T(8,128)}, /*index=5*/bf16[8,16...) while((s32[]{:T(128)}, f32[1,9216]{1,0:T(1,128)}, ...), condition=%wide.region_29.30_spmd.clone, body=%wide.region_16.29_spmd.clone.sunk | while | flops 39832624 | bytes 28125452 | solution.py:75
  398.4 7.3 fusion.146
  424.7 7.3 fusion.146
  451.7 7.3 fusion.146
  478.7 7.3 fusion.146
  505.8 7.3 fusion.146
  532.8 7.3 fusion.146
  559.9 7.3 fusion.146
  586.9 7.3 fusion.146
  612.6 18.5 %psum.107 = bf16[128,104]{0,1:T(8,128)(2,1)S(1)} all-reduce(bf16[128,104]{0,1:T(8,128)(2,1)S(1)} %pad_maximum_fusion.1), channel_id=1, replica_groups=mesh['dp'=8,'tensor'=4] {'tensor'}, use_global_device_ids=true, to_apply=%region_30.31 | all-reduce | flops 13312 | bytes 53248 | tf_op jit(solution)/shard_map/psum | solution.py:279
  656.0 19.9 %all-to-all-done.6 = bf16[8,144,768]{2,1,0:T(8,128)(2,1)S(1)} async-done(((bf16[8,144,768]{2,1,0:T(8,128)(2,1)}), bf16[8,144,768]{2,1,0:T(8,128)(2,1)S(1)}, u32[]{:S(2)}, u32[]{:S(2)}) %all-to-all-start.6) | async-done | bytes 1769504 | tf_op jit(solution)/shard_map/all_to_all | solution.py:248
  686.7 54.3 %all-reduce.15 = (f32[1152]{0:T(1024)}, f32[4,576]{1,0:T(4,128)}, f32[576]{0:T(1024)}, f32[576]{0:T(1024)}, f32[16,576]{1,0:T(8,128)}, /*index=5*/f32[576]{0:T(1024)}, f32[1152]{0:T(1024)}) all-reduce(f32[1152]{0:T(1024)S(1)} %get-tuple-element.694, f32[4,576]{1,0:T(4,128)S(1)} %pad_add_fusion.1, ...), channel_id=1, replica_groups=mesh['dp'=8,'tensor'=4] {'dp'}, use_global_device_ids=true, to_apply=%region_34.35 | all-reduce | flops 15552 | bytes 124416 | tf_op jit(solution)/shard_map/psum | solution.py:298
  746.8 75.8 %all-reduce.25.cloned.1.call-done = (f32[2,1152,576]{1,2,0:T(8,128)}, f32[576,104]{0,1:T(8,128)}, f32[72,576]{1,0:T(8,128)}, f32[576,1152]{1,0:T(8,128)}) async-done(((f32[2,1152,576]{1,2,0:T(8,128)}, f32[576,104]{0,1:T(8,128)}, f32[72,576]{1,0:T(8,128)}, f32[576,1152]{1,0:T(8,128)}), (f32[2,1152,576]{1,2,0:T(8,128)}, f32[576,104]{0,1:T(8,128)}, f32[72,576]{1,0:T(8,128)}, ...) | async-done | bytes 8368144 | tf_op jit(solution)/shard_map/psum | solution.py:298
  822.6 5.4 copy.192
  (818 shorter events, 429.4 us)
Async XLA Ops:
  7.2 207.5 %copy-start = (bf16[576,1152]{1,0:T(8,128)(2,1)S(1)}, bf16[576,1152]{1,0:T(8,128)(2,1)}, u32[]{:S(2)}) copy-start(bf16[576,1152]{1,0:T(8,128)(2,1)} %param.33) | copy-start | bytes 3981316
  7.2 242.8 %all-reduce.21.cloned.1.call-start = ((), (), s32[]{:S(2)}) async-start(), calls=%async_computation.10 | async-start | bytes 589824 | tf_op jit(solution)/shard_map/psum | solution.py:183
  58.4 153.4 %copy-start.38 = (f32[1152]{0:T(1024)S(1)}, f32[1152]{0:T(1024)}, u32[]{:S(2)}) copy-start(f32[1152]{0:T(1024)} %param.24) | copy-start | bytes 13828
  217.4 33.8 %copy-start.37 = (f32[1152]{0:T(1024)S(1)}, f32[1152]{0:T(1024)}, u32[]{:S(2)}) copy-start(f32[1152]{0:T(1024)} %param.34) | copy-start | bytes 13828
  219.4 34.1 %all-to-all-start.4 = ((bf16[8,32,1152]{2,1,0:T(8,128)(2,1)}), bf16[8,32,1152]{2,1,0:T(8,128)(2,1)S(1)}, u32[]{:S(2)}, u32[]{:S(2)}) async-start(bf16[8,32,1152]{2,1,0:T(8,128)(2,1)} %bitcast.16), calls=%async_computation.4 | async-start | bytes 1179648 | tf_op jit(solution)/shard_map/all_to_all | solution.py:228
  295.2 34.9 %copy-start.6 = (bf16[8,144,768]{2,1,0:T(8,128)(2,1)}, bf16[8,144,768]{2,1,0:T(8,128)(2,1)S(1)}, u32[]{:S(2)}) copy-start(bf16[8,144,768]{2,1,0:T(8,128)(2,1)S(1)} %all_to_all.41) | copy-start | bytes 5308420
  295.2 27.5 %all-to-all-start.1 = ((bf16[8,144,768]{2,1,0:T(8,128)(2,1)}), bf16[8,144,768]{2,1,0:T(8,128)(2,1)}, u32[]{:S(2)}, u32[]{:S(2)}) async-start(bf16[8,144,768]{2,1,0:T(8,128)(2,1)} %param.35), calls=%async_computation.1 | async-start | bytes 3538944 | tf_op jit(solution)/shard_map/all_to_all | solution.py:135
  330.1 13.9 %all-to-all-start.5 = ((bf16[8,32,1152]{2,1,0:T(8,128)(2,1)}), bf16[8,32,1152]{2,1,0:T(8,128)(2,1)S(1)}, u32[]{:S(2)}, u32[]{:S(2)}) async-start(bf16[8,32,1152]{2,1,0:T(8,128)(2,1)} %convolution_convert_fusion), calls=%async_computation.5 | async-start | bytes 1179648 | tf_op jit(solution)/shard_map/all_to_all | solution.py:241
  333.7 31.2 %reduce-scatter.9.cloned.1.call-start = ((), (), s32[]{:S(2)}) async-start(), calls=%async_computation.13 | async-start | bytes 368640
  348.9 31.0 %copy-start.9 = (bf16[128,1152]{1,0:T(8,128)(2,1)S(1)}, bf16[128,1152]{1,0:T(8,128)(2,1)}, u32[]{:S(2)}) copy-start(bf16[128,1152]{1,0:T(8,128)(2,1)} %all-reduce.21.cloned.1.call-done) | copy-start | bytes 884740
  348.9 14.1 %all-to-all-start.3 = ((bf16[8,32,1152]{2,1,0:T(8,128)(2,1)}), bf16[8,32,1152]{2,1,0:T(8,128)(2,1)S(1)}, u32[]{:S(2)}, u32[]{:S(2)}) async-start(bf16[8,32,1152]{2,1,0:T(8,128)(2,1)} %convolution_convert_fusion.1), calls=%async_computation.3 | async-start | bytes 1179648 | tf_op jit(solution)/shard_map/all_to_all | solution.py:216
  352.5 327.8 %reduce-scatter.7.cloned.1.call-start = ((), (), s32[]{:S(2)}) async-start(), calls=%async_computation.12 | async-start | bytes 368640
  364.8 318.7 %all-reduce.23.cloned.1.call-start = ((), (), s32[]{:S(2)}) async-start(), calls=%async_computation.11 | async-start | bytes 589824 | tf_op jit(solution)/shard_map/psum | solution.py:288
  605.7 27.5 %copy-start.3 = (f32[128,576]{0,1:T(8,128)S(1)}, f32[128,576]{0,1:T(8,128)}, u32[]{:S(2)}) copy-start(f32[128,576]{0,1:T(8,128)} %copy-done.2) | copy-start | bytes 884740
  605.7 27.5 %copy-start.20 = (f32[128,576]{0,1:T(8,128)S(1)}, f32[128,576]{0,1:T(8,128)}, u32[]{:S(2)}) copy-start(f32[128,576]{0,1:T(8,128)} %copy-done.19) | copy-start | bytes 884740
  605.7 27.5 %copy-start.21 = (f32[128,576]{0,1:T(8,128)S(1)}, f32[128,576]{0,1:T(8,128)}, u32[]{:S(2)}) copy-start(f32[128,576]{0,1:T(8,128)} %get-tuple-element.778) | copy-start | bytes 884740
  605.7 27.5 %copy-start.27 = (bf16[576,104]{0,1:T(8,128)(2,1)S(1)}, bf16[576,104]{0,1:T(8,128)(2,1)}, u32[]{:S(2)}) copy-start(bf16[576,104]{0,1:T(8,128)(2,1)} %param.28) | copy-start | bytes 359428
  605.7 27.5 %copy-start.45 = (f32[128]{0:T(128)S(1)}, f32[128]{0:T(128)}, u32[]{:S(2)}) copy-start(f32[128]{0:T(128)} %copy-done.44) | copy-start | bytes 1540
  605.7 27.5 %copy-start.47 = (f32[128]{0:T(128)S(1)}, f32[128]{0:T(128)}, u32[]{:S(2)}) copy-start(f32[128]{0:T(128)} %copy-done.46) | copy-start | bytes 1540
  605.7 27.5 %copy-start.49 = (f32[128]{0:T(128)S(1)}, f32[128]{0:T(128)}, u32[]{:S(2)}) copy-start(f32[128]{0:T(128)} %copy-done.48) | copy-start | bytes 1540
  639.5 183.1 %all-reduce.25.cloned.1.call-start = ((), (), s32[]{:S(2)}) async-start(), calls=%async_computation.14 | async-start | bytes 16826368 | tf_op jit(solution)/shard_map/psum | solution.py:298
  649.3 26.7 %all-to-all-start.6 = ((bf16[8,144,768]{2,1,0:T(8,128)(2,1)}), bf16[8,144,768]{2,1,0:T(8,128)(2,1)S(1)}, u32[]{:S(2)}, u32[]{:S(2)}) async-start(bf16[8,144,768]{2,1,0:T(8,128)(2,1)} %convolution_convert_fusion.4), calls=%async_computation.6 | async-start | bytes 3538944 | tf_op jit(solution)/shard_map/all_to_all | solution.py:248
  656.0 28.7 %copy-start.55 = (f32[128]{0:T(128)S(1)}, f32[128]{0:T(128)}, u32[]{:S(2)}) copy-start(f32[128]{0:T(128)} %copy-done.54) | copy-start | bytes 1540
  675.9 67.3 %all-to-all-start.7 = ((bf16[8,144,768]{2,1,0:T(8,128)(2,1)}), bf16[8,144,768]{2,1,0:T(8,128)(2,1)}, u32[]{:S(2)}, u32[]{:S(2)}) async-start(bf16[8,144,768]{2,1,0:T(8,128)(2,1)} %convolution_convert_fusion.3), calls=%async_computation.7 | async-start | bytes 3538944 | tf_op jit(solution)/shard_map/all_to_all | solution.py:255
  (58 other events, 509.7 us)
Sparse Core Ops, SparseCore 0:
  215.9 34.0 all-reduce.20
  346.0 17.7 reduce-scatter.8
  366.1 18.8 reduce-scatter.6
  639.6 33.1 all-reduce.22
  677.8 144.7 all-reduce.24
where the time goes:
time: 847 us; the launch traced here: 837 us
  other arithmetic  236 us (28%)
  local copies, waits for them, and re-layouts  176 us (21%)
  blocking collectives  164 us (19%)
  waiting for transfers between devices  164 us (19%)
  matrix products  58.1 us (7%)
  starting transfers between devices  23.3 us (3%)
  between operations  14.6 us (2%)
    psum x1, waiting for transfers between devices, body(): lax.psum((grad_norm_one, grad_in_proj, grad_conv_weight, grad_conv_bias,...  75.8 us
    reduce_sum x8, other arithmetic, block_fn(): diff = cum[:, None, :] - cum[None, :, :]  58.4 us
    psum x1, blocking collectives, body(): lax.psum((grad_norm_one, grad_in_proj, grad_conv_weight, grad_conv_bias,...  54.3 us
    reduce_sum x8, other arithmetic, block_fn(): from_block = jnp.sum(weights * drive_in[None, :, :], axis=1)  34.8 us
    dynamic_update_slice x32, local copies, waits for them, and re-layouts, scan_piece(): lax.scan(jax.checkpoint(block_fn), start_state, pieces)  29.3 us
    another operation x24, other arithmetic, block_fn(): cum = jnp.cumsum(log_decay, axis=0)  28.1 us
    psum x1, waiting for transfers between devices, body(): lax.psum(jnp.dot(gated_low, out_proj, preferred_element_type=jnp.float32)...  26.9 us
    all_to_all x1, blocking collectives, body(): lax.all_to_all(jnp.tile(expert_out, (tile_count, 1, 1)), 'dp', split_axis...  26.8 us
  transfers between devices with their start and end apart: 11, of which 6 were waited for; matrix products, arithmetic and copies ran while one was open for 33% of the time, Pallas kernels for 0%

commit v1 on v0

v1 whole, which is shorter than its diff:
```python
import functools
import math

import jax
import jax.numpy as jnp
from jax import lax
from jax.experimental import pallas as pl
from jax.experimental.pallas import tpu as pltpu
from jax.sharding import PartitionSpec as P

EPSILON = 1e-05
F32 = jnp.float32
BF16 = jnp.bfloat16
NEVER = 1e4
LOG2E = 1.4426950408889634
GELU_SCALE = math.sqrt(2.0 / math.pi)
GELU_CUBE = 0.044715
VMEM_BYTES = 56 * 1024 * 1024
WIDEST_GATHER = 8


def run_kernel(kernel, outs, args, scratch=(), scalars=0):
    return pl.pallas_call(
        kernel,
        out_shape=[jax.ShapeDtypeStruct(shape, dtype) for shape, dtype in outs],
        in_specs=[pl.BlockSpec(memory_space=pltpu.SMEM)] * scalars
        + [pl.BlockSpec(memory_space=pltpu.VMEM)] * (len(args) - scalars),
        out_specs=[pl.BlockSpec(memory_space=pltpu.VMEM)] * len(outs),
        scratch_shapes=[pltpu.VMEM(shape, dtype) for shape, dtype in scratch],
        compiler_params=pltpu.CompilerParams(vmem_limit_bytes=VMEM_BYTES),
    )(*args)


def dot_nn(left, right):
    return lax.dot_general(left, right, (((1,), (0,)), ((), ())), preferred_element_type=F32)


def dot_nt(left, right):
    return lax.dot_general(left, right, (((1,), (1,)), ((), ())), preferred_element_type=F32)


def dot_tn(left, right):
    return lax.dot_general(left, right, (((0,), (0,)), ((), ())), preferred_element_type=F32)


def lane_tiles(column, tiles):
    return jnp.concatenate([column] * tiles, axis=1)


def fold_tiles(values):
    total = values[:, :128]
    for tile in range(1, values.shape[1] // 128):
        total = total + values[:, 128 * tile : 128 * (tile + 1)]
    return total


def wide_masks(masks, index, chans):
    return lane_tiles(masks[index], -(-chans // 128))[:, :chans]


def rms_rate(values):
    return lax.rsqrt(jnp.mean(values * values, axis=-1, keepdims=True) + EPSILON)


def prepare_kernel(
    experts, capacity, block_rows, resets, route_col, route_row, cotangent, masks, choose, slots
):
    length = route_col.shape[0]
    square = (length, length)
    earlier = lax.broadcasted_iota(jnp.int32, square, 0)
    later = lax.broadcasted_iota(jnp.int32, square, 1)
    route_of = jnp.broadcast_to(route_row[...], square)
    same = (jnp.broadcast_to(route_col[...], square) == route_of) & (earlier < later)
    if block_rows < length:
        same = same & (earlier // block_rows == later // block_rows)
    rank = jnp.sum(same.astype(F32), axis=0, keepdims=True).astype(jnp.int32)
    place = route_row[...]
    if block_rows < length:
        place = place + experts * (later[:1] // block_rows)
    slot = place * capacity + rank
    slot_count = choose.shape[0]
    slot_ids = lax.broadcasted_iota(jnp.int32, (slot_count, length), 0)
    chosen = (slot_ids == jnp.broadcast_to(slot, (slot_count, length))).astype(F32).astype(BF16)
    choose[...] = chosen
    slots[...] = dot_nn(chosen, cotangent[...]).astype(BF16)
    keep = jnp.where(jnp.broadcast_to(resets[...], square) == 0, 1.0, 0.0)
    joined = jnp.where(earlier > 0, keep, 0.0)
    one_back = pltpu.roll(joined, 1, 0)
    two_back = pltpu.roll(joined, 2, 0)
    masks[0] = keep
    masks[1] = joined
    masks[2] = joined * one_back
    masks[3] = joined * one_back * two_back


def enter_kernel(
    place,
    piece_0,
    piece_1,
    piece_2,
    piece_3,
    gain,
    in_proj,
    conv_weight,
    conv_bias,
    x_proj,
    masks,
    rows_out,
    share_out,
    inner_out,
    conv_out,
    gate_out,
    mixed_out,
    held,
):
    pieces = (piece_0, piece_1, piece_2, piece_3)
    count = len(pieces)
    for step, piece in enumerate(pieces):
        held[lax.rem(place[0] - step + count, count)] = piece[...].astype(F32)
    rows = jnp.concatenate([held[index] for index in range(count)], axis=1)
    rows_out[...] = rows.astype(BF16)
    normed = (rows * rms_rate(rows) * gain[...]).astype(BF16)
    width = rows.shape[1]
    share_out[:, :width] = normed
    inner = dot_nn(normed, in_proj[0])
    gate_out[...] = dot_nn(normed, in_proj[1])
    chans = inner.shape[1]
    inner_out[...] = inner
    total = conv_bias[...] + conv_weight[3:4, :] * inner
    for shift in (1, 2, 3):
        moved = pltpu.roll(inner, shift, 0) * wide_masks(masks, shift, chans)
        total = total + conv_weight[3 - shift : 4 - shift, :] * moved
    conv_out[...] = total
    act = (total * jax.nn.sigmoid(total)).astype(BF16)
    share_out[:, width : width + chans] = act
    mixed_out[...] = dot_nn(act, x_proj[...]).astype(BF16)


def sum_pieces(place, pieces, held):
    count = len(pieces)
    for step, piece in enumerate(pieces):
        held[lax.rem(place[0] - step + count, count)] = piece[...]
    total = held[0].astype(F32)
    for index in range(1, count):
        total = total + held[index].astype(F32)
    return total


def put_row_chunks(place, source, outs):
    count = len(outs)
    rows = source.shape[0] // count
    for step, out in enumerate(outs):
        start = pl.multiple_of(lax.rem(place[0] + step, count) * rows, rows)
        out[...] = source[pl.ds(start, rows), :].astype(out.dtype)


def take_row_pieces(place, pieces, target):
    count = len(pieces)
    rows = target.shape[0] // count
    for step, piece in enumerate(pieces):
        start = pl.multiple_of(lax.rem(place[0] - step + count, count) * rows, rows)
        target[pl.ds(start, rows), :] = piece[...].astype(target.dtype)


def block_columns(transposed, block):
    length = transposed.shape[1]
    return pltpu.roll(transposed, lax.rem(length - 8 * block, length), 1)


def spread_column(columns, row, tiles):
    return lane_tiles(jnp.broadcast_to(columns[:, row : row + 1], (columns.shape[0], 128)), tiles)


def padded_copy(target, values):
    target[...] = jnp.zeros(target.shape, target.dtype)
    target[:, : values.shape[1]] = values


def softplus(values):
    return jnp.maximum(values, 0.0) + jnp.log1p(jnp.exp(-jnp.abs(values)))


def scan_forward_kernel(
    place,
    piece_0,
    piece_1,
    piece_2,
    piece_3,
    dt_proj,
    dt_bias,
    decay_log,
    skip_gain,
    share,
    gate_in,
    masks,
    out_proj,
    out_0,
    out_1,
    out_2,
    out_3,
    mixed_out,
    share_out,
    y_out,
    held,
    rate,
    step_rows,
    drive_rows,
    y_rows,
    partial,
):
    rank = dt_proj.shape[0]
    states = decay_log.shape[0]
    length, chans = y_out.shape
    tiles = step_rows.shape[1] // 128
    mixed = sum_pieces(place, (piece_0, piece_1, piece_2, piece_3), held)
    padded_copy(mixed_out, mixed)
    dt_low = mixed[:, :rank].astype(BF16)
    step_size = softplus(dot_nn(dt_low, dt_proj[...]) + dt_bias[...])
    act = share[:, share.shape[1] - chans :].astype(F32)
    reset = NEVER * (1.0 - wide_masks(masks, 0, chans))
    padded_copy(rate, -LOG2E * jnp.exp(decay_log[...]))
    padded_copy(step_rows, step_size + reset)
    padded_copy(drive_rows, step_size * act)
    turned = mixed_out[...].T
    b_turned = turned[rank : rank + states]
    c_turned = turned[rank + states : rank + 2 * states]

    def block(index, state):
        start = pl.multiple_of(index * 8, 8)
        b_cols = block_columns(b_turned, index)
        c_cols = block_columns(c_turned, index)
        steps = step_rows[pl.ds(start, 8), :]
        drives = drive_rows[pl.ds(start, 8), :]
        rows = []
        for row in range(8):
            decay = jnp.exp2(rate[...] * steps[row : row + 1])
            state = decay * state + spread_column(b_cols, row, tiles) * drives[row : row + 1]
            rows.append(
                jnp.sum(spread_column(c_cols, row, tiles) * state, axis=0, keepdims=True)
            )
        y_rows[pl.ds(start, 8), :] = jnp.concatenate(rows, axis=0)
        return state

    lax.fori_loop(0, length // 8, block, jnp.zeros((states, 128 * tiles), F32))
    y = y_rows[:, :chans] + skip_gain[...] * act
    y_out[...] = y
    gate = gate_in[...]
    gated = (y * (gate * jax.nn.sigmoid(gate))).astype(BF16)
    share_out[...] = jnp.zeros(share_out.shape, BF16)
    share_out[:, :chans] = gated
    share_out[:, 128 * tiles : 128 * tiles + rank] = dt_low
    partial[...] = dot_nn(gated, out_proj[...])
    put_row_chunks(place, partial, (out_0, out_1, out_2, out_3))


def dispatch_kernel(
    place,
    piece_0,
    piece_1,
    piece_2,
    piece_3,
    rows_in,
    gain,
    choose,
    residual_out,
    columns_out,
    slots,
    held,
):
    take_row_pieces(place, (piece_0, piece_1, piece_2, piece_3), residual_out)
    residual = rows_in[...].astype(F32) + residual_out[...]
    residual_out[...] = residual
    width = columns_out.shape[1]
    for index in range(held.shape[0]):
        held[index] = residual[:, index * width : (index + 1) * width]
    columns_out[...] = held[place[0]]
    send = (residual * rms_rate(residual) * gain[...]).astype(BF16)
    slots[...] = dot_nn(choose[...], send).astype(BF16)


def hidden_back_kernel(grad_slots, second_w, d_hidden):
    d_hidden[...] = dot_nn(grad_slots[...], second_w[...])


def expert_kernel(arrived, first_w, d_hidden, hidden_out, d_pre_out, d_slots):
    value = dot_nn(arrived[...], first_w[...])
    square = value * value
    bend = jnp.tanh(GELU_SCALE * (value + GELU_CUBE * value * square))
    half = 0.5 * (1.0 + bend)
    hidden_out[...] = (value * half).astype(BF16)
    slope = half + 0.5 * value * (1.0 - bend * bend) * GELU_SCALE * (
        1.0 + 3.0 * GELU_CUBE * square
    )
    d_pre = (slope * d_hidden[...]).astype(BF16)
    d_pre_out[...] = d_pre
    d_slots[...] = dot_nt(d_pre, first_w[...]).astype(BF16)


def expert_grads_kernel(arrived, grad_slots, hidden, d_pre, second_w, first_out, second_out, moe):
    first_out[...] = dot_tn(arrived[...], d_pre[...]).astype(BF16)
    second_out[...] = dot_tn(grad_slots[...], hidden[...]).astype(BF16)
    moe[...] = dot_nt(hidden[...], second_w[...]).astype(BF16)


def back_rows_kernel(place, choose, slots, out_0, out_1, out_2, out_3, partial):
    partial[...] = dot_tn(choose[...], slots[...])
    put_row_chunks(place, partial, (out_0, out_1, out_2, out_3))


def back_columns_kernel(place, choose, slots, out_0, out_1, out_2, out_3, held):
    rows = dot_tn(choose[...], slots[...])
    put_column_chunks(place, rows, (out_0, out_1, out_2, out_3), held)


def put_column_chunks(place, rows, outs, held):
    count = len(outs)
    width = rows.shape[1] // count
    for index in range(count):
        held[index] = rows[:, index * width : (index + 1) * width]
    for step, out in enumerate(outs):
        out[:, :width] = held[lax.rem(place[0] + step, count)].astype(out.dtype)


def mixer_grad_kernel(
    place,
    piece_0,
    piece_1,
    piece_2,
    piece_3,
    residual_in,
    gain,
    cotangent,
    out_proj,
    columns_out,
    mix_out,
    d_gated,
    gain_grad,
    d_send,
    held,
):
    take_row_pieces(place, (piece_0, piece_1, piece_2, piece_3), d_send)
    residual = residual_in[...]
    inverse = rms_rate(residual)
    scaled = residual * inverse
    grad = d_send[...]
    gain_grad[...] = jnp.sum(grad * scaled, axis=0, keepdims=True)
    pulled = grad * gain[...]
    along = jnp.mean(pulled * scaled, axis=-1, keepdims=True)
    d_residual = cotangent[...].astype(F32) + inverse * (pulled - scaled * along)
    width = columns_out.shape[1]
    for index in range(held.shape[0]):
        held[index] = d_residual[:, index * width : (index + 1) * width]
    columns_out[...] = held[place[0]]
    d_mix = d_residual.astype(BF16)
    mix_out[...] = d_mix
    d_gated[...] = dot_nt(d_mix, out_proj[...])


def scan_backward_kernel(
    d_gated,
    y_in,
    gate_in,
    share,
    mixed_in,
    masks,
    dt_proj,
    dt_bias,
    decay_log,
    skip_gain,
    d_mixed_out,
    d_act_out,
    share_out,
    small_out,
    rate,
    step_rows,
    decay_rows,
    drive_rows,
    dy_rows,
    du_rows,
    dl_rows,
    decays,
    history,
):
    rank = dt_proj.shape[0]
    states = decay_log.shape[0]
    length, chans = y_in.shape
    tiles = step_rows.shape[1] // 128
    full = 128 * tiles
    dt_low = mixed_in[:, :rank].astype(BF16)
    raw_step = dot_nn(dt_low, dt_proj[...]) + dt_bias[...]
    step_size = softplus(raw_step)
    act = share[:, share.shape[1] - chans :].astype(F32)
    reset = NEVER * (1.0 - wide_masks(masks, 0, chans))
    padded_copy(rate, -jnp.exp(decay_log[...]))
    padded_copy(step_rows, step_size)
    padded_copy(decay_rows, LOG2E * (step_size + reset))
    padded_copy(drive_rows, step_size * act)
    gate = gate_in[...]
    gate_sig = jax.nn.sigmoid(gate)
    d_out = d_gated[...]
    d_y = d_out * (gate * gate_sig)
    padded_copy(dy_rows, d_y)
    d_gate = d_out * y_in[...] * gate_sig * (1.0 + gate * (1.0 - gate_sig))
    turned = mixed_in[...].T
    b_turned = turned[rank : rank + states]
    c_turned = turned[rank + states : rank + 2 * states]
    history[pl.ds(0, states), :] = jnp.zeros((states, full), F32)

    def forward_block(index, state):
        start = pl.multiple_of(index * 8, 8)
        b_cols = block_columns(b_turned, index)
        steps = decay_rows[pl.ds(start, 8), :]
        drives = drive_rows[pl.ds(start, 8), :]
        for row in range(8):
            decay = jnp.exp2(rate[...] * steps[row : row + 1])
            state = decay * state + spread_column(b_cols, row, tiles) * drives[row : row + 1]
            at = pl.multiple_of((start + row) * states, states)
            decays[pl.ds(at, states), :] = decay
            history[pl.ds(at + states, states), :] = state
        return state

    lax.fori_loop(0, length // 8, forward_block, jnp.zeros((states, full), F32))
    lanes = lax.broadcasted_iota(jnp.int32, (states, length), 1)

    def backward_block(count, carry):
        carried, d_rate, d_b, d_c = carry
        index = length // 8 - 1 - count
        start = pl.multiple_of(index * 8, 8)
        b_cols = block_columns(b_turned, index)
        c_cols = block_columns(c_turned, index)
        steps = step_rows[pl.ds(start, 8), :]
        drives = drive_rows[pl.ds(start, 8), :]
        dys = dy_rows[pl.ds(start, 8), :]
        du = [None] * 8
        dl = [None] * 8
        for row in reversed(range(8)):
            at = pl.multiple_of((start + row) * states, states)
            before = history[pl.ds(at, states), :]
            after = history[pl.ds(at + states, states), :]
            decay = decays[pl.ds(at, states), :]
            here = lanes == start + row
            dy_row = jnp.broadcast_to(dys[row : row + 1], (states, full))
            grad = spread_column(c_cols, row, tiles) * dy_row + carried
            c_part = jnp.sum(fold_tiles(dy_row * after), axis=1, keepdims=True)
            d_c = jnp.where(here, c_part, d_c)
            b_part = jnp.sum(fold_tiles(grad * drives[row : row + 1]), axis=1, keepdims=True)
            d_b = jnp.where(here, b_part, d_b)
            du[row] = jnp.sum(grad * spread_column(b_cols, row, tiles), axis=0, keepdims=True)
            carried = grad * decay
            d_log = carried * before
            dl[row] = jnp.sum(d_log * rate[...], axis=0, keepdims=True)
            d_rate = d_rate + d_log * steps[row : row + 1]
        du_rows[pl.ds(start, 8), :] = jnp.concatenate(du, axis=0)
        dl_rows[pl.ds(start, 8), :] = jnp.concatenate(dl, axis=0)
        return carried, d_rate, d_b, d_c

    nothing = jnp.zeros((states, full), F32)
    thin = jnp.zeros((states, length), F32)
    _, d_rate, d_b, d_c = lax.fori_loop(
        0, length // 8, backward_block, (nothing, nothing, thin, thin)
    )
    du = du_rows[:, :chans]
    d_act_out[...] = du * step_size + skip_gain[...] * d_y
    d_step = (dl_rows[:, :chans] + du * act) * jax.nn.sigmoid(raw_step)
    d_step_low = d_step.astype(BF16)
    share_out[:length] = d_gate.astype(BF16)
    share_out[length:] = d_step_low
    small_out[...] = jnp.zeros(small_out.shape, F32)
    small_out[:states] = (d_rate * rate[...])[:, :chans]
    small_out[states : states + 1] = jnp.sum(d_step, axis=0, keepdims=True)
    small_out[states + 1 : states + 2] = jnp.sum(d_y * act, axis=0, keepdims=True)
    low_turned = dot_nt(dt_proj[...], d_step_low)
    used = rank + 2 * states
    d_turned = jnp.concatenate(
        [low_turned, d_b, d_c, jnp.zeros((128 - used, length), F32)], axis=0
    )
    d_mixed_out[...] = d_turned.T[:, :used].astype(BF16)


def leave_kernel(
    place,
    piece_0,
    piece_1,
    piece_2,
    piece_3,
    d_act_scan,
    d_gate,
    conv_in,
    inner_in,
    masks,
    x_proj,
    conv_weight,
    in_proj,
    rows_in,
    gain,
    small_in,
    gain_two,
    out_0,
    out_1,
    out_2,
    out_3,
    message,
    held,
    held_columns,
):
    length, chans = inner_in.shape
    width = gain.shape[1]
    d_mixed = sum_pieces(place, (piece_0, piece_1, piece_2, piece_3), held).astype(BF16)
    d_act = d_act_scan[...] + dot_nt(d_mixed, x_proj[...])
    conv = conv_in[...]
    sig = jax.nn.sigmoid(conv)
    d_conv = d_act * sig * (1.0 + conv * (1.0 - sig))
    inner = inner_in[...]
    d_inner = conv_weight[3:4, :] * d_conv
    weight_grads = [jnp.sum(d_conv * inner, axis=0, keepdims=True)]
    for shift in (1, 2, 3):
        masked = d_conv * wide_masks(masks, shift, chans)
        weight_grads.append(
            jnp.sum(masked * pltpu.roll(inner, shift, 0), axis=0, keepdims=True)
        )
        d_inner = d_inner + conv_weight[3 - shift : 4 - shift, :] * pltpu.roll(
            masked, length - shift, 0
        )
    d_inner_low = d_inner.astype(BF16)
    message[...] = jnp.zeros(message.shape, BF16)
    message[:length, :chans] = d_inner_low
    lane = -(-chans // 128) * 128
    message[:length, lane : lane + d_mixed.shape[1]] = d_mixed
    d_normed = dot_nt(d_inner_low, in_proj[0]) + dot_nt(d_gate[:length], in_proj[1])
    rows = rows_in[...].astype(F32)
    scaled = rows * rms_rate(rows)
    norm_grad = jnp.sum(d_normed * scaled, axis=0, keepdims=True)
    along = jnp.mean(d_normed * gain[...] * scaled, axis=-1, keepdims=True)
    outs = (out_0, out_1, out_2, out_3)
    put_column_chunks(place, d_normed, outs, held_columns)
    column = width // len(outs)
    high = along.astype(BF16)
    for out in outs:
        out[:, column : column + 1] = high
        out[:, column + 1 : column + 2] = (along - high.astype(F32)).astype(BF16)
    small = small_in[...]
    states = 16
    sent = jnp.concatenate(
        [
            small[: states + 2],
            weight_grads[3],
            weight_grads[2],
            weight_grads[1],
            weight_grads[0],
            jnp.sum(d_conv, axis=0, keepdims=True),
            norm_grad[:, :chans],
            norm_grad[:, chans:],
            gain_two[:, :chans],
            gain_two[:, chans:],
            jnp.zeros((5, chans), F32),
        ],
        axis=0,
    )
    upper = sent.astype(BF16)
    message[length : length + 32, :chans] = upper
    message[length + 32 : length + 64, :chans] = (sent - upper.astype(F32)).astype(BF16)


def finish_rows_kernel(
    piece_0, piece_1, piece_2, piece_3, d_columns, tokens, scale, gain, grad_tokens
):
    width = tokens.shape[1]
    total = piece_0[...].astype(F32)
    for piece in (piece_1, piece_2, piece_3):
        total = total + piece[...].astype(F32)
    along = total[:, width : width + 1] + total[:, width + 1 : width + 2]
    inverse = scale[:, :1]
    pulled = total[:, :width] * gain[...]
    scaled = tokens[...].astype(F32) * inverse
    grad_tokens[...] = d_columns[...] + inverse * (pulled - scaled * along)


def send_chunks(chunks):
    count = len(chunks)
    pairs = [[(i, (i + s) % count) for i in range(count)] for s in range(count)]
    return [chunks[0]] + [lax.ppermute(chunks[s], "tensor", pairs[s]) for s in range(1, count)]


def share_rows(values, count):
    return send_chunks([values] * count)


def add_low(pieces):
    total = pieces[0].astype(F32)
    for piece in pieces[1:]:
        total = total + piece.astype(F32)
    return total.astype(BF16)


def near_gather(values, groups):
    def swap(array, bits):
        return lax.ppermute(array, "dp", [(i, i ^ bits) for i in range(groups)])

    far = [values] + [swap(values, bits) for bits in range(2, groups, 2)]
    near = [swap(piece, 1) for piece in far]
    order = [None] * groups
    for index, (piece, other) in enumerate(zip(far, near)):
        order[2 * index] = piece
        order[2 * index + 1] = other
    return order


def body(
    tokens,
    resets,
    routes,
    norm_one,
    in_proj,
    conv_weight,
    conv_bias,
    x_proj,
    dt_proj,
    dt_bias,
    decay_log,
    skip_gain,
    out_proj,
    norm_two,
    expert_in,
    expert_out,
    cotangent,
):
    groups = lax.axis_size("dp")
    parts = lax.axis_size("tensor")
    place = lax.axis_index("tensor").astype(jnp.int32).reshape(1)
    length, column = tokens.shape
    width = norm_one.shape[0]
    rank, chans = dt_proj.shape
    states = decay_log.shape[0]
    experts, share, hidden_units = expert_in.shape
    proj = x_proj.shape[1]
    tile_count = groups // experts
    block_rows = length * experts // groups
    capacity = max(2, block_rows // 4)
    slot_count = groups * capacity
    full = -(-chans // 128) * 128
    tiles = full // 128
    gain_one = norm_one.reshape(1, width)
    gain_two = norm_two.reshape(1, width)
    bias_row = conv_bias.reshape(1, chans)
    dt_row = dt_bias.reshape(1, chans)
    skip_row = skip_gain.reshape(1, chans)

    def exchange(values):
        return lax.all_to_all(values, "dp", split_axis=0, concat_axis=0, tiled=True)

    first_w = exchange(jnp.tile(expert_in, (tile_count, 1, 1))).reshape(width, hidden_units)
    second_w = exchange(jnp.tile(expert_out, (tile_count, 1, 1))).reshape(width, hidden_units)

    token_pieces = share_rows(tokens, parts)
    masks, choose, grad_send = run_kernel(
        functools.partial(prepare_kernel, experts, capacity, block_rows),
        [
            ((4, length, 128), F32),
            ((slot_count, length), BF16),
            ((slot_count, width), BF16),
        ],
        [resets.reshape(length, 1), routes, routes.reshape(1, length), cotangent],
    )
    grad_slots = exchange(grad_send.reshape(groups, capacity, width)).reshape(slot_count, width)

    rows, share_one, inner, conv, gate, mixed_part = run_kernel(
        enter_kernel,
        [
            ((length, width), BF16),
            ((length, width + chans), BF16),
            ((length, chans), F32),
            ((length, chans), F32),
            ((length, chans), F32),
            ((length, proj), BF16),
        ],
        [place, *token_pieces, gain_one, in_proj, conv_weight, bias_row, x_proj, masks],
        [((parts, length, column), F32)],
        scalars=1,
    )
    mixed_pieces = share_rows(mixed_part, parts)
    *mix_chunks, mixed, share_two, y = run_kernel(
        scan_forward_kernel,
        [((length // parts, width), BF16)] * parts
        + [
            ((length, 128), F32),
            ((length, full + 128), BF16),
            ((length, chans), F32),
        ],
        [
            place,
            *mixed_pieces,
            dt_proj,
            dt_row,
            decay_log,
            skip_row,
            share_one,
            gate,
            masks,
            out_proj,
        ],
        [
            ((parts, length, proj), BF16),
            ((states, full), F32),
            ((length, full), F32),
            ((length, full), F32),
            ((length, full), F32),
            ((length, width), F32),
        ],
        scalars=1,
    )
    mixer_pieces = share_rows(add_low(send_chunks(mix_chunks)), parts)
    residual, residual_columns, send_slots = run_kernel(
        dispatch_kernel,
        [
            ((length, width), F32),
            ((length, column), F32),
            ((slot_count, width), BF16),
        ],
        [place, *mixer_pieces, rows, gain_two, choose],
        [((parts, length, column), F32)],
        scalars=1,
    )
    arrived = exchange(send_slots.reshape(groups, capacity, width)).reshape(slot_count, width)
    (d_hidden,) = run_kernel(
        hidden_back_kernel, [((slot_count, hidden_units), F32)], [grad_slots, second_w]
    )
    hidden, d_pre, d_slots = run_kernel(
        expert_kernel,
        [
            ((slot_count, hidden_units), BF16),
            ((slot_count, hidden_units), BF16),
            ((slot_count, width), BF16),
        ],
        [arrived, first_w, d_hidden],
    )
    back_slots = exchange(d_slots.reshape(groups, capacity, width)).reshape(slot_count, width)
    grad_first, grad_second, moe_slots = run_kernel(
        expert_grads_kernel,
        [
            ((width, hidden_units), BF16),
            ((width, hidden_units), BF16),
            ((slot_count, width), BF16),
        ],
        [arrived, grad_slots, hidden, d_pre, second_w],
    )
    back_chunks = run_kernel(
        back_rows_kernel,
        [((length // parts, width), BF16)] * parts,
        [place, choose, back_slots],
        [((length, width), F32)],
        scalars=1,
    )
    send_pieces = share_rows(add_low(send_chunks(back_chunks)), parts)
    d_columns, d_mix, d_gated, gain_grad_two = run_kernel(
        mixer_grad_kernel,
        [
            ((length, column), F32),
            ((length, width), BF16),
            ((length, chans), F32),
            ((1, width), F32),
        ],
        [place, *send_pieces, residual, gain_two, cotangent, out_proj],
        [((length, width), F32), ((parts, length, column), F32)],
        scalars=1,
    )
    d_mixed_part, d_act_scan, share_three, small = run_kernel(
        scan_backward_kernel,
        [
            ((length, proj), BF16),
            ((length, chans), F32),
            ((2 * length, chans), BF16),
            ((24, chans), F32),
        ],
        [
            d_gated,
            y,
            gate,
            share_one,
            mixed,
            masks,
            dt_proj,
            dt_row,
            decay_log,
            skip_row,
        ],
        [
            ((states, full), F32),
            ((length, full), F32),
            ((length, full), F32),
            ((length, full), F32),
            ((length, full), F32),
            ((length, full), F32),
            ((length, full), F32),
            ((length * states, full), F32),
            (((length + 1) * states, full), F32),
        ],
    )
    d_mixed_pieces = share_rows(d_mixed_part, parts)
    *normed_chunks, message = run_kernel(
        leave_kernel,
        [((length, column + 2), BF16)] * parts + [((length + 64, full + 128), BF16)],
        [
            place,
            *d_mixed_pieces,
            d_act_scan,
            share_three,
            conv,
            inner,
            masks,
            x_proj,
            conv_weight,
            in_proj,
            rows,
            gain_one,
            small,
            gain_grad_two,
        ],
        [((parts, length, proj), BF16), ((parts, length, column), F32)],
        scalars=1,
    )
    normed_pieces = send_chunks(normed_chunks)
    row_scale = rms_rate(rows.astype(F32))
    gain_columns = lax.dynamic_slice_in_dim(gain_one, place[0] * column, column, 1)
    (grad_tokens,) = run_kernel(
        finish_rows_kernel,
        [((length, column), F32)],
        [*normed_pieces, d_columns, tokens, jnp.broadcast_to(row_scale, (length, 128)), gain_columns],
    )

    returned = exchange(moe_slots.reshape(groups, capacity, width)).reshape(slot_count, width)
    moe_chunks = run_kernel(
        back_columns_kernel,
        [((length, column), BF16)] * parts,
        [place, choose, returned],
        [((parts, length, column), F32)],
        scalars=1,
    )
    moe_pieces = send_chunks(moe_chunks)
    outcome = residual_columns
    for piece in moe_pieces:
        outcome = outcome + piece.astype(F32)
    outcome = outcome.astype(BF16)

    def owner_sum(values):
        got = exchange(values.reshape(groups, share, hidden_units)).astype(F32)
        return jnp.sum(got.reshape(tile_count, experts, share, hidden_units), axis=0)

    grad_expert_in = owner_sum(grad_first)
    grad_expert_out = owner_sum(grad_second)

    if groups <= WIDEST_GATHER:
        def gather(values):
            return lax.all_gather(values, "dp", axis=0, tiled=True)

        all_one = gather(share_one)
        all_two = gather(share_two)
        all_mix = gather(d_mix)
        all_three = lax.all_gather(share_three, "dp", axis=0, tiled=False)
        all_gate = all_three[:, :length].reshape(groups * length, chans)
        all_step = all_three[:, length:].reshape(groups * length, chans)
        grad_out_proj = dot_tn(all_two[:, :chans], all_mix)
        grad_dt_proj = dot_tn(all_two[:, full : full + rank], all_step)
        all_message = lax.all_gather(message, "dp", axis=0, tiled=False)
        all_inner = all_message[:, :length, :chans].reshape(groups * length, chans)
        all_mixed = all_message[:, :length, full : full + proj].reshape(groups * length, proj)
        grad_in_proj = jnp.stack(
            [dot_tn(all_one[:, :width], all_inner), dot_tn(all_one[:, :width], all_gate)]
        )
        grad_x_proj = dot_tn(all_one[:, width:], all_mixed)
        sent = jnp.sum(all_message[:, length:, :chans].astype(F32), axis=0)
        vectors = sent[:32] + sent[32:]
    else:
        d_inner = message[:length, :chans]
        d_mixed = message[:length, full : full + proj]
        sent = message[length:, :chans].astype(F32)
        grad_in_proj, grad_x_proj, grad_dt_proj, grad_out_proj, vectors = lax.psum(
            (
                jnp.stack(
                    [
                        dot_tn(share_one[:, :width], d_inner),
                        dot_tn(share_one[:, :width], share_three[:length]),
                    ]
                ),
                dot_tn(share_one[:, width:], d_mixed),
                dot_tn(share_two[:, full : full + rank], share_three[length:]),
                dot_tn(share_two[:, :chans], d_mix),
                sent[:32] + sent[32:],
            ),
            "dp",
        )
    first_vector = states + 2
    norm_part = vectors[first_vector + 5 : first_vector + 7].reshape(width)
    grad_norm_one = sum(share_rows(norm_part.reshape(1, width), parts)).reshape(width)
    grad_norm_two = vectors[first_vector + 7 : first_vector + 9].reshape(width)
    return (
        outcome,
        grad_tokens,
        grad_norm_one,
        grad_in_proj,
        vectors[first_vector : first_vector + 4],
        vectors[first_vector + 4],
        grad_x_proj,
        grad_dt_proj,
        vectors[states],
        vectors[:states],
        vectors[states + 1],
        grad_out_proj,
        grad_norm_two,
        grad_expert_in,
        grad_expert_out,
    )


def solution(mesh):
    placed = (
        P("dp", "tensor"),
        P("dp"),
        P("dp", None),
        P(),
        P(None, None, "tensor"),
        P(None, "tensor"),
        P("tensor"),
        P("tensor", None),
        P(None, "tensor"),
        P("tensor"),
        P(None, "tensor"),
        P("tensor"),
        P("tensor", None),
        P(),
        P(None, "dp", "tensor"),
        P(None, "dp", "tensor"),
        P("dp", None),
    )
    return jax.shard_map(
        body,
        mesh=mesh,
        in_specs=placed,
        out_specs=(
            P("dp", "tensor"),
            P("dp", "tensor"),
            P(),
            P(None, None, "tensor"),
            P(None, "tensor"),
            P("tensor"),
            P("tensor", None),
            P(None, "tensor"),
            P("tensor"),
            P(None, "tensor"),
            P("tensor"),
            P("tensor", None),
            P(),
            P(None, "dp", "tensor"),
            P(None, "dp", "tensor"),
        ),
        check_vma=False,
    )
```

time: 847 us -> 394 us (0.47)
  other arithmetic: 236 us -> 13.8 us
  local copies, waits for them, and re-layouts: 176 us -> 32.2 us
  blocking collectives: 164 us -> 72.1 us
  Pallas kernels: 0 us -> 56.6 us
  matrix products: 58.1 us -> 16.7 us
  waiting for transfers between devices: 164 us -> 132 us
  starting transfers between devices: 23.3 us -> 54.9 us
    reduce_sum x55 -> x2, other arithmetic: 109 us -> 2.31 us  [the longest x1 1.21 us: body(): sent = jnp.sum(all_message[:, length:, :chans].astype(F32), axis=0)]
    psum x3 -> x0, waiting for transfers between devices: 103 us -> none  [the longest x1 75.8 us: body(): lax.psum((grad_norm_one, grad_in_proj, grad_conv_weight, grad_conv_bias,...]
    psum x3 -> x0, blocking collectives: 92.6 us -> none  [the longest x1 54.3 us: body(): lax.psum((grad_norm_one, grad_in_proj, grad_conv_weight, grad_conv_bias,...]
    all_gather x0 -> x5, waiting for transfers between devices: none -> 63.2 us  [the longest x3 36.2 us: gather(): return lax.all_gather(values, 'dp', axis=0, tiled=True)]
    pallas_call x0 -> x13, Pallas kernels: none -> 56.6 us  [run_kernel(): pl.pallas_call(kernel, out_shape=[jax.ShapeDtypeStruct(shape, dtype) for...]
    another operation x76 -> x1, other arithmetic: 47.6 us -> 3.06 us  [body(): jnp.stack([dot_tn(all_one[:, :width], all_inner), dot_tn(all_one[:, :widt...]
    dot_general x37 -> x5, matrix products: 58.1 us -> 16.7 us  [dot_tn(): lax.dot_general(left, right, (((0,), (0,)), ((), ())), preferred_element_...]
    ppermute x0 -> x30, starting transfers between devices: none -> 40.1 us  [send_chunks(): lax.ppermute(chunks[s], 'tensor', pairs[s])]
  transfers between devices with their start and end apart: 11 -> 39, of which waited for: 6 -> 19; matrix products, arithmetic and copies ran while one was open for 33% -> 14% of each run, Pallas kernels for 0% -> 6%
where the time goes in v1:
time: 394 us; the launch traced here: 392 us
  waiting for transfers between devices  132 us (34%)
  blocking collectives  72.1 us (18%)
  Pallas kernels  56.6 us (14%)
  starting transfers between devices  54.9 us (14%)
  local copies, waits for them, and re-layouts  32.2 us (8%)
  matrix products  16.7 us (4%)
  between operations  14.1 us (4%)
  other arithmetic  13.8 us (4%)
    all_to_all x4, blocking collectives, exchange(): return lax.all_to_all(values, 'dp', split_axis=0, concat_axis=0, tiled=True)  72.1 us
    pallas_call x13, Pallas kernels, run_kernel(): pl.pallas_call(kernel, out_shape=[jax.ShapeDtypeStruct(shape, dtype) for...  56.6 us
    ppermute x30, starting transfers between devices, send_chunks(): lax.ppermute(chunks[s], 'tensor', pairs[s])  40.1 us
    all_gather x3, waiting for transfers between devices, gather(): return lax.all_gather(values, 'dp', axis=0, tiled=True)  36.2 us
    ppermute x30, waiting for transfers between devices, send_chunks(): lax.ppermute(chunks[s], 'tensor', pairs[s])  34.2 us
    all_to_all x4, waiting for transfers between devices, exchange(): return lax.all_to_all(values, 'dp', split_axis=0, concat_axis=0, tiled=True)  32.6 us
    all_gather x1, waiting for transfers between devices, body(): all_message = lax.all_gather(message, 'dp', axis=0, tiled=False)  27 us
    dot_general x5, matrix products, dot_tn(): lax.dot_general(left, right, (((0,), (0,)), ((), ())), preferred_element_...  16.7 us
  transfers between devices with their start and end apart: 39, of which 19 were waited for; matrix products, arithmetic and copies ran while one was open for 14% of the time, Pallas kernels for 6%

profile of v1, /device:TPU:0, one launch (start us, length us, event | category | flops | bytes accessed | tf_op | source)
XLA Modules:
  0.0 392.1 jit_solution(14891593226604832084)
XLA Ops:
  8.2 5.1 %collective-permute-start.2 = (bf16[128,288]{1,0:T(8,128)(2,1)S(1)}, bf16[128,288]{1,0:T(8,128)(2,1)S(1)}, u32[]{:S(2)}, u32[]{:S(2)}) collective-permute-start(bf16[128,288]{1,0:T(8,128)(2,1)S(1)} %copy.37.piece_0.tokens), channel_id=1, source_target_pairs={{0,3},{1,0},{2,1},{3,2},{4,7},{5,4},{6,5},{7,6},{8,11},{9,8},{10,9... | collective-permute-start | bytes 221192 | tf_op jit(solution)/shard_map/ppermute | solution.py:581
  21.3 4.6 %copy.38.in_proj = bf16[2,1152,576]{2,1,0:T(8,128)(2,1)} copy(bf16[2,1152,576]{1,2,0:T(8,128)(2,1)} %param.21) | data formatting | bytes 5308416 | tf_op args[4]
  28.9 4.2 %shard_map.281 = (bf16[128,1152]{1,0:T(8,128)(2,1)}, bf16[128,1728]{1,0:T(8,128)(2,1)}, f32[128,576]{1,0:T(8,128)}, f32[128,576]{1,0:T(8,128)}, f32[128,576]{1,0:T(8,128)}, /*index=5*/bf16[128,104]{1,0:T(8,128)(2,1)}) custom-call(s32[1]{0:T(128)} %bitcast.place, bf16[128,288]{1,0:T(8,128)(2,1)} %copy-done.4, bf16[128,288]{1,0:T(8,128)(2,1)} %copy-done.9, ...), custom_call_target="tpu_custom_call" | custom-call | tf_op jit(solution)/shard_map/pallas_call | solution.py:23
  43.7 7.1 %shard_map.282 = (bf16[32,1152]{1,0:T(8,128)(2,1)}, bf16[32,1152]{1,0:T(8,128)(2,1)}, bf16[32,1152]{1,0:T(8,128)(2,1)}, bf16[32,1152]{1,0:T(8,128)(2,1)}, f32[12...) custom-call(s32[1]{0:T(128)} %bitcast.place, bf16[128,104]{1,0:T(8,128)(2,1)} %get-tuple-element.62.piece_0, ...), custom_call_target="tpu_custom_call" | custom-call | tf_op jit(solution)/shard_map/pallas_call | solution.py:23
  54.7 3.7 all-to-all-start.1
  64.4 5.1 %collective-permute-done.10.piece_2 = bf16[32,1152]{1,0:T(8,128)(2,1)S(1)} collective-permute-done((bf16[32,1152]{1,0:T(8,128)(2,1)S(1)}, bf16[32,1152]{1,0:T(8,128)(2,1)S(1)}, u32[]{:S(2)}, u32[]{:S(2)}) %collective-permute-start.10) | collective-permute-done | bytes 73760 | tf_op jit(solution)/shard_map/ppermute | solution.py:581
  72.6 14.6 %all_to_all.40 = bf16[8,32,1152]{2,1,0:T(8,128)(2,1)} all-to-all(bf16[8,32,1152]{2,1,0:T(8,128)(2,1)} %bitcast.48), channel_id=1, replica_groups=mesh['dp'=8,'tensor'=4] {'dp'}, dimensions={0} | all-to-all | bytes 1179648 | tf_op jit(solution)/shard_map/all_to_all | solution.py:649
  87.3 26.2 %all_to_all.41 = bf16[8,144,768]{2,1,0:T(8,128)(2,1)} all-to-all(bf16[8,144,768]{2,1,0:T(8,128)(2,1)S(1)} %copy-done.2), channel_id=1, replica_groups=mesh['dp'=8,'tensor'=4] {'dp'}, dimensions={0} | all-to-all | bytes 3538944 | tf_op jit(solution)/shard_map/all_to_all | solution.py:649
  120.4 19.8 %all-to-all-done.2 = bf16[8,144,768]{2,1,0:T(8,128)(2,1)S(1)} async-done(((bf16[8,144,768]{2,1,0:T(8,128)(2,1)}), bf16[8,144,768]{2,1,0:T(8,128)(2,1)S(1)}, u32[]{:S(2)}, u32[]{:S(2)}) %all-to-all-start.2) | async-done | bytes 1769504 | tf_op jit(solution)/shard_map/all_to_all | solution.py:649
  141.4 4.2 %shard_map.285 = (bf16[256,768]{1,0:T(8,128)(2,1)}, bf16[256,768]{1,0:T(8,128)(2,1)}, bf16[256,1152]{1,0:T(8,128)(2,1)}) custom-call(bf16[256,1152]{1,0:T(8,128)(2,1)} %bitcast.35, bf16[1152,768]{1,0:T(8,128)(2,1)} %bitcast.32, f32[256,768]{1,0:T(8,128)} %shard_map.284.d_hidden), custom_call_target="tpu_custom_call" | custom-call | tf_op jit(solution)/shard_map/pallas_call | solution.py:23
  145.6 14.6 %all_to_all.42 = bf16[8,32,1152]{2,1,0:T(8,128)(2,1)} all-to-all(bf16[8,32,1152]{2,1,0:T(8,128)(2,1)} %bitcast.50), channel_id=1, replica_groups=mesh['dp'=8,'tensor'=4] {'dp'}, dimensions={0} | all-to-all | bytes 1179648 | tf_op jit(solution)/shard_map/all_to_all | solution.py:649
  177.6 4.4 %collective-permute-done.19.piece_2 = bf16[32,1152]{1,0:T(8,128)(2,1)S(1)} collective-permute-done((bf16[32,1152]{1,0:T(8,128)(2,1)S(1)}, bf16[32,1152]{1,0:T(8,128)(2,1)S(1)}, u32[]{:S(2)}, u32[]{:S(2)}) %collective-permute-start.19) | collective-permute-done | bytes 73760 | tf_op jit(solution)/shard_map/ppermute | solution.py:581
  185.9 13.5 %shard_map.290 = (bf16[128,104]{1,0:T(8,128)(2,1)}, f32[128,576]{1,0:T(8,128)}, bf16[256,576]{1,0:T(8,128)(2,1)}, f32[24,576]{1,0:T(8,128)}) custom-call(f32[128,576]{1,0:T(8,128)} %get-tuple-element.87.d_gated, f32[128,576]{1,0:T(8,128)} %get-tuple-element.88.y_in, f32[128,576]{1,0:T(8,128)} %get-tuple-element.64.gate_in, ...), custom_call_target="tpu_custom_call" | custom-call | tf_op jit(solution)/shard_map/pallas_call | solution.py:23
  201.5 4.8 %shard_map.286 = (bf16[1152,768]{1,0:T(8,128)(2,1)}, bf16[1152,768]{1,0:T(8,128)(2,1)}, bf16[256,1152]{1,0:T(8,128)(2,1)}) custom-call(bf16[256,1152]{1,0:T(8,128)(2,1)} %bitcast.36, bf16[256,1152]{1,0:T(8,128)(2,1)} %bitcast.34, bf16[256,768]{1,0:T(8,128)(2,1)} %get-tuple-element.74.hidden, bf16[256,768]{1,0:T(8,128)(2,1)} %get-tuple-element.75.d_pre, ...), custom_call_target="tpu_custom_call" | custom-call | tf_op jit(solution)/shard_map/pallas_call | solution.py:23
  206.3 16.6 %all_to_all.43 = bf16[8,32,1152]{2,1,0:T(8,128)(2,1)} all-to-all(bf16[8,32,1152]{2,1,0:T(8,128)(2,1)} %bitcast.49), channel_id=1, replica_groups=mesh['dp'=8,'tensor'=4] {'dp'}, dimensions={0} | all-to-all | bytes 1179648 | tf_op jit(solution)/shard_map/all_to_all | solution.py:649
  222.9 3.6 all-to-all-start.7
  233.9 5.0 %shard_map.291 = (bf16[128,290]{1,0:T(8,128)(2,1)}, bf16[128,290]{1,0:T(8,128)(2,1)}, bf16[128,290]{1,0:T(8,128)(2,1)}, bf16[128,290]{1,0:T(8,128)(2,1)}, bf16[192,768]{1,0:T(8,128)(2,1)}) custom-call(s32[1]{0:T(128)} %bitcast.place, bf16[128,104]{1,0:T(8,128)(2,1)} %get-tuple-element.90.piece_0, bf16[128,104]{1,0:T(8,128)(2,1)} %copy-done.20, ...), custom_call_target="tpu_custom_call" | custom-call | tf_op jit(solution)/shard_map/pallas_call | solution.py:23
  238.8 12.9 %all-to-all-done.7 = bf16[8,144,768]{2,1,0:T(8,128)(2,1)S(1)} async-done(((bf16[8,144,768]{2,1,0:T(8,128)(2,1)}), bf16[8,144,768]{2,1,0:T(8,128)(2,1)S(1)}, u32[]{:S(2)}, u32[]{:S(2)}) %all-to-all-start.7) | async-done | bytes 1769504 | tf_op jit(solution)/shard_map/all_to_all | solution.py:649
  274.5 5.0 %collective-permute-done.25.piece_2 = bf16[128,290]{1,0:T(8,128)(2,1)} collective-permute-done((bf16[128,290]{1,0:T(8,128)(2,1)}, bf16[128,290]{1,0:T(8,128)(2,1)}, u32[]{:S(2)}, u32[]{:S(2)}) %collective-permute-start.25) | collective-permute-done | bytes 74272 | tf_op jit(solution)/shard_map/ppermute | solution.py:581
  293.4 4.8 %all-gather.12.cloned.1.call-done = bf16[1024,1152]{1,0:T(8,128)(2,1)} async-done(((bf16[128,1152]{1,0:T(8,128)(2,1)}), bf16[1024,1152]{1,0:T(8,128)(2,1)}) %all-gather.12.cloned.1.call-update) | async-done | bytes 2359312 | tf_op jit(solution)/shard_map/all_gather | solution.py:853
  298.2 4.9 %fusion.2 = f32[576,1152]{1,0:T(8,128)} fusion(bf16[1024,1152]{1,0:T(8,128)(2,1)} %all-gather.12.cloned.1.call-done, bf16[1024,768]{1,0:T(8,128)(2,1)S(1)} %copy-done.3), kind=kOutput, calls=%fused_computation.5 | convolution fusion | flops 1358954496 | bytes 6324224 | tf_op jit(solution)/shard_map/dot_general | solution.py:43
  303.1 31.4 %all-gather.8.cloned.1.call-done = bf16[1024,1728]{1,0:T(8,128)(2,1)} async-done(((bf16[128,1728]{1,0:T(8,128)(2,1)}), bf16[1024,1728]{1,0:T(8,128)(2,1)}) %all-gather.8.cloned.1.call-update) | async-done | bytes 3538960 | tf_op jit(solution)/shard_map/all_gather | solution.py:853
  334.5 3.8 convolution_bitcast_fusion
  338.2 27.0 %all-gather.14.cloned.1.call-done = bf16[1536,768]{1,0:T(8,128)(2,1)} async-done(((bf16[192,768]{1,0:T(8,128)(2,1)}), bf16[1536,768]{1,0:T(8,128)(2,1)}) %all-gather.14.cloned.1.call-update) | async-done | bytes 2359312 | tf_op jit(solution)/shard_map/all_gather | solution.py:863
  (168 shorter events, 131.2 us)
Async XLA Ops:
  8.2 20.0 %collective-permute-start.2 = (bf16[128,288]{1,0:T(8,128)(2,1)S(1)}, bf16[128,288]{1,0:T(8,128)(2,1)S(1)}, u32[]{:S(2)}, u32[]{:S(2)}) collective-permute-start(bf16[128,288]{1,0:T(8,128)(2,1)S(1)} %copy.37.piece_0.tokens), channel_id=1, source_target_pairs={{0,3},{1,0},{2,1},{3,2},{4,7},{5,4},{6,5},{7,6},{8,11},{9,8},{10,9... | collective-permute-start | bytes 221192 | tf_op jit(solution)/shard_map/ppermute | solution.py:581
  13.3 14.9 %collective-permute-start.1 = (bf16[128,288]{1,0:T(8,128)(2,1)S(1)}, bf16[128,288]{1,0:T(8,128)(2,1)S(1)}, u32[]{:S(2)}, u32[]{:S(2)}) collective-permute-start(bf16[128,288]{1,0:T(8,128)(2,1)S(1)} %copy.37.piece_0.tokens), channel_id=1, source_target_pairs={{0,2},{1,3},{2,0},{3,1},{4,6},{5,7},{6,4},{7,5},{8,10},{9,11},{10,... | collective-permute-start | bytes 221192 | tf_op jit(solution)/shard_map/ppermute | solution.py:581
  13.3 14.9 %collective-permute-start = (bf16[128,288]{1,0:T(8,128)(2,1)S(1)}, bf16[128,288]{1,0:T(8,128)(2,1)S(1)}, u32[]{:S(2)}, u32[]{:S(2)}) collective-permute-start(bf16[128,288]{1,0:T(8,128)(2,1)S(1)} %copy.37.piece_0.tokens), channel_id=1, source_target_pairs={{0,1},{1,2},{2,3},{3,0},{4,5},{5,6},{6,7},{7,4},{8,9},{9,10},{10,1... | collective-permute-start | bytes 221192 | tf_op jit(solution)/shard_map/ppermute | solution.py:581
  50.8 7.6 %collective-permute-start.6 = (bf16[32,1152]{1,0:T(8,128)(2,1)}, bf16[32,1152]{1,0:T(8,128)(2,1)S(1)}, u32[]{:S(2)}, u32[]{:S(2)}) collective-permute-start(bf16[32,1152]{1,0:T(8,128)(2,1)} %get-tuple-element.66), channel_id=1, source_target_pairs={{0,1},{1,2},{2,3},{3,0},{4,5},{5,6},{6,7},{7,4},{8,9},{9,10},{10,1... | collective-permute-start | bytes 221192 | tf_op jit(solution)/shard_map/ppermute | solution.py:581
  50.8 7.5 %collective-permute-start.7 = (bf16[32,1152]{1,0:T(8,128)(2,1)}, bf16[32,1152]{1,0:T(8,128)(2,1)S(1)}, u32[]{:S(2)}, u32[]{:S(2)}) collective-permute-start(bf16[32,1152]{1,0:T(8,128)(2,1)} %get-tuple-element.67), channel_id=1, source_target_pairs={{0,2},{1,3},{2,0},{3,1},{4,6},{5,7},{6,4},{7,5},{8,10},{9,11},{10,... | collective-permute-start | bytes 221192 | tf_op jit(solution)/shard_map/ppermute | solution.py:581
  54.7 18.0 %all-to-all-start.1 = ((bf16[8,32,1152]{2,1,0:T(8,128)(2,1)}), bf16[8,32,1152]{2,1,0:T(8,128)(2,1)S(1)}, u32[]{:S(2)}, u32[]{:S(2)}) async-start(bf16[8,32,1152]{2,1,0:T(8,128)(2,1)} %bitcast.5), calls=%async_computation.1 | async-start | bytes 1179648 | tf_op jit(solution)/shard_map/all_to_all | solution.py:649
  113.5 26.7 %all-to-all-start.2 = ((bf16[8,144,768]{2,1,0:T(8,128)(2,1)}), bf16[8,144,768]{2,1,0:T(8,128)(2,1)S(1)}, u32[]{:S(2)}, u32[]{:S(2)}) async-start(bf16[8,144,768]{2,1,0:T(8,128)(2,1)} %param.31), calls=%async_computation.2 | async-start | bytes 3538944 | tf_op jit(solution)/shard_map/all_to_all | solution.py:649
  117.1 171.1 %all-gather.16.cloned.1.call-start = ((), (), s32[]{:S(2)}) async-start(), calls=%async_computation.12 | async-start | bytes 2949120 | tf_op jit(solution)/shard_map/all_gather | solution.py:858
  162.3 9.0 %collective-permute-start.16 = (bf16[32,1152]{1,0:T(8,128)(2,1)}, bf16[32,1152]{1,0:T(8,128)(2,1)S(1)}, u32[]{:S(2)}, u32[]{:S(2)}) collective-permute-start(bf16[32,1152]{1,0:T(8,128)(2,1)} %get-tuple-element.84), channel_id=1, source_target_pairs={{0,2},{1,3},{2,0},{3,1},{4,6},{5,7},{6,4},{7,5},{8,10},{9,11},{10,... | collective-permute-start | bytes 221192 | tf_op jit(solution)/shard_map/ppermute | solution.py:581
  199.5 91.8 %all-gather.10.cloned.1.call-start = ((), (), s32[]{:S(2)}) async-start(), calls=%async_computation.9 | async-start | bytes 1769472 | tf_op jit(solution)/shard_map/all_gather | solution.py:853
  200.2 98.0 %all-gather.12.cloned.1.call-start = ((), (), s32[]{:S(2)}) async-start(), calls=%async_computation.10 | async-start | bytes 2654208 | tf_op jit(solution)/shard_map/all_gather | solution.py:853
  200.9 133.5 %all-gather.8.cloned.1.call-start = ((), (), s32[]{:S(2)}) async-start(), calls=%async_computation.8 | async-start | bytes 4128768 | tf_op jit(solution)/shard_map/all_gather | solution.py:853
  222.9 28.8 %all-to-all-start.7 = ((bf16[8,144,768]{2,1,0:T(8,128)(2,1)}), bf16[8,144,768]{2,1,0:T(8,128)(2,1)S(1)}, u32[]{:S(2)}, u32[]{:S(2)}) async-start(bf16[8,144,768]{2,1,0:T(8,128)(2,1)} %bitcast.45), calls=%async_computation.7 | async-start | bytes 3538944 | tf_op jit(solution)/shard_map/all_to_all | solution.py:649
  226.5 138.7 %all-gather.14.cloned.1.call-start = ((), (), s32[]{:S(2)}) async-start(), calls=%async_computation.11 | async-start | bytes 2654208 | tf_op jit(solution)/shard_map/all_gather | solution.py:863
  251.7 34.4 %all-to-all-start.6 = ((bf16[8,144,768]{2,1,0:T(8,128)(2,1)}), bf16[8,144,768]{2,1,0:T(8,128)(2,1)S(1)}, u32[]{:S(2)}, u32[]{:S(2)}) async-start(bf16[8,144,768]{2,1,0:T(8,128)(2,1)} %bitcast.44), calls=%async_computation.6 | async-start | bytes 3538944 | tf_op jit(solution)/shard_map/all_to_all | solution.py:649
  260.1 7.7 %collective-permute-start.12 = (bf16[128,288]{1,0:T(8,128)(2,1)}, bf16[128,288]{1,0:T(8,128)(2,1)S(1)}, u32[]{:S(2)}, u32[]{:S(2)}) collective-permute-start(bf16[128,288]{1,0:T(8,128)(2,1)} %get-tuple-element.78), channel_id=1, source_target_pairs={{0,1},{1,2},{2,3},{3,0},{4,5},{5,6},{6,7},{7,4},{8,9},{9,10},{10,1... | collective-permute-start | bytes 221192 | tf_op jit(solution)/shard_map/ppermute | solution.py:581
  260.1 11.1 %collective-permute-start.13 = (bf16[128,288]{1,0:T(8,128)(2,1)}, bf16[128,288]{1,0:T(8,128)(2,1)S(1)}, u32[]{:S(2)}, u32[]{:S(2)}) collective-permute-start(bf16[128,288]{1,0:T(8,128)(2,1)} %get-tuple-element.79), channel_id=1, source_target_pairs={{0,2},{1,3},{2,0},{3,1},{4,6},{5,7},{6,4},{7,5},{8,10},{9,11},{10,... | collective-permute-start | bytes 221192 | tf_op jit(solution)/shard_map/ppermute | solution.py:581
  261.0 10.2 %collective-permute-start.14 = (bf16[128,288]{1,0:T(8,128)(2,1)}, bf16[128,288]{1,0:T(8,128)(2,1)S(1)}, u32[]{:S(2)}, u32[]{:S(2)}) collective-permute-start(bf16[128,288]{1,0:T(8,128)(2,1)} %get-tuple-element.80), channel_id=1, source_target_pairs={{0,3},{1,0},{2,1},{3,2},{4,7},{5,4},{6,5},{7,6},{8,11},{9,8},{10,9... | collective-permute-start | bytes 221192 | tf_op jit(solution)/shard_map/ppermute | solution.py:581
  264.0 10.6 %collective-permute-start.24 = (bf16[128,290]{1,0:T(8,128)(2,1)}, bf16[128,290]{1,0:T(8,128)(2,1)}, u32[]{:S(2)}, u32[]{:S(2)}) collective-permute-start(bf16[128,290]{1,0:T(8,128)(2,1)} %get-tuple-element.98), channel_id=1, source_target_pairs={{0,1},{1,2},{2,3},{3,0},{4,5},{5,6},{6,7},{7,4},{8,9},{9,10},{10,1... | collective-permute-start | bytes 222728 | tf_op jit(solution)/shard_map/ppermute | solution.py:581
  264.5 15.1 %collective-permute-start.25 = (bf16[128,290]{1,0:T(8,128)(2,1)}, bf16[128,290]{1,0:T(8,128)(2,1)}, u32[]{:S(2)}, u32[]{:S(2)}) collective-permute-start(bf16[128,290]{1,0:T(8,128)(2,1)} %get-tuple-element.99), channel_id=1, source_target_pairs={{0,2},{1,3},{2,0},{3,1},{4,6},{5,7},{6,4},{7,5},{8,10},{9,11},{10,... | collective-permute-start | bytes 222728 | tf_op jit(solution)/shard_map/ppermute | solution.py:581
  267.8 11.7 %collective-permute-start.26 = (bf16[128,290]{1,0:T(8,128)(2,1)}, bf16[128,290]{1,0:T(8,128)(2,1)}, u32[]{:S(2)}, u32[]{:S(2)}) collective-permute-start(bf16[128,290]{1,0:T(8,128)(2,1)} %get-tuple-element.100), channel_id=1, source_target_pairs={{0,3},{1,0},{2,1},{3,2},{4,7},{5,4},{6,5},{7,6},{8,11},{9,8},{10,9... | collective-permute-start | bytes 222728 | tf_op jit(solution)/shard_map/ppermute | solution.py:581
  366.6 18.4 %collective-permute-start.29 = (f32[1,1152]{1,0:T(1,128)S(1)}, f32[1,1152]{1,0:T(1,128)S(1)}, u32[]{:S(2)}, u32[]{:S(2)}) collective-permute-start(f32[1,1152]{1,0:T(1,128)S(1)} %reshape_reshape.3), channel_id=1, source_target_pairs={{0,3},{1,0},{2,1},{3,2},{4,7},{5,4},{6,5},{7,6},{8,11},{9,8},{10,9... | collective-permute-start | bytes 13832 | tf_op jit(solution)/shard_map/ppermute | solution.py:581
  369.9 15.0 %collective-permute-start.28 = (f32[1,1152]{1,0:T(1,128)S(1)}, f32[1,1152]{1,0:T(1,128)S(1)}, u32[]{:S(2)}, u32[]{:S(2)}) collective-permute-start(f32[1,1152]{1,0:T(1,128)S(1)} %reshape_reshape.3), channel_id=1, source_target_pairs={{0,2},{1,3},{2,0},{3,1},{4,6},{5,7},{6,4},{7,5},{8,10},{9,11},{10,... | collective-permute-start | bytes 13832 | tf_op jit(solution)/shard_map/ppermute | solution.py:581
  369.9 15.0 %collective-permute-start.27 = (f32[1,1152]{1,0:T(1,128)S(1)}, f32[1,1152]{1,0:T(1,128)S(1)}, u32[]{:S(2)}, u32[]{:S(2)}) collective-permute-start(f32[1,1152]{1,0:T(1,128)S(1)} %reshape_reshape.3), channel_id=1, source_target_pairs={{0,1},{1,2},{2,3},{3,0},{4,5},{5,6},{6,7},{7,4},{8,9},{9,10},{10,1... | collective-permute-start | bytes 13832 | tf_op jit(solution)/shard_map/ppermute | solution.py:581
  (41 other events, 314.4 us)
Sparse Core Ops, SparseCore 0:
  199.6 29.1 all-gather.15
  230.6 28.6 all-gather.9
  261.2 36.9 all-gather.11
  299.9 34.5 all-gather.7
  336.2 29.0 all-gather.13

commit v2 on v1

v2 whole, which is shorter than its diff:
```python
import functools
import math

import jax
import jax.numpy as jnp
from jax import lax
from jax.experimental import pallas as pl
from jax.experimental.pallas import tpu as pltpu
from jax.sharding import PartitionSpec as P

EPSILON = 1e-05
F32 = jnp.float32
BF16 = jnp.bfloat16
NEVER = 1e4
LOG2E = 1.4426950408889634
GELU_SCALE = math.sqrt(2.0 / math.pi)
GELU_CUBE = 0.044715
VMEM_BYTES = 56 * 1024 * 1024
NEAR_GROUPS = 8
VECTORS_ONE = 24
VECTORS_TWO = 8


def run_kernel(kernel, outs, args, scratch=(), scalars=0, far_args=(), far_outs=(), alias=None):
    def spec(index, far):
        return pl.BlockSpec(memory_space=pl.ANY if index in far else pltpu.VMEM)

    return pl.pallas_call(
        kernel,
        out_shape=[jax.ShapeDtypeStruct(shape, dtype) for shape, dtype in outs],
        in_specs=[
            pl.BlockSpec(memory_space=pltpu.SMEM) if index < scalars else spec(index, far_args)
            for index in range(len(args))
        ],
        out_specs=[spec(index, far_outs) for index in range(len(outs))],
        scratch_shapes=[
            shape if not isinstance(shape, tuple) else pltpu.VMEM(*shape) for shape in scratch
        ],
        input_output_aliases=alias or {},
        compiler_params=pltpu.CompilerParams(vmem_limit_bytes=VMEM_BYTES),
    )(*args)


def dot_nn(left, right):
    return lax.dot_general(left, right, (((1,), (0,)), ((), ())), preferred_element_type=F32)


def dot_nt(left, right):
    return lax.dot_general(left, right, (((1,), (1,)), ((), ())), preferred_element_type=F32)


def dot_tn(left, right):
    return lax.dot_general(left, right, (((0,), (0,)), ((), ())), preferred_element_type=F32)


def lane_tiles(column, tiles):
    return jnp.concatenate([column] * tiles, axis=1)


def fold_tiles(values):
    total = values[:, :128]
    for tile in range(1, values.shape[1] // 128):
        total = total + values[:, 128 * tile : 128 * (tile + 1)]
    return total


def wide_masks(masks, index, chans):
    return lane_tiles(masks[index], -(-chans // 128))[:, :chans]


def rms_rate(values):
    return lax.rsqrt(jnp.mean(values * values, axis=-1, keepdims=True) + EPSILON)


def as_row(ref):
    return ref[...].reshape(1, ref.shape[0])


def softplus(values):
    return jnp.maximum(values, 0.0) + jnp.log1p(jnp.exp(-jnp.abs(values)))


def padded_copy(target, values):
    target[...] = jnp.zeros(target.shape, target.dtype)
    target[:, : values.shape[1]] = values


def put_row_chunks(place, source, outs):
    count = len(outs)
    rows = source.shape[0] // count
    for step, out in enumerate(outs):
        start = pl.multiple_of(lax.rem(place[0] + step, count) * rows, rows)
        out[pl.ds(0, rows), :] = source[pl.ds(start, rows), :].astype(out.dtype)


def take_row_pieces(place, pieces, target):
    count = len(pieces)
    rows = target.shape[0] // count
    for step, piece in enumerate(pieces):
        start = pl.multiple_of(lax.rem(place[0] - step + count, count) * rows, rows)
        target[pl.ds(start, rows), :] = piece[...].astype(target.dtype)


def sum_pieces(place, pieces, held):
    count = len(pieces)
    for step, piece in enumerate(pieces):
        held[lax.rem(place[0] - step + count, count)] = piece[...]
    total = held[0].astype(F32)
    for index in range(1, count):
        total = total + held[index].astype(F32)
    return total


def run_copies(copies, semaphores):
    started = []
    for index, (source, target) in enumerate(copies):
        copy = pltpu.make_async_copy(source, target, semaphores.at[index])
        copy.start()
        started.append(copy)
    return started


def fill_masks(resets, masks):
    length = resets.shape[1]
    square = (length, length)
    earlier = lax.broadcasted_iota(jnp.int32, square, 0)
    reset = jnp.broadcast_to(resets[...].astype(F32), square).T
    keep = jnp.where(reset == 0.0, 1.0, 0.0)
    joined = jnp.where(earlier > 0, keep, 0.0)
    one_back = pltpu.roll(joined, 1, 0)
    two_back = pltpu.roll(joined, 2, 0)
    masks[0] = keep
    masks[1] = joined
    masks[2] = joined * one_back
    masks[3] = joined * one_back * two_back


def fill_choose(capacity, block_rows, experts, routes, choose):
    length = routes.shape[1]
    square = (length, length)
    earlier = lax.broadcasted_iota(jnp.int32, square, 0)
    later = lax.broadcasted_iota(jnp.int32, square, 1)
    route_of = jnp.broadcast_to(routes[...].astype(F32), square)
    same = (route_of.T == route_of) & (earlier < later)
    if block_rows < length:
        same = same & (earlier // block_rows == later // block_rows)
    rank = jnp.sum(jnp.where(same, 1.0, 0.0), axis=0, keepdims=True).astype(jnp.int32)
    group = routes[...]
    if block_rows < length:
        group = group + experts * (later[:1] // block_rows)
    slot = group * capacity + rank
    slot_count = choose.shape[0]
    slot_ids = lax.broadcasted_iota(jnp.int32, (slot_count, length), 0)
    hit = slot_ids == jnp.broadcast_to(slot, (slot_count, length))
    choose[...] = jnp.where(hit, 1.0, 0.0).astype(BF16)


def prepare_kernel(
    experts, capacity, block_rows, resets, routes, cotangent, masks, choose, slots
):
    fill_masks(resets, masks)
    fill_choose(capacity, block_rows, experts, routes, choose)
    slots[...] = dot_nn(choose[...], cotangent[...]).astype(BF16)


def put_folded(target, slots):
    rows, width = slots.shape
    units = target.shape[1]
    half = rows // 2
    rest = width - units
    target[:rows, :] = slots[:, :units]
    target[rows:, :rest] = slots[:half, units:]
    target[rows:, rest:] = slots[half:, units:]


def unfold_copies(source, target, top, rows):
    units = source.shape[1]
    half = rows // 2
    rest = target.shape[1] - units
    copies = [(source.at[pl.ds(0, rows)], target.at[pl.ds(top, rows), pl.ds(0, units)])]
    for part in range(2):
        copies.append(
            (
                source.at[pl.ds(rows, half), pl.ds(part * rest, rest)],
                target.at[pl.ds(top + part * half, half), pl.ds(units, rest)],
            )
        )
    return copies


def pack_kernel(
    capacity,
    resets,
    routes,
    cotangent,
    expert_in,
    expert_out,
    masks,
    choose,
    message,
    packed,
    semaphores,
):
    experts, share, units = expert_in.shape
    length, width = cotangent.shape
    copies = []
    for index in range(experts):
        target = message.at[index]
        copies.append((expert_in.at[index], target.at[pl.ds(0, share)]))
        copies.append((expert_out.at[index], target.at[pl.ds(share, share)]))
    started = run_copies(copies, semaphores)
    fill_choose(capacity, length, experts, routes, choose)
    slots = dot_nn(choose[...], cotangent[...]).astype(BF16)
    copies = []
    for index in range(experts):
        put_folded(packed.at[index], slots[index * capacity : (index + 1) * capacity])
        target = message.at[index]
        copies.append((packed.at[index], target.at[pl.ds(2 * share, packed.shape[1])]))
    started += run_copies(copies, semaphores.at[pl.ds(2 * experts, experts)])
    fill_masks(resets, masks)
    for copy in started:
        copy.wait()


def unpack_kernel(share, capacity, message, first_w, second_w, grad_slots, d_hidden, semaphores):
    folded = capacity + capacity // 2
    copies = []
    for index in range(message.shape[0]):
        piece = message.at[index]
        rows = pl.ds(index * share, share)
        copies.append((piece.at[pl.ds(share, share)], second_w.at[rows]))
        copies += unfold_copies(
            piece.at[pl.ds(2 * share, folded)], grad_slots, index * capacity, capacity
        )
        copies.append((piece.at[pl.ds(0, share)], first_w.at[rows]))
    for copy in run_copies(copies, semaphores):
        copy.wait()
    d_hidden[...] = dot_nn(grad_slots[...], second_w[...])


def put_blocks(target, values):
    length = values.shape[0]
    for start in range(0, values.shape[1], 128):
        target[start : start + length, :] = values[:, start : start + 128]


def enter_kernel(
    place,
    piece_0,
    piece_1,
    piece_2,
    piece_3,
    gain_ref,
    in_proj,
    conv_weight,
    conv_bias,
    x_proj,
    masks,
    rows_out,
    normed_out,
    act_out,
    inner_out,
    conv_out,
    gate_out,
    scale_out,
    gain_out,
    mixed_out,
    turned,
):
    take_row_pieces(place, (piece_0, piece_1, piece_2, piece_3), turned)
    rows = turned[...].T
    gain = as_row(gain_ref)
    rows_out[...] = rows.astype(BF16)
    normed = (rows * rms_rate(rows) * gain).astype(BF16)
    put_blocks(normed_out, normed)
    inner = dot_nt(normed, in_proj[0])
    chans = inner.shape[1]
    inner_out[...] = inner
    total = as_row(conv_bias) + conv_weight[3:4, :] * inner
    for shift in (1, 2, 3):
        moved = pltpu.roll(inner, shift, 0) * wide_masks(masks, shift, chans)
        total = total + conv_weight[3 - shift : 4 - shift, :] * moved
    conv_out[...] = total
    act = (total * jax.nn.sigmoid(total)).astype(BF16)
    act_out[...] = act
    mixed_out[...] = dot_nt(x_proj[...], act).astype(BF16)
    gate_out[...] = dot_nt(normed, in_proj[1])
    raw = turned[...]
    scale_out[...] = lax.rsqrt(jnp.mean(raw * raw, axis=0, keepdims=True) + EPSILON)
    turned[...] = jnp.broadcast_to(gain, rows.shape).T
    column = gain_out.shape[0]
    gain_out[...] = turned[pl.ds(pl.multiple_of(place[0] * column, column), column), :]


def block_columns(transposed, block):
    length = transposed.shape[1]
    return pltpu.roll(transposed, lax.rem(length - 8 * block, length), 1)


def spread_column(columns, row, tiles):
    return lane_tiles(jnp.broadcast_to(columns[:, row : row + 1], (columns.shape[0], 128)), tiles)


def scan_forward_kernel(
    place,
    piece_0,
    piece_1,
    piece_2,
    piece_3,
    dt_proj,
    dt_bias,
    decay_log,
    skip_gain,
    act_in,
    gate_in,
    masks,
    out_proj,
    normed,
    out_0,
    out_1,
    out_2,
    out_3,
    mixed_out,
    share_out,
    y_out,
    held,
    rate,
    step_rows,
    drive_rows,
    y_rows,
    partial,
):
    rank = dt_proj.shape[0]
    states = decay_log.shape[0]
    length, chans = y_out.shape
    tiles = step_rows.shape[1] // 128
    mixed = sum_pieces(place, (piece_0, piece_1, piece_2, piece_3), held)
    mixed_out[...] = mixed
    step_size = softplus(dot_tn(mixed[:rank].astype(BF16), dt_proj[...]) + as_row(dt_bias))
    act = act_in[...].astype(F32)
    reset = NEVER * (1.0 - wide_masks(masks, 0, chans))
    padded_copy(rate, -LOG2E * jnp.exp(decay_log[...]))
    padded_copy(step_rows, step_size + reset)
    padded_copy(drive_rows, step_size * act)
    b_turned = mixed[rank : rank + states]
    c_turned = mixed[rank + states : rank + 2 * states]

    def block(index, state):
        start = pl.multiple_of(index * 8, 8)
        b_cols = block_columns(b_turned, index)
        c_cols = block_columns(c_turned, index)
        steps = step_rows[pl.ds(start, 8), :]
        drives = drive_rows[pl.ds(start, 8), :]
        rows = []
        for row in range(8):
            decay = jnp.exp2(rate[...] * steps[row : row + 1])
            state = decay * state + spread_column(b_cols, row, tiles) * drives[row : row + 1]
            rows.append(
                jnp.sum(spread_column(c_cols, row, tiles) * state, axis=0, keepdims=True)
            )
        y_rows[pl.ds(start, 8), :] = jnp.concatenate(rows, axis=0)
        return state

    lax.fori_loop(0, length // 8, block, jnp.zeros((states, 128 * tiles), F32))
    y = y_rows[:, :chans] + as_row(skip_gain) * act
    y_out[...] = y
    gate = gate_in[...]
    gated = (y * (gate * jax.nn.sigmoid(gate))).astype(BF16)
    partial[...] = dot_nn(gated, out_proj[...])
    put_row_chunks(place, partial, (out_0, out_1, out_2, out_3))
    width = normed.shape[0]
    share_out[:width] = normed[...]
    padded_copy(step_rows, gated.astype(F32))
    share_out[width : width + chans] = step_rows[...].T[:chans].astype(BF16)
    padded_copy(step_rows, act)
    share_out[width + chans :] = step_rows[...].T[:chans].astype(BF16)


def dispatch_kernel(
    place,
    piece_0,
    piece_1,
    piece_2,
    piece_3,
    rows_in,
    gain,
    choose,
    residual_out,
    columns_out,
    slots,
    turned,
):
    take_row_pieces(place, (piece_0, piece_1, piece_2, piece_3), residual_out)
    residual = rows_in[...].astype(F32) + residual_out[...]
    residual_out[...] = residual
    send = (residual * rms_rate(residual) * as_row(gain)).astype(BF16)
    slots[...] = dot_nn(choose[...], send).astype(BF16)
    turned[...] = residual.T
    column = columns_out.shape[0]
    columns_out[...] = turned[pl.ds(pl.multiple_of(place[0] * column, column), column), :]


def hidden_back_kernel(grad_slots, second_w, d_hidden):
    d_hidden[...] = dot_nn(grad_slots[...], second_w[...])


def expert_kernel(arrived, first_w, d_hidden, hidden_out, d_pre_out, d_slots):
    value = dot_nn(arrived[...], first_w[...])
    square = value * value
    bend = jnp.tanh(GELU_SCALE * (value + GELU_CUBE * value * square))
    half = 0.5 * (1.0 + bend)
    slope = half + 0.5 * value * (1.0 - bend * bend) * GELU_SCALE * (
        1.0 + 3.0 * GELU_CUBE * square
    )
    d_pre = (slope * d_hidden[...]).astype(BF16)
    d_pre_out[...] = d_pre
    d_slots[...] = dot_nt(d_pre, first_w[...]).astype(BF16)
    hidden_out[...] = (value * half).astype(BF16)


def expert_grads_kernel(arrived, grad_slots, hidden, d_pre, second_w, first_out, second_out, moe):
    first_out[...] = dot_tn(arrived[...], d_pre[...]).astype(BF16)
    second_out[...] = dot_tn(grad_slots[...], hidden[...]).astype(BF16)
    moe[...] = dot_nt(hidden[...], second_w[...]).astype(BF16)


def expert_grads_pack_kernel(
    share, capacity, arrived, grad_slots, hidden, d_pre, second_w, message, grads, packed, semaphores
):
    experts = message.shape[0]
    started = []
    for which, (left, right) in enumerate(((arrived, d_pre), (grad_slots, hidden))):
        grads[which] = dot_tn(left[...], right[...]).astype(BF16)
        copies = [
            (
                grads.at[which, pl.ds(index * share, share)],
                message.at[index, pl.ds(which * share, share)],
            )
            for index in range(experts)
        ]
        started += run_copies(copies, semaphores.at[pl.ds(which * experts, experts)])
    moe = dot_nt(hidden[...], second_w[...]).astype(BF16)
    copies = []
    for index in range(experts):
        put_folded(packed.at[index], moe[index * capacity : (index + 1) * capacity])
        copies.append(
            (packed.at[index], message.at[index, pl.ds(2 * share, packed.shape[1])])
        )
    started += run_copies(copies, semaphores.at[pl.ds(2 * experts, experts)])
    for copy in started:
        copy.wait()


def owner_kernel(share, message, first_out, second_out, low, wide, arrivals, semaphores):
    count = message.shape[0]
    arriving = run_copies(
        [(message.at[index, pl.ds(0, 2 * share)], low.at[index]) for index in range(count)],
        arrivals,
    )
    started = []
    for index in range(count):
        arriving[index].wait()
        wide[index] = low[index].astype(F32)
        copies = [
            (wide.at[index, pl.ds(0, share)], first_out.at[index]),
            (wide.at[index, pl.ds(share, share)], second_out.at[index]),
        ]
        started += run_copies(copies, semaphores.at[pl.ds(2 * index, 2)])
    for copy in started:
        copy.wait()


def back_rows_kernel(place, choose, slots, out_0, out_1, out_2, out_3, partial):
    partial[...] = dot_tn(choose[...], slots[...])
    put_row_chunks(place, partial, (out_0, out_1, out_2, out_3))


def back_columns_kernel(place, choose, slots, out_0, out_1, out_2, out_3, turned):
    turned[...] = dot_tn(slots[...], choose[...])
    put_row_chunks(place, turned, (out_0, out_1, out_2, out_3))


def back_folded_kernel(
    share, place, choose, message, out_0, out_1, out_2, out_3, slots, turned, semaphores
):
    count = message.shape[0]
    capacity = slots.shape[0] // count
    folded = message.shape[1] - 2 * share
    copies = []
    for index in range(count):
        copies += unfold_copies(
            message.at[index, pl.ds(2 * share, folded)], slots, index * capacity, capacity
        )
    for copy in run_copies(copies, semaphores):
        copy.wait()
    back_columns_kernel(place, choose, slots, out_0, out_1, out_2, out_3, turned)


def mixer_grad_kernel(
    place,
    piece_0,
    piece_1,
    piece_2,
    piece_3,
    residual_in,
    gain_ref,
    cotangent,
    out_proj,
    columns_out,
    mix_out,
    d_gated,
    gain_grad,
    d_send,
    turned,
):
    take_row_pieces(place, (piece_0, piece_1, piece_2, piece_3), d_send)
    residual = residual_in[...]
    inverse = rms_rate(residual)
    scaled = residual * inverse
    grad = d_send[...]
    pulled = grad * as_row(gain_ref)
    along = jnp.mean(pulled * scaled, axis=-1, keepdims=True)
    d_residual = cotangent[...].astype(F32) + inverse * (pulled - scaled * along)
    d_mix = d_residual.astype(BF16)
    put_blocks(mix_out, d_mix)
    d_gated[...] = dot_nt(d_mix, out_proj[...])
    gain_grad[...] = jnp.sum(grad * scaled, axis=0, keepdims=True)
    turned[...] = d_residual.T
    column = columns_out.shape[0]
    columns_out[...] = turned[pl.ds(pl.multiple_of(place[0] * column, column), column), :]


def split_vectors(vectors):
    upper = vectors.astype(BF16).astype(F32)
    return upper, vectors - upper


def scan_backward_kernel(
    d_gated,
    y_in,
    gate_in,
    act_in,
    mixed_in,
    masks,
    dt_proj,
    dt_bias,
    decay_log,
    skip_gain,
    gain_grad,
    d_mix,
    d_mixed_out,
    d_act_out,
    d_gate_out,
    share_out,
    rate,
    step_rows,
    decay_rows,
    drive_rows,
    dy_rows,
    du_rows,
    dl_rows,
    decays,
    history,
):
    rank = dt_proj.shape[0]
    states = decay_log.shape[0]
    length, chans = y_in.shape
    tiles = step_rows.shape[1] // 128
    full = 128 * tiles
    mixed = mixed_in[...]
    dt_low = mixed[:rank].astype(BF16)
    raw_step = dot_tn(dt_low, dt_proj[...]) + as_row(dt_bias)
    step_size = softplus(raw_step)
    act = act_in[...].astype(F32)
    reset = NEVER * (1.0 - wide_masks(masks, 0, chans))
    padded_copy(rate, -jnp.exp(decay_log[...]))
    padded_copy(step_rows, step_size)
    padded_copy(decay_rows, LOG2E * (step_size + reset))
    padded_copy(drive_rows, step_size * act)
    gate = gate_in[...]
    gate_sig = jax.nn.sigmoid(gate)
    d_out = d_gated[...]
    d_y = d_out * (gate * gate_sig)
    padded_copy(dy_rows, d_y)
    d_gate = d_out * y_in[...] * gate_sig * (1.0 + gate * (1.0 - gate_sig))
    b_turned = mixed[rank : rank + states]
    c_turned = mixed[rank + states : rank + 2 * states]
    history[pl.ds(0, states), :] = jnp.zeros((states, full), F32)

    def forward_block(index, state):
        start = pl.multiple_of(index * 8, 8)
        b_cols = block_columns(b_turned, index)
        steps = decay_rows[pl.ds(start, 8), :]
        drives = drive_rows[pl.ds(start, 8), :]
        for row in range(8):
            decay = jnp.exp2(rate[...] * steps[row : row + 1])
            state = decay * state + spread_column(b_cols, row, tiles) * drives[row : row + 1]
            at = pl.multiple_of((start + row) * states, states)
            decays[pl.ds(at, states), :] = decay
            history[pl.ds(at + states, states), :] = state
        return state

    lax.fori_loop(0, length // 8, forward_block, jnp.zeros((states, full), F32))
    lanes = lax.broadcasted_iota(jnp.int32, (states, length), 1)

    def backward_block(count, carry):
        carried, d_rate, d_b, d_c = carry
        index = length // 8 - 1 - count
        start = pl.multiple_of(index * 8, 8)
        b_cols = block_columns(b_turned, index)
        c_cols = block_columns(c_turned, index)
        steps = step_rows[pl.ds(start, 8), :]
        drives = drive_rows[pl.ds(start, 8), :]
        dys = dy_rows[pl.ds(start, 8), :]
        du = [None] * 8
        dl = [None] * 8
        for row in reversed(range(8)):
            at = pl.multiple_of((start + row) * states, states)
            before = history[pl.ds(at, states), :]
            after = history[pl.ds(at + states, states), :]
            decay = decays[pl.ds(at, states), :]
            here = lanes == start + row
            dy_row = jnp.broadcast_to(dys[row : row + 1], (states, full))
            grad = spread_column(c_cols, row, tiles) * dy_row + carried
            c_part = jnp.sum(fold_tiles(dy_row * after), axis=1, keepdims=True)
            d_c = jnp.where(here, c_part, d_c)
            b_part = jnp.sum(fold_tiles(grad * drives[row : row + 1]), axis=1, keepdims=True)
            d_b = jnp.where(here, b_part, d_b)
            du[row] = jnp.sum(grad * spread_column(b_cols, row, tiles), axis=0, keepdims=True)
            carried = grad * decay
            d_log = carried * before
            dl[row] = jnp.sum(d_log * rate[...], axis=0, keepdims=True)
            d_rate = d_rate + d_log * steps[row : row + 1]
        du_rows[pl.ds(start, 8), :] = jnp.concatenate(du, axis=0)
        dl_rows[pl.ds(start, 8), :] = jnp.concatenate(dl, axis=0)
        return carried, d_rate, d_b, d_c

    nothing = jnp.zeros((states, full), F32)
    thin = jnp.zeros((states, length), F32)
    _, d_rate, d_b, d_c = lax.fori_loop(
        0, length // 8, backward_block, (nothing, nothing, thin, thin)
    )
    du = du_rows[:, :chans]
    d_step = (dl_rows[:, :chans] + du * act) * jax.nn.sigmoid(raw_step)
    d_step_low = d_step.astype(BF16)
    low_turned = dot_nt(dt_proj[...], d_step_low)
    d_mixed_out[...] = jnp.concatenate([low_turned, d_b, d_c], axis=0).astype(BF16)
    d_act_out[...] = du * step_size + as_row(skip_gain) * d_y
    d_gate_low = d_gate.astype(BF16)
    d_gate_out[...] = d_gate_low
    width = d_mix.shape[0]
    share_out[:width] = d_mix[...]
    padded_copy(du_rows, d_gate_low.astype(F32))
    share_out[width : width + chans] = du_rows[...].T[:chans].astype(BF16)
    gain_rows = gain_grad[...]
    upper, lower = split_vectors(
        jnp.concatenate(
            [
                (d_rate * rate[...])[:, :chans],
                jnp.sum(d_step, axis=0, keepdims=True),
                jnp.sum(d_y * act, axis=0, keepdims=True),
                gain_rows[:, :chans],
                gain_rows[:, chans:],
                jnp.zeros((VECTORS_ONE - states - 4, chans), F32),
            ],
            axis=0,
        )
    )
    dl_rows[...] = jnp.zeros(dl_rows.shape, F32)
    dl_rows[:rank, :chans] = dot_nn(dt_low, d_step_low)
    dl_rows[rank : rank + VECTORS_ONE, :chans] = upper
    dl_rows[rank + VECTORS_ONE : rank + 2 * VECTORS_ONE, :chans] = lower
    share_out[width + chans :] = dl_rows[...].T[:chans].astype(BF16)


def leave_kernel(
    place,
    piece_0,
    piece_1,
    piece_2,
    piece_3,
    d_act_scan,
    d_gate,
    conv_in,
    inner_in,
    masks,
    x_proj,
    conv_weight,
    in_proj,
    rows_in,
    gain,
    out_0,
    out_1,
    out_2,
    out_3,
    message,
    held,
    turned,
    padded,
):
    length, chans = inner_in.shape
    width = rows_in.shape[1]
    full = padded.shape[1]
    d_mixed = sum_pieces(place, (piece_0, piece_1, piece_2, piece_3), held).astype(BF16)
    d_act = d_act_scan[...] + dot_tn(d_mixed, x_proj[...])
    conv = conv_in[...]
    sig = jax.nn.sigmoid(conv)
    d_conv = d_act * sig * (1.0 + conv * (1.0 - sig))
    inner = inner_in[...]
    d_inner = conv_weight[3:4, :] * d_conv
    weight_grads = [jnp.sum(d_conv * inner, axis=0, keepdims=True)]
    for shift in (1, 2, 3):
        masked = d_conv * wide_masks(masks, shift, chans)
        weight_grads.append(
            jnp.sum(masked * pltpu.roll(inner, shift, 0), axis=0, keepdims=True)
        )
        d_inner = d_inner + conv_weight[3 - shift : 4 - shift, :] * pltpu.roll(
            masked, length - shift, 0
        )
    d_inner_low = d_inner.astype(BF16)
    padded_copy(padded, d_inner_low.astype(F32))
    message[:chans] = padded[...].T[:chans].astype(BF16)
    proj = d_mixed.shape[0]
    top = message.shape[0] - full // 128 * 2 * VECTORS_TWO
    message[chans:top] = jnp.concatenate(
        [d_mixed.astype(F32), jnp.zeros((top - chans - proj, length), F32)], axis=0
    ).astype(BF16)
    d_normed = dot_nn(d_inner_low, in_proj[0]) + dot_nn(d_gate[...], in_proj[1])
    rows = rows_in[...].astype(F32)
    scaled = rows * rms_rate(rows)
    norm_grad = jnp.sum(d_normed * scaled, axis=0, keepdims=True)
    upper, lower = split_vectors(
        jnp.concatenate(
            [
                weight_grads[3],
                weight_grads[2],
                weight_grads[1],
                weight_grads[0],
                jnp.sum(d_conv, axis=0, keepdims=True),
                norm_grad[:, :chans],
                norm_grad[:, chans:],
                jnp.zeros((VECTORS_TWO - 7, chans), F32),
            ],
            axis=0,
        )
    )
    padded_copy(padded, jnp.zeros((length, chans), F32))
    padded[:VECTORS_TWO, :chans] = upper
    padded[VECTORS_TWO : 2 * VECTORS_TWO, :chans] = lower
    for tile in range(full // 128):
        message[top + tile * 2 * VECTORS_TWO : top + (tile + 1) * 2 * VECTORS_TWO] = padded[
            : 2 * VECTORS_TWO, tile * 128 : (tile + 1) * 128
        ].astype(BF16)
    along = jnp.mean(d_normed * as_row(gain) * scaled, axis=-1, keepdims=True)
    along = jnp.broadcast_to(along, (length, length)).T[:8]
    high = along.astype(BF16)
    low = (along - high.astype(F32)).astype(BF16)
    turned[...] = d_normed.T
    outs = (out_0, out_1, out_2, out_3)
    put_row_chunks(place, turned, outs)
    column = width // len(outs)
    for out in outs:
        out[column:, :] = jnp.concatenate([high, low], axis=0)


def finish_rows_kernel(
    piece_0, piece_1, piece_2, piece_3, d_columns, tokens, scale, gain, grad_tokens
):
    column = tokens.shape[0]
    total = piece_0[...].astype(F32)
    for piece in (piece_1, piece_2, piece_3):
        total = total + piece[...].astype(F32)
    along = total[column : column + 1] + total[column + 8 : column + 9]
    inverse = scale[...]
    pulled = total[:column] * gain[...]
    scaled = tokens[...].astype(F32) * inverse
    grad_tokens[...] = d_columns[...] + inverse * (pulled - scaled * along)


def take_blocks(target, pieces):
    for index, piece in enumerate(pieces):
        for start in range(0, target.shape[1], 128):
            target[index * 128 : (index + 1) * 128, start : start + 128] = piece[
                start : start + 128
            ]


def take_turned(target, pieces, start):
    rows = target.shape[0]
    for index, piece in enumerate(pieces):
        target[:, index * 128 : (index + 1) * 128] = piece[start : start + rows]


def first_sets_kernel(firsts, normed, gated, acts):
    chans = gated.shape[0]
    width = normed.shape[1]
    take_blocks(normed, firsts)
    take_turned(gated, firsts, width)
    take_turned(acts, firsts, width + chans)


def wide_grads_kernel(
    sizes,
    seconds,
    normed,
    gated,
    out_grad,
    in_grad,
    dt_grad,
    bias_grad,
    decay_grad,
    skip_grad,
    norm_grad,
    mixed,
    d_gate,
    total,
    gate_grad,
    semaphore,
):
    rank, states = sizes
    chans, width = out_grad.shape
    take_turned(d_gate, seconds, width)
    gate_grad[...] = dot_nn(d_gate[...], normed[...])
    last = pltpu.make_async_copy(gate_grad, in_grad.at[1], semaphore)
    last.start()
    take_blocks(mixed, seconds)
    out_grad[...] = dot_nn(gated[...], mixed[...])
    vectors = seconds[0][width + chans :].astype(F32)
    for piece in seconds[1:]:
        vectors = vectors + piece[width + chans :].astype(F32)
    total[...] = jnp.zeros(total.shape, F32)
    total[:chans] = vectors
    rows = total[...].T[:, :chans]
    dt_grad[...] = rows[:rank]
    rows = rows[rank : rank + VECTORS_ONE] + rows[rank + VECTORS_ONE : rank + 2 * VECTORS_ONE]
    decay_grad[...] = rows[:states]
    bias_grad[...] = rows[states].reshape(chans)
    skip_grad[...] = rows[states + 1].reshape(chans)
    norm_grad[...] = jnp.concatenate(
        [rows[states + 2 : states + 3], rows[states + 3 : states + 4]], axis=1
    )
    last.wait()


def late_grads_kernel(
    widths,
    lasts,
    normed,
    acts,
    kept_grad,
    in_grad,
    x_grad,
    weight_grad,
    bias_grad,
    norm_grad,
    d_inner,
    d_mixed,
    inner_grad,
    semaphore,
):
    chans, proj = widths
    rows = d_mixed.shape[0]
    take_turned(d_inner, lasts, 0)
    inner_grad[...] = dot_nn(d_inner[...], normed[...])
    last = pltpu.make_async_copy(inner_grad, in_grad.at[0], semaphore)
    last.start()
    take_turned(d_mixed, lasts, chans)
    x_grad[...] = dot_nt(d_mixed[...], acts[...])[:proj]
    total = lasts[0][chans + rows :].astype(F32)
    for piece in lasts[1:]:
        total = total + piece[chans + rows :].astype(F32)
    deep = 2 * VECTORS_TWO
    vectors = jnp.concatenate(
        [total[start : start + deep] for start in range(0, total.shape[0], deep)], axis=1
    )[:, :chans]
    vectors = vectors[:VECTORS_TWO] + vectors[VECTORS_TWO:]
    weight_grad[...] = vectors[:4]
    bias_grad[...] = vectors[4].reshape(chans)
    norm_grad[...] = jnp.concatenate([vectors[5:6], vectors[6:7]], axis=1)
    last.wait()


def send_chunks(chunks):
    count = len(chunks)
    pairs = [[(i, (i + s) % count) for i in range(count)] for s in range(count)]
    return [chunks[0]] + [lax.ppermute(chunks[s], "tensor", pairs[s]) for s in range(1, count)]


def share_rows(values, count):
    return send_chunks([values] * count)


def add_low(pieces):
    total = pieces[0].astype(F32)
    for piece in pieces[1:]:
        total = total + piece.astype(F32)
    return total.astype(BF16)


def after(values, *events):
    return list(lax.optimization_barrier((tuple(values), events))[0])


def swap(values, bits):
    return lax.ppermute(values, "dp", [(i, i ^ bits) for i in range(NEAR_GROUPS)])


def swap_near(fars):
    return [*fars, *[swap(far, 1) for far in fars]]


def body(
    tokens,
    resets,
    routes,
    norm_one,
    in_proj,
    conv_weight,
    conv_bias,
    x_proj,
    dt_proj,
    dt_bias,
    decay_log,
    skip_gain,
    out_proj,
    norm_two,
    expert_in,
    expert_out,
    cotangent,
):
    groups = lax.axis_size("dp")
    parts = lax.axis_size("tensor")
    place = lax.axis_index("tensor").astype(jnp.int32).reshape(1)
    length, column = tokens.shape
    width = norm_one.shape[0]
    rank, chans = dt_proj.shape
    states = decay_log.shape[0]
    experts, share, hidden_units = expert_in.shape
    proj = x_proj.shape[1]
    tile_count = groups // experts
    block_rows = length * experts // groups
    capacity = max(2, block_rows // 4)
    slot_count = groups * capacity
    tiles = -(-chans // 128)
    full = 128 * tiles
    near = groups == NEAR_GROUPS and experts == groups
    tokens_turned = tokens.T
    in_turned = jnp.swapaxes(in_proj, 1, 2)
    x_turned = x_proj.T
    resets_row = resets.reshape(1, length)
    routes_row = routes.reshape(1, length)

    def exchange(values):
        return lax.all_to_all(values, "dp", split_axis=0, concat_axis=0, tiled=True)

    def exchange_slots(slots):
        return exchange(slots.reshape(groups, capacity, width)).reshape(slot_count, width)

    token_pieces = share_rows(tokens_turned, parts)
    mask_out = ((4, length, 128), F32)
    choose_out = ((slot_count, length), BF16)
    weight_outs = [((width, hidden_units), BF16)] * 2
    slots_out = ((slot_count, width), BF16)
    hidden_out = ((slot_count, hidden_units), BF16)
    folded = capacity + capacity // 2
    message_out = ((groups, 2 * share + folded, hidden_units), BF16)
    if near:
        masks, choose, packed = run_kernel(
            functools.partial(pack_kernel, capacity),
            [mask_out, choose_out, message_out],
            [resets_row, routes_row, cotangent, expert_in, expert_out],
            [
                ((groups, folded, hidden_units), BF16),
                pltpu.SemaphoreType.DMA((3 * experts,)),
            ],
            far_outs=(2,),
        )
        first_w, second_w, grad_slots, d_hidden = run_kernel(
            functools.partial(unpack_kernel, share, capacity),
            weight_outs + [slots_out, ((slot_count, hidden_units), F32)],
            [exchange(packed)],
            [pltpu.SemaphoreType.DMA((5 * groups,))],
            far_args=(0,),
        )
    else:
        masks, choose, grad_send = run_kernel(
            functools.partial(prepare_kernel, experts, capacity, block_rows),
            [mask_out, choose_out, slots_out],
            [resets_row, routes_row, cotangent],
        )
        first_w = exchange(jnp.tile(expert_in, (tile_count, 1, 1))).reshape(weight_outs[0][0])
        second_w = exchange(jnp.tile(expert_out, (tile_count, 1, 1))).reshape(weight_outs[0][0])
        grad_slots = exchange_slots(grad_send)
        (d_hidden,) = run_kernel(
            hidden_back_kernel, [((slot_count, hidden_units), F32)], [grad_slots, second_w]
        )

    rows, normed, act, inner, conv, gate, scale, gain_columns, mixed_part = run_kernel(
        enter_kernel,
        [
            ((length, width), BF16),
            ((width, length), BF16),
            ((length, chans), BF16),
            ((length, chans), F32),
            ((length, chans), F32),
            ((length, chans), F32),
            ((1, length), F32),
            ((column, length), F32),
            ((proj, length), BF16),
        ],
        [place, *token_pieces, norm_one, in_turned, conv_weight, conv_bias, x_turned, masks],
        [((width, length), F32)],
        scalars=1,
    )
    mixed_pieces = share_rows(mixed_part, parts)
    *mix_chunks, mixed, first, y = run_kernel(
        scan_forward_kernel,
        [((length // parts, width), BF16)] * parts
        + [
            ((proj, length), F32),
            ((width + 2 * chans, length), BF16),
            ((length, chans), F32),
        ],
        [
            place,
            *mixed_pieces,
            dt_proj,
            dt_bias,
            decay_log,
            skip_gain,
            act,
            gate,
            masks,
            out_proj,
            normed,
        ],
        [
            ((parts, proj, length), BF16),
            ((states, full), F32),
            ((length, full), F32),
            ((length, full), F32),
            ((length, full), F32),
            ((length, width), F32),
        ],
        scalars=1,
    )
    mixer_pieces = share_rows(add_low(send_chunks(mix_chunks)), parts)
    residual, residual_columns, send_slots = run_kernel(
        dispatch_kernel,
        [((length, width), F32), ((column, length), F32), slots_out],
        [place, *mixer_pieces, rows, norm_two, choose],
        [((width, length), F32)],
        scalars=1,
    )
    arrived = exchange_slots(send_slots)
    if near:
        first_x = swap(after([first], d_hidden)[0], 2)
        arrived = after([arrived], first_x)[0]
    hidden, d_pre, d_slots = run_kernel(
        expert_kernel, [hidden_out, hidden_out, slots_out], [arrived, first_w, d_hidden]
    )
    back_slots = exchange_slots(d_slots)
    grad_args = [arrived, grad_slots, hidden, d_pre, second_w]
    grad_out = ((experts, share, hidden_units), F32)
    if near:
        (packed,) = run_kernel(
            functools.partial(expert_grads_pack_kernel, share, capacity),
            [message_out],
            grad_args,
            [
                ((2, width, hidden_units), BF16),
                ((groups, folded, hidden_units), BF16),
                pltpu.SemaphoreType.DMA((3 * groups,)),
            ],
            far_outs=(0,),
        )
        first_y = swap(after([first], hidden)[0], 4)
        packed, back_slots = after([packed, back_slots], first_y)
        back_slots = after([back_slots], packed)[0]
        owned = exchange(packed)
    else:
        grad_first, grad_second, moe_slots = run_kernel(
            expert_grads_kernel, weight_outs + [slots_out], grad_args
        )
    back_chunks = run_kernel(
        back_rows_kernel,
        [((length // parts, width), BF16)] * parts,
        [place, choose, back_slots],
        [((length, width), F32)],
        scalars=1,
    )
    send_pieces = share_rows(add_low(send_chunks(back_chunks)), parts)
    d_columns, d_mix, d_gated, gain_grad_two = run_kernel(
        mixer_grad_kernel,
        [
            ((column, length), F32),
            ((width, length), BF16),
            ((length, chans), F32),
            ((1, width), F32),
        ],
        [place, *send_pieces, residual, norm_two, cotangent, out_proj],
        [((length, width), F32), ((width, length), F32)],
        scalars=1,
    )
    d_mixed_part, d_act_scan, d_gate, second = run_kernel(
        scan_backward_kernel,
        [
            ((proj, length), BF16),
            ((length, chans), F32),
            ((length, chans), BF16),
            ((width + 2 * chans, length), BF16),
        ],
        [
            d_gated,
            y,
            gate,
            act,
            mixed,
            masks,
            dt_proj,
            dt_bias,
            decay_log,
            skip_gain,
            gain_grad_two,
            d_mix,
        ],
        [
            ((states, full), F32),
            ((length, full), F32),
            ((length, full), F32),
            ((length, full), F32),
            ((length, full), F32),
            ((length, full), F32),
            ((length, full), F32),
            ((length * states, full), F32),
            (((length + 1) * states, full), F32),
        ],
    )
    d_mixed_pieces = share_rows(d_mixed_part, parts)
    if near:
        second_x, second_y = swap(second, 2), swap(second, 4)
    last_rows = chans + -(-proj // 16) * 16 + tiles * 2 * VECTORS_TWO
    *normed_chunks, message = run_kernel(
        leave_kernel,
        [((column + 16, length), BF16)] * parts
        + [((last_rows, length), BF16)],
        [
            place,
            *d_mixed_pieces,
            d_act_scan,
            d_gate,
            conv,
            inner,
            masks,
            x_turned,
            conv_weight,
            in_turned,
            rows,
            norm_one,
        ],
        [((parts, proj, length), BF16), ((width, length), F32), ((length, full), F32)],
        scalars=1,
    )
    normed_pieces = send_chunks(normed_chunks)
    (grad_tokens,) = run_kernel(
        finish_rows_kernel,
        [((column, length), F32)],
        [*normed_pieces, d_columns, tokens_turned, scale, gain_columns],
    )

    chunk_outs = [((column, length), BF16)] * parts
    if near:
        moe_chunks = run_kernel(
            functools.partial(back_folded_kernel, share),
            chunk_outs,
            [place, choose, owned],
            [slots_out, ((width, length), F32), pltpu.SemaphoreType.DMA((3 * groups,))],
            scalars=1,
            far_args=(2,),
        )
        grad_expert_in, grad_expert_out = run_kernel(
            functools.partial(owner_kernel, share),
            [grad_out] * 2,
            [owned],
            [
                ((groups, 2 * share, hidden_units), BF16),
                ((groups, 2 * share, hidden_units), F32),
                pltpu.SemaphoreType.DMA((groups,)),
                pltpu.SemaphoreType.DMA((2 * groups,)),
            ],
            far_args=(0,),
            far_outs=(0, 1),
        )
    else:
        moe_chunks = run_kernel(
            back_columns_kernel,
            chunk_outs,
            [place, choose, exchange_slots(moe_slots)],
            [((width, length), F32)],
            scalars=1,
        )

        def owner_sum(values):
            got = exchange(values.reshape(groups, share, hidden_units)).astype(F32)
            return jnp.sum(got.reshape(tile_count, experts, share, hidden_units), axis=0)

        grad_expert_in = owner_sum(grad_first)
        grad_expert_out = owner_sum(grad_second)
    outcome = residual_columns
    for piece in send_chunks(moe_chunks):
        outcome = outcome + piece.astype(F32)
    outcome = outcome.astype(BF16)

    if near:
        first_y, second_x, second_y = after([first_y, second_x, second_y], message)
        firsts = swap_near([first, first_x, first_y, swap(first_y, 2)])
        seconds = swap_near([second, second_x, second_y, swap(second_x, 4)])

        def first_sets(*refs):
            first_sets_kernel(refs[:groups], *refs[groups:])

        all_normed, all_gated, all_act = run_kernel(
            first_sets,
            [
                ((groups * length, width), BF16),
                ((chans, groups * length), BF16),
                ((chans, groups * length), BF16),
            ],
            firsts,
        )

        def wide_grads(*refs):
            wide_grads_kernel((rank, states), refs[:groups], *refs[groups:])

        (
            grad_out_proj,
            grad_in_turned,
            grad_dt_proj,
            grad_dt_bias,
            grad_decay_log,
            grad_skip_gain,
            grad_norm_two,
        ) = run_kernel(
            wide_grads,
            [
                ((chans, width), F32),
                ((2, chans, width), F32),
                ((rank, chans), F32),
                ((chans,), F32),
                ((states, chans), F32),
                ((chans,), F32),
                ((1, width), F32),
            ],
            [*seconds, all_normed, all_gated],
            [
                ((groups * length, width), BF16),
                ((chans, groups * length), BF16),
                ((full, length), F32),
                ((chans, width), F32),
                pltpu.SemaphoreType.DMA,
            ],
            far_outs=(1,),
        )
        message = after([message], second_x, second_y)[0]
        lasts = swap_near([message, swap(message, 2), swap(message, 4), swap(message, 6)])

        def late_grads(*refs):
            late_grads_kernel((chans, proj), refs[:groups], *refs[groups:])

        grad_in_turned, grad_x_turned, grad_conv_weight, grad_conv_bias, norm_part = run_kernel(
            late_grads,
            [
                ((2, chans, width), F32),
                ((proj, chans), F32),
                ((4, chans), F32),
                ((chans,), F32),
                ((1, width), F32),
            ],
            [*lasts, all_normed, all_act, grad_in_turned],
            [
                ((chans, groups * length), BF16),
                ((-(-proj // 16) * 16, groups * length), BF16),
                ((chans, width), F32),
                pltpu.SemaphoreType.DMA,
            ],
            far_args=(groups + 2,),
            far_outs=(0,),
            alias={groups + 2: 0},
        )
    else:
        top = last_rows - tiles * 2 * VECTORS_TWO
        ones = second[width + chans :].astype(F32).T
        twos = message[top:].astype(F32).reshape(tiles, 2 * VECTORS_TWO, length)
        twos = jnp.swapaxes(twos, 0, 1).reshape(2 * VECTORS_TWO, full)[:, :chans]
        plain_normed = jnp.swapaxes(normed.reshape(-1, length, 128), 0, 1).reshape(length, width)
        plain_mix = jnp.swapaxes(d_mix.reshape(-1, length, 128), 0, 1).reshape(length, width)
        grad_in_turned, grad_x_turned, grad_dt_proj, grad_out_proj, ones, twos = lax.psum(
            (
                jnp.stack(
                    [
                        dot_nn(message[:chans], plain_normed),
                        dot_nn(second[width : width + chans], plain_normed),
                    ]
                ),
                dot_nn(message[chans : chans + proj], act),
                ones[:rank],
                dot_nn(first[width : width + chans], plain_mix),
                ones[rank : rank + VECTORS_ONE]
                + ones[rank + VECTORS_ONE : rank + 2 * VECTORS_ONE],
                twos[:VECTORS_TWO] + twos[VECTORS_TWO:],
            ),
            "dp",
        )
        grad_decay_log = ones[:states]
        grad_dt_bias = ones[states]
        grad_skip_gain = ones[states + 1]
        grad_norm_two = ones[states + 2 : states + 4]
        grad_conv_weight = twos[:4]
        grad_conv_bias = twos[4]
        norm_part = twos[5:7].reshape(1, width)
    grad_norm_one = sum(share_rows(norm_part, parts))
    return (
        outcome.T,
        grad_tokens.T,
        grad_norm_one.reshape(width),
        jnp.swapaxes(grad_in_turned, 1, 2),
        grad_conv_weight,
        grad_conv_bias,
        grad_x_turned.T,
        grad_dt_proj,
        grad_dt_bias,
        grad_decay_log,
        grad_skip_gain,
        grad_out_proj,
        grad_norm_two.reshape(width),
        grad_expert_in,
        grad_expert_out,
    )


def solution(mesh):
    placed = (
        P("dp", "tensor"),
        P("dp"),
        P("dp", None),
        P(),
        P(None, None, "tensor"),
        P(None, "tensor"),
        P("tensor"),
        P("tensor", None),
        P(None, "tensor"),
        P("tensor"),
        P(None, "tensor"),
        P("tensor"),
        P("tensor", None),
        P(),
        P(None, "dp", "tensor"),
        P(None, "dp", "tensor"),
        P("dp", None),
    )
    return jax.shard_map(
        body,
        mesh=mesh,
        in_specs=placed,
        out_specs=(
            P("dp", "tensor"),
            P("dp", "tensor"),
            P(),
            P(None, None, "tensor"),
            P(None, "tensor"),
            P("tensor"),
            P("tensor", None),
            P(None, "tensor"),
            P("tensor"),
            P(None, "tensor"),
            P("tensor"),
            P("tensor", None),
            P(),
            P(None, "dp", "tensor"),
            P(None, "dp", "tensor"),
        ),
        check_vma=False,
    )
```

time: 394 us -> 256 us (0.65)
  blocking collectives: 72.1 us -> 16.7 us
  waiting for transfers between devices: 132 us -> 76.7 us
  Pallas kernels: 56.6 us -> 87.6 us
  local copies, waits for them, and re-layouts: 32.2 us -> 5.33 us
  matrix products: 16.7 us -> 0 us
  between operations: 14.1 us -> 1.15 us
  other arithmetic: 13.8 us -> 3.78 us
  starting transfers between devices: 54.9 us -> 64 us
    all_gather x5 -> x0, waiting for transfers between devices: 63.2 us -> none  [the longest x3 36.2 us: gather(): return lax.all_gather(values, 'dp', axis=0, tiled=True)]
    all_to_all x4 -> x1, blocking collectives: 72.1 us -> 16.7 us  [exchange(): return lax.all_to_all(values, 'dp', split_axis=0, concat_axis=0, tiled=True)]
    pallas_call x13 -> x17, Pallas kernels: 56.6 us -> 87.6 us  [run_kernel(): pl.pallas_call(kernel, out_shape=[jax.ShapeDtypeStruct(shape, dtype) for...]
    ppermute x0 -> x21, waiting for transfers between devices: none -> 23.9 us  [swap(): lax.ppermute(values, 'dp', [(i, i ^ bits) for i in range(NEAR_GROUPS)])]
    all_to_all x4 -> x3, waiting for transfers between devices: 32.6 us -> 15.1 us  [exchange(): return lax.all_to_all(values, 'dp', split_axis=0, concat_axis=0, tiled=True)]
    dot_general x5 -> x0, matrix products: 16.7 us -> none  [dot_tn(): lax.dot_general(left, right, (((0,), (0,)), ((), ())), preferred_element_...]
    ppermute x0 -> x21, starting transfers between devices: none -> 11.4 us  [swap(): lax.ppermute(values, 'dp', [(i, i ^ bits) for i in range(NEAR_GROUPS)])]
    unnamed x58 -> x90, local copies, waits for them, and re-layouts: 16.4 us -> 5.33 us
  transfers between devices with their start and end apart: 39 -> 54, of which waited for: 19 -> 24; matrix products, arithmetic and copies ran while one was open for 14% -> 1% of each run, Pallas kernels for 6% -> 31%
where the time goes in v2:
time: 256 us; the launch traced here: 255 us
  Pallas kernels  87.6 us (34%)
  waiting for transfers between devices  76.7 us (30%)
  starting transfers between devices  64 us (25%)
  blocking collectives  16.7 us (7%)
  local copies, waits for them, and re-layouts  5.33 us (2%)
  other arithmetic  3.78 us (1%)
    pallas_call x17, Pallas kernels, run_kernel(): pl.pallas_call(kernel, out_shape=[jax.ShapeDtypeStruct(shape, dtype) for...  87.6 us
    ppermute x30, starting transfers between devices, send_chunks(): lax.ppermute(chunks[s], 'tensor', pairs[s])  39.2 us
    ppermute x30, waiting for transfers between devices, send_chunks(): lax.ppermute(chunks[s], 'tensor', pairs[s])  37.7 us
    ppermute x21, waiting for transfers between devices, swap(): lax.ppermute(values, 'dp', [(i, i ^ bits) for i in range(NEAR_GROUPS)])  23.9 us
    all_to_all x1, blocking collectives, exchange(): return lax.all_to_all(values, 'dp', split_axis=0, concat_axis=0, tiled=True)  16.7 us
    all_to_all x3, waiting for transfers between devices, exchange(): return lax.all_to_all(values, 'dp', split_axis=0, concat_axis=0, tiled=True)  15.1 us
    all_to_all x3, starting transfers between devices, exchange(): return lax.all_to_all(values, 'dp', split_axis=0, concat_axis=0, tiled=True)  13.4 us
    ppermute x21, starting transfers between devices, swap(): lax.ppermute(values, 'dp', [(i, i ^ bits) for i in range(NEAR_GROUPS)])  11.4 us
  transfers between devices with their start and end apart: 54, of which 24 were waited for; matrix products, arithmetic and copies ran while one was open for 1% of the time, Pallas kernels for 31%

profile of v2, /device:TPU:0, one launch (start us, length us, event | category | flops | bytes accessed | tf_op | source)
XLA Modules:
  0.0 255.2 jit_solution(15507558451279420624)
XLA Ops:
  0.6 5.0 %shard_map.280 = (f32[4,128,128]{2,1,0:T(8,128)}, bf16[256,128]{1,0:T(8,128)(2,1)}, bf16[8,336,768]{2,1,0:T(8,128)(2,1)}) custom-call(s32[1,128]{1,0:T(1,128)} %bitcast.31, s32[1,128]{1,0:T(1,128)} %bitcast.32, bf16[128,1152]{1,0:T(8,128)(2,1)} %cotangent.3, bf16[8,144,768]{2,1,0:T(8,128)(2,1)} %expert_in.1, bf16[8,144,768]{2,1,0:T(8,128)(2,1)} %expert_out.1), custom_call_target="tpu_custom_call" | custom-call | tf_op jit(solution)/shard_map/pallas_call | solution.py:28
  5.7 5.3 %all-to-all-start.1 = ((bf16[8,336,768]{2,1,0:T(8,128)(2,1)}), bf16[8,336,768]{2,1,0:T(8,128)(2,1)}, u32[]{:S(2)}, u32[]{:S(2)}) async-start(bf16[8,336,768]{2,1,0:T(8,128)(2,1)} %get-tuple-element.106), calls=%async_computation.1 | async-start | bytes 8257536 | tf_op jit(solution)/shard_map/all_to_all | solution.py:954
  11.0 4.5 %collective-permute-start.2 = (bf16[288,128]{1,0:T(8,128)(2,1)S(1)}, bf16[288,128]{1,0:T(8,128)(2,1)S(1)}, u32[]{:S(2)}, u32[]{:S(2)}) collective-permute-start(bf16[288,128]{1,0:T(8,128)(2,1)S(1)} %bitcast.27), channel_id=1, source_target_pairs={{0,3},{1,0},{2,1},{3,2},{4,7},{5,4},{6,5},{7,6},{8,11},{9,8},{10,9... | collective-permute-start | bytes 221192 | tf_op jit(solution)/shard_map/ppermute | solution.py:886
  18.2 5.0 %collective-permute-done.1.piece_2 = bf16[288,128]{1,0:T(8,128)(2,1)S(1)} collective-permute-done((bf16[288,128]{1,0:T(8,128)(2,1)S(1)}, bf16[288,128]{1,0:T(8,128)(2,1)S(1)}, u32[]{:S(2)}, u32[]{:S(2)}) %collective-permute-start.1) | collective-permute-done | bytes 73760 | tf_op jit(solution)/shard_map/ppermute | solution.py:886
  23.8 4.2 %shard_map.281 = (bf16[128,1152]{1,0:T(8,128)(2,1)}, bf16[1152,128]{1,0:T(8,128)(2,1)}, bf16[128,576]{1,0:T(8,128)(2,1)}, f32[128,576]{1,0:T(8,128)}, f32[128,57...) custom-call(s32[1]{0:T(128)} %bitcast.place, ...), custom_call_target="tpu_custom_call" | custom-call | tf_op jit(solution)/shard_map/pallas_call | solution.py:28
  36.3 7.4 %shard_map.282 = (bf16[32,1152]{1,0:T(8,128)(2,1)}, bf16[32,1152]{1,0:T(8,128)(2,1)}, bf16[32,1152]{1,0:T(8,128)(2,1)}, bf16[32,1152]{1,0:T(8,128)(2,1)}, f32[10...) custom-call(s32[1]{0:T(128)} %bitcast.place, bf16[104,128]{1,0:T(8,128)(2,1)} %get-tuple-element.93.piece_0, ...), custom_call_target="tpu_custom_call" | custom-call | tf_op jit(solution)/shard_map/pallas_call | solution.py:28
  55.8 3.7 %all-to-all-done.1.message = bf16[8,336,768]{2,1,0:T(8,128)(2,1)} async-done(((bf16[8,336,768]{2,1,0:T(8,128)(2,1)}), bf16[8,336,768]{2,1,0:T(8,128)(2,1)}, u32[]{:S(2)}, u32[]{:S(2)}) %all-to-all-start.1) | async-done | bytes 4128800 | tf_op jit(solution)/shard_map/all_to_all | solution.py:954
  59.5 4.9 %shard_map.284 = (bf16[1152,768]{1,0:T(8,128)(2,1)}, bf16[1152,768]{1,0:T(8,128)(2,1)}, bf16[256,1152]{1,0:T(8,128)(2,1)}, f32[256,768]{1,0:T(8,128)}) custom-call(bf16[8,336,768]{2,1,0:T(8,128)(2,1)} %all-to-all-done.1.message), custom_call_target="tpu_custom_call" | custom-call | tf_op jit(solution)/shard_map/pallas_call | solution.py:28
  68.2 16.7 %all_to_all.20 = bf16[8,32,1152]{2,1,0:T(8,128)(2,1)} all-to-all(bf16[8,32,1152]{2,1,0:T(8,128)(2,1)} %bitcast.22), channel_id=1, replica_groups=mesh['dp'=8,'tensor'=4] {'dp'}, dimensions={0} | all-to-all | bytes 1179648 | tf_op jit(solution)/shard_map/all_to_all | solution.py:954
  84.9 4.4 %shard_map.285 = (bf16[256,768]{1,0:T(8,128)(2,1)}, bf16[256,768]{1,0:T(8,128)(2,1)}, bf16[256,1152]{1,0:T(8,128)(2,1)}) custom-call(bf16[256,1152]{1,0:T(8,128)(2,1)} %bitcast.18, bf16[1152,768]{1,0:T(8,128)(2,1)} %get-tuple-element.111.first_w, f32[256,768]{1,0:T(8,128)} %get-tuple-element.107.d_hidden), custom_call_target="tpu_custom_call" | custom-call | tf_op jit(solution)/shard_map/pallas_call | solution.py:28
  90.8 3.5 %all-to-all-start.2 = ((bf16[8,32,1152]{2,1,0:T(8,128)(2,1)}), bf16[8,32,1152]{2,1,0:T(8,128)(2,1)S(1)}, u32[]{:S(2)}, u32[]{:S(2)}) async-start(bf16[8,32,1152]{2,1,0:T(8,128)(2,1)} %bitcast.21), calls=%async_computation.2 | async-start | bytes 1179648 | tf_op jit(solution)/shard_map/all_to_all | solution.py:954
  94.4 5.0 %shard_map.286 = bf16[8,336,768]{2,1,0:T(8,128)(2,1)} custom-call(bf16[256,1152]{1,0:T(8,128)(2,1)} %bitcast.19, bf16[256,1152]{1,0:T(8,128)(2,1)} %get-tuple-element.110.grad_slots, bf16[256,768]{1,0:T(8,128)(2,1)} %get-tuple-element.112.hidden, bf16[256,768]{1,0:T(8,128)(2,1)} %get-tuple-element.113.d_pre, bf16[1152,768]{1,0:T(8,128)(2,1)} %get-tuple-element.114.second_w), custom_call_target="tpu_custom_call" | custom-call | tf_op jit(solution)/shard_map/pallas_call | solution.py:28
  99.4 11.4 %all-to-all-done.2 = bf16[8,32,1152]{2,1,0:T(8,128)(2,1)S(1)} async-done(((bf16[8,32,1152]{2,1,0:T(8,128)(2,1)}), bf16[8,32,1152]{2,1,0:T(8,128)(2,1)S(1)}, u32[]{:S(2)}, u32[]{:S(2)}) %all-to-all-start.2) | async-done | bytes 589856 | tf_op jit(solution)/shard_map/all_to_all | solution.py:954
  111.6 4.5 %all-to-all-start.3 = ((bf16[8,336,768]{2,1,0:T(8,128)(2,1)}), bf16[8,336,768]{2,1,0:T(8,128)(2,1)}, u32[]{:S(2)}, u32[]{:S(2)}) async-start(bf16[8,336,768]{2,1,0:T(8,128)(2,1)} %shard_map.286), calls=%async_computation.3 | async-start | bytes 8257536 | tf_op jit(solution)/shard_map/all_to_all | solution.py:954
  135.7 4.7 %collective-permute-done.21.piece_2 = bf16[32,1152]{1,0:T(8,128)(2,1)S(1)} collective-permute-done((bf16[32,1152]{1,0:T(8,128)(2,1)S(1)}, bf16[32,1152]{1,0:T(8,128)(2,1)S(1)}, u32[]{:S(2)}, u32[]{:S(2)}) %collective-permute-start.21) | collective-permute-done | bytes 73760 | tf_op jit(solution)/shard_map/ppermute | solution.py:886
  144.4 13.9 %shard_map.290 = (bf16[104,128]{1,0:T(8,128)(2,1)}, f32[128,576]{1,0:T(8,128)}, bf16[128,576]{1,0:T(8,128)(2,1)}, bf16[2304,128]{1,0:T(8,128)(2,1)}) custom-call(f32[128,576]{1,0:T(8,128)} %get-tuple-element.129.d_gated, f32[128,576]{1,0:T(8,128)} %get-tuple-element.130.y_in, f32[128,576]{1,0:T(8,128)} %get-tuple-element.95.gate_in, ...), custom_call_target="tpu_custom_call" | custom-call | tf_op jit(solution)/shard_map/pallas_call | solution.py:28
  166.6 4.2 %collective-permute-done.24.piece_2 = bf16[104,128]{1,0:T(8,128)(2,1)S(1)} collective-permute-done((bf16[104,128]{1,0:T(8,128)(2,1)}, bf16[104,128]{1,0:T(8,128)(2,1)S(1)}, u32[]{:S(2)}, u32[]{:S(2)}) %collective-permute-start.24) | collective-permute-done | bytes 26656 | tf_op jit(solution)/shard_map/ppermute | solution.py:886
  171.2 5.5 %collective-permute-done.23.piece_1 = bf16[104,128]{1,0:T(8,128)(2,1)S(1)} collective-permute-done((bf16[104,128]{1,0:T(8,128)(2,1)}, bf16[104,128]{1,0:T(8,128)(2,1)S(1)}, u32[]{:S(2)}, u32[]{:S(2)}) %collective-permute-start.23) | collective-permute-done | bytes 26656 | tf_op jit(solution)/shard_map/ppermute | solution.py:886
  177.3 4.5 %shard_map.291 = (bf16[304,128]{1,0:T(8,128)(2,1)}, bf16[304,128]{1,0:T(8,128)(2,1)}, bf16[304,128]{1,0:T(8,128)(2,1)}, bf16[304,128]{1,0:T(8,128)(2,1)}, bf16[768,128]{1,0:T(8,128)(2,1)}) custom-call(s32[1]{0:T(128)} %bitcast.place, bf16[104,128]{1,0:T(8,128)(2,1)} %get-tuple-element.134.piece_0, bf16[104,128]{1,0:T(8,128)(2,1)} %copy-done.41, ...), custom_call_target="tpu_custom_call" | custom-call | tf_op jit(solution)/shard_map/pallas_call | solution.py:28
  186.4 15.9 %collective-permute-done.33.refs_3_ = bf16[768,128]{1,0:T(8,128)(2,1)S(1)} collective-permute-done((bf16[768,128]{1,0:T(8,128)(2,1)}, bf16[768,128]{1,0:T(8,128)(2,1)S(1)}, u32[]{:S(2)}, u32[]{:S(2)}) %collective-permute-start.33) | collective-permute-done | bytes 196640 | tf_op jit(solution)/shard_map/ppermute | solution.py:905
  213.4 5.6 %shard_map.293 = (bf16[1024,1152]{1,0:T(8,128)(2,1)}, bf16[576,1024]{1,0:T(8,128)(2,1)}, bf16[576,1024]{1,0:T(8,128)(2,1)}) custom-call(bf16[2304,128]{1,0:T(8,128)(2,1)} %get-tuple-element.116.refs_0_, bf16[2304,128]{1,0:T(8,128)(2,1)} %copy-done.2, bf16[2304,128]{1,0:T(8,128)(2,1)} %copy-done.3, bf16[2304,128]{1,0:T(8,128)(2,1)} %copy-done.10, ...), custom_call_target="tpu_custom_call" | custom-call | tf_op jit(solution)/shard_map/pallas_call | solution.py:28
  219.0 8.6 %shard_map.294 = (f32[576,1152]{1,0:T(8,128)}, f32[2,576,1152]{2,1,0:T(8,128)}, f32[72,576]{1,0:T(8,128)}, f32[576]{0:T(1024)}, f32[16,576]{1,0:T(8,128)}, /*index=5*/f32[576]{0:T(1024)}, f32[1,1152]{1,0:T(1,128)}) custom-call(bf16[2304,128]{1,0:T(8,128)(2,1)} %get-tuple-element.147.refs_0_, bf16[2304,128]{1,0:T(8,128)(2,1)} %copy-done.5, ...), custom_call_target="tpu_custom_call" | custom-call | tf_op jit(solution)/shard_map/pallas_call | solution.py:28
  228.3 6.8 %shard_map.295 = (f32[2,576,1152]{2,1,0:T(8,128)}, f32[104,576]{1,0:T(8,128)}, f32[4,576]{1,0:T(4,128)}, f32[576]{0:T(1024)}, f32[1,1152]{1,0:T(1,128)}) custom-call(bf16[768,128]{1,0:T(8,128)(2,1)} %get-tuple-element.150.refs_0_, bf16[768,128]{1,0:T(8,128)(2,1)} %collective-permute-done.31.refs_1_, ...), custom_call_target="tpu_custom_call", output_to_operand_aliasing={{0}: (10, {})} | custom-call | tf_op jit(solution)/shard_map/pallas_call | solution.py:28
  250.3 4.2 %shard_map.296 = (f32[8,144,768]{2,1,0:T(8,128)}, f32[8,144,768]{2,1,0:T(8,128)}) custom-call(bf16[8,336,768]{2,1,0:T(8,128)(2,1)} %all-to-all-done.3.message), custom_call_target="tpu_custom_call" | custom-call | tf_op jit(solution)/shard_map/pallas_call | solution.py:28
  (197 shorter events, 94.6 us)
Async XLA Ops:
  5.7 53.8 %all-to-all-start.1 = ((bf16[8,336,768]{2,1,0:T(8,128)(2,1)}), bf16[8,336,768]{2,1,0:T(8,128)(2,1)}, u32[]{:S(2)}, u32[]{:S(2)}) async-start(bf16[8,336,768]{2,1,0:T(8,128)(2,1)} %get-tuple-element.106), calls=%async_computation.1 | async-start | bytes 8257536 | tf_op jit(solution)/shard_map/all_to_all | solution.py:954
  52.1 13.0 %collective-permute-start.11 = (bf16[32,1152]{1,0:T(8,128)(2,1)S(1)}, bf16[32,1152]{1,0:T(8,128)(2,1)S(1)}, u32[]{:S(2)}, u32[]{:S(2)}) collective-permute-start(bf16[32,1152]{1,0:T(8,128)(2,1)S(1)} %add_convert_fusion.2.piece_0), channel_id=1, source_target_pairs={{0,3},{1,0},{2,1},{3,2},{4,7},{5,4},{6,5},{7,6},{8,11},{9,8},{10,9... | collective-permute-start | bytes 221192 | tf_op jit(solution)/shard_map/ppermute | solution.py:886
  55.1 9.9 %collective-permute-start.9 = (bf16[32,1152]{1,0:T(8,128)(2,1)S(1)}, bf16[32,1152]{1,0:T(8,128)(2,1)S(1)}, u32[]{:S(2)}, u32[]{:S(2)}) collective-permute-start(bf16[32,1152]{1,0:T(8,128)(2,1)S(1)} %add_convert_fusion.2.piece_0), channel_id=1, source_target_pairs={{0,1},{1,2},{2,3},{3,0},{4,5},{5,6},{6,7},{7,4},{8,9},{9,10},{10,1... | collective-permute-start | bytes 221192 | tf_op jit(solution)/shard_map/ppermute | solution.py:886
  64.4 20.5 %collective-permute-start.12 = (bf16[2304,128]{1,0:T(8,128)(2,1)S(1)}, bf16[2304,128]{1,0:T(8,128)(2,1)S(1)}, u32[]{:S(2)}, u32[]{:S(2)}) collective-permute-start(bf16[2304,128]{1,0:T(8,128)(2,1)S(1)} %copy-done.1), channel_id=1, source_target_pairs={{0,8},{4,12},{8,0},{12,4},{16,24},{20,28},{24,16},{28,20},{1,9},{5... | collective-permute-start | bytes 1769480 | tf_op jit(solution)/shard_map/ppermute | solution.py:905
  89.3 21.5 %collective-permute-start.13 = (bf16[2304,128]{1,0:T(8,128)(2,1)S(1)}, bf16[2304,128]{1,0:T(8,128)(2,1)S(1)}, u32[]{:S(2)}, u32[]{:S(2)}) collective-permute-start(bf16[2304,128]{1,0:T(8,128)(2,1)S(1)} %copy-done.1), channel_id=1, source_target_pairs={{0,16},{4,20},{8,24},{12,28},{16,0},{20,4},{24,8},{28,12},{1,17},{... | collective-permute-start | bytes 1769480 | tf_op jit(solution)/shard_map/ppermute | solution.py:905
  90.8 19.9 %all-to-all-start.2 = ((bf16[8,32,1152]{2,1,0:T(8,128)(2,1)}), bf16[8,32,1152]{2,1,0:T(8,128)(2,1)S(1)}, u32[]{:S(2)}, u32[]{:S(2)}) async-start(bf16[8,32,1152]{2,1,0:T(8,128)(2,1)} %bitcast.21), calls=%async_computation.2 | async-start | bytes 1179648 | tf_op jit(solution)/shard_map/all_to_all | solution.py:954
  111.6 130.8 %all-to-all-start.3 = ((bf16[8,336,768]{2,1,0:T(8,128)(2,1)}), bf16[8,336,768]{2,1,0:T(8,128)(2,1)}, u32[]{:S(2)}, u32[]{:S(2)}) async-start(bf16[8,336,768]{2,1,0:T(8,128)(2,1)} %shard_map.286), calls=%async_computation.3 | async-start | bytes 8257536 | tf_op jit(solution)/shard_map/all_to_all | solution.py:954
  158.3 23.5 %collective-permute-start.30 = (bf16[2304,128]{1,0:T(8,128)(2,1)}, bf16[2304,128]{1,0:T(8,128)(2,1)S(1)}, u32[]{:S(2)}, u32[]{:S(2)}) collective-permute-start(bf16[2304,128]{1,0:T(8,128)(2,1)} %get-tuple-element.147.refs_0_), channel_id=1, source_target_pairs={{0,16},{4,20},{8,24},{12,28},{16,0},{20,4},{24,8},{28,12},{1,17},{... | collective-permute-start | bytes 1769480 | tf_op jit(solution)/shard_map/ppermute | solution.py:905
  160.0 21.8 %collective-permute-start.29 = (bf16[2304,128]{1,0:T(8,128)(2,1)}, bf16[2304,128]{1,0:T(8,128)(2,1)S(1)}, u32[]{:S(2)}, u32[]{:S(2)}) collective-permute-start(bf16[2304,128]{1,0:T(8,128)(2,1)} %get-tuple-element.147.refs_0_), channel_id=1, source_target_pairs={{0,8},{4,12},{8,0},{12,4},{16,24},{20,28},{24,16},{28,20},{1,9},{5... | collective-permute-start | bytes 1769480 | tf_op jit(solution)/shard_map/ppermute | solution.py:905
  161.5 21.3 %collective-permute-start.39 = (bf16[2304,128]{1,0:T(8,128)(2,1)S(1)}, bf16[2304,128]{1,0:T(8,128)(2,1)S(1)}, u32[]{:S(2)}, u32[]{:S(2)}) collective-permute-start(bf16[2304,128]{1,0:T(8,128)(2,1)S(1)} %copy-done.1), channel_id=1, source_target_pairs={{0,4},{4,0},{8,12},{12,8},{16,20},{20,16},{24,28},{28,24},{1,5},{5... | collective-permute-start | bytes 1769480 | tf_op jit(solution)/shard_map/ppermute | solution.py:905
  162.6 20.2 %collective-permute-start.40 = (bf16[2304,128]{1,0:T(8,128)(2,1)S(1)}, bf16[2304,128]{1,0:T(8,128)(2,1)S(1)}, u32[]{:S(2)}, u32[]{:S(2)}) collective-permute-start(bf16[2304,128]{1,0:T(8,128)(2,1)S(1)} %collective-permute-done.12.refs_1_), channel_id=1, source_target_pairs={{0,4},{4,0},{8,12},{12,8},{16,20},{20,16},{24,28},{28,24},{1,5},{5... | collective-permute-start | bytes 1769480 | tf_op jit(solution)/shard_map/ppermute | solution.py:905
  181.8 24.5 %collective-permute-start.38 = (bf16[2304,128]{1,0:T(8,128)(2,1)S(1)}, bf16[2304,128]{1,0:T(8,128)(2,1)S(1)}, u32[]{:S(2)}, u32[]{:S(2)}) collective-permute-start(bf16[2304,128]{1,0:T(8,128)(2,1)S(1)} %collective-permute-done.13.refs_2_), channel_id=1, source_target_pairs={{0,8},{4,12},{8,0},{12,4},{16,24},{20,28},{24,16},{28,20},{1,9},{5... | collective-permute-start | bytes 1769480 | tf_op jit(solution)/shard_map/ppermute | solution.py:905
  182.5 24.3 %collective-permute-start.43 = (bf16[2304,128]{1,0:T(8,128)(2,1)S(1)}, bf16[2304,128]{1,0:T(8,128)(2,1)S(1)}, u32[]{:S(2)}, u32[]{:S(2)}) collective-permute-start(bf16[2304,128]{1,0:T(8,128)(2,1)S(1)} %collective-permute-done.29.refs_1_), channel_id=1, source_target_pairs={{0,16},{4,20},{8,24},{12,28},{16,0},{20,4},{24,8},{28,12},{1,17},{... | collective-permute-start | bytes 1769480 | tf_op jit(solution)/shard_map/ppermute | solution.py:905
  182.8 19.5 %collective-permute-start.33 = (bf16[768,128]{1,0:T(8,128)(2,1)}, bf16[768,128]{1,0:T(8,128)(2,1)S(1)}, u32[]{:S(2)}, u32[]{:S(2)}) collective-permute-start(bf16[768,128]{1,0:T(8,128)(2,1)} %get-tuple-element.150.refs_0_), channel_id=1, source_target_pairs={{0,24},{4,28},{8,16},{12,20},{16,8},{20,12},{24,0},{28,4},{1,25},{... | collective-permute-start | bytes 589832 | tf_op jit(solution)/shard_map/ppermute | solution.py:905
  185.5 20.3 %collective-permute-start.32 = (bf16[768,128]{1,0:T(8,128)(2,1)}, bf16[768,128]{1,0:T(8,128)(2,1)S(1)}, u32[]{:S(2)}, u32[]{:S(2)}) collective-permute-start(bf16[768,128]{1,0:T(8,128)(2,1)} %get-tuple-element.150.refs_0_), channel_id=1, source_target_pairs={{0,16},{4,20},{8,24},{12,28},{16,0},{20,4},{24,8},{28,12},{1,17},{... | collective-permute-start | bytes 589832 | tf_op jit(solution)/shard_map/ppermute | solution.py:905
  186.0 19.7 %collective-permute-start.31 = (bf16[768,128]{1,0:T(8,128)(2,1)}, bf16[768,128]{1,0:T(8,128)(2,1)}, u32[]{:S(2)}, u32[]{:S(2)}) collective-permute-start(bf16[768,128]{1,0:T(8,128)(2,1)} %get-tuple-element.150.refs_0_), channel_id=1, source_target_pairs={{0,8},{4,12},{8,0},{12,4},{16,24},{20,28},{24,16},{28,20},{1,9},{5... | collective-permute-start | bytes 589832 | tf_op jit(solution)/shard_map/ppermute | solution.py:905
  207.8 19.8 %collective-permute-start.36 = (bf16[768,128]{1,0:T(8,128)(2,1)S(1)}, bf16[768,128]{1,0:T(8,128)(2,1)}, u32[]{:S(2)}, u32[]{:S(2)}) collective-permute-start(bf16[768,128]{1,0:T(8,128)(2,1)S(1)} %collective-permute-done.32.refs_2_), channel_id=1, source_target_pairs={{0,4},{4,0},{8,12},{12,8},{16,20},{20,16},{24,28},{28,24},{1,5},{5... | collective-permute-start | bytes 589832 | tf_op jit(solution)/shard_map/ppermute | solution.py:905
  208.6 19.0 %collective-permute-start.35 = (bf16[768,128]{1,0:T(8,128)(2,1)}, bf16[768,128]{1,0:T(8,128)(2,1)S(1)}, u32[]{:S(2)}, u32[]{:S(2)}) collective-permute-start(bf16[768,128]{1,0:T(8,128)(2,1)} %collective-permute-done.31.refs_1_), channel_id=1, source_target_pairs={{0,4},{4,0},{8,12},{12,8},{16,20},{20,16},{24,28},{28,24},{1,5},{5... | collective-permute-start | bytes 589832 | tf_op jit(solution)/shard_map/ppermute | solution.py:905
  209.5 27.9 %collective-permute-start.26 = (bf16[304,128]{1,0:T(8,128)(2,1)}, bf16[304,128]{1,0:T(8,128)(2,1)S(1)}, u32[]{:S(2)}, u32[]{:S(2)}) collective-permute-start(bf16[304,128]{1,0:T(8,128)(2,1)} %get-tuple-element.140), channel_id=1, source_target_pairs={{0,1},{1,2},{2,3},{3,0},{4,5},{5,6},{6,7},{7,4},{8,9},{9,10},{10,1... | collective-permute-start | bytes 233480 | tf_op jit(solution)/shard_map/ppermute | solution.py:886
  210.9 28.3 %collective-permute-start.27 = (bf16[304,128]{1,0:T(8,128)(2,1)}, bf16[304,128]{1,0:T(8,128)(2,1)S(1)}, u32[]{:S(2)}, u32[]{:S(2)}) collective-permute-start(bf16[304,128]{1,0:T(8,128)(2,1)} %get-tuple-element.141), channel_id=1, source_target_pairs={{0,2},{1,3},{2,0},{3,1},{4,6},{5,7},{6,4},{7,5},{8,10},{9,11},{10,... | collective-permute-start | bytes 233480 | tf_op jit(solution)/shard_map/ppermute | solution.py:886
  211.7 27.5 %collective-permute-start.28 = (bf16[304,128]{1,0:T(8,128)(2,1)}, bf16[304,128]{1,0:T(8,128)(2,1)S(1)}, u32[]{:S(2)}, u32[]{:S(2)}) collective-permute-start(bf16[304,128]{1,0:T(8,128)(2,1)} %get-tuple-element.142), channel_id=1, source_target_pairs={{0,3},{1,0},{2,1},{3,2},{4,7},{5,4},{6,5},{7,6},{8,11},{9,8},{10,9... | collective-permute-start | bytes 233480 | tf_op jit(solution)/shard_map/ppermute | solution.py:886
  235.2 13.2 %collective-permute-start.50 = (f32[1,1152]{1,0:T(1,128)}, f32[1,1152]{1,0:T(1,128)S(1)}, u32[]{:S(2)}, u32[]{:S(2)}) collective-permute-start(f32[1,1152]{1,0:T(1,128)} %get-tuple-element.156), channel_id=1, source_target_pairs={{0,3},{1,0},{2,1},{3,2},{4,7},{5,4},{6,5},{7,6},{8,11},{9,8},{10,9... | collective-permute-start | bytes 13832 | tf_op jit(solution)/shard_map/ppermute | solution.py:886
  237.1 12.6 %collective-permute-start.49 = (f32[1,1152]{1,0:T(1,128)}, f32[1,1152]{1,0:T(1,128)S(1)}, u32[]{:S(2)}, u32[]{:S(2)}) collective-permute-start(f32[1,1152]{1,0:T(1,128)} %get-tuple-element.156), channel_id=1, source_target_pairs={{0,2},{1,3},{2,0},{3,1},{4,6},{5,7},{6,4},{7,5},{8,10},{9,11},{10,... | collective-permute-start | bytes 13832 | tf_op jit(solution)/shard_map/ppermute | solution.py:886
  237.4 12.3 %collective-permute-start.48 = (f32[1,1152]{1,0:T(1,128)}, f32[1,1152]{1,0:T(1,128)S(1)}, u32[]{:S(2)}, u32[]{:S(2)}) collective-permute-start(f32[1,1152]{1,0:T(1,128)} %get-tuple-element.156), channel_id=1, source_target_pairs={{0,1},{1,2},{2,3},{3,0},{4,5},{5,6},{6,7},{7,4},{8,9},{9,10},{10,1... | collective-permute-start | bytes 13832 | tf_op jit(solution)/shard_map/ppermute | solution.py:886
  (75 other events, 801.4 us)

commit v3 on v2

--- a/solution.py
+++ b/solution.py
@@ -15,30 +15,74 @@
 LOG2E = 1.4426950408889634
 GELU_SCALE = math.sqrt(2.0 / math.pi)
 GELU_CUBE = 0.044715
-VMEM_BYTES = 56 * 1024 * 1024
+VMEM_SPARE = 6 * 1024 * 1024
 NEAR_GROUPS = 8
 VECTORS_ONE = 24
 VECTORS_TWO = 8
 
 
-def run_kernel(kernel, outs, args, scratch=(), scalars=0, far_args=(), far_outs=(), alias=None):
+def run_kernel(
+    kernel,
+    outs,
+    args,
+    scratch=(),
+    scalars=0,
+    far_args=(),
+    staged=(),
+    far_outs=(),
+    loose_outs=(),
+    held_outs=(),
+    alias=None,
+):
+    staged = tuple(staged)
+    outside = {*far_args, *staged}
+
     def spec(index, far):
-        return pl.BlockSpec(memory_space=pl.ANY if index in far else pltpu.VMEM)
-
+        return pl.BlockSpec(memory_space=pltpu.HBM if index in far else pltpu.VMEM)
+
+    def held(index, shape, dtype):
+        if index in loose_outs:
+            return jax.ShapeDtypeStruct(shape, dtype)
+        return (pltpu.VMEM if index in held_outs else pltpu.HBM)(shape, dtype)
+
+    def body(*refs):
+        refs = list(refs)
+        if staged:
+            *refs, semaphores = refs
+            places = refs[len(refs) - len(staged) :]
+            refs = refs[: len(refs) - len(staged)]
+            copies = run_copies(list(zip([refs[index] for index in staged], places)), semaphores)
+            for index, place in zip(staged, places):
+                refs[index] = place
+            for copy in copies:
+                copy.wait()
+        kernel(*refs)
+
+    sizes = [(arg.shape, arg.dtype) for index, arg in enumerate(args) if index not in far_args]
+    sizes += [out for index, out in enumerate(outs) if index not in far_outs]
+    sizes += [shape for shape in scratch if isinstance(shape, tuple)]
+    scratch = [pltpu.VMEM(*shape) if isinstance(shape, tuple) else shape for shape in scratch]
+    if staged:
+        scratch += [pltpu.VMEM(args[index].shape, args[index].dtype) for index in staged]
+        scratch += [pltpu.SemaphoreType.DMA((len(staged),))]
+    needed = sum(math.prod(shape) * jnp.dtype(dtype).itemsize for shape, dtype in sizes)
     return pl.pallas_call(
-        kernel,
-        out_shape=[jax.ShapeDtypeStruct(shape, dtype) for shape, dtype in outs],
+        body,
+        out_shape=[held(index, shape, dtype) for index, (shape, dtype) in enumerate(outs)],
         in_specs=[
-            pl.BlockSpec(memory_space=pltpu.SMEM) if index < scalars else spec(index, far_args)
+            pl.BlockSpec(memory_space=pltpu.SMEM) if index < scalars else spec(index, outside)
             for index in range(len(args))
         ],
         out_specs=[spec(index, far_outs) for index in range(len(outs))],
-        scratch_shapes=[
-            shape if not isinstance(shape, tuple) else pltpu.VMEM(*shape) for shape in scratch
-        ],
+        scratch_shapes=scratch,
         input_output_aliases=alias or {},
-        compiler_params=pltpu.CompilerParams(vmem_limit_bytes=VMEM_BYTES),
-    )(*args)
+        compiler_params=pltpu.CompilerParams(vmem_limit_bytes=VMEM_SPARE + needed * 5 // 4),
+    )(
+        *[
+            pltpu.with_memory_space_constraint(arg, pltpu.HBM) if index in outside else arg
+            for index, arg in enumerate(args)
+        ]
+    )
 
 
 def dot_nn(left, right):
@@ -199,18 +243,27 @@
     choose,
     message,
     packed,
+    staged,
+    arrivals,
     semaphores,
 ):
     experts, share, units = expert_in.shape
     length, width = cotangent.shape
     copies = []
     for index in range(experts):
-        target = message.at[index]
-        copies.append((expert_in.at[index], target.at[pl.ds(0, share)]))
-        copies.append((expert_out.at[index], target.at[pl.ds(share, share)]))
-    started = run_copies(copies, semaphores)
+        copies.append((expert_in.at[index], staged.at[index, 0]))
+        copies.append((expert_out.at[index], staged.at[index, 1]))
+    arriving = run_copies(copies, arrivals)
     fill_choose(capacity, length, experts, routes, choose)
     slots = dot_nn(choose[...], cotangent[...]).astype(BF16)
+    started = []
+    for index in range(experts):
+        copies = []
+        for which in range(2):
+            arriving[2 * index + which].wait()
+            target = message.at[index, pl.ds(which * share, share)]
+            copies.append((staged.at[index, which], target))
+        started += run_copies(copies, semaphores.at[pl.ds(2 * index, 2)])
     copies = []
     for index in range(experts):
         put_folded(packed.at[index], slots[index * capacity : (index + 1) * capacity])
@@ -222,7 +275,19 @@
         copy.wait()
 
 
-def unpack_kernel(share, capacity, message, first_w, second_w, grad_slots, d_hidden, semaphores):
+def unpack_kernel(
+    share,
+    capacity,
+    message,
+    first_out,
+    second_out,
+    slots_out,
+    d_hidden,
+    first_w,
+    second_w,
+    grad_slots,
+    semaphores,
+):
     folded = capacity + capacity // 2
     copies = []
     for index in range(message.shape[0]):
@@ -235,7 +300,11 @@
         copies.append((piece.at[pl.ds(0, share)], first_w.at[rows]))
     for copy in run_copies(copies, semaphores):
         copy.wait()
+    copies = [(first_w, first_out), (second_w, second_out), (grad_slots, slots_out)]
+    started = run_copies(copies, semaphores)
     d_hidden[...] = dot_nn(grad_slots[...], second_w[...])
+    for copy in started:
+        copy.wait()
 
 
 def put_blocks(target, values):
@@ -475,14 +544,16 @@
     put_row_chunks(place, partial, (out_0, out_1, out_2, out_3))
 
 
-def back_columns_kernel(place, choose, slots, out_0, out_1, out_2, out_3, turned):
-    turned[...] = dot_tn(slots[...], choose[...])
-    put_row_chunks(place, turned, (out_0, out_1, out_2, out_3))
-
-
-def back_folded_kernel(
-    share, place, choose, message, out_0, out_1, out_2, out_3, slots, turned, semaphores
-):
+def back_columns_kernel(choose, shares, slots, out):
+    rows = dot_tn(slots[...], choose[...]).astype(BF16)
+    count, top, _ = shares.shape
+    column = rows.shape[0] // count
+    for index in range(count):
+        out[index, :top, :] = shares[index]
+        out[index, top:, :] = rows[index * column : (index + 1) * column]
+
+
+def back_folded_kernel(share, choose, shares, message, out, slots, semaphores):
     count = message.shape[0]
     capacity = slots.shape[0] // count
     folded = message.shape[1] - 2 * share
@@ -493,7 +564,28 @@
         )
     for copy in run_copies(copies, semaphores):
         copy.wait()
-    back_columns_kernel(place, choose, slots, out_0, out_1, out_2, out_3, turned)
+    back_columns_kernel(choose, shares, slots, out)
+
+
+def late_vectors_kernel(refs, weight_grad, bias_grad, norm_out, staged, semaphores):
+    deep = 2 * VECTORS_TWO
+    rows = staged.shape[1]
+    top = refs[0].shape[0] - rows
+    copies = [(ref.at[pl.ds(top, rows)], staged.at[index]) for index, ref in enumerate(refs)]
+    for copy in run_copies(copies, semaphores):
+        copy.wait()
+    total = staged[0].astype(F32)
+    for index in range(1, staged.shape[0]):
+        total = total + staged[index].astype(F32)
+    chans = weight_grad.shape[1]
+    vectors = jnp.concatenate(
+        [total[start : start + deep] for start in range(0, rows, deep)], axis=1
+    )[:, :chans]
+    vectors = vectors[:VECTORS_TWO] + vectors[VECTORS_TWO:]
+    weight_grad[...] = vectors[:4]
+    bias_grad[...] = vectors[4].reshape(chans)
+    norm_grad = jnp.concatenate([vectors[5:6], vectors[6:7]], axis=1)
+    norm_out[...] = norm_grad
 
 
 def mixer_grad_kernel(
@@ -689,10 +781,7 @@
     in_proj,
     rows_in,
     gain,
-    out_0,
-    out_1,
-    out_2,
-    out_3,
+    shares,
     message,
     held,
     turned,
@@ -756,25 +845,25 @@
     high = along.astype(BF16)
     low = (along - high.astype(F32)).astype(BF16)
     turned[...] = d_normed.T
-    outs = (out_0, out_1, out_2, out_3)
-    put_row_chunks(place, turned, outs)
-    column = width // len(outs)
-    for out in outs:
-        out[column:, :] = jnp.concatenate([high, low], axis=0)
-
-
-def finish_rows_kernel(
-    piece_0, piece_1, piece_2, piece_3, d_columns, tokens, scale, gain, grad_tokens
-):
+    count, rows, _ = shares.shape
+    column = width // count
+    ends = jnp.concatenate([high, low], axis=0)
+    for index in range(count):
+        shares[index, :column, :] = turned[index * column : (index + 1) * column].astype(BF16)
+        shares[index, column:, :] = ends
+
+
+def finish_rows_kernel(pieces, residual, d_columns, tokens, scale, gain, outcome, grad_tokens):
     column = tokens.shape[0]
-    total = piece_0[...].astype(F32)
-    for piece in (piece_1, piece_2, piece_3):
-        total = total + piece[...].astype(F32)
+    total = pieces[0].astype(F32)
+    for index in range(1, pieces.shape[0]):
+        total = total + pieces[index].astype(F32)
     along = total[column : column + 1] + total[column + 8 : column + 9]
     inverse = scale[...]
     pulled = total[:column] * gain[...]
     scaled = tokens[...].astype(F32) * inverse
     grad_tokens[...] = d_columns[...] + inverse * (pulled - scaled * along)
+    outcome[...] = (residual[...] + total[column + 16 :]).astype(BF16)
 
 
 def take_blocks(target, pieces):
@@ -791,9 +880,25 @@
         target[:, index * 128 : (index + 1) * 128] = piece[start : start + rows]
 
 
-def first_sets_kernel(firsts, normed, gated, acts):
+def stage_pieces(refs, staged, semaphores, rows=None):
+    copies = []
+    parts = len(refs) // 2
+    for index, ref in enumerate(refs):
+        side, part = divmod(index, parts)
+        target = staged.at[4 * side + min(part, 3)]
+        if part >= 3 and parts > 4:
+            height = staged.shape[1] // (parts - 3)
+            target = target.at[pl.ds((part - 3) * height, height)]
+        copies.append((ref if rows is None else ref.at[pl.ds(*rows)], target))
+    return run_copies(copies, semaphores), [staged.at[index] for index in range(8)]
+
+
+def first_sets_kernel(refs, normed, gated, acts, staged, semaphores):
     chans = gated.shape[0]
     width = normed.shape[1]
+    arriving, firsts = stage_pieces(refs, staged, semaphores)
+    for copy in arriving:
+        copy.wait()
     take_blocks(normed, firsts)
     take_turned(gated, firsts, width)
     take_turned(acts, firsts, width + chans)
@@ -801,30 +906,54 @@
 
 def wide_grads_kernel(
     sizes,
-    seconds,
+    second_refs,
+    last_refs,
     normed,
     gated,
+    acts,
     out_grad,
     in_grad,
+    x_grad,
     dt_grad,
     bias_grad,
     decay_grad,
     skip_grad,
     norm_grad,
+    staged,
+    staged_last,
     mixed,
     d_gate,
+    d_mixed,
     total,
-    gate_grad,
-    semaphore,
+    wide_grad,
+    second_arrivals,
+    last_arrivals,
+    semaphores,
 ):
-    rank, states = sizes
+    rank, states, proj = sizes
     chans, width = out_grad.shape
+    arriving_last, lasts = stage_pieces(last_refs, staged_last, last_arrivals)
+    arriving, seconds = stage_pieces(second_refs, staged, second_arrivals)
+    for copy in arriving_last:
+        copy.wait()
+    take_turned(d_gate, lasts, 0)
+    wide_grad[0] = dot_nn(d_gate[...], normed[...])
+    started = run_copies([(wide_grad.at[0], in_grad.at[0])], semaphores)
+    take_turned(d_mixed, lasts, chans)
+    x_grad[...] = dot_nt(d_mixed[...], acts[...])[:proj]
+    for copy in arriving:
+        copy.wait()
     take_turned(d_gate, seconds, width)
-    gate_grad[...] = dot_nn(d_gate[...], normed[...])
-    last = pltpu.make_async_copy(gate_grad, in_grad.at[1], semaphore)
-    last.start()
+    wide_grad[1] = dot_nn(d_gate[...], normed[...])
+    started += run_copies([(wide_grad.at[1], in_grad.at[1])], semaphores.at[pl.ds(1, 1)])
     take_blocks(mixed, seconds)
-    out_grad[...] = dot_nn(gated[...], mixed[...])
+    half = chans // 2
+    for index in range(2):
+        rows = pl.ds(index * half, half)
+        wide_grad[2, rows] = dot_nn(gated[rows], mixed[...])
+        started += run_copies(
+            [(wide_grad.at[2, rows], out_grad.at[rows])], semaphores.at[pl.ds(2 + index, 1)]
+        )
     vectors = seconds[0][width + chans :].astype(F32)
     for piece in seconds[1:]:
         vectors = vectors + piece[width + chans :].astype(F32)
@@ -839,45 +968,8 @@
     norm_grad[...] = jnp.concatenate(
         [rows[states + 2 : states + 3], rows[states + 3 : states + 4]], axis=1
     )
-    last.wait()
-
-
-def late_grads_kernel(
-    widths,
-    lasts,
-    normed,
-    acts,
-    kept_grad,
-    in_grad,
-    x_grad,
-    weight_grad,
-    bias_grad,
-    norm_grad,
-    d_inner,
-    d_mixed,
-    inner_grad,
-    semaphore,
-):
-    chans, proj = widths
-    rows = d_mixed.shape[0]
-    take_turned(d_inner, lasts, 0)
-    inner_grad[...] = dot_nn(d_inner[...], normed[...])
-    last = pltpu.make_async_copy(inner_grad, in_grad.at[0], semaphore)
-    last.start()
-    take_turned(d_mixed, lasts, chans)
-    x_grad[...] = dot_nt(d_mixed[...], acts[...])[:proj]
-    total = lasts[0][chans + rows :].astype(F32)
-    for piece in lasts[1:]:
-        total = total + piece[chans + rows :].astype(F32)
-    deep = 2 * VECTORS_TWO
-    vectors = jnp.concatenate(
-        [total[start : start + deep] for start in range(0, total.shape[0], deep)], axis=1
-    )[:, :chans]
-    vectors = vectors[:VECTORS_TWO] + vectors[VECTORS_TWO:]
-    weight_grad[...] = vectors[:4]
-    bias_grad[...] = vectors[4].reshape(chans)
-    norm_grad[...] = jnp.concatenate([vectors[5:6], vectors[6:7]], axis=1)
-    last.wait()
+    for copy in started:
+        copy.wait()
 
 
 def send_chunks(chunks):
@@ -905,8 +997,17 @@
     return lax.ppermute(values, "dp", [(i, i ^ bits) for i in range(NEAR_GROUPS)])
 
 
-def swap_near(fars):
-    return [*fars, *[swap(far, 1) for far in fars]]
+def split_beside(along_x, along_y):
+    half = along_x.shape[0] // 2
+    return along_y[:half], along_x[half:]
+
+
+def swap_across(halves):
+    return [swap(halves[0], 2), swap(halves[1], 4)]
+
+
+def swap_near(values):
+    return [*values, *[swap(part, 1) for part in values]]
 
 
 def body(
@@ -971,23 +1072,18 @@
             [resets_row, routes_row, cotangent, expert_in, expert_out],
             [
                 ((groups, folded, hidden_units), BF16),
+                ((experts, 2, share, hidden_units), BF16),
+                pltpu.SemaphoreType.DMA((2 * experts,)),
                 pltpu.SemaphoreType.DMA((3 * experts,)),
             ],
-            far_outs=(2,),
-        )
-        first_w, second_w, grad_slots, d_hidden = run_kernel(
-            functools.partial(unpack_kernel, share, capacity),
-            weight_outs + [slots_out, ((slot_count, hidden_units), F32)],
-            [exchange(packed)],
-            [pltpu.SemaphoreType.DMA((5 * groups,))],
-            far_args=(0,),
-        )
+            far_args=(3, 4),
+            far_outs=(2,), staged=(0, 1, 2))
+        weights = exchange(packed)
     else:
         masks, choose, grad_send = run_kernel(
             functools.partial(prepare_kernel, experts, capacity, block_rows),
             [mask_out, choose_out, slots_out],
-            [resets_row, routes_row, cotangent],
-        )
+            [resets_row, routes_row, cotangent], loose_outs=(2,))
         first_w = exchange(jnp.tile(expert_in, (tile_count, 1, 1))).reshape(weight_outs[0][0])
         second_w = exchange(jnp.tile(expert_out, (tile_count, 1, 1))).reshape(weight_outs[0][0])
         grad_slots = exchange_slots(grad_send)
@@ -1010,8 +1106,7 @@
         ],
         [place, *token_pieces, norm_one, in_turned, conv_weight, conv_bias, x_turned, masks],
         [((width, length), F32)],
-        scalars=1,
-    )
+        scalars=1, loose_outs=(8,), staged=(1, 2, 3, 4, 10))
     mixed_pieces = share_rows(mixed_part, parts)
     *mix_chunks, mixed, first, y = run_kernel(
         scan_forward_kernel,
@@ -1042,23 +1137,28 @@
             ((length, full), F32),
             ((length, width), F32),
         ],
-        scalars=1,
-    )
+        scalars=1, loose_outs=(0, 1, 2, 3, 5), staged=(1, 2, 3, 4, 9, 10, 11, 13))
     mixer_pieces = share_rows(add_low(send_chunks(mix_chunks)), parts)
+    if near:
+        first_x, first_y = swap(first, 2), swap(first, 4)
     residual, residual_columns, send_slots = run_kernel(
         dispatch_kernel,
         [((length, width), F32), ((column, length), F32), slots_out],
         [place, *mixer_pieces, rows, norm_two, choose],
         [((width, length), F32)],
-        scalars=1,
-    )
+        scalars=1, loose_outs=(2,), staged=(1, 2, 3, 4, 5, 7))
+    if near:
+        first_w, second_w, grad_slots, d_hidden = run_kernel(
+            functools.partial(unpack_kernel, share, capacity),
+            weight_outs + [slots_out, ((slot_count, hidden_units), F32)],
+            after([weights], send_slots, first_x, first_y),
+            [*weight_outs, slots_out, pltpu.SemaphoreType.DMA((5 * groups,))],
+            far_args=(0,),
+            far_outs=(0, 1, 2),
+        )
     arrived = exchange_slots(send_slots)
-    if near:
-        first_x = swap(after([first], d_hidden)[0], 2)
-        arrived = after([arrived], first_x)[0]
     hidden, d_pre, d_slots = run_kernel(
-        expert_kernel, [hidden_out, hidden_out, slots_out], [arrived, first_w, d_hidden]
-    )
+        expert_kernel, [hidden_out, hidden_out, slots_out], [arrived, first_w, d_hidden], loose_outs=(2,), staged=(0, 1, 2))
     back_slots = exchange_slots(d_slots)
     grad_args = [arrived, grad_slots, hidden, d_pre, second_w]
     grad_out = ((experts, share, hidden_units), F32)
@@ -1072,24 +1172,25 @@
                 ((groups, folded, hidden_units), BF16),
                 pltpu.SemaphoreType.DMA((3 * groups,)),
             ],
-            far_outs=(0,),
-        )
-        first_y = swap(after([first], hidden)[0], 4)
-        packed, back_slots = after([packed, back_slots], first_y)
-        back_slots = after([back_slots], packed)[0]
+            far_outs=(0,), staged=range(5))
+        first_d = swap_across(split_beside(*after([first_x, first_y], arrived)))
+        back_slots = after([back_slots], packed, first_d)[0]
+        packed = after([packed], back_slots)[0]
         owned = exchange(packed)
     else:
         grad_first, grad_second, moe_slots = run_kernel(
-            expert_grads_kernel, weight_outs + [slots_out], grad_args
-        )
+            expert_grads_kernel, weight_outs + [slots_out], grad_args, loose_outs=(0, 1, 2))
     back_chunks = run_kernel(
         back_rows_kernel,
         [((length // parts, width), BF16)] * parts,
         [place, choose, back_slots],
         [((length, width), F32)],
-        scalars=1,
-    )
+        scalars=1, loose_outs=(0, 1, 2, 3), staged=(1, 2))
     send_pieces = share_rows(add_low(send_chunks(back_chunks)), parts)
+    if near:
+        firsts = swap_near([first, first_x, first_y, *first_d])
+
+        send_pieces = after(send_pieces, firsts)
     d_columns, d_mix, d_gated, gain_grad_two = run_kernel(
         mixer_grad_kernel,
         [
@@ -1100,8 +1201,7 @@
         ],
         [place, *send_pieces, residual, norm_two, cotangent, out_proj],
         [((length, width), F32), ((width, length), F32)],
-        scalars=1,
-    )
+        scalars=1, staged=(1, 2, 3, 4, 5, 7, 8), held_outs=(1, 2, 3))
     d_mixed_part, d_act_scan, d_gate, second = run_kernel(
         scan_backward_kernel,
         [
@@ -1134,16 +1234,14 @@
             ((length, full), F32),
             ((length * states, full), F32),
             (((length + 1) * states, full), F32),
-        ],
-    )
+        ], loose_outs=(0, 3), staged=(1, 2, 3, 4, 5, 6), held_outs=(1, 2))
     d_mixed_pieces = share_rows(d_mixed_part, parts)
     if near:
         second_x, second_y = swap(second, 2), swap(second, 4)
     last_rows = chans + -(-proj // 16) * 16 + tiles * 2 * VECTORS_TWO
-    *normed_chunks, message = run_kernel(
+    normed_shares, message = run_kernel(
         leave_kernel,
-        [((column + 16, length), BF16)] * parts
-        + [((last_rows, length), BF16)],
+        [((parts, column + 16, length), BF16), ((last_rows, length), BF16)],
         [
             place,
             *d_mixed_pieces,
@@ -1159,29 +1257,22 @@
             norm_one,
         ],
         [((parts, proj, length), BF16), ((width, length), F32), ((length, full), F32)],
-        scalars=1,
-    )
-    normed_pieces = send_chunks(normed_chunks)
-    (grad_tokens,) = run_kernel(
-        finish_rows_kernel,
-        [((column, length), F32)],
-        [*normed_pieces, d_columns, tokens_turned, scale, gain_columns],
-    )
-
-    chunk_outs = [((column, length), BF16)] * parts
+        scalars=1, loose_outs=(0, 1), staged=(1, 2, 3, 4, 7, 8, 9, 13))
+    shares_out = ((parts, 2 * column + 16, length), BF16)
     if near:
-        moe_chunks = run_kernel(
+        (shares,) = run_kernel(
             functools.partial(back_folded_kernel, share),
-            chunk_outs,
-            [place, choose, owned],
-            [slots_out, ((width, length), F32), pltpu.SemaphoreType.DMA((3 * groups,))],
-            scalars=1,
+            [shares_out],
+            [choose, normed_shares, owned],
+            [slots_out, pltpu.SemaphoreType.DMA((3 * groups,))],
+            staged=(0,),
             far_args=(2,),
+            loose_outs=(0,),
         )
         grad_expert_in, grad_expert_out = run_kernel(
             functools.partial(owner_kernel, share),
             [grad_out] * 2,
-            [owned],
+            after([owned], shares),
             [
                 ((groups, 2 * share, hidden_units), BF16),
                 ((groups, 2 * share, hidden_units), F32),
@@ -1191,33 +1282,16 @@
             far_args=(0,),
             far_outs=(0, 1),
         )
-    else:
-        moe_chunks = run_kernel(
-            back_columns_kernel,
-            chunk_outs,
-            [place, choose, exchange_slots(moe_slots)],
-            [((width, length), F32)],
-            scalars=1,
-        )
-
-        def owner_sum(values):
-            got = exchange(values.reshape(groups, share, hidden_units)).astype(F32)
-            return jnp.sum(got.reshape(tile_count, experts, share, hidden_units), axis=0)
-
-        grad_expert_in = owner_sum(grad_first)
-        grad_expert_out = owner_sum(grad_second)
-    outcome = residual_columns
-    for piece in send_chunks(moe_chunks):
-        outcome = outcome + piece.astype(F32)
-    outcome = outcome.astype(BF16)
-
-    if near:
-        first_y, second_x, second_y = after([first_y, second_x, second_y], message)
-        firsts = swap_near([first, first_x, first_y, swap(first_y, 2)])
-        seconds = swap_near([second, second_x, second_y, swap(second_x, 4)])
+        second, second_x, second_y = after([second, second_x, second_y], grad_expert_in)
+        halves = split_beside(second_x, second_y)
+        last = after([message], second_x, second_y)[0]
+        lasts = [last, swap(last, 2), swap(last, 4), swap(last, 6)]
+        second_d = swap_across(halves)
+        *seconds, near_own, near_x, near_y = swap_near([second, second_x, second_y])
+        firsts = after(firsts, halves, near_own, near_x, near_y)
 
         def first_sets(*refs):
-            first_sets_kernel(refs[:groups], *refs[groups:])
+            first_sets_kernel(refs[:10], *refs[10:])
 
         all_normed, all_gated, all_act = run_kernel(
             first_sets,
@@ -1227,14 +1301,64 @@
                 ((chans, groups * length), BF16),
             ],
             firsts,
-        )
+            [((groups, width + 2 * chans, length), BF16), pltpu.SemaphoreType.DMA((10,))],
+            far_args=range(10),
+        )
+    else:
+        (shares,) = run_kernel(
+            back_columns_kernel,
+            [shares_out],
+            [choose, normed_shares, exchange_slots(moe_slots)],
+            loose_outs=(0,),
+        )
+
+        def owner_sum(values):
+            got = exchange(values.reshape(groups, share, hidden_units)).astype(F32)
+            return jnp.sum(got.reshape(tile_count, experts, share, hidden_units), axis=0)
+
+        grad_expert_in = owner_sum(grad_first)
+        grad_expert_out = owner_sum(grad_second)
+    shares_made = shares
+    shares = lax.all_to_all(shares, "tensor", split_axis=0, concat_axis=0, tiled=True)
+    outcome, grad_tokens = run_kernel(
+        finish_rows_kernel,
+        [((column, length), BF16), ((column, length), F32)],
+        [shares, residual_columns, d_columns, tokens_turned, scale, gain_columns],
+        staged=range(6),
+        loose_outs=(0, 1),
+    )
+
+    if near:
+        lasts, second_d = after([lasts, second_d], all_normed, grad_tokens)
+        lasts = swap_near(lasts)
+        near_d = [swap(part, 1) for part in second_d]
+        seconds = [*seconds, *second_d, near_own, near_x, near_y, *near_d]
+
+        def late_vectors(*refs):
+            late_vectors_kernel(refs[:groups], *refs[groups:])
+
+        grad_conv_weight, grad_conv_bias, norm_shares = run_kernel(
+            late_vectors,
+            [((4, chans), F32), ((chans,), F32), ((1, width), F32)],
+            lasts,
+            [
+                ((groups, tiles * 2 * VECTORS_TWO, length), BF16),
+                pltpu.SemaphoreType.DMA((groups,)),
+            ],
+            far_args=range(groups),
+            loose_outs=(0, 1, 2),
+        )
+        norm_parts = share_rows(after([norm_shares], near_d)[0], parts)
 
         def wide_grads(*refs):
-            wide_grads_kernel((rank, states), refs[:groups], *refs[groups:])
+            wide_grads_kernel(
+                (rank, states, proj), refs[:10], refs[10 : 10 + groups], *refs[10 + groups :]
+            )
 
         (
             grad_out_proj,
             grad_in_turned,
+            grad_x_turned,
             grad_dt_proj,
             grad_dt_bias,
             grad_decay_log,
@@ -1245,48 +1369,31 @@
             [
                 ((chans, width), F32),
                 ((2, chans, width), F32),
+                ((proj, chans), F32),
                 ((rank, chans), F32),
                 ((chans,), F32),
                 ((states, chans), F32),
                 ((chans,), F32),
                 ((1, width), F32),
             ],
-            [*seconds, all_normed, all_gated],
+            [*after(seconds, norm_shares), *lasts, all_normed, all_gated, all_act],
             [
+                ((groups, width + 2 * chans, length), BF16),
+                ((groups, last_rows, length), BF16),
                 ((groups * length, width), BF16),
                 ((chans, groups * length), BF16),
+                ((-(-proj // 16) * 16, groups * length), BF16),
                 ((full, length), F32),
-                ((chans, width), F32),
-                pltpu.SemaphoreType.DMA,
+                ((3, chans, width), F32),
+                pltpu.SemaphoreType.DMA((10,)),
+                pltpu.SemaphoreType.DMA((groups,)),
+                pltpu.SemaphoreType.DMA((4,)),
             ],
-            far_outs=(1,),
-        )
-        message = after([message], second_x, second_y)[0]
-        lasts = swap_near([message, swap(message, 2), swap(message, 4), swap(message, 6)])
-
-        def late_grads(*refs):
-            late_grads_kernel((chans, proj), refs[:groups], *refs[groups:])
-
-        grad_in_turned, grad_x_turned, grad_conv_weight, grad_conv_bias, norm_part = run_kernel(
-            late_grads,
-            [
-                ((2, chans, width), F32),
-                ((proj, chans), F32),
-                ((4, chans), F32),
-                ((chans,), F32),
-                ((1, width), F32),
-            ],
-            [*lasts, all_normed, all_act, grad_in_turned],
-            [
-                ((chans, groups * length), BF16),
-                ((-(-proj // 16) * 16, groups * length), BF16),
-                ((chans, width), F32),
-                pltpu.SemaphoreType.DMA,
-            ],
-            far_args=(groups + 2,),
-            far_outs=(0,),
-            alias={groups + 2: 0},
-        )
+            far_args=range(10 + groups),
+            far_outs=(0, 1),
+            loose_outs=range(8),
+        )
+        grad_norm_one = sum(norm_parts).reshape(width)
     else:
         top = last_rows - tiles * 2 * VECTORS_TWO
         ones = second[width + chans :].astype(F32).T
@@ -1317,12 +1424,11 @@
         grad_norm_two = ones[states + 2 : states + 4]
         grad_conv_weight = twos[:4]
         grad_conv_bias = twos[4]
-        norm_part = twos[5:7].reshape(1, width)
-    grad_norm_one = sum(share_rows(norm_part, parts))
+        grad_norm_one = sum(share_rows(twos[5:7].reshape(1, width), parts)).reshape(width)
     return (
         outcome.T,
         grad_tokens.T,
-        grad_norm_one.reshape(width),
+        grad_norm_one,
         jnp.swapaxes(grad_in_turned, 1, 2),
         grad_conv_weight,
         grad_conv_bias,

time: 256 us -> 225 us (0.88)
  waiting for transfers between devices: 76.7 us -> 50.3 us
  blocking collectives: 16.7 us -> 0 us
  starting transfers between devices: 64 us -> 75.6 us
  local copies, waits for them, and re-layouts: 5.33 us -> 16.1 us
  Pallas kernels: 87.6 us -> 79.5 us
    all_to_all x1 -> x0, blocking collectives: 16.7 us -> none  [exchange(): return lax.all_to_all(values, 'dp', split_axis=0, concat_axis=0, tiled=True)]
    all_to_all x3 -> x4, waiting for transfers between devices: 15.1 us -> 0.73 us  [exchange(): return lax.all_to_all(values, 'dp', split_axis=0, concat_axis=0, tiled=True)]
    pallas_call x17, Pallas kernels: 87.6 us -> 79.5 us  [run_kernel(): pl.pallas_call(body, out_shape=[held(index, shape, dtype) for index, (sha...]
    ppermute x30 -> x24, waiting for transfers between devices: 37.7 us -> 31.5 us  [send_chunks(): lax.ppermute(chunks[s], 'tensor', pairs[s])]
    ppermute x21 -> x25, waiting for transfers between devices: 23.9 us -> 18.1 us  [swap(): lax.ppermute(values, 'dp', [(i, i ^ bits) for i in range(NEAR_GROUPS)])]
    unnamed x90 -> x124, local copies, waits for them, and re-layouts: 5.33 us -> 10.7 us
    slice x0 -> x4, local copies, waits for them, and re-layouts: none -> 5.38 us  [split_beside(): return (along_y[:half], along_x[half:])]
    ppermute x21 -> x25, starting transfers between devices: 11.4 us -> 16.8 us  [swap(): lax.ppermute(values, 'dp', [(i, i ^ bits) for i in range(NEAR_GROUPS)])]
  transfers between devices with their start and end apart: 54 -> 54, of which waited for: 24 -> 26; matrix products, arithmetic and copies ran while one was open for 1% -> 3% of each run, Pallas kernels for 31% -> 31%
where the time goes in v3:
time: 225 us; the launch traced here: 224 us
  Pallas kernels  79.5 us (35%)
  starting transfers between devices  75.6 us (34%)
  waiting for transfers between devices  50.3 us (22%)
  local copies, waits for them, and re-layouts  16.1 us (7%)
    pallas_call x17, Pallas kernels, run_kernel(): pl.pallas_call(body, out_shape=[held(index, shape, dtype) for index, (sha...  79.5 us
    ppermute x24, starting transfers between devices, send_chunks(): lax.ppermute(chunks[s], 'tensor', pairs[s])  36.3 us
    ppermute x24, waiting for transfers between devices, send_chunks(): lax.ppermute(chunks[s], 'tensor', pairs[s])  31.5 us
    all_to_all x4, starting transfers between devices, exchange(): return lax.all_to_all(values, 'dp', split_axis=0, concat_axis=0, tiled=True)  18.4 us
    ppermute x25, waiting for transfers between devices, swap(): lax.ppermute(values, 'dp', [(i, i ^ bits) for i in range(NEAR_GROUPS)])  18.1 us
    ppermute x25, starting transfers between devices, swap(): lax.ppermute(values, 'dp', [(i, i ^ bits) for i in range(NEAR_GROUPS)])  16.8 us
    unnamed x124, local copies, waits for them, and re-layouts  10.7 us
    slice x4, local copies, waits for them, and re-layouts, split_beside(): return (along_y[:half], along_x[half:])  5.38 us
  transfers between devices with their start and end apart: 54, of which 26 were waited for; matrix products, arithmetic and copies ran while one was open for 3% of the time, Pallas kernels for 31%

profile of v3, /device:TPU:0, one launch (start us, length us, event | category | flops | bytes accessed | tf_op | source)
XLA Modules:
  0.0 224.2 jit_solution(1843619994685605946)
XLA Ops:
  0.6 5.4 %shard_map.280 = (f32[4,128,128]{2,1,0:T(8,128)}, bf16[256,128]{1,0:T(8,128)(2,1)}, bf16[8,336,768]{2,1,0:T(8,128)(2,1)}) custom-call(s32[1,128]{1,0:T(1,128)} %bitcast.25, s32[1,128]{1,0:T(1,128)} %bitcast.26, bf16[128,1152]{1,0:T(8,128)(2,1)} %refs_7_.6, bf16[8,144,768]{2,1,0:T(8,128)(2,1)} %refs_3_.1, bf16[8,144,768]{2,1,0:T(8,128)(2,1)} %refs_4_.1), custom_call_target="tpu_custom_call" | custom-call | tf_op jit(solution)/shard_map/pallas_call | solution.py:69
  6.1 5.4 %all-to-all-start.1 = ((bf16[8,336,768]{2,1,0:T(8,128)(2,1)}), bf16[8,336,768]{2,1,0:T(8,128)(2,1)}, u32[]{:S(2)}, u32[]{:S(2)}) async-start(bf16[8,336,768]{2,1,0:T(8,128)(2,1)} %get-tuple-element.129), calls=%async_computation.1 | async-start | bytes 8257536 | tf_op jit(solution)/shard_map/all_to_all | solution.py:1055
  11.6 4.5 %collective-permute-start.2 = (bf16[288,128]{1,0:T(8,128)(2,1)S(1)}, bf16[288,128]{1,0:T(8,128)(2,1)S(1)}, u32[]{:S(2)}, u32[]{:S(2)}) collective-permute-start(bf16[288,128]{1,0:T(8,128)(2,1)S(1)} %bitcast.22), channel_id=1, source_target_pairs={{0,3},{1,0},{2,1},{3,2},{4,7},{5,4},{6,5},{7,6},{8,11},{9,8},{10,9... | collective-permute-start | bytes 221192 | tf_op jit(solution)/shard_map/ppermute | solution.py:978
  18.8 5.0 %collective-permute-done.1.refs_3_ = bf16[288,128]{1,0:T(8,128)(2,1)S(1)} collective-permute-done((bf16[288,128]{1,0:T(8,128)(2,1)S(1)}, bf16[288,128]{1,0:T(8,128)(2,1)S(1)}, u32[]{:S(2)}, u32[]{:S(2)}) %collective-permute-start.1) | collective-permute-done | bytes 73760 | tf_op jit(solution)/shard_map/ppermute | solution.py:978
  24.5 3.8 %shard_map.281 = (bf16[128,1152]{1,0:T(8,128)(2,1)}, bf16[1152,128]{1,0:T(8,128)(2,1)}, bf16[128,576]{1,0:T(8,128)(2,1)}, f32[128,576]{1,0:T(8,128)}, f32[128,57...) custom-call(s32[1]{0:T(128)} %bitcast.2.refs_0_, ...), custom_call_target="tpu_custom_call" | custom-call | tf_op jit(solution)/shard_map/pallas_call | solution.py:69
  36.4 6.5 %shard_map.282 = (bf16[32,1152]{1,0:T(8,128)(2,1)S(1)}, bf16[32,1152]{1,0:T(8,128)(2,1)S(1)}, bf16[32,1152]{1,0:T(8,128)(2,1)S(1)}, bf16[32,1152]{1,0:T(8,128)(2...) custom-call(s32[1]{0:T(128)} %bitcast.2.refs_0_, bf16[104,128]{1,0:T(8,128)(2,1)} %copy-done.21, ...), custom_call_target="tpu_custom_call" | custom-call | tf_op jit(solution)/shard_map/pallas_call | solution.py:69
  63.4 4.2 %all-to-all-start = ((bf16[8,32,1152]{2,1,0:T(8,128)(2,1)}), bf16[8,32,1152]{2,1,0:T(8,128)(2,1)}, u32[]{:S(2)}, u32[]{:S(2)}) async-start(bf16[8,32,1152]{2,1,0:T(8,128)(2,1)} %bitcast.17), calls=%async_computation | async-start | bytes 1179648 | tf_op jit(solution)/shard_map/all_to_all | solution.py:1055
  67.6 5.2 %collective-permute-done.13.refs_2_ = bf16[2304,128]{1,0:T(8,128)(2,1)} collective-permute-done((bf16[2304,128]{1,0:T(8,128)(2,1)S(1)}, bf16[2304,128]{1,0:T(8,128)(2,1)}, u32[]{:S(2)}, u32[]{:S(2)}) %collective-permute-start.13) | collective-permute-done | bytes 589856 | tf_op jit(solution)/shard_map/ppermute | solution.py:997
  72.8 5.5 %shard_map.284 = (bf16[1152,768]{1,0:T(8,128)(2,1)}, bf16[1152,768]{1,0:T(8,128)(2,1)}, bf16[256,1152]{1,0:T(8,128)(2,1)}, f32[256,768]{1,0:T(8,128)}) custom-call(bf16[8,336,768]{2,1,0:T(8,128)(2,1)} %all-to-all-done.1.refs_0_), custom_call_target="tpu_custom_call" | custom-call | tf_op jit(solution)/shard_map/pallas_call | solution.py:69
  79.1 3.8 %shard_map.285 = (bf16[256,768]{1,0:T(8,128)(2,1)}, bf16[256,768]{1,0:T(8,128)(2,1)}, bf16[256,1152]{1,0:T(8,128)(2,1)S(1)}) custom-call(bf16[256,1152]{1,0:T(8,128)(2,1)} %bitcast.7.refs_0_, bf16[1152,768]{1,0:T(8,128)(2,1)} %get-tuple-element.132.refs_1_, f32[256,768]{1,0:T(8,128)} %get-tuple-element.133.refs_2_), custom_call_target="tpu_custom_call" | custom-call | tf_op jit(solution)/shard_map/pallas_call | solution.py:69
  83.7 4.2 %all-to-all-start.2 = ((bf16[8,32,1152]{2,1,0:T(8,128)(2,1)}), bf16[8,32,1152]{2,1,0:T(8,128)(2,1)}, u32[]{:S(2)}, u32[]{:S(2)}) async-start(bf16[8,32,1152]{2,1,0:T(8,128)(2,1)} %bitcast.16), calls=%async_computation.2 | async-start | bytes 1179648 | tf_op jit(solution)/shard_map/all_to_all | solution.py:1055
  93.3 5.0 %shard_map.286 = bf16[8,336,768]{2,1,0:T(8,128)(2,1)} custom-call(bf16[256,1152]{1,0:T(8,128)(2,1)} %bitcast.7.refs_0_, bf16[256,1152]{1,0:T(8,128)(2,1)} %get-tuple-element.135.refs_1_, bf16[256,768]{1,0:T(8,128)(2,1)} %get-tuple-element.136.refs_2_, bf16[256,768]{1,0:T(8,128)(2,1)} %get-tuple-element.137.refs_3_, bf16[1152,768]{1,0:T(8,128)(2,1)} %get-tuple-element.138.refs_4_), custom_call_target="tpu_custom_call" | custom-call | tf_op jit(solution)/shard_map/pallas_call | solution.py:69
  98.3 5.4 %collective-permute-done.15.refs_4_ = bf16[1152,128]{1,0:T(8,128)(2,1)} collective-permute-done((bf16[1152,128]{1,0:T(8,128)(2,1)S(1)}, bf16[1152,128]{1,0:T(8,128)(2,1)}, u32[]{:S(2)}, u32[]{:S(2)}) %collective-permute-start.15) | collective-permute-done | bytes 294944 | tf_op jit(solution)/shard_map/ppermute | solution.py:997
  103.8 4.5 %all-to-all-start.3 = ((bf16[8,336,768]{2,1,0:T(8,128)(2,1)}), bf16[8,336,768]{2,1,0:T(8,128)(2,1)}, u32[]{:S(2)}, u32[]{:S(2)}) async-start(bf16[8,336,768]{2,1,0:T(8,128)(2,1)} %shard_map.286), calls=%async_computation.3 | async-start | bytes 8257536 | tf_op jit(solution)/shard_map/all_to_all | solution.py:1055
  121.8 3.2 %collective-permute-start.21 = (bf16[32,1152]{1,0:T(8,128)(2,1)S(1)}, bf16[32,1152]{1,0:T(8,128)(2,1)S(1)}, u32[]{:S(2)}, u32[]{:S(2)}) collective-permute-start(bf16[32,1152]{1,0:T(8,128)(2,1)S(1)} %add_convert_fusion.refs_1_), channel_id=1, source_target_pairs={{0,3},{1,0},{2,1},{3,2},{4,7},{5,4},{6,5},{7,6},{8,11},{9,8},{10,9... | collective-permute-start | bytes 221192 | tf_op jit(solution)/shard_map/ppermute | solution.py:978
  127.7 5.0 %collective-permute-done.20.refs_3_ = bf16[32,1152]{1,0:T(8,128)(2,1)S(1)} collective-permute-done((bf16[32,1152]{1,0:T(8,128)(2,1)S(1)}, bf16[32,1152]{1,0:T(8,128)(2,1)S(1)}, u32[]{:S(2)}, u32[]{:S(2)}) %collective-permute-start.20) | collective-permute-done | bytes 73760 | tf_op jit(solution)/shard_map/ppermute | solution.py:978
  136.6 12.9 %shard_map.289 = (bf16[104,128]{1,0:T(8,128)(2,1)S(1)}, f32[128,576]{1,0:T(8,128)S(1)}, bf16[128,576]{1,0:T(8,128)(2,1)S(1)}, bf16[2304,128]{1,0:T(8,128)(2,1)S(1)}) custom-call(f32[128,576]{1,0:T(8,128)S(1)} %get-tuple-element.151.refs_0_, f32[128,576]{1,0:T(8,128)} %get-tuple-element.152.refs_1_, f32[128,576]{1,0:T(8,128)} %get-tuple-element.121.refs_10_.refs_2_, ...), custom_call_target="tpu_custom_call" | custom-call | tf_op jit(solution)/shard_map/pallas_call | solution.py:69
  165.5 3.3 %shard_map.291 = bf16[4,592,128]{2,1,0:T(8,128)(2,1)} custom-call(bf16[256,128]{1,0:T(8,128)(2,1)} %get-tuple-element.117.refs_7_.refs_1_.refs_0_, bf16[4,304,128]{2,1,0:T(8,128)(2,1)S(1)} %copy-done.14, bf16[8,336,768]{2,1,0:T(8,128)(2,1)} %all-to-all-done.3.refs_2_.refs_0_), custom_call_target="tpu_custom_call" | custom-call | tf_op jit(solution)/shard_map/pallas_call | solution.py:69
  168.8 4.2 %all-to-all-start.4 = ((bf16[4,592,128]{2,1,0:T(8,128)(2,1)}), bf16[4,592,128]{2,1,0:T(8,128)(2,1)}, u32[]{:S(2)}, u32[]{:S(2)}) async-start(bf16[4,592,128]{2,1,0:T(8,128)(2,1)} %shard_map.291), calls=%async_computation.4 | async-start | bytes 1212416 | tf_op jit(solution)/shard_map/all_to_all | solution.py:1322
  173.0 4.2 %shard_map.293 = (f32[8,144,768]{2,1,0:T(8,128)}, f32[8,144,768]{2,1,0:T(8,128)}) custom-call(bf16[8,336,768]{2,1,0:T(8,128)(2,1)} %all-to-all-done.3.refs_2_.refs_0_), custom_call_target="tpu_custom_call" | custom-call | tf_op jit(solution)/shard_map/pallas_call | solution.py:69
  186.1 5.7 %shard_map.294 = (bf16[1024,1152]{1,0:T(8,128)(2,1)}, bf16[576,1024]{1,0:T(8,128)(2,1)}, bf16[576,1024]{1,0:T(8,128)(2,1)}) custom-call(bf16[2304,128]{1,0:T(8,128)(2,1)} %copy-done.6, bf16[2304,128]{1,0:T(8,128)(2,1)} %collective-permute-done.12.refs_1_, bf16[2304,128]{1,0:T(8,128)(2,1)} %collective-permute-done.13.refs_2_, ...), custom_call_target="tpu_custom_call" | custom-call | tf_op jit(solution)/shard_map/pallas_call | solution.py:69
  195.5 4.0 %collective-permute-done.33.refs_2_.refs_12_ = bf16[768,128]{1,0:T(8,128)(2,1)S(1)} collective-permute-done((bf16[768,128]{1,0:T(8,128)(2,1)S(1)}, bf16[768,128]{1,0:T(8,128)(2,1)S(1)}, u32[]{:S(2)}, u32[]{:S(2)}) %collective-permute-start.33) | collective-permute-done | bytes 196640 | tf_op jit(solution)/shard_map/ppermute | solution.py:997
  205.4 3.8 %collective-permute-start.48 = (f32[1,1152]{1,0:T(1,128)S(1)}, f32[1,1152]{1,0:T(1,128)S(1)}, u32[]{:S(2)}, u32[]{:S(2)}) collective-permute-start(f32[1,1152]{1,0:T(1,128)S(1)} %get-tuple-element.195), channel_id=1, source_target_pairs={{0,3},{1,0},{2,1},{3,2},{4,7},{5,4},{6,5},{7,6},{8,11},{9,8},{10,9... | collective-permute-start | bytes 13832 | tf_op jit(solution)/shard_map/ppermute | solution.py:978
  212.9 10.0 %shard_map.296 = (f32[576,1152]{1,0:T(8,128)}, f32[2,576,1152]{2,1,0:T(8,128)}, f32[104,576]{1,0:T(8,128)}, f32[72,576]{1,0:T(8,128)}, f32[576]{0:T(1024)}, /*in...) custom-call(bf16[2304,128]{1,0:T(8,128)(2,1)} %copy-done.9, bf16[2304,128]{1,0:T(8,128)(2,1)} %collective-permute-done.30.refs_1_, ...), custom_call_target="tpu_custom_call" | custom-call | tf_op jit(solution)/shard_map/pallas_call | solution.py:69
  (233 shorter events, 98.0 us)
Async XLA Ops:
  6.1 57.3 %all-to-all-start.1 = ((bf16[8,336,768]{2,1,0:T(8,128)(2,1)}), bf16[8,336,768]{2,1,0:T(8,128)(2,1)}, u32[]{:S(2)}, u32[]{:S(2)}) async-start(bf16[8,336,768]{2,1,0:T(8,128)(2,1)} %get-tuple-element.129), calls=%async_computation.1 | async-start | bytes 8257536 | tf_op jit(solution)/shard_map/all_to_all | solution.py:1055
  16.1 7.7 %collective-permute-start.1 = (bf16[288,128]{1,0:T(8,128)(2,1)S(1)}, bf16[288,128]{1,0:T(8,128)(2,1)S(1)}, u32[]{:S(2)}, u32[]{:S(2)}) collective-permute-start(bf16[288,128]{1,0:T(8,128)(2,1)S(1)} %bitcast.23), channel_id=1, source_target_pairs={{0,2},{1,3},{2,0},{3,1},{4,6},{5,7},{6,4},{7,5},{8,10},{9,11},{10,... | collective-permute-start | bytes 221192 | tf_op jit(solution)/shard_map/ppermute | solution.py:978
  16.1 7.7 %collective-permute-start = (bf16[288,128]{1,0:T(8,128)(2,1)S(1)}, bf16[288,128]{1,0:T(8,128)(2,1)S(1)}, u32[]{:S(2)}, u32[]{:S(2)}) collective-permute-start(bf16[288,128]{1,0:T(8,128)(2,1)S(1)} %bitcast.24), channel_id=1, source_target_pairs={{0,1},{1,2},{2,3},{3,0},{4,5},{5,6},{6,7},{7,4},{8,9},{9,10},{10,1... | collective-permute-start | bytes 221192 | tf_op jit(solution)/shard_map/ppermute | solution.py:978
  53.9 18.9 %collective-permute-start.13 = (bf16[2304,128]{1,0:T(8,128)(2,1)S(1)}, bf16[2304,128]{1,0:T(8,128)(2,1)}, u32[]{:S(2)}, u32[]{:S(2)}) collective-permute-start(bf16[2304,128]{1,0:T(8,128)(2,1)S(1)} %get-tuple-element.177.refs_0_), channel_id=1, source_target_pairs={{0,16},{4,20},{8,24},{12,28},{16,0},{20,4},{24,8},{28,12},{1,17},{... | collective-permute-start | bytes 1769480 | tf_op jit(solution)/shard_map/ppermute | solution.py:997
  55.6 17.2 %collective-permute-start.12 = (bf16[2304,128]{1,0:T(8,128)(2,1)S(1)}, bf16[2304,128]{1,0:T(8,128)(2,1)}, u32[]{:S(2)}, u32[]{:S(2)}) collective-permute-start(bf16[2304,128]{1,0:T(8,128)(2,1)S(1)} %get-tuple-element.177.refs_0_), channel_id=1, source_target_pairs={{0,8},{4,12},{8,0},{12,4},{16,24},{20,28},{24,16},{28,20},{1,9},{5... | collective-permute-start | bytes 1769480 | tf_op jit(solution)/shard_map/ppermute | solution.py:997
  63.4 15.7 %all-to-all-start = ((bf16[8,32,1152]{2,1,0:T(8,128)(2,1)}), bf16[8,32,1152]{2,1,0:T(8,128)(2,1)}, u32[]{:S(2)}, u32[]{:S(2)}) async-start(bf16[8,32,1152]{2,1,0:T(8,128)(2,1)} %bitcast.17), calls=%async_computation | async-start | bytes 1179648 | tf_op jit(solution)/shard_map/all_to_all | solution.py:1055
  83.7 20.1 %all-to-all-start.2 = ((bf16[8,32,1152]{2,1,0:T(8,128)(2,1)}), bf16[8,32,1152]{2,1,0:T(8,128)(2,1)}, u32[]{:S(2)}, u32[]{:S(2)}) async-start(bf16[8,32,1152]{2,1,0:T(8,128)(2,1)} %bitcast.16), calls=%async_computation.2 | async-start | bytes 1179648 | tf_op jit(solution)/shard_map/all_to_all | solution.py:1055
  89.9 13.9 %collective-permute-start.15 = (bf16[1152,128]{1,0:T(8,128)(2,1)S(1)}, bf16[1152,128]{1,0:T(8,128)(2,1)}, u32[]{:S(2)}, u32[]{:S(2)}) collective-permute-start(bf16[1152,128]{1,0:T(8,128)(2,1)S(1)} %slice.13), channel_id=1, source_target_pairs={{0,16},{4,20},{8,24},{12,28},{16,0},{20,4},{24,8},{28,12},{1,17},{... | collective-permute-start | bytes 884744 | tf_op jit(solution)/shard_map/ppermute | solution.py:997
  91.8 11.9 %collective-permute-start.14 = (bf16[1152,128]{1,0:T(8,128)(2,1)S(1)}, bf16[1152,128]{1,0:T(8,128)(2,1)}, u32[]{:S(2)}, u32[]{:S(2)}) collective-permute-start(bf16[1152,128]{1,0:T(8,128)(2,1)S(1)} %slice.12), channel_id=1, source_target_pairs={{0,8},{4,12},{8,0},{12,4},{16,24},{20,28},{24,16},{28,20},{1,9},{5... | collective-permute-start | bytes 884744 | tf_op jit(solution)/shard_map/ppermute | solution.py:997
  103.8 60.6 %all-to-all-start.3 = ((bf16[8,336,768]{2,1,0:T(8,128)(2,1)}), bf16[8,336,768]{2,1,0:T(8,128)(2,1)}, u32[]{:S(2)}, u32[]{:S(2)}) async-start(bf16[8,336,768]{2,1,0:T(8,128)(2,1)} %shard_map.286), calls=%async_computation.3 | async-start | bytes 8257536 | tf_op jit(solution)/shard_map/all_to_all | solution.py:1055
  112.2 9.6 %collective-permute-start.22 = (bf16[2304,128]{1,0:T(8,128)(2,1)S(1)}, bf16[2304,128]{1,0:T(8,128)(2,1)S(1)}, u32[]{:S(2)}, u32[]{:S(2)}) collective-permute-start(bf16[2304,128]{1,0:T(8,128)(2,1)S(1)} %get-tuple-element.177.refs_0_), channel_id=1, source_target_pairs={{0,4},{4,0},{8,12},{12,8},{16,20},{20,16},{24,28},{28,24},{1,5},{5... | collective-permute-start | bytes 1769480 | tf_op jit(solution)/shard_map/ppermute | solution.py:997
  112.3 12.8 %collective-permute-start.24 = (bf16[2304,128]{1,0:T(8,128)(2,1)}, bf16[2304,128]{1,0:T(8,128)(2,1)S(1)}, u32[]{:S(2)}, u32[]{:S(2)}) collective-permute-start(bf16[2304,128]{1,0:T(8,128)(2,1)} %collective-permute-done.13.refs_2_), channel_id=1, source_target_pairs={{0,4},{4,0},{8,12},{12,8},{16,20},{20,16},{24,28},{28,24},{1,5},{5... | collective-permute-start | bytes 1769480 | tf_op jit(solution)/shard_map/ppermute | solution.py:997
  112.7 12.3 %collective-permute-start.23 = (bf16[2304,128]{1,0:T(8,128)(2,1)}, bf16[2304,128]{1,0:T(8,128)(2,1)S(1)}, u32[]{:S(2)}, u32[]{:S(2)}) collective-permute-start(bf16[2304,128]{1,0:T(8,128)(2,1)} %collective-permute-done.12.refs_1_), channel_id=1, source_target_pairs={{0,4},{4,0},{8,12},{12,8},{16,20},{20,16},{24,28},{28,24},{1,5},{5... | collective-permute-start | bytes 1769480 | tf_op jit(solution)/shard_map/ppermute | solution.py:997
  149.5 27.6 %collective-permute-start.31 = (bf16[2304,128]{1,0:T(8,128)(2,1)S(1)}, bf16[2304,128]{1,0:T(8,128)(2,1)}, u32[]{:S(2)}, u32[]{:S(2)}) collective-permute-start(bf16[2304,128]{1,0:T(8,128)(2,1)S(1)} %get-tuple-element.196.refs_0_), channel_id=1, source_target_pairs={{0,16},{4,20},{8,24},{12,28},{16,0},{20,4},{24,8},{28,12},{1,17},{... | collective-permute-start | bytes 1769480 | tf_op jit(solution)/shard_map/ppermute | solution.py:997
  151.3 25.8 %collective-permute-start.30 = (bf16[2304,128]{1,0:T(8,128)(2,1)S(1)}, bf16[2304,128]{1,0:T(8,128)(2,1)}, u32[]{:S(2)}, u32[]{:S(2)}) collective-permute-start(bf16[2304,128]{1,0:T(8,128)(2,1)S(1)} %get-tuple-element.196.refs_0_), channel_id=1, source_target_pairs={{0,8},{4,12},{8,0},{12,4},{16,24},{20,28},{24,16},{28,20},{1,9},{5... | collective-permute-start | bytes 1769480 | tf_op jit(solution)/shard_map/ppermute | solution.py:997
  168.8 23.0 %all-to-all-start.4 = ((bf16[4,592,128]{2,1,0:T(8,128)(2,1)}), bf16[4,592,128]{2,1,0:T(8,128)(2,1)}, u32[]{:S(2)}, u32[]{:S(2)}) async-start(bf16[4,592,128]{2,1,0:T(8,128)(2,1)} %shard_map.291), calls=%async_computation.4 | async-start | bytes 1212416 | tf_op jit(solution)/shard_map/all_to_all | solution.py:1322
  181.2 18.3 %collective-permute-start.35 = (bf16[1152,128]{1,0:T(8,128)(2,1)}, bf16[1152,128]{1,0:T(8,128)(2,1)}, u32[]{:S(2)}, u32[]{:S(2)}) collective-permute-start(bf16[1152,128]{1,0:T(8,128)(2,1)} %slice.14), channel_id=1, source_target_pairs={{0,8},{4,12},{8,0},{12,4},{16,24},{20,28},{24,16},{28,20},{1,9},{5... | collective-permute-start | bytes 884744 | tf_op jit(solution)/shard_map/ppermute | solution.py:997
  181.8 17.7 %collective-permute-start.36 = (bf16[1152,128]{1,0:T(8,128)(2,1)}, bf16[1152,128]{1,0:T(8,128)(2,1)}, u32[]{:S(2)}, u32[]{:S(2)}) collective-permute-start(bf16[1152,128]{1,0:T(8,128)(2,1)} %slice.15), channel_id=1, source_target_pairs={{0,16},{4,20},{8,24},{12,28},{16,0},{20,4},{24,8},{28,12},{1,17},{... | collective-permute-start | bytes 884744 | tf_op jit(solution)/shard_map/ppermute | solution.py:997
  182.1 13.4 %collective-permute-start.34 = (bf16[768,128]{1,0:T(8,128)(2,1)S(1)}, bf16[768,128]{1,0:T(8,128)(2,1)S(1)}, u32[]{:S(2)}, u32[]{:S(2)}) collective-permute-start(bf16[768,128]{1,0:T(8,128)(2,1)S(1)} %get-tuple-element.188.refs_0_.refs_10_), channel_id=1, source_target_pairs={{0,24},{4,28},{8,16},{12,20},{16,8},{20,12},{24,0},{28,4},{1,25},{... | collective-permute-start | bytes 589832 | tf_op jit(solution)/shard_map/ppermute | solution.py:997
  184.7 14.8 %collective-permute-start.33 = (bf16[768,128]{1,0:T(8,128)(2,1)S(1)}, bf16[768,128]{1,0:T(8,128)(2,1)S(1)}, u32[]{:S(2)}, u32[]{:S(2)}) collective-permute-start(bf16[768,128]{1,0:T(8,128)(2,1)S(1)} %get-tuple-element.188.refs_0_.refs_10_), channel_id=1, source_target_pairs={{0,16},{4,20},{8,24},{12,28},{16,0},{20,4},{24,8},{28,12},{1,17},{... | collective-permute-start | bytes 589832 | tf_op jit(solution)/shard_map/ppermute | solution.py:997
  185.3 14.2 %collective-permute-start.32 = (bf16[768,128]{1,0:T(8,128)(2,1)S(1)}, bf16[768,128]{1,0:T(8,128)(2,1)S(1)}, u32[]{:S(2)}, u32[]{:S(2)}) collective-permute-start(bf16[768,128]{1,0:T(8,128)(2,1)S(1)} %get-tuple-element.188.refs_0_.refs_10_), channel_id=1, source_target_pairs={{0,8},{4,12},{8,0},{12,4},{16,24},{20,28},{24,16},{28,20},{1,9},{5... | collective-permute-start | bytes 589832 | tf_op jit(solution)/shard_map/ppermute | solution.py:997
  205.4 18.2 %collective-permute-start.48 = (f32[1,1152]{1,0:T(1,128)S(1)}, f32[1,1152]{1,0:T(1,128)S(1)}, u32[]{:S(2)}, u32[]{:S(2)}) collective-permute-start(f32[1,1152]{1,0:T(1,128)S(1)} %get-tuple-element.195), channel_id=1, source_target_pairs={{0,3},{1,0},{2,1},{3,2},{4,7},{5,4},{6,5},{7,6},{8,11},{9,8},{10,9... | collective-permute-start | bytes 13832 | tf_op jit(solution)/shard_map/ppermute | solution.py:978
  209.2 14.3 %collective-permute-start.47 = (f32[1,1152]{1,0:T(1,128)S(1)}, f32[1,1152]{1,0:T(1,128)S(1)}, u32[]{:S(2)}, u32[]{:S(2)}) collective-permute-start(f32[1,1152]{1,0:T(1,128)S(1)} %get-tuple-element.195), channel_id=1, source_target_pairs={{0,2},{1,3},{2,0},{3,1},{4,6},{5,7},{6,4},{7,5},{8,10},{9,11},{10,... | collective-permute-start | bytes 13832 | tf_op jit(solution)/shard_map/ppermute | solution.py:978
  209.2 14.3 %collective-permute-start.46 = (f32[1,1152]{1,0:T(1,128)S(1)}, f32[1,1152]{1,0:T(1,128)S(1)}, u32[]{:S(2)}, u32[]{:S(2)}) collective-permute-start(f32[1,1152]{1,0:T(1,128)S(1)} %get-tuple-element.195), channel_id=1, source_target_pairs={{0,1},{1,2},{2,3},{3,0},{4,5},{5,6},{6,7},{7,4},{8,9},{9,10},{10,1... | collective-permute-start | bytes 13832 | tf_op jit(solution)/shard_map/ppermute | solution.py:978
  (92 other events, 857.1 us)

commit v4 on v3

--- a/solution.py
+++ b/solution.py
@@ -19,6 +19,7 @@
 NEAR_GROUPS = 8
 VECTORS_ONE = 24
 VECTORS_TWO = 8
+NORM_ROWS = 16
 
 
 def run_kernel(
@@ -275,19 +276,45 @@
         copy.wait()
 
 
+def pass_on(along_x, along_y, pass_y, pass_x, passed, arrivals, semaphores):
+    half = passed.shape[1]
+    copies = [
+        (along_y.at[pl.ds(0, half)], passed.at[0]),
+        (along_x.at[pl.ds(half, half)], passed.at[1]),
+    ]
+    for copy in run_copies(copies, arrivals):
+        copy.wait()
+    return run_copies([(passed.at[0], pass_y), (passed.at[1], pass_x)], semaphores)
+
+
 def unpack_kernel(
     share,
     capacity,
     message,
+    along_x,
+    along_y,
     first_out,
     second_out,
     slots_out,
+    pass_y,
+    pass_x,
     d_hidden,
     first_w,
     second_w,
     grad_slots,
+    passed,
+    pass_semaphores,
     semaphores,
 ):
+    started = pass_on(
+        along_x,
+        along_y,
+        pass_y,
+        pass_x,
+        passed,
+        pass_semaphores.at[pl.ds(0, 2)],
+        pass_semaphores.at[pl.ds(2, 2)],
+    )
     folded = capacity + capacity // 2
     copies = []
     for index in range(message.shape[0]):
@@ -301,7 +328,7 @@
     for copy in run_copies(copies, semaphores):
         copy.wait()
     copies = [(first_w, first_out), (second_w, second_out), (grad_slots, slots_out)]
-    started = run_copies(copies, semaphores)
+    started += run_copies(copies, semaphores)
     d_hidden[...] = dot_nn(grad_slots[...], second_w[...])
     for copy in started:
         copy.wait()
@@ -520,13 +547,35 @@
         copy.wait()
 
 
-def owner_kernel(share, message, first_out, second_out, low, wide, arrivals, semaphores):
+def owner_kernel(
+    share,
+    message,
+    along_x,
+    along_y,
+    first_out,
+    second_out,
+    pass_y,
+    pass_x,
+    low,
+    wide,
+    passed,
+    arrivals,
+    semaphores,
+):
     count = message.shape[0]
     arriving = run_copies(
         [(message.at[index, pl.ds(0, 2 * share)], low.at[index]) for index in range(count)],
-        arrivals,
+        arrivals.at[pl.ds(2, count)],
     )
-    started = []
+    started = pass_on(
+        along_x,
+        along_y,
+        pass_y,
+        pass_x,
+        passed,
+        arrivals.at[pl.ds(0, 2)],
+        semaphores.at[pl.ds(0, 2)],
+    )
     for index in range(count):
         arriving[index].wait()
         wide[index] = low[index].astype(F32)
@@ -534,7 +583,7 @@
             (wide.at[index, pl.ds(0, share)], first_out.at[index]),
             (wide.at[index, pl.ds(share, share)], second_out.at[index]),
         ]
-        started += run_copies(copies, semaphores.at[pl.ds(2 * index, 2)])
+        started += run_copies(copies, semaphores.at[pl.ds(2 + 2 * index, 2)])
     for copy in started:
         copy.wait()
 
@@ -544,16 +593,35 @@
     put_row_chunks(place, partial, (out_0, out_1, out_2, out_3))
 
 
-def back_columns_kernel(choose, shares, slots, out):
-    rows = dot_tn(slots[...], choose[...]).astype(BF16)
+def back_columns_kernel(place, choose, shares, slots, out_0, out_1, out_2, out_3, rows):
+    rows[...] = dot_tn(slots[...], choose[...]).astype(BF16)
+    outs = (out_0, out_1, out_2, out_3)
     count, top, _ = shares.shape
     column = rows.shape[0] // count
-    for index in range(count):
-        out[index, :top, :] = shares[index]
-        out[index, top:, :] = rows[index * column : (index + 1) * column]
-
-
-def back_folded_kernel(share, choose, shares, message, out, slots, semaphores):
+    for step, out in enumerate(outs):
+        whose = lax.rem(place[0] + step, count)
+        out[:top, :] = shares[whose]
+        out[top:, :] = rows[pl.ds(pl.multiple_of(whose * column, column), column), :]
+
+
+def back_folded_kernel(
+    share,
+    place,
+    choose,
+    shares,
+    message,
+    refs,
+    out_0,
+    out_1,
+    out_2,
+    out_3,
+    weight_grad,
+    bias_grad,
+    slots,
+    rows,
+    staged,
+    semaphores,
+):
     count = message.shape[0]
     capacity = slots.shape[0] // count
     folded = message.shape[1] - 2 * share
@@ -562,16 +630,10 @@
         copies += unfold_copies(
             message.at[index, pl.ds(2 * share, folded)], slots, index * capacity, capacity
         )
-    for copy in run_copies(copies, semaphores):
-        copy.wait()
-    back_columns_kernel(choose, shares, slots, out)
-
-
-def late_vectors_kernel(refs, weight_grad, bias_grad, norm_out, staged, semaphores):
     deep = 2 * VECTORS_TWO
-    rows = staged.shape[1]
-    top = refs[0].shape[0] - rows
-    copies = [(ref.at[pl.ds(top, rows)], staged.at[index]) for index, ref in enumerate(refs)]
+    height = staged.shape[1]
+    top = refs[0].shape[0] - height
+    copies += [(ref.at[pl.ds(top, height)], staged.at[index]) for index, ref in enumerate(refs)]
     for copy in run_copies(copies, semaphores):
         copy.wait()
     total = staged[0].astype(F32)
@@ -579,13 +641,23 @@
         total = total + staged[index].astype(F32)
     chans = weight_grad.shape[1]
     vectors = jnp.concatenate(
-        [total[start : start + deep] for start in range(0, rows, deep)], axis=1
+        [total[start : start + deep] for start in range(0, height, deep)], axis=1
     )[:, :chans]
     vectors = vectors[:VECTORS_TWO] + vectors[VECTORS_TWO:]
     weight_grad[...] = vectors[:4]
     bias_grad[...] = vectors[4].reshape(chans)
     norm_grad = jnp.concatenate([vectors[5:6], vectors[6:7]], axis=1)
-    norm_out[...] = norm_grad
+    norm_rows = [norm_grad[:, start : start + 128] for start in range(0, norm_grad.shape[1], 128)]
+    spare = jnp.zeros((NORM_ROWS - len(norm_rows), 128), F32)
+    upper, lower = split_vectors(jnp.concatenate([*norm_rows, spare], axis=0))
+    norm_low = jnp.concatenate([upper, lower], axis=0).astype(BF16)
+    outs = (out_0, out_1, out_2, out_3)
+    plain = out_0.shape[0] - 2 * NORM_ROWS
+    back_columns_kernel(
+        place, choose, shares, slots, *[out.at[pl.ds(0, plain)] for out in outs], rows
+    )
+    for out in outs:
+        out[plain:, :] = norm_low
 
 
 def mixer_grad_kernel(
@@ -627,8 +699,7 @@
     return upper, vectors - upper
 
 
-def scan_backward_kernel(
-    d_gated,
+def scan_states_kernel(
     y_in,
     gate_in,
     act_in,
@@ -637,22 +708,15 @@
     dt_proj,
     dt_bias,
     decay_log,
-    skip_gain,
-    gain_grad,
-    d_mix,
-    d_mixed_out,
-    d_act_out,
-    d_gate_out,
-    share_out,
-    rate,
-    step_rows,
-    decay_rows,
-    drive_rows,
-    dy_rows,
-    du_rows,
-    dl_rows,
     decays,
     history,
+    step_rows,
+    drive_rows,
+    step_slope,
+    y_slope,
+    gate_slope,
+    rate,
+    decay_rows,
 ):
     rank = dt_proj.shape[0]
     states = decay_log.shape[0]
@@ -660,23 +724,19 @@
     tiles = step_rows.shape[1] // 128
     full = 128 * tiles
     mixed = mixed_in[...]
-    dt_low = mixed[:rank].astype(BF16)
-    raw_step = dot_tn(dt_low, dt_proj[...]) + as_row(dt_bias)
+    raw_step = dot_tn(mixed[:rank].astype(BF16), dt_proj[...]) + as_row(dt_bias)
     step_size = softplus(raw_step)
-    act = act_in[...].astype(F32)
+    step_slope[...] = jax.nn.sigmoid(raw_step)
     reset = NEVER * (1.0 - wide_masks(masks, 0, chans))
-    padded_copy(rate, -jnp.exp(decay_log[...]))
+    padded_copy(rate, -LOG2E * jnp.exp(decay_log[...]))
     padded_copy(step_rows, step_size)
-    padded_copy(decay_rows, LOG2E * (step_size + reset))
-    padded_copy(drive_rows, step_size * act)
+    padded_copy(decay_rows, step_size + reset)
+    padded_copy(drive_rows, step_size * act_in[...].astype(F32))
     gate = gate_in[...]
     gate_sig = jax.nn.sigmoid(gate)
-    d_out = d_gated[...]
-    d_y = d_out * (gate * gate_sig)
-    padded_copy(dy_rows, d_y)
-    d_gate = d_out * y_in[...] * gate_sig * (1.0 + gate * (1.0 - gate_sig))
+    y_slope[...] = gate * gate_sig
+    gate_slope[...] = y_in[...] * gate_sig * (1.0 + gate * (1.0 - gate_sig))
     b_turned = mixed[rank : rank + states]
-    c_turned = mixed[rank + states : rank + 2 * states]
     history[pl.ds(0, states), :] = jnp.zeros((states, full), F32)
 
     def forward_block(index, state):
@@ -693,6 +753,48 @@
         return state
 
     lax.fori_loop(0, length // 8, forward_block, jnp.zeros((states, full), F32))
+
+
+def scan_backward_kernel(
+    d_gated,
+    y_slope,
+    gate_slope,
+    act_in,
+    mixed_in,
+    dt_proj,
+    decay_log,
+    skip_gain,
+    gain_grad,
+    d_mix,
+    decays,
+    history,
+    step_rows,
+    drive_rows,
+    step_slope,
+    d_mixed_out,
+    d_act_out,
+    d_gate_out,
+    share_out,
+    rate,
+    dy_rows,
+    du_rows,
+    dl_rows,
+):
+    rank = dt_proj.shape[0]
+    states = decay_log.shape[0]
+    length, chans = y_slope.shape
+    tiles = step_rows.shape[1] // 128
+    full = 128 * tiles
+    mixed = mixed_in[...]
+    dt_low = mixed[:rank].astype(BF16)
+    act = act_in[...].astype(F32)
+    padded_copy(rate, -jnp.exp(decay_log[...]))
+    d_out = d_gated[...]
+    d_y = d_out * y_slope[...]
+    padded_copy(dy_rows, d_y)
+    d_gate = d_out * gate_slope[...]
+    b_turned = mixed[rank : rank + states]
+    c_turned = mixed[rank + states : rank + 2 * states]
     lanes = lax.broadcasted_iota(jnp.int32, (states, length), 1)
 
     def backward_block(count, carry):
@@ -733,11 +835,11 @@
         0, length // 8, backward_block, (nothing, nothing, thin, thin)
     )
     du = du_rows[:, :chans]
-    d_step = (dl_rows[:, :chans] + du * act) * jax.nn.sigmoid(raw_step)
+    d_step = (dl_rows[:, :chans] + du * act) * step_slope[...]
     d_step_low = d_step.astype(BF16)
     low_turned = dot_nt(dt_proj[...], d_step_low)
     d_mixed_out[...] = jnp.concatenate([low_turned, d_b, d_c], axis=0).astype(BF16)
-    d_act_out[...] = du * step_size + as_row(skip_gain) * d_y
+    d_act_out[...] = du * step_rows[:, :chans] + as_row(skip_gain) * d_y
     d_gate_low = d_gate.astype(BF16)
     d_gate_out[...] = d_gate_low
     width = d_mix.shape[0]
@@ -853,17 +955,37 @@
         shares[index, column:, :] = ends
 
 
-def finish_rows_kernel(pieces, residual, d_columns, tokens, scale, gain, outcome, grad_tokens):
+def finish_rows_kernel(
+    piece_0,
+    piece_1,
+    piece_2,
+    piece_3,
+    residual,
+    d_columns,
+    tokens,
+    scale,
+    gain,
+    outcome,
+    grad_tokens,
+    *norm_out,
+):
     column = tokens.shape[0]
-    total = pieces[0].astype(F32)
-    for index in range(1, pieces.shape[0]):
-        total = total + pieces[index].astype(F32)
+    total = piece_0[...].astype(F32)
+    for piece in (piece_1, piece_2, piece_3):
+        total = total + piece[...].astype(F32)
     along = total[column : column + 1] + total[column + 8 : column + 9]
     inverse = scale[...]
     pulled = total[:column] * gain[...]
     scaled = tokens[...].astype(F32) * inverse
     grad_tokens[...] = d_columns[...] + inverse * (pulled - scaled * along)
-    outcome[...] = (residual[...] + total[column + 16 :]).astype(BF16)
+    plain = 2 * column + 16
+    outcome[...] = (residual[...] + total[column + 16 : plain]).astype(BF16)
+    for out in norm_out:
+        norm = total[plain : plain + NORM_ROWS] + total[plain + NORM_ROWS :]
+        width = out.shape[0]
+        out[...] = jnp.concatenate(
+            [norm[row : row + 1] for row in range(width // 128)], axis=1
+        ).reshape(width)
 
 
 def take_blocks(target, pieces):
@@ -939,8 +1061,6 @@
     take_turned(d_gate, lasts, 0)
     wide_grad[0] = dot_nn(d_gate[...], normed[...])
     started = run_copies([(wide_grad.at[0], in_grad.at[0])], semaphores)
-    take_turned(d_mixed, lasts, chans)
-    x_grad[...] = dot_nt(d_mixed[...], acts[...])[:proj]
     for copy in arriving:
         copy.wait()
     take_turned(d_gate, seconds, width)
@@ -954,6 +1074,8 @@
         started += run_copies(
             [(wide_grad.at[2, rows], out_grad.at[rows])], semaphores.at[pl.ds(2 + index, 1)]
         )
+    take_turned(d_mixed, lasts, chans)
+    x_grad[...] = dot_nt(d_mixed[...], acts[...])[:proj]
     vectors = seconds[0][width + chans :].astype(F32)
     for piece in seconds[1:]:
         vectors = vectors + piece[width + chans :].astype(F32)
@@ -967,7 +1089,7 @@
     skip_grad[...] = rows[states + 1].reshape(chans)
     norm_grad[...] = jnp.concatenate(
         [rows[states + 2 : states + 3], rows[states + 3 : states + 4]], axis=1
-    )
+    ).reshape(width)
     for copy in started:
         copy.wait()
 
@@ -995,11 +1117,6 @@
 
 def swap(values, bits):
     return lax.ppermute(values, "dp", [(i, i ^ bits) for i in range(NEAR_GROUPS)])
-
-
-def split_beside(along_x, along_y):
-    half = along_x.shape[0] // 2
-    return along_y[:half], along_x[half:]
 
 
 def swap_across(halves):
@@ -1148,17 +1265,28 @@
         [((width, length), F32)],
         scalars=1, loose_outs=(2,), staged=(1, 2, 3, 4, 5, 7))
     if near:
-        first_w, second_w, grad_slots, d_hidden = run_kernel(
+        half_out = (((width + 2 * chans) // 2, length), BF16)
+        first_w, second_w, grad_slots, *halves, d_hidden = run_kernel(
             functools.partial(unpack_kernel, share, capacity),
-            weight_outs + [slots_out, ((slot_count, hidden_units), F32)],
-            after([weights], send_slots, first_x, first_y),
-            [*weight_outs, slots_out, pltpu.SemaphoreType.DMA((5 * groups,))],
-            far_args=(0,),
-            far_outs=(0, 1, 2),
+            weight_outs
+            + [slots_out, half_out, half_out, ((slot_count, hidden_units), F32)],
+            [*after([weights], send_slots), first_x, first_y],
+            [
+                *weight_outs,
+                slots_out,
+                ((2, *half_out[0]), BF16),
+                pltpu.SemaphoreType.DMA((4,)),
+                pltpu.SemaphoreType.DMA((5 * groups,)),
+            ],
+            far_args=(0, 1, 2),
+            far_outs=(0, 1, 2, 3, 4),
         )
+        first_d = swap_across(halves)
     arrived = exchange_slots(send_slots)
     hidden, d_pre, d_slots = run_kernel(
         expert_kernel, [hidden_out, hidden_out, slots_out], [arrived, first_w, d_hidden], loose_outs=(2,), staged=(0, 1, 2))
+    if near:
+        d_slots = after([d_slots], first_d)[0]
     back_slots = exchange_slots(d_slots)
     grad_args = [arrived, grad_slots, hidden, d_pre, second_w]
     grad_out = ((experts, share, hidden_units), F32)
@@ -1173,8 +1301,7 @@
                 pltpu.SemaphoreType.DMA((3 * groups,)),
             ],
             far_outs=(0,), staged=range(5))
-        first_d = swap_across(split_beside(*after([first_x, first_y], arrived)))
-        back_slots = after([back_slots], packed, first_d)[0]
+        back_slots = after([back_slots], packed)[0]
         packed = after([packed], back_slots)[0]
         owned = exchange(packed)
     else:
@@ -1191,6 +1318,23 @@
         firsts = swap_near([first, first_x, first_y, *first_d])
 
         send_pieces = after(send_pieces, firsts)
+    decays, history, step_rows, drive_rows, step_slope, y_slope, gate_slope = run_kernel(
+        scan_states_kernel,
+        [
+            ((length * states, full), F32),
+            (((length + 1) * states, full), F32),
+            ((length, full), F32),
+            ((length, full), F32),
+            ((length, chans), F32),
+            ((length, chans), F32),
+            ((length, chans), F32),
+        ],
+        [y, gate, act, *after([mixed], back_chunks[0]), masks, dt_proj, dt_bias, decay_log],
+        [((states, full), F32), ((length, full), F32)],
+        staged=range(5),
+        held_outs=range(7),
+    )
+    send_pieces = after(send_pieces, decays)
     d_columns, d_mix, d_gated, gain_grad_two = run_kernel(
         mixer_grad_kernel,
         [
@@ -1212,29 +1356,31 @@
         ],
         [
             d_gated,
-            y,
-            gate,
+            y_slope,
+            gate_slope,
             act,
             mixed,
-            masks,
             dt_proj,
-            dt_bias,
             decay_log,
             skip_gain,
             gain_grad_two,
             d_mix,
+            decays,
+            history,
+            step_rows,
+            drive_rows,
+            step_slope,
         ],
         [
             ((states, full), F32),
             ((length, full), F32),
             ((length, full), F32),
             ((length, full), F32),
-            ((length, full), F32),
-            ((length, full), F32),
-            ((length, full), F32),
-            ((length * states, full), F32),
-            (((length + 1) * states, full), F32),
-        ], loose_outs=(0, 3), staged=(1, 2, 3, 4, 5, 6), held_outs=(1, 2))
+        ],
+        staged=(3, 4),
+        loose_outs=(0, 3),
+        held_outs=(1, 2),
+    )
     d_mixed_pieces = share_rows(d_mixed_part, parts)
     if near:
         second_x, second_y = swap(second, 2), swap(second, 4)
@@ -1257,39 +1403,10 @@
             norm_one,
         ],
         [((parts, proj, length), BF16), ((width, length), F32), ((length, full), F32)],
-        scalars=1, loose_outs=(0, 1), staged=(1, 2, 3, 4, 7, 8, 9, 13))
-    shares_out = ((parts, 2 * column + 16, length), BF16)
+        scalars=1, loose_outs=(1,), staged=(1, 2, 3, 4, 7, 8, 9, 13))
+    share_outs = [((2 * column + 16, length), BF16)] * parts
     if near:
-        (shares,) = run_kernel(
-            functools.partial(back_folded_kernel, share),
-            [shares_out],
-            [choose, normed_shares, owned],
-            [slots_out, pltpu.SemaphoreType.DMA((3 * groups,))],
-            staged=(0,),
-            far_args=(2,),
-            loose_outs=(0,),
-        )
-        grad_expert_in, grad_expert_out = run_kernel(
-            functools.partial(owner_kernel, share),
-            [grad_out] * 2,
-            after([owned], shares),
-            [
-                ((groups, 2 * share, hidden_units), BF16),
-                ((groups, 2 * share, hidden_units), F32),
-                pltpu.SemaphoreType.DMA((groups,)),
-                pltpu.SemaphoreType.DMA((2 * groups,)),
-            ],
-            far_args=(0,),
-            far_outs=(0, 1),
-        )
-        second, second_x, second_y = after([second, second_x, second_y], grad_expert_in)
-        halves = split_beside(second_x, second_y)
-        last = after([message], second_x, second_y)[0]
-        lasts = [last, swap(last, 2), swap(last, 4), swap(last, 6)]
-        second_d = swap_across(halves)
-        *seconds, near_own, near_x, near_y = swap_near([second, second_x, second_y])
-        firsts = after(firsts, halves, near_own, near_x, near_y)
-
+        lasts = [message, swap(message, 2), swap(message, 4), swap(message, 6)]
         def first_sets(*refs):
             first_sets_kernel(refs[:10], *refs[10:])
 
@@ -1300,17 +1417,60 @@
                 ((chans, groups * length), BF16),
                 ((chans, groups * length), BF16),
             ],
-            firsts,
+            after(firsts, message, owned),
             [((groups, width + 2 * chans, length), BF16), pltpu.SemaphoreType.DMA((10,))],
             far_args=range(10),
+            held_outs=(0, 1, 2),
         )
+        second_x, second_y = after([second_x, second_y], all_normed)
+        grad_expert_in, grad_expert_out, *halves = run_kernel(
+            functools.partial(owner_kernel, share),
+            [grad_out, grad_out, half_out, half_out],
+            [owned, second_x, second_y],
+            [
+                ((groups, 2 * share, hidden_units), BF16),
+                ((groups, 2 * share, hidden_units), F32),
+                ((2, *half_out[0]), BF16),
+                pltpu.SemaphoreType.DMA((2 + groups,)),
+                pltpu.SemaphoreType.DMA((2 + 2 * groups,)),
+            ],
+            far_args=(0, 1, 2),
+            far_outs=(0, 1, 2, 3),
+        )
+        second_d = swap_across(halves)
+        lasts = swap_near(after(lasts, halves))
+
+        def back_folded(*refs):
+            back_folded_kernel(share, *refs[:4], refs[4 : 4 + groups], *refs[4 + groups :])
+
+        *shares, grad_conv_weight, grad_conv_bias = run_kernel(
+            back_folded,
+            [((2 * column + 16 + 2 * NORM_ROWS, length), BF16)] * parts
+            + [((4, chans), F32), ((chans,), F32)],
+            [place, choose, normed_shares, owned, *lasts],
+            [
+                slots_out,
+                ((width, length), BF16),
+                ((groups, tiles * 2 * VECTORS_TWO, length), BF16),
+                pltpu.SemaphoreType.DMA((4 * groups,)),
+            ],
+            scalars=1,
+            staged=(1, 2),
+            far_args=range(3, 4 + groups),
+            loose_outs=range(parts + 2),
+        )
+        norm_out = [((width,), F32)]
     else:
-        (shares,) = run_kernel(
+        shares = run_kernel(
             back_columns_kernel,
-            [shares_out],
-            [choose, normed_shares, exchange_slots(moe_slots)],
-            loose_outs=(0,),
+            share_outs,
+            [place, choose, normed_shares, exchange_slots(moe_slots)],
+            [((width, length), BF16)],
+            scalars=1,
+            loose_outs=(0, 1, 2, 3),
         )
+
+        norm_out = []
 
         def owner_sum(values):
             got = exchange(values.reshape(groups, share, hidden_units)).astype(F32)
@@ -1318,37 +1478,10 @@
 
         grad_expert_in = owner_sum(grad_first)
         grad_expert_out = owner_sum(grad_second)
-    shares_made = shares
-    shares = lax.all_to_all(shares, "tensor", split_axis=0, concat_axis=0, tiled=True)
-    outcome, grad_tokens = run_kernel(
-        finish_rows_kernel,
-        [((column, length), BF16), ((column, length), F32)],
-        [shares, residual_columns, d_columns, tokens_turned, scale, gain_columns],
-        staged=range(6),
-        loose_outs=(0, 1),
-    )
-
+    pieces = send_chunks(shares)
     if near:
-        lasts, second_d = after([lasts, second_d], all_normed, grad_tokens)
-        lasts = swap_near(lasts)
-        near_d = [swap(part, 1) for part in second_d]
-        seconds = [*seconds, *second_d, near_own, near_x, near_y, *near_d]
-
-        def late_vectors(*refs):
-            late_vectors_kernel(refs[:groups], *refs[groups:])
-
-        grad_conv_weight, grad_conv_bias, norm_shares = run_kernel(
-            late_vectors,
-            [((4, chans), F32), ((chans,), F32), ((1, width), F32)],
-            lasts,
-            [
-                ((groups, tiles * 2 * VECTORS_TWO, length), BF16),
-                pltpu.SemaphoreType.DMA((groups,)),
-            ],
-            far_args=range(groups),
-            loose_outs=(0, 1, 2),
-        )
-        norm_parts = share_rows(after([norm_shares], near_d)[0], parts)
+        seconds = [second, second_x, second_y, *second_d]
+        seconds = swap_near(after(seconds, grad_conv_weight))
 
         def wide_grads(*refs):
             wide_grads_kernel(
@@ -1374,9 +1507,9 @@
                 ((chans,), F32),
                 ((states, chans), F32),
                 ((chans,), F32),
-                ((1, width), F32),
+                ((width,), F32),
             ],
-            [*after(seconds, norm_shares), *lasts, all_normed, all_gated, all_act],
+            [*seconds, *lasts, all_normed, all_gated, all_act],
             [
                 ((groups, width + 2 * chans, length), BF16),
                 ((groups, last_rows, length), BF16),
@@ -1393,7 +1526,7 @@
             far_outs=(0, 1),
             loose_outs=range(8),
         )
-        grad_norm_one = sum(norm_parts).reshape(width)
+        pieces = after(pieces, grad_out_proj)
     else:
         top = last_rows - tiles * 2 * VECTORS_TWO
         ones = second[width + chans :].astype(F32).T
@@ -1425,6 +1558,15 @@
         grad_conv_weight = twos[:4]
         grad_conv_bias = twos[4]
         grad_norm_one = sum(share_rows(twos[5:7].reshape(1, width), parts)).reshape(width)
+    outcome, grad_tokens, *norm_one_grad = run_kernel(
+        finish_rows_kernel,
+        [((column, length), BF16), ((column, length), F32)] + norm_out,
+        [*pieces, residual_columns, d_columns, tokens_turned, scale, gain_columns],
+        staged=range(9),
+        loose_outs=(0, 1, 2),
+    )
+    if near:
+        (grad_norm_one,) = norm_one_grad
     return (
         outcome.T,
         grad_tokens.T,

time: 225 us -> 213 us (0.947)
  local copies, waits for them, and re-layouts: 16.1 us -> 7.64 us
  starting transfers between devices: 75.6 us -> 71.6 us
    slice x4 -> x0, local copies, waits for them, and re-layouts: 5.38 us -> none  [split_beside(): return (along_y[:half], along_x[half:])]
    ppermute x24, waiting for transfers between devices: 31.5 us -> 26.5 us  [send_chunks(): lax.ppermute(chunks[s], 'tensor', pairs[s])]
    all_to_all x4, waiting for transfers between devices: 0.73 us -> 5.44 us  [exchange(): return lax.all_to_all(values, 'dp', split_axis=0, concat_axis=0, tiled=True)]
    all_to_all x1 -> x0, starting transfers between devices: 4.16 us -> none  [body(): lax.all_to_all(shares, 'tensor', split_axis=0, concat_axis=0, tiled=True)]
    unnamed x124 -> x120, local copies, waits for them, and re-layouts: 10.7 us -> 7.64 us
  transfers between devices with their start and end apart: 54 -> 53, of which waited for: 26 -> 27; matrix products, arithmetic and copies ran while one was open for 3% -> 0% of each run, Pallas kernels for 31% -> 34%
where the time goes in v4:
time: 213 us; the launch traced here: 212 us
  Pallas kernels  80.1 us (38%)
  starting transfers between devices  71.6 us (34%)
  waiting for transfers between devices  51.4 us (24%)
  local copies, waits for them, and re-layouts  7.64 us (4%)
    pallas_call x17, Pallas kernels, run_kernel(): pl.pallas_call(body, out_shape=[held(index, shape, dtype) for index, (sha...  80.1 us
    ppermute x24, starting transfers between devices, send_chunks(): lax.ppermute(chunks[s], 'tensor', pairs[s])  37.7 us
    ppermute x24, waiting for transfers between devices, send_chunks(): lax.ppermute(chunks[s], 'tensor', pairs[s])  26.5 us
    ppermute x25, waiting for transfers between devices, swap(): lax.ppermute(values, 'dp', [(i, i ^ bits) for i in range(NEAR_GROUPS)])  19.5 us
    all_to_all x4, starting transfers between devices, exchange(): return lax.all_to_all(values, 'dp', split_axis=0, concat_axis=0, tiled=True)  18.4 us
    ppermute x25, starting transfers between devices, swap(): lax.ppermute(values, 'dp', [(i, i ^ bits) for i in range(NEAR_GROUPS)])  15.5 us
    unnamed x120, local copies, waits for them, and re-layouts  7.64 us
    all_to_all x4, waiting for transfers between devices, exchange(): return lax.all_to_all(values, 'dp', split_axis=0, concat_axis=0, tiled=True)  5.44 us
  transfers between devices with their start and end apart: 53, of which 27 were waited for; matrix products, arithmetic and copies ran while one was open for 0% of the time, Pallas kernels for 34%

profile of v4, /device:TPU:0, one launch (start us, length us, event | category | flops | bytes accessed | tf_op | source)
XLA Modules:
  0.0 212.3 jit_solution(2868147982459826567)
XLA Ops:
  0.6 5.4 %shard_map.280 = (f32[4,128,128]{2,1,0:T(8,128)}, bf16[256,128]{1,0:T(8,128)(2,1)}, bf16[8,336,768]{2,1,0:T(8,128)(2,1)}) custom-call(s32[1,128]{1,0:T(1,128)} %bitcast.25, s32[1,128]{1,0:T(1,128)} %bitcast.26, bf16[128,1152]{1,0:T(8,128)(2,1)} %refs_7_.8, bf16[8,144,768]{2,1,0:T(8,128)(2,1)} %refs_3_.1, bf16[8,144,768]{2,1,0:T(8,128)(2,1)} %refs_4_.1), custom_call_target="tpu_custom_call" | custom-call | tf_op jit(solution)/shard_map/pallas_call | solution.py:70
  6.1 5.4 %all-to-all-start.1 = ((bf16[8,336,768]{2,1,0:T(8,128)(2,1)}), bf16[8,336,768]{2,1,0:T(8,128)(2,1)}, u32[]{:S(2)}, u32[]{:S(2)}) async-start(bf16[8,336,768]{2,1,0:T(8,128)(2,1)} %get-tuple-element.141), calls=%async_computation.1 | async-start | bytes 8257536 | tf_op jit(solution)/shard_map/all_to_all | solution.py:1172
  11.6 4.5 %collective-permute-start.2 = (bf16[288,128]{1,0:T(8,128)(2,1)S(1)}, bf16[288,128]{1,0:T(8,128)(2,1)S(1)}, u32[]{:S(2)}, u32[]{:S(2)}) collective-permute-start(bf16[288,128]{1,0:T(8,128)(2,1)S(1)} %bitcast.22), channel_id=1, source_target_pairs={{0,3},{1,0},{2,1},{3,2},{4,7},{5,4},{6,5},{7,6},{8,11},{9,8},{10,9... | collective-permute-start | bytes 221192 | tf_op jit(solution)/shard_map/ppermute | solution.py:1100
  18.8 5.0 %collective-permute-done.1.refs_3_ = bf16[288,128]{1,0:T(8,128)(2,1)S(1)} collective-permute-done((bf16[288,128]{1,0:T(8,128)(2,1)S(1)}, bf16[288,128]{1,0:T(8,128)(2,1)S(1)}, u32[]{:S(2)}, u32[]{:S(2)}) %collective-permute-start.1) | collective-permute-done | bytes 73760 | tf_op jit(solution)/shard_map/ppermute | solution.py:1100
  24.5 3.7 %shard_map.281 = (bf16[128,1152]{1,0:T(8,128)(2,1)}, bf16[1152,128]{1,0:T(8,128)(2,1)}, bf16[128,576]{1,0:T(8,128)(2,1)}, f32[128,576]{1,0:T(8,128)}, f32[128,57...) custom-call(s32[1]{0:T(128)} %bitcast.refs_0_, ...), custom_call_target="tpu_custom_call" | custom-call | tf_op jit(solution)/shard_map/pallas_call | solution.py:70
  36.4 6.5 %shard_map.282 = (bf16[32,1152]{1,0:T(8,128)(2,1)S(1)}, bf16[32,1152]{1,0:T(8,128)(2,1)S(1)}, bf16[32,1152]{1,0:T(8,128)(2,1)S(1)}, bf16[32,1152]{1,0:T(8,128)(2...) custom-call(s32[1]{0:T(128)} %bitcast.refs_0_, bf16[104,128]{1,0:T(8,128)(2,1)} %copy-done.17, ...), custom_call_target="tpu_custom_call" | custom-call | tf_op jit(solution)/shard_map/pallas_call | solution.py:70
  50.3 3.0 %collective-permute-start.11 = (bf16[32,1152]{1,0:T(8,128)(2,1)S(1)}, bf16[32,1152]{1,0:T(8,128)(2,1)S(1)}, u32[]{:S(2)}, u32[]{:S(2)}) collective-permute-start(bf16[32,1152]{1,0:T(8,128)(2,1)S(1)} %add_convert_fusion.1.refs_1_), channel_id=1, source_target_pairs={{0,3},{1,0},{2,1},{3,2},{4,7},{5,4},{6,5},{7,6},{8,11},{9,8},{10,9... | collective-permute-start | bytes 221192 | tf_op jit(solution)/shard_map/ppermute | solution.py:1100
  63.5 4.2 %all-to-all-start = ((bf16[8,32,1152]{2,1,0:T(8,128)(2,1)}), bf16[8,32,1152]{2,1,0:T(8,128)(2,1)}, u32[]{:S(2)}, u32[]{:S(2)}) async-start(bf16[8,32,1152]{2,1,0:T(8,128)(2,1)} %bitcast.16), calls=%async_computation | async-start | bytes 1179648 | tf_op jit(solution)/shard_map/all_to_all | solution.py:1172
  67.7 4.9 %collective-permute-done.13.refs_2_ = bf16[2304,128]{1,0:T(8,128)(2,1)} collective-permute-done((bf16[2304,128]{1,0:T(8,128)(2,1)S(1)}, bf16[2304,128]{1,0:T(8,128)(2,1)}, u32[]{:S(2)}, u32[]{:S(2)}) %collective-permute-start.13) | collective-permute-done | bytes 589856 | tf_op jit(solution)/shard_map/ppermute | solution.py:1119
  72.6 6.8 %shard_map.284 = (bf16[1152,768]{1,0:T(8,128)(2,1)}, bf16[1152,768]{1,0:T(8,128)(2,1)}, bf16[256,1152]{1,0:T(8,128)(2,1)}, bf16[1152,128]{1,0:T(8,128)(2,1)}, bf...) custom-call(bf16[8,336,768]{2,1,0:T(8,128)(2,1)} %all-to-all-done.1.refs_0_, ...), custom_call_target="tpu_custom_call" | custom-call | tf_op jit(solution)/shard_map/pallas_call | solution.py:70
  81.5 3.8 %shard_map.285 = (bf16[256,768]{1,0:T(8,128)(2,1)}, bf16[256,768]{1,0:T(8,128)(2,1)}, bf16[256,1152]{1,0:T(8,128)(2,1)S(1)}) custom-call(bf16[256,1152]{1,0:T(8,128)(2,1)} %bitcast.7.refs_0_, bf16[1152,768]{1,0:T(8,128)(2,1)} %get-tuple-element.144.refs_1_, f32[256,768]{1,0:T(8,128)} %get-tuple-element.145.refs_2_), custom_call_target="tpu_custom_call" | custom-call | tf_op jit(solution)/shard_map/pallas_call | solution.py:70
  89.6 4.2 %all-to-all-start.2 = ((bf16[8,32,1152]{2,1,0:T(8,128)(2,1)}), bf16[8,32,1152]{2,1,0:T(8,128)(2,1)}, u32[]{:S(2)}, u32[]{:S(2)}) async-start(bf16[8,32,1152]{2,1,0:T(8,128)(2,1)} %bitcast.17), calls=%async_computation.2 | async-start | bytes 1179648 | tf_op jit(solution)/shard_map/all_to_all | solution.py:1172
  93.8 5.0 %shard_map.286 = bf16[8,336,768]{2,1,0:T(8,128)(2,1)} custom-call(bf16[256,1152]{1,0:T(8,128)(2,1)} %bitcast.7.refs_0_, bf16[256,1152]{1,0:T(8,128)(2,1)} %get-tuple-element.150.refs_1_, bf16[256,768]{1,0:T(8,128)(2,1)} %get-tuple-element.151.refs_2_, bf16[256,768]{1,0:T(8,128)(2,1)} %get-tuple-element.152.refs_3_, bf16[1152,768]{1,0:T(8,128)(2,1)} %get-tuple-element.153.refs_4_), custom_call_target="tpu_custom_call" | custom-call | tf_op jit(solution)/shard_map/pallas_call | solution.py:70
  98.9 5.4 %all-to-all-done.2 = bf16[8,32,1152]{2,1,0:T(8,128)(2,1)} async-done(((bf16[8,32,1152]{2,1,0:T(8,128)(2,1)}), bf16[8,32,1152]{2,1,0:T(8,128)(2,1)}, u32[]{:S(2)}, u32[]{:S(2)}) %all-to-all-start.2) | async-done | bytes 589856 | tf_op jit(solution)/shard_map/all_to_all | solution.py:1172
  104.3 4.6 %all-to-all-start.3 = ((bf16[8,336,768]{2,1,0:T(8,128)(2,1)}), bf16[8,336,768]{2,1,0:T(8,128)(2,1)}, u32[]{:S(2)}, u32[]{:S(2)}) async-start(bf16[8,336,768]{2,1,0:T(8,128)(2,1)} %shard_map.286), calls=%async_computation.3 | async-start | bytes 8257536 | tf_op jit(solution)/shard_map/all_to_all | solution.py:1172
  122.2 3.2 %collective-permute-start.21 = (bf16[32,1152]{1,0:T(8,128)(2,1)S(1)}, bf16[32,1152]{1,0:T(8,128)(2,1)S(1)}, u32[]{:S(2)}, u32[]{:S(2)}) collective-permute-start(bf16[32,1152]{1,0:T(8,128)(2,1)S(1)} %add_convert_fusion.refs_1_), channel_id=1, source_target_pairs={{0,3},{1,0},{2,1},{3,2},{4,7},{5,4},{6,5},{7,6},{8,11},{9,8},{10,9... | collective-permute-start | bytes 221192 | tf_op jit(solution)/shard_map/ppermute | solution.py:1100
  126.4 4.6 %shard_map.288 = (f32[2048,640]{1,0:T(8,128)S(1)}, f32[2064,640]{1,0:T(8,128)S(1)}, f32[128,640]{1,0:T(8,128)S(1)}, f32[128,640]{1,0:T(8,128)S(1)}, f32[128,576]...) custom-call(f32[128,576]{1,0:T(8,128)} %get-tuple-element.163.refs_0_, ...), custom_call_target="tpu_custom_call" | custom-call | tf_op jit(solution)/shard_map/pallas_call | solution.py:70
  133.8 3.1 %shard_map.289 = (f32[288,128]{1,0:T(8,128)}, bf16[1152,128]{1,0:T(8,128)(2,1)S(1)}, f32[128,576]{1,0:T(8,128)S(1)}, f32[1,1152]{1,0:T(1,128)S(1)}) custom-call(s32[1]{0:T(128)} %bitcast.refs_0_, bf16[32,1152]{1,0:T(8,128)(2,1)} %copy-done.40, bf16[32,1152]{1,0:T(8,128)(2,1)} %copy-done.47, bf16[32,1152]{1,0:T(8,128)(2,1)} %copy-done.46, ...), custom_call_target="tpu_custom_call" | custom-call | tf_op jit(solution)/shard_map/pallas_call | solution.py:70
  136.9 9.2 %shard_map.290 = (bf16[104,128]{1,0:T(8,128)(2,1)S(1)}, f32[128,576]{1,0:T(8,128)S(1)}, bf16[128,576]{1,0:T(8,128)(2,1)S(1)}, bf16[2304,128]{1,0:T(8,128)(2,1)S(1)}) custom-call(f32[128,576]{1,0:T(8,128)S(1)} %get-tuple-element.172.refs_0_, f32[128,576]{1,0:T(8,128)S(1)} %get-tuple-element.173.refs_1_, f32[128,576]{1,0:T(8,128)S(1)} %get-tuple-element.174.refs_2_, ...), custom_call_target="tpu_custom_call" | custom-call | tf_op jit(solution)/shard_map/pallas_call | solution.py:70
  157.8 3.5 %shard_map.291 = (bf16[4,304,128]{2,1,0:T(8,128)(2,1)}, bf16[768,128]{1,0:T(8,128)(2,1)S(1)}) custom-call(s32[1]{0:T(128)} %bitcast.refs_0_, bf16[104,128]{1,0:T(8,128)(2,1)} %copy-done.16, bf16[104,128]{1,0:T(8,128)(2,1)} %copy-done.58, bf16[104,128]{1,0:T(8,128)(2,1)} %copy-done.56, bf16[104,128]{1,0:T(8,128)(2,1)} %copy-done.54, ...), custom_call_target="tpu_custom_call" | custom-call | tf_op jit(solution)/shard_map/pallas_call | solution.py:70
  164.8 3.5 %shard_map.292 = (bf16[1024,1152]{1,0:T(8,128)(2,1)S(1)}, bf16[576,1024]{1,0:T(8,128)(2,1)S(1)}, bf16[576,1024]{1,0:T(8,128)(2,1)S(1)}) custom-call(bf16[2304,128]{1,0:T(8,128)(2,1)} %copy-done.4, bf16[2304,128]{1,0:T(8,128)(2,1)} %collective-permute-done.12.refs_1_, bf16[2304,128]{1,0:T(8,128)(2,1)} %collective-permute-done.13.refs_2_, ...), custom_call_target="tpu_custom_call" | custom-call | tf_op jit(solution)/shard_map/pallas_call | solution.py:70
  170.5 5.4 %shard_map.293 = (f32[8,144,768]{2,1,0:T(8,128)}, f32[8,144,768]{2,1,0:T(8,128)}, bf16[1152,128]{1,0:T(8,128)(2,1)}, bf16[1152,128]{1,0:T(8,128)(2,1)}) custom-call(bf16[8,336,768]{2,1,0:T(8,128)(2,1)} %all-to-all-done.3.refs_0_.refs_3_, bf16[2304,128]{1,0:T(8,128)(2,1)} %collective-permute-done.33.refs_1_, bf16[2304,128]{1,0:T(8,128)(2,1)} %collective-permute-done.34.refs_2_), custom_call_target="tpu_custom_call" | custom-call | tf_op jit(solution)/shard_map/pallas_call | solution.py:70
  182.2 3.3 %shard_map.294 = (bf16[624,128]{1,0:T(8,128)(2,1)S(1)}, bf16[624,128]{1,0:T(8,128)(2,1)S(1)}, bf16[624,128]{1,0:T(8,128)(2,1)S(1)}, bf16[624,128]{1,0:T(8,128)(2,1)S(1)}, f32[4,576]{1,0:T(4,128)}, /*index=5*/f32[576]{0:T(1024)}) custom-call(s32[1]{0:T(128)} %bitcast.refs_0_, bf16[256,128]{1,0:T(8,128)(2,1)} %get-tuple-element.129.refs_7_.refs_1_, ...), custom_call_target="tpu_custom_call" | custom-call | tf_op jit(solution)/shard_map/pallas_call | solution.py:70
  198.7 10.4 %shard_map.295 = (f32[576,1152]{1,0:T(8,128)}, f32[2,576,1152]{2,1,0:T(8,128)}, f32[104,576]{1,0:T(8,128)}, f32[72,576]{1,0:T(8,128)}, f32[576]{0:T(1024)}, /*in...) custom-call(bf16[2304,128]{1,0:T(8,128)(2,1)} %copy-done.7, bf16[2304,128]{1,0:T(8,128)(2,1)} %collective-permute-done.33.refs_1_, ...), custom_call_target="tpu_custom_call" | custom-call | tf_op jit(solution)/shard_map/pallas_call | solution.py:70
  (221 shorter events, 92.0 us)
Async XLA Ops:
  6.1 57.3 %all-to-all-start.1 = ((bf16[8,336,768]{2,1,0:T(8,128)(2,1)}), bf16[8,336,768]{2,1,0:T(8,128)(2,1)}, u32[]{:S(2)}, u32[]{:S(2)}) async-start(bf16[8,336,768]{2,1,0:T(8,128)(2,1)} %get-tuple-element.141), calls=%async_computation.1 | async-start | bytes 8257536 | tf_op jit(solution)/shard_map/all_to_all | solution.py:1172
  47.0 25.6 %collective-permute-start.13 = (bf16[2304,128]{1,0:T(8,128)(2,1)S(1)}, bf16[2304,128]{1,0:T(8,128)(2,1)}, u32[]{:S(2)}, u32[]{:S(2)}) collective-permute-start(bf16[2304,128]{1,0:T(8,128)(2,1)S(1)} %get-tuple-element.190.refs_0_), channel_id=1, source_target_pairs={{0,16},{4,20},{8,24},{12,28},{16,0},{20,4},{24,8},{28,12},{1,17},{... | collective-permute-start | bytes 1769480 | tf_op jit(solution)/shard_map/ppermute | solution.py:1119
  48.7 23.9 %collective-permute-start.12 = (bf16[2304,128]{1,0:T(8,128)(2,1)S(1)}, bf16[2304,128]{1,0:T(8,128)(2,1)}, u32[]{:S(2)}, u32[]{:S(2)}) collective-permute-start(bf16[2304,128]{1,0:T(8,128)(2,1)S(1)} %get-tuple-element.190.refs_0_), channel_id=1, source_target_pairs={{0,8},{4,12},{8,0},{12,4},{16,24},{20,28},{24,16},{28,20},{1,9},{5... | collective-permute-start | bytes 1769480 | tf_op jit(solution)/shard_map/ppermute | solution.py:1119
  63.5 18.0 %all-to-all-start = ((bf16[8,32,1152]{2,1,0:T(8,128)(2,1)}), bf16[8,32,1152]{2,1,0:T(8,128)(2,1)}, u32[]{:S(2)}, u32[]{:S(2)}) async-start(bf16[8,32,1152]{2,1,0:T(8,128)(2,1)} %bitcast.16), calls=%async_computation | async-start | bytes 1179648 | tf_op jit(solution)/shard_map/all_to_all | solution.py:1172
  89.6 14.7 %all-to-all-start.2 = ((bf16[8,32,1152]{2,1,0:T(8,128)(2,1)}), bf16[8,32,1152]{2,1,0:T(8,128)(2,1)}, u32[]{:S(2)}, u32[]{:S(2)}) async-start(bf16[8,32,1152]{2,1,0:T(8,128)(2,1)} %bitcast.17), calls=%async_computation.2 | async-start | bytes 1179648 | tf_op jit(solution)/shard_map/all_to_all | solution.py:1172
  104.3 60.6 %all-to-all-start.3 = ((bf16[8,336,768]{2,1,0:T(8,128)(2,1)}), bf16[8,336,768]{2,1,0:T(8,128)(2,1)}, u32[]{:S(2)}, u32[]{:S(2)}) async-start(bf16[8,336,768]{2,1,0:T(8,128)(2,1)} %shard_map.286), calls=%async_computation.3 | async-start | bytes 8257536 | tf_op jit(solution)/shard_map/all_to_all | solution.py:1172
  112.6 9.6 %collective-permute-start.22 = (bf16[2304,128]{1,0:T(8,128)(2,1)S(1)}, bf16[2304,128]{1,0:T(8,128)(2,1)S(1)}, u32[]{:S(2)}, u32[]{:S(2)}) collective-permute-start(bf16[2304,128]{1,0:T(8,128)(2,1)S(1)} %get-tuple-element.190.refs_0_), channel_id=1, source_target_pairs={{0,4},{4,0},{8,12},{12,8},{16,20},{20,16},{24,28},{28,24},{1,5},{5... | collective-permute-start | bytes 1769480 | tf_op jit(solution)/shard_map/ppermute | solution.py:1119
  112.7 12.8 %collective-permute-start.24 = (bf16[2304,128]{1,0:T(8,128)(2,1)}, bf16[2304,128]{1,0:T(8,128)(2,1)S(1)}, u32[]{:S(2)}, u32[]{:S(2)}) collective-permute-start(bf16[2304,128]{1,0:T(8,128)(2,1)} %collective-permute-done.13.refs_2_), channel_id=1, source_target_pairs={{0,4},{4,0},{8,12},{12,8},{16,20},{20,16},{24,28},{28,24},{1,5},{5... | collective-permute-start | bytes 1769480 | tf_op jit(solution)/shard_map/ppermute | solution.py:1119
  113.1 12.3 %collective-permute-start.23 = (bf16[2304,128]{1,0:T(8,128)(2,1)}, bf16[2304,128]{1,0:T(8,128)(2,1)S(1)}, u32[]{:S(2)}, u32[]{:S(2)}) collective-permute-start(bf16[2304,128]{1,0:T(8,128)(2,1)} %collective-permute-done.12.refs_1_), channel_id=1, source_target_pairs={{0,4},{4,0},{8,12},{12,8},{16,20},{20,16},{24,28},{28,24},{1,5},{5... | collective-permute-start | bytes 1769480 | tf_op jit(solution)/shard_map/ppermute | solution.py:1119
  120.8 10.3 %collective-permute-start.25 = (bf16[1152,128]{1,0:T(8,128)(2,1)}, bf16[1152,128]{1,0:T(8,128)(2,1)S(1)}, u32[]{:S(2)}, u32[]{:S(2)}) collective-permute-start(bf16[1152,128]{1,0:T(8,128)(2,1)} %collective-permute-done.14.refs_3_), channel_id=1, source_target_pairs={{0,4},{4,0},{8,12},{12,8},{16,20},{20,16},{24,28},{28,24},{1,5},{5... | collective-permute-start | bytes 884744 | tf_op jit(solution)/shard_map/ppermute | solution.py:1119
  122.1 9.0 %collective-permute-start.26 = (bf16[1152,128]{1,0:T(8,128)(2,1)}, bf16[1152,128]{1,0:T(8,128)(2,1)S(1)}, u32[]{:S(2)}, u32[]{:S(2)}) collective-permute-start(bf16[1152,128]{1,0:T(8,128)(2,1)} %collective-permute-done.15.refs_4_), channel_id=1, source_target_pairs={{0,4},{4,0},{8,12},{12,8},{16,20},{20,16},{24,28},{28,24},{1,5},{5... | collective-permute-start | bytes 884744 | tf_op jit(solution)/shard_map/ppermute | solution.py:1119
  122.2 8.9 %collective-permute-start.21 = (bf16[32,1152]{1,0:T(8,128)(2,1)S(1)}, bf16[32,1152]{1,0:T(8,128)(2,1)S(1)}, u32[]{:S(2)}, u32[]{:S(2)}) collective-permute-start(bf16[32,1152]{1,0:T(8,128)(2,1)S(1)} %add_convert_fusion.refs_1_), channel_id=1, source_target_pairs={{0,3},{1,0},{2,1},{3,2},{4,7},{5,4},{6,5},{7,6},{8,11},{9,8},{10,9... | collective-permute-start | bytes 221192 | tf_op jit(solution)/shard_map/ppermute | solution.py:1100
  146.1 24.4 %collective-permute-start.34 = (bf16[2304,128]{1,0:T(8,128)(2,1)S(1)}, bf16[2304,128]{1,0:T(8,128)(2,1)}, u32[]{:S(2)}, u32[]{:S(2)}) collective-permute-start(bf16[2304,128]{1,0:T(8,128)(2,1)S(1)} %get-tuple-element.214.refs_0_), channel_id=1, source_target_pairs={{0,16},{4,20},{8,24},{12,28},{16,0},{20,4},{24,8},{28,12},{1,17},{... | collective-permute-start | bytes 1769480 | tf_op jit(solution)/shard_map/ppermute | solution.py:1119
  147.9 22.6 %collective-permute-start.33 = (bf16[2304,128]{1,0:T(8,128)(2,1)S(1)}, bf16[2304,128]{1,0:T(8,128)(2,1)}, u32[]{:S(2)}, u32[]{:S(2)}) collective-permute-start(bf16[2304,128]{1,0:T(8,128)(2,1)S(1)} %get-tuple-element.214.refs_0_), channel_id=1, source_target_pairs={{0,8},{4,12},{8,0},{12,4},{16,24},{20,28},{24,16},{28,20},{1,9},{5... | collective-permute-start | bytes 1769480 | tf_op jit(solution)/shard_map/ppermute | solution.py:1119
  161.3 14.6 %collective-permute-start.32 = (bf16[768,128]{1,0:T(8,128)(2,1)S(1)}, bf16[768,128]{1,0:T(8,128)(2,1)S(1)}, u32[]{:S(2)}, u32[]{:S(2)}) collective-permute-start(bf16[768,128]{1,0:T(8,128)(2,1)S(1)} %get-tuple-element.205.refs_4_.refs_10_), channel_id=1, source_target_pairs={{0,24},{4,28},{8,16},{12,20},{16,8},{20,12},{24,0},{28,4},{1,25},{... | collective-permute-start | bytes 589832 | tf_op jit(solution)/shard_map/ppermute | solution.py:1119
  161.6 16.7 %collective-permute-start.31 = (bf16[768,128]{1,0:T(8,128)(2,1)S(1)}, bf16[768,128]{1,0:T(8,128)(2,1)}, u32[]{:S(2)}, u32[]{:S(2)}) collective-permute-start(bf16[768,128]{1,0:T(8,128)(2,1)S(1)} %get-tuple-element.205.refs_4_.refs_10_), channel_id=1, source_target_pairs={{0,16},{4,20},{8,24},{12,28},{16,0},{20,4},{24,8},{28,12},{1,17},{... | collective-permute-start | bytes 589832 | tf_op jit(solution)/shard_map/ppermute | solution.py:1119
  163.4 15.0 %collective-permute-start.30 = (bf16[768,128]{1,0:T(8,128)(2,1)S(1)}, bf16[768,128]{1,0:T(8,128)(2,1)}, u32[]{:S(2)}, u32[]{:S(2)}) collective-permute-start(bf16[768,128]{1,0:T(8,128)(2,1)S(1)} %get-tuple-element.205.refs_4_.refs_10_), channel_id=1, source_target_pairs={{0,8},{4,12},{8,0},{12,4},{16,24},{20,28},{24,16},{28,20},{1,9},{5... | collective-permute-start | bytes 589832 | tf_op jit(solution)/shard_map/ppermute | solution.py:1119
  178.4 9.6 %collective-permute-start.42 = (bf16[1152,128]{1,0:T(8,128)(2,1)}, bf16[1152,128]{1,0:T(8,128)(2,1)S(1)}, u32[]{:S(2)}, u32[]{:S(2)}) collective-permute-start(bf16[1152,128]{1,0:T(8,128)(2,1)} %get-tuple-element.203), channel_id=1, source_target_pairs={{0,8},{4,12},{8,0},{12,4},{16,24},{20,28},{24,16},{28,20},{1,9},{5... | collective-permute-start | bytes 884744 | tf_op jit(solution)/shard_map/ppermute | solution.py:1119
  178.9 9.3 %collective-permute-start.43 = (bf16[1152,128]{1,0:T(8,128)(2,1)}, bf16[1152,128]{1,0:T(8,128)(2,1)S(1)}, u32[]{:S(2)}, u32[]{:S(2)}) collective-permute-start(bf16[1152,128]{1,0:T(8,128)(2,1)} %get-tuple-element.204), channel_id=1, source_target_pairs={{0,16},{4,20},{8,24},{12,28},{16,0},{20,4},{24,8},{28,12},{1,17},{... | collective-permute-start | bytes 884744 | tf_op jit(solution)/shard_map/ppermute | solution.py:1119
  188.2 9.5 %collective-permute-start.45 = (bf16[2304,128]{1,0:T(8,128)(2,1)}, bf16[2304,128]{1,0:T(8,128)(2,1)S(1)}, u32[]{:S(2)}, u32[]{:S(2)}) collective-permute-start(bf16[2304,128]{1,0:T(8,128)(2,1)} %collective-permute-done.33.refs_1_), channel_id=1, source_target_pairs={{0,4},{4,0},{8,12},{12,8},{16,20},{20,16},{24,28},{28,24},{1,5},{5... | collective-permute-start | bytes 1769480 | tf_op jit(solution)/shard_map/ppermute | solution.py:1119
  188.7 9.0 %collective-permute-start.46 = (bf16[2304,128]{1,0:T(8,128)(2,1)}, bf16[2304,128]{1,0:T(8,128)(2,1)S(1)}, u32[]{:S(2)}, u32[]{:S(2)}) collective-permute-start(bf16[2304,128]{1,0:T(8,128)(2,1)} %collective-permute-done.34.refs_2_), channel_id=1, source_target_pairs={{0,4},{4,0},{8,12},{12,8},{16,20},{20,16},{24,28},{28,24},{1,5},{5... | collective-permute-start | bytes 1769480 | tf_op jit(solution)/shard_map/ppermute | solution.py:1119
  191.5 17.6 %collective-permute-start.39 = (bf16[624,128]{1,0:T(8,128)(2,1)S(1)}, bf16[624,128]{1,0:T(8,128)(2,1)S(1)}, u32[]{:S(2)}, u32[]{:S(2)}) collective-permute-start(bf16[624,128]{1,0:T(8,128)(2,1)S(1)} %get-tuple-element.210), channel_id=1, source_target_pairs={{0,1},{1,2},{2,3},{3,0},{4,5},{5,6},{6,7},{7,4},{8,9},{9,10},{10,1... | collective-permute-start | bytes 479240 | tf_op jit(solution)/shard_map/ppermute | solution.py:1100
  193.7 15.4 %collective-permute-start.40 = (bf16[624,128]{1,0:T(8,128)(2,1)S(1)}, bf16[624,128]{1,0:T(8,128)(2,1)S(1)}, u32[]{:S(2)}, u32[]{:S(2)}) collective-permute-start(bf16[624,128]{1,0:T(8,128)(2,1)S(1)} %get-tuple-element.211), channel_id=1, source_target_pairs={{0,2},{1,3},{2,0},{3,1},{4,6},{5,7},{6,4},{7,5},{8,10},{9,11},{10,... | collective-permute-start | bytes 479240 | tf_op jit(solution)/shard_map/ppermute | solution.py:1100
  196.3 12.9 %collective-permute-start.41 = (bf16[624,128]{1,0:T(8,128)(2,1)S(1)}, bf16[624,128]{1,0:T(8,128)(2,1)S(1)}, u32[]{:S(2)}, u32[]{:S(2)}) collective-permute-start(bf16[624,128]{1,0:T(8,128)(2,1)S(1)} %get-tuple-element.212), channel_id=1, source_target_pairs={{0,3},{1,0},{2,1},{3,2},{4,7},{5,4},{6,5},{7,6},{8,11},{9,8},{10,9... | collective-permute-start | bytes 479240 | tf_op jit(solution)/shard_map/ppermute | solution.py:1100
  (89 other events, 768.5 us)

commit v5 on v4

--- a/solution.py
+++ b/solution.py
@@ -235,9 +235,9 @@
 
 def pack_kernel(
     capacity,
-    resets,
-    routes,
-    cotangent,
+    resets_in,
+    routes_in,
+    cotangent_in,
     expert_in,
     expert_out,
     masks,
@@ -245,6 +245,10 @@
     message,
     packed,
     staged,
+    resets,
+    routes,
+    cotangent,
+    early_arrivals,
     arrivals,
     semaphores,
 ):
@@ -254,7 +258,12 @@
     for index in range(experts):
         copies.append((expert_in.at[index], staged.at[index, 0]))
         copies.append((expert_out.at[index], staged.at[index, 1]))
+    early = run_copies(
+        [(resets_in, resets), (routes_in, routes), (cotangent_in, cotangent)], early_arrivals
+    )
     arriving = run_copies(copies, arrivals)
+    for copy in early:
+        copy.wait()
     fill_choose(capacity, length, experts, routes, choose)
     slots = dot_nn(choose[...], cotangent[...]).astype(BF16)
     started = []
@@ -287,34 +296,24 @@
     return run_copies([(passed.at[0], pass_y), (passed.at[1], pass_x)], semaphores)
 
 
+def pass_kernel(along_x, along_y, pass_y, pass_x, passed, arrivals, semaphores):
+    for copy in pass_on(along_x, along_y, pass_y, pass_x, passed, arrivals, semaphores):
+        copy.wait()
+
+
 def unpack_kernel(
     share,
     capacity,
     message,
-    along_x,
-    along_y,
     first_out,
     second_out,
     slots_out,
-    pass_y,
-    pass_x,
     d_hidden,
     first_w,
     second_w,
     grad_slots,
-    passed,
-    pass_semaphores,
     semaphores,
 ):
-    started = pass_on(
-        along_x,
-        along_y,
-        pass_y,
-        pass_x,
-        passed,
-        pass_semaphores.at[pl.ds(0, 2)],
-        pass_semaphores.at[pl.ds(2, 2)],
-    )
     folded = capacity + capacity // 2
     copies = []
     for index in range(message.shape[0]):
@@ -328,7 +327,7 @@
     for copy in run_copies(copies, semaphores):
         copy.wait()
     copies = [(first_w, first_out), (second_w, second_out), (grad_slots, slots_out)]
-    started += run_copies(copies, semaphores)
+    started = run_copies(copies, semaphores)
     d_hidden[...] = dot_nn(grad_slots[...], second_w[...])
     for copy in started:
         copy.wait()
@@ -1055,9 +1054,9 @@
     rank, states, proj = sizes
     chans, width = out_grad.shape
     arriving_last, lasts = stage_pieces(last_refs, staged_last, last_arrivals)
-    arriving, seconds = stage_pieces(second_refs, staged, second_arrivals)
     for copy in arriving_last:
         copy.wait()
+    arriving, seconds = stage_pieces(second_refs, staged, second_arrivals)
     take_turned(d_gate, lasts, 0)
     wide_grad[0] = dot_nn(d_gate[...], normed[...])
     started = run_copies([(wide_grad.at[0], in_grad.at[0])], semaphores)
@@ -1190,11 +1189,15 @@
             [
                 ((groups, folded, hidden_units), BF16),
                 ((experts, 2, share, hidden_units), BF16),
+                ((1, length), jnp.int32),
+                ((1, length), jnp.int32),
+                ((length, width), BF16),
+                pltpu.SemaphoreType.DMA((3,)),
                 pltpu.SemaphoreType.DMA((2 * experts,)),
                 pltpu.SemaphoreType.DMA((3 * experts,)),
             ],
-            far_args=(3, 4),
-            far_outs=(2,), staged=(0, 1, 2))
+            far_args=range(5),
+            far_outs=(2,), )
         weights = exchange(packed)
     else:
         masks, choose, grad_send = run_kernel(
@@ -1263,28 +1266,34 @@
         [((length, width), F32), ((column, length), F32), slots_out],
         [place, *mixer_pieces, rows, norm_two, choose],
         [((width, length), F32)],
-        scalars=1, loose_outs=(2,), staged=(1, 2, 3, 4, 5, 7))
+        scalars=1, staged=(1, 5, 7))
     if near:
         half_out = (((width + 2 * chans) // 2, length), BF16)
-        first_w, second_w, grad_slots, *halves, d_hidden = run_kernel(
+        first_w, second_w, grad_slots, d_hidden = run_kernel(
             functools.partial(unpack_kernel, share, capacity),
-            weight_outs
-            + [slots_out, half_out, half_out, ((slot_count, hidden_units), F32)],
-            [*after([weights], send_slots), first_x, first_y],
+            weight_outs + [slots_out, ((slot_count, hidden_units), F32)],
+            after([weights], send_slots),
+            [*weight_outs, slots_out, pltpu.SemaphoreType.DMA((5 * groups,))],
+            far_args=(0,),
+            far_outs=(0, 1, 2),
+        )
+        first_x, first_y = after([first_x, first_y], d_hidden)
+        halves = run_kernel(
+            pass_kernel,
+            [half_out, half_out],
+            [first_x, first_y],
             [
-                *weight_outs,
-                slots_out,
                 ((2, *half_out[0]), BF16),
-                pltpu.SemaphoreType.DMA((4,)),
-                pltpu.SemaphoreType.DMA((5 * groups,)),
+                pltpu.SemaphoreType.DMA((2,)),
+                pltpu.SemaphoreType.DMA((2,)),
             ],
-            far_args=(0, 1, 2),
-            far_outs=(0, 1, 2, 3, 4),
+            far_args=(0, 1),
+            far_outs=(0, 1),
         )
         first_d = swap_across(halves)
     arrived = exchange_slots(send_slots)
     hidden, d_pre, d_slots = run_kernel(
-        expert_kernel, [hidden_out, hidden_out, slots_out], [arrived, first_w, d_hidden], loose_outs=(2,), staged=(0, 1, 2))
+        expert_kernel, [hidden_out, hidden_out, slots_out], [arrived, first_w, d_hidden], staged=(0, 1, 2))
     if near:
         d_slots = after([d_slots], first_d)[0]
     back_slots = exchange_slots(d_slots)
@@ -1301,7 +1310,8 @@
                 pltpu.SemaphoreType.DMA((3 * groups,)),
             ],
             far_outs=(0,), staged=range(5))
-        back_slots = after([back_slots], packed)[0]
+        firsts = swap_near([first, first_x, first_y, *first_d])
+        back_slots = after([back_slots], packed, firsts)[0]
         packed = after([packed], back_slots)[0]
         owned = exchange(packed)
     else:
@@ -1314,10 +1324,6 @@
         [((length, width), F32)],
         scalars=1, loose_outs=(0, 1, 2, 3), staged=(1, 2))
     send_pieces = share_rows(add_low(send_chunks(back_chunks)), parts)
-    if near:
-        firsts = swap_near([first, first_x, first_y, *first_d])
-
-        send_pieces = after(send_pieces, firsts)
     decays, history, step_rows, drive_rows, step_slope, y_slope, gate_slope = run_kernel(
         scan_states_kernel,
         [
@@ -1345,7 +1351,7 @@
         ],
         [place, *send_pieces, residual, norm_two, cotangent, out_proj],
         [((length, width), F32), ((width, length), F32)],
-        scalars=1, staged=(1, 2, 3, 4, 5, 7, 8), held_outs=(1, 2, 3))
+        scalars=1, staged=(1, 5, 7, 8), held_outs=(1, 2, 3))
     d_mixed_part, d_act_scan, d_gate, second = run_kernel(
         scan_backward_kernel,
         [
@@ -1403,7 +1409,7 @@
             norm_one,
         ],
         [((parts, proj, length), BF16), ((width, length), F32), ((length, full), F32)],
-        scalars=1, loose_outs=(1,), staged=(1, 2, 3, 4, 7, 8, 9, 13))
+        scalars=1, loose_outs=(1,), staged=(1, 7, 8, 9, 13))
     share_outs = [((2 * column + 16, length), BF16)] * parts
     if near:
         lasts = [message, swap(message, 2), swap(message, 4), swap(message, 6)]
@@ -1457,7 +1463,7 @@
             scalars=1,
             staged=(1, 2),
             far_args=range(3, 4 + groups),
-            loose_outs=range(parts + 2),
+            loose_outs=(parts, parts + 1),
         )
         norm_out = [((width,), F32)]
     else:
@@ -1562,7 +1568,7 @@
         finish_rows_kernel,
         [((column, length), BF16), ((column, length), F32)] + norm_out,
         [*pieces, residual_columns, d_columns, tokens_turned, scale, gain_columns],
-        staged=range(9),
+        staged=range(4, 9),
         loose_outs=(0, 1, 2),
     )
     if near:

time: 213 us -> 208 us (0.977)
  local copies, waits for them, and re-layouts: 7.64 us -> 3.08 us
    unnamed x120 -> x82, local copies, waits for them, and re-layouts: 7.64 us -> 3.08 us
    ppermute x25, waiting for transfers between devices: 19.5 us -> 15.8 us  [swap(): lax.ppermute(values, 'dp', [(i, i ^ bits) for i in range(NEAR_GROUPS)])]
    pallas_call x17 -> x18, Pallas kernels: 80.1 us -> 80.8 us  [run_kernel(): pl.pallas_call(body, out_shape=[held(index, shape, dtype) for index, (sha...]
  transfers between devices with their start and end apart: 53 -> 53, of which waited for: 27 -> 29; matrix products, arithmetic and copies ran while one was open for 0% -> 0% of each run, Pallas kernels for 34% -> 35%
where the time goes in v5:
time: 208 us; the launch traced here: 207 us
  Pallas kernels  80.8 us (39%)
  starting transfers between devices  71.5 us (34%)
  waiting for transfers between devices  50 us (24%)
  local copies, waits for them, and re-layouts  3.08 us (1%)
    pallas_call x18, Pallas kernels, run_kernel(): pl.pallas_call(body, out_shape=[held(index, shape, dtype) for index, (sha...  80.8 us
    ppermute x24, starting transfers between devices, send_chunks(): lax.ppermute(chunks[s], 'tensor', pairs[s])  36.4 us
    ppermute x24, waiting for transfers between devices, send_chunks(): lax.ppermute(chunks[s], 'tensor', pairs[s])  27.2 us
    all_to_all x4, starting transfers between devices, exchange(): return lax.all_to_all(values, 'dp', split_axis=0, concat_axis=0, tiled=True)  18.4 us
    ppermute x25, starting transfers between devices, swap(): lax.ppermute(values, 'dp', [(i, i ^ bits) for i in range(NEAR_GROUPS)])  16.6 us
    ppermute x25, waiting for transfers between devices, swap(): lax.ppermute(values, 'dp', [(i, i ^ bits) for i in range(NEAR_GROUPS)])  15.8 us
    all_to_all x4, waiting for transfers between devices, exchange(): return lax.all_to_all(values, 'dp', split_axis=0, concat_axis=0, tiled=True)  6.96 us
  transfers between devices with their start and end apart: 53, of which 29 were waited for; matrix products, arithmetic and copies ran while one was open for 0% of the time, Pallas kernels for 35%

profile of v5, /device:TPU:0, one launch (start us, length us, event | category | flops | bytes accessed | tf_op | source)
XLA Modules:
  0.0 206.8 jit_solution(5478123120465830552)
XLA Ops:
  0.6 5.6 %shard_map.280 = (f32[4,128,128]{2,1,0:T(8,128)}, bf16[256,128]{1,0:T(8,128)(2,1)}, bf16[8,336,768]{2,1,0:T(8,128)(2,1)}) custom-call(s32[1,128]{1,0:T(1,128)} %bitcast.25, s32[1,128]{1,0:T(1,128)} %bitcast.26, bf16[128,1152]{1,0:T(8,128)(2,1)} %refs_7_.8, bf16[8,144,768]{2,1,0:T(8,128)(2,1)} %refs_3_.1, bf16[8,144,768]{2,1,0:T(8,128)(2,1)} %refs_4_.1), custom_call_target="tpu_custom_call" | custom-call | tf_op jit(solution)/shard_map/pallas_call | solution.py:70
  6.3 5.4 %all-to-all-start.1 = ((bf16[8,336,768]{2,1,0:T(8,128)(2,1)}), bf16[8,336,768]{2,1,0:T(8,128)(2,1)}, u32[]{:S(2)}, u32[]{:S(2)}) async-start(bf16[8,336,768]{2,1,0:T(8,128)(2,1)} %get-tuple-element.139), calls=%async_computation.1 | async-start | bytes 8257536 | tf_op jit(solution)/shard_map/all_to_all | solution.py:1171
  11.8 4.5 %collective-permute-start.2 = (bf16[288,128]{1,0:T(8,128)(2,1)S(1)}, bf16[288,128]{1,0:T(8,128)(2,1)S(1)}, u32[]{:S(2)}, u32[]{:S(2)}) collective-permute-start(bf16[288,128]{1,0:T(8,128)(2,1)S(1)} %bitcast.22), channel_id=1, source_target_pairs={{0,3},{1,0},{2,1},{3,2},{4,7},{5,4},{6,5},{7,6},{8,11},{9,8},{10,9... | collective-permute-start | bytes 221192 | tf_op jit(solution)/shard_map/ppermute | solution.py:1099
  18.9 5.0 %collective-permute-done.1.refs_3_ = bf16[288,128]{1,0:T(8,128)(2,1)S(1)} collective-permute-done((bf16[288,128]{1,0:T(8,128)(2,1)S(1)}, bf16[288,128]{1,0:T(8,128)(2,1)S(1)}, u32[]{:S(2)}, u32[]{:S(2)}) %collective-permute-start.1) | collective-permute-done | bytes 73760 | tf_op jit(solution)/shard_map/ppermute | solution.py:1099
  24.7 3.7 %shard_map.281 = (bf16[128,1152]{1,0:T(8,128)(2,1)}, bf16[1152,128]{1,0:T(8,128)(2,1)}, bf16[128,576]{1,0:T(8,128)(2,1)}, f32[128,576]{1,0:T(8,128)}, f32[128,57...) custom-call(s32[1]{0:T(128)} %bitcast.refs_0_, ...), custom_call_target="tpu_custom_call" | custom-call | tf_op jit(solution)/shard_map/pallas_call | solution.py:70
  36.5 6.5 %shard_map.282 = (bf16[32,1152]{1,0:T(8,128)(2,1)S(1)}, bf16[32,1152]{1,0:T(8,128)(2,1)S(1)}, bf16[32,1152]{1,0:T(8,128)(2,1)S(1)}, bf16[32,1152]{1,0:T(8,128)(2...) custom-call(s32[1]{0:T(128)} %bitcast.refs_0_, bf16[104,128]{1,0:T(8,128)(2,1)} %copy-done.14, ...), custom_call_target="tpu_custom_call" | custom-call | tf_op jit(solution)/shard_map/pallas_call | solution.py:70
  50.4 3.0 %collective-permute-start.11 = (bf16[32,1152]{1,0:T(8,128)(2,1)S(1)}, bf16[32,1152]{1,0:T(8,128)(2,1)S(1)}, u32[]{:S(2)}, u32[]{:S(2)}) collective-permute-start(bf16[32,1152]{1,0:T(8,128)(2,1)S(1)} %add_convert_fusion.1.refs_1_), channel_id=1, source_target_pairs={{0,3},{1,0},{2,1},{3,2},{4,7},{5,4},{6,5},{7,6},{8,11},{9,8},{10,9... | collective-permute-start | bytes 221192 | tf_op jit(solution)/shard_map/ppermute | solution.py:1099
  62.2 4.2 %all-to-all-start = ((bf16[8,32,1152]{2,1,0:T(8,128)(2,1)}), bf16[8,32,1152]{2,1,0:T(8,128)(2,1)}, u32[]{:S(2)}, u32[]{:S(2)}) async-start(bf16[8,32,1152]{2,1,0:T(8,128)(2,1)} %bitcast.18), calls=%async_computation | async-start | bytes 1179648 | tf_op jit(solution)/shard_map/all_to_all | solution.py:1171
  66.4 5.5 %shard_map.284 = (bf16[1152,768]{1,0:T(8,128)(2,1)}, bf16[1152,768]{1,0:T(8,128)(2,1)}, bf16[256,1152]{1,0:T(8,128)(2,1)}, f32[256,768]{1,0:T(8,128)}) custom-call(bf16[8,336,768]{2,1,0:T(8,128)(2,1)} %all-to-all-done.1.refs_0_), custom_call_target="tpu_custom_call" | custom-call | tf_op jit(solution)/shard_map/pallas_call | solution.py:70
  80.0 4.2 %shard_map.285 = (bf16[256,768]{1,0:T(8,128)(2,1)}, bf16[256,768]{1,0:T(8,128)(2,1)}, bf16[256,1152]{1,0:T(8,128)(2,1)}) custom-call(bf16[256,1152]{1,0:T(8,128)(2,1)} %bitcast.7.refs_0_, bf16[1152,768]{1,0:T(8,128)(2,1)} %get-tuple-element.141.refs_1_, f32[256,768]{1,0:T(8,128)} %get-tuple-element.142.refs_2_), custom_call_target="tpu_custom_call" | custom-call | tf_op jit(solution)/shard_map/pallas_call | solution.py:70
  85.6 4.2 %all-to-all-start.2 = ((bf16[8,32,1152]{2,1,0:T(8,128)(2,1)}), bf16[8,32,1152]{2,1,0:T(8,128)(2,1)}, u32[]{:S(2)}, u32[]{:S(2)}) async-start(bf16[8,32,1152]{2,1,0:T(8,128)(2,1)} %bitcast.19), calls=%async_computation.2 | async-start | bytes 1179648 | tf_op jit(solution)/shard_map/all_to_all | solution.py:1171
  90.4 5.0 %shard_map.287 = bf16[8,336,768]{2,1,0:T(8,128)(2,1)} custom-call(bf16[256,1152]{1,0:T(8,128)(2,1)} %bitcast.7.refs_0_, bf16[256,1152]{1,0:T(8,128)(2,1)} %get-tuple-element.150.refs_1_, bf16[256,768]{1,0:T(8,128)(2,1)} %get-tuple-element.151.refs_2_, bf16[256,768]{1,0:T(8,128)(2,1)} %get-tuple-element.152.refs_3_, bf16[1152,768]{1,0:T(8,128)(2,1)} %get-tuple-element.153.refs_4_), custom_call_target="tpu_custom_call" | custom-call | tf_op jit(solution)/shard_map/pallas_call | solution.py:70
  95.5 4.8 %all-to-all-done.2 = bf16[8,32,1152]{2,1,0:T(8,128)(2,1)} async-done(((bf16[8,32,1152]{2,1,0:T(8,128)(2,1)}), bf16[8,32,1152]{2,1,0:T(8,128)(2,1)}, u32[]{:S(2)}, u32[]{:S(2)}) %all-to-all-start.2) | async-done | bytes 589856 | tf_op jit(solution)/shard_map/all_to_all | solution.py:1171
  100.3 4.6 %all-to-all-start.3 = ((bf16[8,336,768]{2,1,0:T(8,128)(2,1)}), bf16[8,336,768]{2,1,0:T(8,128)(2,1)}, u32[]{:S(2)}, u32[]{:S(2)}) async-start(bf16[8,336,768]{2,1,0:T(8,128)(2,1)} %shard_map.287), calls=%async_computation.3 | async-start | bytes 8257536 | tf_op jit(solution)/shard_map/all_to_all | solution.py:1171
  113.8 2.9 %collective-permute-done.22 = bf16[32,1152]{1,0:T(8,128)(2,1)S(1)} collective-permute-done((bf16[32,1152]{1,0:T(8,128)(2,1)S(1)}, bf16[32,1152]{1,0:T(8,128)(2,1)S(1)}, u32[]{:S(2)}, u32[]{:S(2)}) %collective-permute-start.22) | collective-permute-done | bytes 73760 | tf_op jit(solution)/shard_map/ppermute | solution.py:1099
  120.6 4.6 %shard_map.289 = (f32[2048,640]{1,0:T(8,128)S(1)}, f32[2064,640]{1,0:T(8,128)S(1)}, f32[128,640]{1,0:T(8,128)S(1)}, f32[128,640]{1,0:T(8,128)S(1)}, f32[128,576]...) custom-call(f32[128,576]{1,0:T(8,128)} %get-tuple-element.159.refs_0_, ...), custom_call_target="tpu_custom_call" | custom-call | tf_op jit(solution)/shard_map/pallas_call | solution.py:70
  127.4 3.0 %shard_map.290 = (f32[288,128]{1,0:T(8,128)}, bf16[1152,128]{1,0:T(8,128)(2,1)S(1)}, f32[128,576]{1,0:T(8,128)S(1)}, f32[1,1152]{1,0:T(1,128)S(1)}) custom-call(s32[1]{0:T(128)} %bitcast.refs_0_, bf16[32,1152]{1,0:T(8,128)(2,1)} %copy-done.33, bf16[32,1152]{1,0:T(8,128)(2,1)S(1)} %collective-permute-done.24.refs_2_, ...), custom_call_target="tpu_custom_call" | custom-call | tf_op jit(solution)/shard_map/pallas_call | solution.py:70
  130.4 9.2 %shard_map.291 = (bf16[104,128]{1,0:T(8,128)(2,1)S(1)}, f32[128,576]{1,0:T(8,128)S(1)}, bf16[128,576]{1,0:T(8,128)(2,1)S(1)}, bf16[2304,128]{1,0:T(8,128)(2,1)S(1)}) custom-call(f32[128,576]{1,0:T(8,128)S(1)} %get-tuple-element.168.refs_0_, f32[128,576]{1,0:T(8,128)S(1)} %get-tuple-element.169.refs_1_, f32[128,576]{1,0:T(8,128)S(1)} %get-tuple-element.170.refs_2_, ...), custom_call_target="tpu_custom_call" | custom-call | tf_op jit(solution)/shard_map/pallas_call | solution.py:70
  150.7 3.4 %shard_map.292 = (bf16[4,304,128]{2,1,0:T(8,128)(2,1)}, bf16[768,128]{1,0:T(8,128)(2,1)S(1)}) custom-call(s32[1]{0:T(128)} %bitcast.refs_0_, bf16[104,128]{1,0:T(8,128)(2,1)} %copy-done.13, bf16[104,128]{1,0:T(8,128)(2,1)S(1)} %collective-permute-done.27.refs_2_, bf16[104,128]{1,0:T(8,128)(2,1)S(1)} %collective-permute-done.28.refs_3_, ...), custom_call_target="tpu_custom_call" | custom-call | tf_op jit(solution)/shard_map/pallas_call | solution.py:70
  157.7 3.5 %shard_map.293 = (bf16[1024,1152]{1,0:T(8,128)(2,1)S(1)}, bf16[576,1024]{1,0:T(8,128)(2,1)S(1)}, bf16[576,1024]{1,0:T(8,128)(2,1)S(1)}) custom-call(bf16[2304,128]{1,0:T(8,128)(2,1)} %copy-done.4, bf16[2304,128]{1,0:T(8,128)(2,1)} %collective-permute-done.12.refs_0_.refs_1_, bf16[2304,128]{1,0:T(8,128)(2,1)} %collective-permute-done.13.refs_1_.refs_2_, ...), custom_call_target="tpu_custom_call" | custom-call | tf_op jit(solution)/shard_map/pallas_call | solution.py:70
  161.2 5.3 %collective-permute-done.34.refs_2_ = bf16[2304,128]{1,0:T(8,128)(2,1)} collective-permute-done((bf16[2304,128]{1,0:T(8,128)(2,1)S(1)}, bf16[2304,128]{1,0:T(8,128)(2,1)}, u32[]{:S(2)}, u32[]{:S(2)}) %collective-permute-start.34) | collective-permute-done | bytes 589856 | tf_op jit(solution)/shard_map/ppermute | solution.py:1118
  166.5 5.4 %shard_map.294 = (f32[8,144,768]{2,1,0:T(8,128)}, f32[8,144,768]{2,1,0:T(8,128)}, bf16[1152,128]{1,0:T(8,128)(2,1)}, bf16[1152,128]{1,0:T(8,128)(2,1)}) custom-call(bf16[8,336,768]{2,1,0:T(8,128)(2,1)} %all-to-all-done.3.refs_0_.refs_3_, bf16[2304,128]{1,0:T(8,128)(2,1)} %collective-permute-done.33.refs_1_, bf16[2304,128]{1,0:T(8,128)(2,1)} %collective-permute-done.34.refs_2_), custom_call_target="tpu_custom_call" | custom-call | tf_op jit(solution)/shard_map/pallas_call | solution.py:70
  178.2 3.7 %shard_map.295 = (bf16[624,128]{1,0:T(8,128)(2,1)}, bf16[624,128]{1,0:T(8,128)(2,1)}, bf16[624,128]{1,0:T(8,128)(2,1)}, bf16[624,128]{1,0:T(8,128)(2,1)}, f32[4,576]{1,0:T(4,128)}, /*index=5*/f32[576]{0:T(1024)}) custom-call(s32[1]{0:T(128)} %bitcast.refs_0_, bf16[256,128]{1,0:T(8,128)(2,1)} %get-tuple-element.127.refs_7_.refs_1_, ...), custom_call_target="tpu_custom_call" | custom-call | tf_op jit(solution)/shard_map/pallas_call | solution.py:70
  194.8 9.8 %shard_map.296 = (f32[576,1152]{1,0:T(8,128)}, f32[2,576,1152]{2,1,0:T(8,128)}, f32[104,576]{1,0:T(8,128)}, f32[72,576]{1,0:T(8,128)}, f32[576]{0:T(1024)}, /*in...) custom-call(bf16[2304,128]{1,0:T(8,128)(2,1)} %copy-done.5, bf16[2304,128]{1,0:T(8,128)(2,1)} %collective-permute-done.33.refs_1_, ...), custom_call_target="tpu_custom_call" | custom-call | tf_op jit(solution)/shard_map/pallas_call | solution.py:70
  (184 shorter events, 88.3 us)
Async XLA Ops:
  6.3 55.9 %all-to-all-start.1 = ((bf16[8,336,768]{2,1,0:T(8,128)(2,1)}), bf16[8,336,768]{2,1,0:T(8,128)(2,1)}, u32[]{:S(2)}, u32[]{:S(2)}) async-start(bf16[8,336,768]{2,1,0:T(8,128)(2,1)} %get-tuple-element.139), calls=%async_computation.1 | async-start | bytes 8257536 | tf_op jit(solution)/shard_map/all_to_all | solution.py:1171
  47.1 25.9 %collective-permute-start.13 = (bf16[2304,128]{1,0:T(8,128)(2,1)S(1)}, bf16[2304,128]{1,0:T(8,128)(2,1)}, u32[]{:S(2)}, u32[]{:S(2)}) collective-permute-start(bf16[2304,128]{1,0:T(8,128)(2,1)S(1)} %get-tuple-element.186.refs_0_), channel_id=1, source_target_pairs={{0,16},{4,20},{8,24},{12,28},{16,0},{20,4},{24,8},{28,12},{1,17},{... | collective-permute-start | bytes 1769480 | tf_op jit(solution)/shard_map/ppermute | solution.py:1118
  48.8 24.2 %collective-permute-start.12 = (bf16[2304,128]{1,0:T(8,128)(2,1)S(1)}, bf16[2304,128]{1,0:T(8,128)(2,1)}, u32[]{:S(2)}, u32[]{:S(2)}) collective-permute-start(bf16[2304,128]{1,0:T(8,128)(2,1)S(1)} %get-tuple-element.186.refs_0_), channel_id=1, source_target_pairs={{0,8},{4,12},{8,0},{12,4},{16,24},{20,28},{24,16},{28,20},{1,9},{5... | collective-permute-start | bytes 1769480 | tf_op jit(solution)/shard_map/ppermute | solution.py:1118
  62.2 17.8 %all-to-all-start = ((bf16[8,32,1152]{2,1,0:T(8,128)(2,1)}), bf16[8,32,1152]{2,1,0:T(8,128)(2,1)}, u32[]{:S(2)}, u32[]{:S(2)}) async-start(bf16[8,32,1152]{2,1,0:T(8,128)(2,1)} %bitcast.18), calls=%async_computation | async-start | bytes 1179648 | tf_op jit(solution)/shard_map/all_to_all | solution.py:1171
  75.0 9.7 %collective-permute-start.14 = (bf16[1152,128]{1,0:T(8,128)(2,1)}, bf16[1152,128]{1,0:T(8,128)(2,1)}, u32[]{:S(2)}, u32[]{:S(2)}) collective-permute-start(bf16[1152,128]{1,0:T(8,128)(2,1)} %get-tuple-element.147), channel_id=1, source_target_pairs={{0,8},{4,12},{8,0},{12,4},{16,24},{20,28},{24,16},{28,20},{1,9},{5... | collective-permute-start | bytes 884744 | tf_op jit(solution)/shard_map/ppermute | solution.py:1118
  76.1 9.5 %collective-permute-start.15 = (bf16[1152,128]{1,0:T(8,128)(2,1)}, bf16[1152,128]{1,0:T(8,128)(2,1)}, u32[]{:S(2)}, u32[]{:S(2)}) collective-permute-start(bf16[1152,128]{1,0:T(8,128)(2,1)} %get-tuple-element.148), channel_id=1, source_target_pairs={{0,16},{4,20},{8,24},{12,28},{16,0},{20,4},{24,8},{28,12},{1,17},{... | collective-permute-start | bytes 884744 | tf_op jit(solution)/shard_map/ppermute | solution.py:1118
  77.3 18.1 %collective-permute-start.16 = (bf16[2304,128]{1,0:T(8,128)(2,1)S(1)}, bf16[2304,128]{1,0:T(8,128)(2,1)}, u32[]{:S(2)}, u32[]{:S(2)}) collective-permute-start(bf16[2304,128]{1,0:T(8,128)(2,1)S(1)} %get-tuple-element.186.refs_0_), channel_id=1, source_target_pairs={{0,4},{4,0},{8,12},{12,8},{16,20},{20,16},{24,28},{28,24},{1,5},{5... | collective-permute-start | bytes 1769480 | tf_op jit(solution)/shard_map/ppermute | solution.py:1118
  77.4 18.1 %collective-permute-start.17 = (bf16[2304,128]{1,0:T(8,128)(2,1)}, bf16[2304,128]{1,0:T(8,128)(2,1)}, u32[]{:S(2)}, u32[]{:S(2)}) collective-permute-start(bf16[2304,128]{1,0:T(8,128)(2,1)} %collective-permute-done.12.refs_0_.refs_1_), channel_id=1, source_target_pairs={{0,4},{4,0},{8,12},{12,8},{16,20},{20,16},{24,28},{28,24},{1,5},{5... | collective-permute-start | bytes 1769480 | tf_op jit(solution)/shard_map/ppermute | solution.py:1118
  77.9 17.6 %collective-permute-start.18 = (bf16[2304,128]{1,0:T(8,128)(2,1)}, bf16[2304,128]{1,0:T(8,128)(2,1)}, u32[]{:S(2)}, u32[]{:S(2)}) collective-permute-start(bf16[2304,128]{1,0:T(8,128)(2,1)} %collective-permute-done.13.refs_1_.refs_2_), channel_id=1, source_target_pairs={{0,4},{4,0},{8,12},{12,8},{16,20},{20,16},{24,28},{28,24},{1,5},{5... | collective-permute-start | bytes 1769480 | tf_op jit(solution)/shard_map/ppermute | solution.py:1118
  85.6 14.7 %all-to-all-start.2 = ((bf16[8,32,1152]{2,1,0:T(8,128)(2,1)}), bf16[8,32,1152]{2,1,0:T(8,128)(2,1)}, u32[]{:S(2)}, u32[]{:S(2)}) async-start(bf16[8,32,1152]{2,1,0:T(8,128)(2,1)} %bitcast.19), calls=%async_computation.2 | async-start | bytes 1179648 | tf_op jit(solution)/shard_map/all_to_all | solution.py:1171
  100.3 57.4 %all-to-all-start.3 = ((bf16[8,336,768]{2,1,0:T(8,128)(2,1)}), bf16[8,336,768]{2,1,0:T(8,128)(2,1)}, u32[]{:S(2)}, u32[]{:S(2)}) async-start(bf16[8,336,768]{2,1,0:T(8,128)(2,1)} %shard_map.287), calls=%async_computation.3 | async-start | bytes 8257536 | tf_op jit(solution)/shard_map/all_to_all | solution.py:1171
  117.0 8.2 %collective-permute-start.26 = (bf16[32,1152]{1,0:T(8,128)(2,1)S(1)}, bf16[32,1152]{1,0:T(8,128)(2,1)S(1)}, u32[]{:S(2)}, u32[]{:S(2)}) collective-permute-start(bf16[32,1152]{1,0:T(8,128)(2,1)S(1)} %add_convert_fusion.refs_1_), channel_id=1, source_target_pairs={{0,3},{1,0},{2,1},{3,2},{4,7},{5,4},{6,5},{7,6},{8,11},{9,8},{10,9... | collective-permute-start | bytes 221192 | tf_op jit(solution)/shard_map/ppermute | solution.py:1099
  139.7 26.9 %collective-permute-start.34 = (bf16[2304,128]{1,0:T(8,128)(2,1)S(1)}, bf16[2304,128]{1,0:T(8,128)(2,1)}, u32[]{:S(2)}, u32[]{:S(2)}) collective-permute-start(bf16[2304,128]{1,0:T(8,128)(2,1)S(1)} %get-tuple-element.210.refs_0_), channel_id=1, source_target_pairs={{0,16},{4,20},{8,24},{12,28},{16,0},{20,4},{24,8},{28,12},{1,17},{... | collective-permute-start | bytes 1769480 | tf_op jit(solution)/shard_map/ppermute | solution.py:1118
  141.4 25.1 %collective-permute-start.33 = (bf16[2304,128]{1,0:T(8,128)(2,1)S(1)}, bf16[2304,128]{1,0:T(8,128)(2,1)}, u32[]{:S(2)}, u32[]{:S(2)}) collective-permute-start(bf16[2304,128]{1,0:T(8,128)(2,1)S(1)} %get-tuple-element.210.refs_0_), channel_id=1, source_target_pairs={{0,8},{4,12},{8,0},{12,4},{16,24},{20,28},{24,16},{28,20},{1,9},{5... | collective-permute-start | bytes 1769480 | tf_op jit(solution)/shard_map/ppermute | solution.py:1118
  154.2 17.8 %collective-permute-start.32 = (bf16[768,128]{1,0:T(8,128)(2,1)S(1)}, bf16[768,128]{1,0:T(8,128)(2,1)S(1)}, u32[]{:S(2)}, u32[]{:S(2)}) collective-permute-start(bf16[768,128]{1,0:T(8,128)(2,1)S(1)} %get-tuple-element.201.refs_4_.refs_10_), channel_id=1, source_target_pairs={{0,24},{4,28},{8,16},{12,20},{16,8},{20,12},{24,0},{28,4},{1,25},{... | collective-permute-start | bytes 589832 | tf_op jit(solution)/shard_map/ppermute | solution.py:1118
  154.5 19.4 %collective-permute-start.31 = (bf16[768,128]{1,0:T(8,128)(2,1)S(1)}, bf16[768,128]{1,0:T(8,128)(2,1)S(1)}, u32[]{:S(2)}, u32[]{:S(2)}) collective-permute-start(bf16[768,128]{1,0:T(8,128)(2,1)S(1)} %get-tuple-element.201.refs_4_.refs_10_), channel_id=1, source_target_pairs={{0,16},{4,20},{8,24},{12,28},{16,0},{20,4},{24,8},{28,12},{1,17},{... | collective-permute-start | bytes 589832 | tf_op jit(solution)/shard_map/ppermute | solution.py:1118
  156.3 17.7 %collective-permute-start.30 = (bf16[768,128]{1,0:T(8,128)(2,1)S(1)}, bf16[768,128]{1,0:T(8,128)(2,1)S(1)}, u32[]{:S(2)}, u32[]{:S(2)}) collective-permute-start(bf16[768,128]{1,0:T(8,128)(2,1)S(1)} %get-tuple-element.201.refs_4_.refs_10_), channel_id=1, source_target_pairs={{0,8},{4,12},{8,0},{12,4},{16,24},{20,28},{24,16},{28,20},{1,9},{5... | collective-permute-start | bytes 589832 | tf_op jit(solution)/shard_map/ppermute | solution.py:1118
  174.1 9.6 %collective-permute-start.42 = (bf16[1152,128]{1,0:T(8,128)(2,1)}, bf16[1152,128]{1,0:T(8,128)(2,1)S(1)}, u32[]{:S(2)}, u32[]{:S(2)}) collective-permute-start(bf16[1152,128]{1,0:T(8,128)(2,1)} %get-tuple-element.199), channel_id=1, source_target_pairs={{0,8},{4,12},{8,0},{12,4},{16,24},{20,28},{24,16},{28,20},{1,9},{5... | collective-permute-start | bytes 884744 | tf_op jit(solution)/shard_map/ppermute | solution.py:1118
  174.9 9.3 %collective-permute-start.43 = (bf16[1152,128]{1,0:T(8,128)(2,1)}, bf16[1152,128]{1,0:T(8,128)(2,1)S(1)}, u32[]{:S(2)}, u32[]{:S(2)}) collective-permute-start(bf16[1152,128]{1,0:T(8,128)(2,1)} %get-tuple-element.200), channel_id=1, source_target_pairs={{0,16},{4,20},{8,24},{12,28},{16,0},{20,4},{24,8},{28,12},{1,17},{... | collective-permute-start | bytes 884744 | tf_op jit(solution)/shard_map/ppermute | solution.py:1118
  184.2 9.5 %collective-permute-start.45 = (bf16[2304,128]{1,0:T(8,128)(2,1)}, bf16[2304,128]{1,0:T(8,128)(2,1)S(1)}, u32[]{:S(2)}, u32[]{:S(2)}) collective-permute-start(bf16[2304,128]{1,0:T(8,128)(2,1)} %collective-permute-done.33.refs_1_), channel_id=1, source_target_pairs={{0,4},{4,0},{8,12},{12,8},{16,20},{20,16},{24,28},{28,24},{1,5},{5... | collective-permute-start | bytes 1769480 | tf_op jit(solution)/shard_map/ppermute | solution.py:1118
  184.7 9.0 %collective-permute-start.46 = (bf16[2304,128]{1,0:T(8,128)(2,1)}, bf16[2304,128]{1,0:T(8,128)(2,1)S(1)}, u32[]{:S(2)}, u32[]{:S(2)}) collective-permute-start(bf16[2304,128]{1,0:T(8,128)(2,1)} %collective-permute-done.34.refs_2_), channel_id=1, source_target_pairs={{0,4},{4,0},{8,12},{12,8},{16,20},{20,16},{24,28},{28,24},{1,5},{5... | collective-permute-start | bytes 1769480 | tf_op jit(solution)/shard_map/ppermute | solution.py:1118
  187.5 17.1 %collective-permute-start.39 = (bf16[624,128]{1,0:T(8,128)(2,1)}, bf16[624,128]{1,0:T(8,128)(2,1)S(1)}, u32[]{:S(2)}, u32[]{:S(2)}) collective-permute-start(bf16[624,128]{1,0:T(8,128)(2,1)} %get-tuple-element.206), channel_id=1, source_target_pairs={{0,1},{1,2},{2,3},{3,0},{4,5},{5,6},{6,7},{7,4},{8,9},{9,10},{10,1... | collective-permute-start | bytes 479240 | tf_op jit(solution)/shard_map/ppermute | solution.py:1099
  189.8 14.9 %collective-permute-start.40 = (bf16[624,128]{1,0:T(8,128)(2,1)}, bf16[624,128]{1,0:T(8,128)(2,1)S(1)}, u32[]{:S(2)}, u32[]{:S(2)}) collective-permute-start(bf16[624,128]{1,0:T(8,128)(2,1)} %get-tuple-element.207), channel_id=1, source_target_pairs={{0,2},{1,3},{2,0},{3,1},{4,6},{5,7},{6,4},{7,5},{8,10},{9,11},{10,... | collective-permute-start | bytes 479240 | tf_op jit(solution)/shard_map/ppermute | solution.py:1099
  192.4 12.3 %collective-permute-start.41 = (bf16[624,128]{1,0:T(8,128)(2,1)}, bf16[624,128]{1,0:T(8,128)(2,1)S(1)}, u32[]{:S(2)}, u32[]{:S(2)}) collective-permute-start(bf16[624,128]{1,0:T(8,128)(2,1)} %get-tuple-element.208), channel_id=1, source_target_pairs={{0,3},{1,0},{2,1},{3,2},{4,7},{5,4},{6,5},{7,6},{8,11},{9,8},{10,9... | collective-permute-start | bytes 479240 | tf_op jit(solution)/shard_map/ppermute | solution.py:1099
  (70 other events, 636.6 us)

commit v6 on v5

--- a/solution.py
+++ b/solution.py
@@ -546,35 +546,13 @@
         copy.wait()
 
 
-def owner_kernel(
-    share,
-    message,
-    along_x,
-    along_y,
-    first_out,
-    second_out,
-    pass_y,
-    pass_x,
-    low,
-    wide,
-    passed,
-    arrivals,
-    semaphores,
-):
+def owner_kernel(share, message, first_out, second_out, low, wide, arrivals, semaphores):
     count = message.shape[0]
     arriving = run_copies(
         [(message.at[index, pl.ds(0, 2 * share)], low.at[index]) for index in range(count)],
-        arrivals.at[pl.ds(2, count)],
+        arrivals,
     )
-    started = pass_on(
-        along_x,
-        along_y,
-        pass_y,
-        pass_x,
-        passed,
-        arrivals.at[pl.ds(0, 2)],
-        semaphores.at[pl.ds(0, 2)],
-    )
+    started = []
     for index in range(count):
         arriving[index].wait()
         wide[index] = low[index].astype(F32)
@@ -582,7 +560,7 @@
             (wide.at[index, pl.ds(0, share)], first_out.at[index]),
             (wide.at[index, pl.ds(share, share)], second_out.at[index]),
         ]
-        started += run_copies(copies, semaphores.at[pl.ds(2 + 2 * index, 2)])
+        started += run_copies(copies, semaphores.at[pl.ds(2 * index, 2)])
     for copy in started:
         copy.wait()
 
@@ -1172,6 +1150,22 @@
 
     def exchange_slots(slots):
         return exchange(slots.reshape(groups, capacity, width)).reshape(slot_count, width)
+
+    half_out = (((width + 2 * chans) // 2, length), BF16)
+
+    def pass_halves(along_x, along_y):
+        return run_kernel(
+            pass_kernel,
+            [half_out, half_out],
+            [along_x, along_y],
+            [
+                ((2, *half_out[0]), BF16),
+                pltpu.SemaphoreType.DMA((2,)),
+                pltpu.SemaphoreType.DMA((2,)),
+            ],
+            far_args=(0, 1),
+            far_outs=(0, 1),
+        )
 
     token_pieces = share_rows(tokens_turned, parts)
     mask_out = ((4, length, 128), F32)
@@ -1268,7 +1262,6 @@
         [((width, length), F32)],
         scalars=1, staged=(1, 5, 7))
     if near:
-        half_out = (((width + 2 * chans) // 2, length), BF16)
         first_w, second_w, grad_slots, d_hidden = run_kernel(
             functools.partial(unpack_kernel, share, capacity),
             weight_outs + [slots_out, ((slot_count, hidden_units), F32)],
@@ -1278,18 +1271,7 @@
             far_outs=(0, 1, 2),
         )
         first_x, first_y = after([first_x, first_y], d_hidden)
-        halves = run_kernel(
-            pass_kernel,
-            [half_out, half_out],
-            [first_x, first_y],
-            [
-                ((2, *half_out[0]), BF16),
-                pltpu.SemaphoreType.DMA((2,)),
-                pltpu.SemaphoreType.DMA((2,)),
-            ],
-            far_args=(0, 1),
-            far_outs=(0, 1),
-        )
+        halves = pass_halves(first_x, first_y)
         first_d = swap_across(halves)
     arrived = exchange_slots(send_slots)
     hidden, d_pre, d_slots = run_kernel(
@@ -1428,21 +1410,21 @@
             far_args=range(10),
             held_outs=(0, 1, 2),
         )
-        second_x, second_y = after([second_x, second_y], all_normed)
-        grad_expert_in, grad_expert_out, *halves = run_kernel(
+        grad_expert_in, grad_expert_out = run_kernel(
             functools.partial(owner_kernel, share),
-            [grad_out, grad_out, half_out, half_out],
-            [owned, second_x, second_y],
+            [grad_out, grad_out],
+            after([owned], all_normed),
             [
                 ((groups, 2 * share, hidden_units), BF16),
                 ((groups, 2 * share, hidden_units), F32),
-                ((2, *half_out[0]), BF16),
-                pltpu.SemaphoreType.DMA((2 + groups,)),
-                pltpu.SemaphoreType.DMA((2 + 2 * groups,)),
+                pltpu.SemaphoreType.DMA((groups,)),
+                pltpu.SemaphoreType.DMA((2 * groups,)),
             ],
-            far_args=(0, 1, 2),
-            far_outs=(0, 1, 2, 3),
-        )
+            far_args=(0,),
+            far_outs=(0, 1),
+        )
+        second_x, second_y = after([second_x, second_y], grad_expert_in)
+        halves = pass_halves(second_x, second_y)
         second_d = swap_across(halves)
         lasts = swap_near(after(lasts, halves))
 
@@ -1528,7 +1510,7 @@
                 pltpu.SemaphoreType.DMA((groups,)),
                 pltpu.SemaphoreType.DMA((4,)),
             ],
-            far_args=range(10 + groups),
+            far_args=[index for index in range(10 + groups) if index not in range(3, 10)],
             far_outs=(0, 1),
             loose_outs=range(8),
         )

time: 208 us -> 208 us (level)
    pallas_call x18 -> x19, Pallas kernels: 80.8 us -> 81.7 us  [run_kernel(): pl.pallas_call(body, out_shape=[held(index, shape, dtype) for index, (sha...]
  transfers between devices with their start and end apart: 53 -> 53, of which waited for: 29 -> 30; matrix products, arithmetic and copies ran while one was open for 0% -> 0% of each run, Pallas kernels for 35% -> 36%
where the time goes in v6:
time: 208 us; the launch traced here: 206 us
  Pallas kernels  81.7 us (39%)
  starting transfers between devices  71.4 us (34%)
  waiting for transfers between devices  49.7 us (24%)
    pallas_call x19, Pallas kernels, run_kernel(): pl.pallas_call(body, out_shape=[held(index, shape, dtype) for index, (sha...  81.7 us
    ppermute x24, starting transfers between devices, send_chunks(): lax.ppermute(chunks[s], 'tensor', pairs[s])  36.4 us
    ppermute x24, waiting for transfers between devices, send_chunks(): lax.ppermute(chunks[s], 'tensor', pairs[s])  27.2 us
    all_to_all x4, starting transfers between devices, exchange(): return lax.all_to_all(values, 'dp', split_axis=0, concat_axis=0, tiled=True)  18.4 us
    ppermute x25, starting transfers between devices, swap(): lax.ppermute(values, 'dp', [(i, i ^ bits) for i in range(NEAR_GROUPS)])  16.6 us
    ppermute x25, waiting for transfers between devices, swap(): lax.ppermute(values, 'dp', [(i, i ^ bits) for i in range(NEAR_GROUPS)])  15.6 us
    all_to_all x4, waiting for transfers between devices, exchange(): return lax.all_to_all(values, 'dp', split_axis=0, concat_axis=0, tiled=True)  6.95 us
  transfers between devices with their start and end apart: 53, of which 30 were waited for; matrix products, arithmetic and copies ran while one was open for 0% of the time, Pallas kernels for 36%

profile of v6, /device:TPU:0, one launch (start us, length us, event | category | flops | bytes accessed | tf_op | source)
XLA Modules:
  0.0 206.3 jit_solution(1284087980119950800)
XLA Ops:
  0.6 5.6 %shard_map.280 = (f32[4,128,128]{2,1,0:T(8,128)}, bf16[256,128]{1,0:T(8,128)(2,1)}, bf16[8,336,768]{2,1,0:T(8,128)(2,1)}) custom-call(s32[1,128]{1,0:T(1,128)} %bitcast.25, s32[1,128]{1,0:T(1,128)} %bitcast.26, bf16[128,1152]{1,0:T(8,128)(2,1)} %refs_7_.8, bf16[8,144,768]{2,1,0:T(8,128)(2,1)} %refs_3_.1, bf16[8,144,768]{2,1,0:T(8,128)(2,1)} %refs_4_.1), custom_call_target="tpu_custom_call" | custom-call | tf_op jit(solution)/shard_map/pallas_call | solution.py:70
  6.3 5.4 %all-to-all-start.1 = ((bf16[8,336,768]{2,1,0:T(8,128)(2,1)}), bf16[8,336,768]{2,1,0:T(8,128)(2,1)}, u32[]{:S(2)}, u32[]{:S(2)}) async-start(bf16[8,336,768]{2,1,0:T(8,128)(2,1)} %get-tuple-element.140), calls=%async_computation.1 | async-start | bytes 8257536 | tf_op jit(solution)/shard_map/all_to_all | solution.py:1149
  11.8 4.5 %collective-permute-start.2 = (bf16[288,128]{1,0:T(8,128)(2,1)S(1)}, bf16[288,128]{1,0:T(8,128)(2,1)S(1)}, u32[]{:S(2)}, u32[]{:S(2)}) collective-permute-start(bf16[288,128]{1,0:T(8,128)(2,1)S(1)} %bitcast.22), channel_id=1, source_target_pairs={{0,3},{1,0},{2,1},{3,2},{4,7},{5,4},{6,5},{7,6},{8,11},{9,8},{10,9... | collective-permute-start | bytes 221192 | tf_op jit(solution)/shard_map/ppermute | solution.py:1077
  18.9 5.0 %collective-permute-done.1.refs_3_ = bf16[288,128]{1,0:T(8,128)(2,1)S(1)} collective-permute-done((bf16[288,128]{1,0:T(8,128)(2,1)S(1)}, bf16[288,128]{1,0:T(8,128)(2,1)S(1)}, u32[]{:S(2)}, u32[]{:S(2)}) %collective-permute-start.1) | collective-permute-done | bytes 73760 | tf_op jit(solution)/shard_map/ppermute | solution.py:1077
  24.7 3.7 %shard_map.281 = (bf16[128,1152]{1,0:T(8,128)(2,1)}, bf16[1152,128]{1,0:T(8,128)(2,1)}, bf16[128,576]{1,0:T(8,128)(2,1)}, f32[128,576]{1,0:T(8,128)}, f32[128,57...) custom-call(s32[1]{0:T(128)} %bitcast.refs_0_, ...), custom_call_target="tpu_custom_call" | custom-call | tf_op jit(solution)/shard_map/pallas_call | solution.py:70
  36.6 6.4 %shard_map.282 = (bf16[32,1152]{1,0:T(8,128)(2,1)S(1)}, bf16[32,1152]{1,0:T(8,128)(2,1)S(1)}, bf16[32,1152]{1,0:T(8,128)(2,1)S(1)}, bf16[32,1152]{1,0:T(8,128)(2...) custom-call(s32[1]{0:T(128)} %bitcast.refs_0_, bf16[104,128]{1,0:T(8,128)(2,1)} %copy-done.14, ...), custom_call_target="tpu_custom_call" | custom-call | tf_op jit(solution)/shard_map/pallas_call | solution.py:70
  50.4 3.0 %collective-permute-start.11 = (bf16[32,1152]{1,0:T(8,128)(2,1)S(1)}, bf16[32,1152]{1,0:T(8,128)(2,1)S(1)}, u32[]{:S(2)}, u32[]{:S(2)}) collective-permute-start(bf16[32,1152]{1,0:T(8,128)(2,1)S(1)} %add_convert_fusion.1.refs_1_), channel_id=1, source_target_pairs={{0,3},{1,0},{2,1},{3,2},{4,7},{5,4},{6,5},{7,6},{8,11},{9,8},{10,9... | collective-permute-start | bytes 221192 | tf_op jit(solution)/shard_map/ppermute | solution.py:1077
  62.2 4.2 %all-to-all-start = ((bf16[8,32,1152]{2,1,0:T(8,128)(2,1)}), bf16[8,32,1152]{2,1,0:T(8,128)(2,1)}, u32[]{:S(2)}, u32[]{:S(2)}) async-start(bf16[8,32,1152]{2,1,0:T(8,128)(2,1)} %bitcast.18), calls=%async_computation | async-start | bytes 1179648 | tf_op jit(solution)/shard_map/all_to_all | solution.py:1149
  66.4 5.6 %shard_map.284 = (bf16[1152,768]{1,0:T(8,128)(2,1)}, bf16[1152,768]{1,0:T(8,128)(2,1)}, bf16[256,1152]{1,0:T(8,128)(2,1)}, f32[256,768]{1,0:T(8,128)}) custom-call(bf16[8,336,768]{2,1,0:T(8,128)(2,1)} %all-to-all-done.1.refs_0_), custom_call_target="tpu_custom_call" | custom-call | tf_op jit(solution)/shard_map/pallas_call | solution.py:70
  80.0 4.2 %shard_map.285 = (bf16[256,768]{1,0:T(8,128)(2,1)}, bf16[256,768]{1,0:T(8,128)(2,1)}, bf16[256,1152]{1,0:T(8,128)(2,1)}) custom-call(bf16[256,1152]{1,0:T(8,128)(2,1)} %bitcast.7.refs_0_, bf16[1152,768]{1,0:T(8,128)(2,1)} %get-tuple-element.142.refs_1_, f32[256,768]{1,0:T(8,128)} %get-tuple-element.143.refs_2_), custom_call_target="tpu_custom_call" | custom-call | tf_op jit(solution)/shard_map/pallas_call | solution.py:70
  85.7 4.2 %all-to-all-start.2 = ((bf16[8,32,1152]{2,1,0:T(8,128)(2,1)}), bf16[8,32,1152]{2,1,0:T(8,128)(2,1)}, u32[]{:S(2)}, u32[]{:S(2)}) async-start(bf16[8,32,1152]{2,1,0:T(8,128)(2,1)} %bitcast.19), calls=%async_computation.2 | async-start | bytes 1179648 | tf_op jit(solution)/shard_map/all_to_all | solution.py:1149
  90.5 5.0 %shard_map.287 = bf16[8,336,768]{2,1,0:T(8,128)(2,1)} custom-call(bf16[256,1152]{1,0:T(8,128)(2,1)} %bitcast.7.refs_0_, bf16[256,1152]{1,0:T(8,128)(2,1)} %get-tuple-element.151.refs_1_, bf16[256,768]{1,0:T(8,128)(2,1)} %get-tuple-element.152.refs_2_, bf16[256,768]{1,0:T(8,128)(2,1)} %get-tuple-element.153.refs_3_, bf16[1152,768]{1,0:T(8,128)(2,1)} %get-tuple-element.154.refs_4_), custom_call_target="tpu_custom_call" | custom-call | tf_op jit(solution)/shard_map/pallas_call | solution.py:70
  95.5 4.8 %all-to-all-done.2 = bf16[8,32,1152]{2,1,0:T(8,128)(2,1)} async-done(((bf16[8,32,1152]{2,1,0:T(8,128)(2,1)}), bf16[8,32,1152]{2,1,0:T(8,128)(2,1)}, u32[]{:S(2)}, u32[]{:S(2)}) %all-to-all-start.2) | async-done | bytes 589856 | tf_op jit(solution)/shard_map/all_to_all | solution.py:1149
  100.3 4.6 %all-to-all-start.3 = ((bf16[8,336,768]{2,1,0:T(8,128)(2,1)}), bf16[8,336,768]{2,1,0:T(8,128)(2,1)}, u32[]{:S(2)}, u32[]{:S(2)}) async-start(bf16[8,336,768]{2,1,0:T(8,128)(2,1)} %shard_map.287), calls=%async_computation.3 | async-start | bytes 8257536 | tf_op jit(solution)/shard_map/all_to_all | solution.py:1149
  113.8 2.9 %collective-permute-done.22 = bf16[32,1152]{1,0:T(8,128)(2,1)S(1)} collective-permute-done((bf16[32,1152]{1,0:T(8,128)(2,1)S(1)}, bf16[32,1152]{1,0:T(8,128)(2,1)S(1)}, u32[]{:S(2)}, u32[]{:S(2)}) %collective-permute-start.22) | collective-permute-done | bytes 73760 | tf_op jit(solution)/shard_map/ppermute | solution.py:1077
  120.6 4.6 %shard_map.289 = (f32[2048,640]{1,0:T(8,128)S(1)}, f32[2064,640]{1,0:T(8,128)S(1)}, f32[128,640]{1,0:T(8,128)S(1)}, f32[128,640]{1,0:T(8,128)S(1)}, f32[128,576]...) custom-call(f32[128,576]{1,0:T(8,128)} %get-tuple-element.160.refs_0_, ...), custom_call_target="tpu_custom_call" | custom-call | tf_op jit(solution)/shard_map/pallas_call | solution.py:70
  127.4 3.0 %shard_map.290 = (f32[288,128]{1,0:T(8,128)}, bf16[1152,128]{1,0:T(8,128)(2,1)S(1)}, f32[128,576]{1,0:T(8,128)S(1)}, f32[1,1152]{1,0:T(1,128)S(1)}) custom-call(s32[1]{0:T(128)} %bitcast.refs_0_, bf16[32,1152]{1,0:T(8,128)(2,1)} %copy-done.26, bf16[32,1152]{1,0:T(8,128)(2,1)S(1)} %collective-permute-done.24.refs_2_, ...), custom_call_target="tpu_custom_call" | custom-call | tf_op jit(solution)/shard_map/pallas_call | solution.py:70
  130.4 9.2 %shard_map.291 = (bf16[104,128]{1,0:T(8,128)(2,1)S(1)}, f32[128,576]{1,0:T(8,128)S(1)}, bf16[128,576]{1,0:T(8,128)(2,1)S(1)}, bf16[2304,128]{1,0:T(8,128)(2,1)S(1)}) custom-call(f32[128,576]{1,0:T(8,128)S(1)} %get-tuple-element.169.refs_0_, f32[128,576]{1,0:T(8,128)S(1)} %get-tuple-element.170.refs_1_, f32[128,576]{1,0:T(8,128)S(1)} %get-tuple-element.171.refs_2_, ...), custom_call_target="tpu_custom_call" | custom-call | tf_op jit(solution)/shard_map/pallas_call | solution.py:70
  150.8 3.4 %shard_map.292 = (bf16[4,304,128]{2,1,0:T(8,128)(2,1)}, bf16[768,128]{1,0:T(8,128)(2,1)S(1)}) custom-call(s32[1]{0:T(128)} %bitcast.refs_0_, bf16[104,128]{1,0:T(8,128)(2,1)} %copy-done.13, bf16[104,128]{1,0:T(8,128)(2,1)S(1)} %collective-permute-done.27.refs_2_, bf16[104,128]{1,0:T(8,128)(2,1)S(1)} %collective-permute-done.28.refs_3_, ...), custom_call_target="tpu_custom_call" | custom-call | tf_op jit(solution)/shard_map/pallas_call | solution.py:70
  157.8 3.5 %shard_map.293 = (bf16[1024,1152]{1,0:T(8,128)(2,1)S(1)}, bf16[576,1024]{1,0:T(8,128)(2,1)S(1)}, bf16[576,1024]{1,0:T(8,128)(2,1)S(1)}) custom-call(bf16[2304,128]{1,0:T(8,128)(2,1)} %copy-done.4, bf16[2304,128]{1,0:T(8,128)(2,1)} %collective-permute-done.12.refs_0_.refs_1_, bf16[2304,128]{1,0:T(8,128)(2,1)} %collective-permute-done.13.refs_1_.refs_2_, ...), custom_call_target="tpu_custom_call" | custom-call | tf_op jit(solution)/shard_map/pallas_call | solution.py:70
  161.2 4.2 %shard_map.294 = (f32[8,144,768]{2,1,0:T(8,128)}, f32[8,144,768]{2,1,0:T(8,128)}) custom-call(bf16[8,336,768]{2,1,0:T(8,128)(2,1)} %all-to-all-done.3.refs_0_.refs_3_), custom_call_target="tpu_custom_call" | custom-call | tf_op jit(solution)/shard_map/pallas_call | solution.py:70
  170.6 3.4 %collective-permute-done.31.refs_6_.refs_12_ = bf16[768,128]{1,0:T(8,128)(2,1)S(1)} collective-permute-done((bf16[768,128]{1,0:T(8,128)(2,1)S(1)}, bf16[768,128]{1,0:T(8,128)(2,1)S(1)}, u32[]{:S(2)}, u32[]{:S(2)}) %collective-permute-start.31) | collective-permute-done | bytes 196640 | tf_op jit(solution)/shard_map/ppermute | solution.py:1096
  178.2 3.7 %shard_map.296 = (bf16[624,128]{1,0:T(8,128)(2,1)}, bf16[624,128]{1,0:T(8,128)(2,1)}, bf16[624,128]{1,0:T(8,128)(2,1)}, bf16[624,128]{1,0:T(8,128)(2,1)}, f32[4,576]{1,0:T(4,128)}, /*index=5*/f32[576]{0:T(1024)}) custom-call(s32[1]{0:T(128)} %bitcast.refs_0_, bf16[256,128]{1,0:T(8,128)(2,1)} %get-tuple-element.128.refs_7_.refs_1_, ...), custom_call_target="tpu_custom_call" | custom-call | tf_op jit(solution)/shard_map/pallas_call | solution.py:70
  194.1 10.1 %shard_map.297 = (f32[576,1152]{1,0:T(8,128)}, f32[2,576,1152]{2,1,0:T(8,128)}, f32[104,576]{1,0:T(8,128)}, f32[72,576]{1,0:T(8,128)}, f32[576]{0:T(1024)}, /*in...) custom-call(bf16[2304,128]{1,0:T(8,128)(2,1)} %copy-done.5, bf16[2304,128]{1,0:T(8,128)(2,1)} %collective-permute-done.33.refs_0_.refs_1_, ...), custom_call_target="tpu_custom_call" | custom-call | tf_op jit(solution)/shard_map/pallas_call | solution.py:70
  (171 shorter events, 90.8 us)
Async XLA Ops:
  6.3 55.9 %all-to-all-start.1 = ((bf16[8,336,768]{2,1,0:T(8,128)(2,1)}), bf16[8,336,768]{2,1,0:T(8,128)(2,1)}, u32[]{:S(2)}, u32[]{:S(2)}) async-start(bf16[8,336,768]{2,1,0:T(8,128)(2,1)} %get-tuple-element.140), calls=%async_computation.1 | async-start | bytes 8257536 | tf_op jit(solution)/shard_map/all_to_all | solution.py:1149
  47.1 25.9 %collective-permute-start.13 = (bf16[2304,128]{1,0:T(8,128)(2,1)S(1)}, bf16[2304,128]{1,0:T(8,128)(2,1)}, u32[]{:S(2)}, u32[]{:S(2)}) collective-permute-start(bf16[2304,128]{1,0:T(8,128)(2,1)S(1)} %get-tuple-element.187.refs_0_), channel_id=1, source_target_pairs={{0,16},{4,20},{8,24},{12,28},{16,0},{20,4},{24,8},{28,12},{1,17},{... | collective-permute-start | bytes 1769480 | tf_op jit(solution)/shard_map/ppermute | solution.py:1096
  48.8 24.2 %collective-permute-start.12 = (bf16[2304,128]{1,0:T(8,128)(2,1)S(1)}, bf16[2304,128]{1,0:T(8,128)(2,1)}, u32[]{:S(2)}, u32[]{:S(2)}) collective-permute-start(bf16[2304,128]{1,0:T(8,128)(2,1)S(1)} %get-tuple-element.187.refs_0_), channel_id=1, source_target_pairs={{0,8},{4,12},{8,0},{12,4},{16,24},{20,28},{24,16},{28,20},{1,9},{5... | collective-permute-start | bytes 1769480 | tf_op jit(solution)/shard_map/ppermute | solution.py:1096
  62.2 17.8 %all-to-all-start = ((bf16[8,32,1152]{2,1,0:T(8,128)(2,1)}), bf16[8,32,1152]{2,1,0:T(8,128)(2,1)}, u32[]{:S(2)}, u32[]{:S(2)}) async-start(bf16[8,32,1152]{2,1,0:T(8,128)(2,1)} %bitcast.18), calls=%async_computation | async-start | bytes 1179648 | tf_op jit(solution)/shard_map/all_to_all | solution.py:1149
  75.0 9.7 %collective-permute-start.14 = (bf16[1152,128]{1,0:T(8,128)(2,1)}, bf16[1152,128]{1,0:T(8,128)(2,1)}, u32[]{:S(2)}, u32[]{:S(2)}) collective-permute-start(bf16[1152,128]{1,0:T(8,128)(2,1)} %get-tuple-element.148), channel_id=1, source_target_pairs={{0,8},{4,12},{8,0},{12,4},{16,24},{20,28},{24,16},{28,20},{1,9},{5... | collective-permute-start | bytes 884744 | tf_op jit(solution)/shard_map/ppermute | solution.py:1096
  76.2 9.5 %collective-permute-start.15 = (bf16[1152,128]{1,0:T(8,128)(2,1)}, bf16[1152,128]{1,0:T(8,128)(2,1)}, u32[]{:S(2)}, u32[]{:S(2)}) collective-permute-start(bf16[1152,128]{1,0:T(8,128)(2,1)} %get-tuple-element.149), channel_id=1, source_target_pairs={{0,16},{4,20},{8,24},{12,28},{16,0},{20,4},{24,8},{28,12},{1,17},{... | collective-permute-start | bytes 884744 | tf_op jit(solution)/shard_map/ppermute | solution.py:1096
  77.4 18.1 %collective-permute-start.16 = (bf16[2304,128]{1,0:T(8,128)(2,1)S(1)}, bf16[2304,128]{1,0:T(8,128)(2,1)}, u32[]{:S(2)}, u32[]{:S(2)}) collective-permute-start(bf16[2304,128]{1,0:T(8,128)(2,1)S(1)} %get-tuple-element.187.refs_0_), channel_id=1, source_target_pairs={{0,4},{4,0},{8,12},{12,8},{16,20},{20,16},{24,28},{28,24},{1,5},{5... | collective-permute-start | bytes 1769480 | tf_op jit(solution)/shard_map/ppermute | solution.py:1096
  77.4 18.1 %collective-permute-start.17 = (bf16[2304,128]{1,0:T(8,128)(2,1)}, bf16[2304,128]{1,0:T(8,128)(2,1)}, u32[]{:S(2)}, u32[]{:S(2)}) collective-permute-start(bf16[2304,128]{1,0:T(8,128)(2,1)} %collective-permute-done.12.refs_0_.refs_1_), channel_id=1, source_target_pairs={{0,4},{4,0},{8,12},{12,8},{16,20},{20,16},{24,28},{28,24},{1,5},{5... | collective-permute-start | bytes 1769480 | tf_op jit(solution)/shard_map/ppermute | solution.py:1096
  77.9 17.6 %collective-permute-start.18 = (bf16[2304,128]{1,0:T(8,128)(2,1)}, bf16[2304,128]{1,0:T(8,128)(2,1)}, u32[]{:S(2)}, u32[]{:S(2)}) collective-permute-start(bf16[2304,128]{1,0:T(8,128)(2,1)} %collective-permute-done.13.refs_1_.refs_2_), channel_id=1, source_target_pairs={{0,4},{4,0},{8,12},{12,8},{16,20},{20,16},{24,28},{28,24},{1,5},{5... | collective-permute-start | bytes 1769480 | tf_op jit(solution)/shard_map/ppermute | solution.py:1096
  85.7 14.7 %all-to-all-start.2 = ((bf16[8,32,1152]{2,1,0:T(8,128)(2,1)}), bf16[8,32,1152]{2,1,0:T(8,128)(2,1)}, u32[]{:S(2)}, u32[]{:S(2)}) async-start(bf16[8,32,1152]{2,1,0:T(8,128)(2,1)} %bitcast.19), calls=%async_computation.2 | async-start | bytes 1179648 | tf_op jit(solution)/shard_map/all_to_all | solution.py:1149
  100.3 57.4 %all-to-all-start.3 = ((bf16[8,336,768]{2,1,0:T(8,128)(2,1)}), bf16[8,336,768]{2,1,0:T(8,128)(2,1)}, u32[]{:S(2)}, u32[]{:S(2)}) async-start(bf16[8,336,768]{2,1,0:T(8,128)(2,1)} %shard_map.287), calls=%async_computation.3 | async-start | bytes 8257536 | tf_op jit(solution)/shard_map/all_to_all | solution.py:1149
  139.7 26.9 %collective-permute-start.34 = (bf16[2304,128]{1,0:T(8,128)(2,1)S(1)}, bf16[2304,128]{1,0:T(8,128)(2,1)}, u32[]{:S(2)}, u32[]{:S(2)}) collective-permute-start(bf16[2304,128]{1,0:T(8,128)(2,1)S(1)} %get-tuple-element.213.refs_0_), channel_id=1, source_target_pairs={{0,16},{4,20},{8,24},{12,28},{16,0},{20,4},{24,8},{28,12},{1,17},{... | collective-permute-start | bytes 1769480 | tf_op jit(solution)/shard_map/ppermute | solution.py:1096
  141.4 25.2 %collective-permute-start.33 = (bf16[2304,128]{1,0:T(8,128)(2,1)S(1)}, bf16[2304,128]{1,0:T(8,128)(2,1)}, u32[]{:S(2)}, u32[]{:S(2)}) collective-permute-start(bf16[2304,128]{1,0:T(8,128)(2,1)S(1)} %get-tuple-element.213.refs_0_), channel_id=1, source_target_pairs={{0,8},{4,12},{8,0},{12,4},{16,24},{20,28},{24,16},{28,20},{1,9},{5... | collective-permute-start | bytes 1769480 | tf_op jit(solution)/shard_map/ppermute | solution.py:1096
  154.2 16.4 %collective-permute-start.32 = (bf16[768,128]{1,0:T(8,128)(2,1)S(1)}, bf16[768,128]{1,0:T(8,128)(2,1)S(1)}, u32[]{:S(2)}, u32[]{:S(2)}) collective-permute-start(bf16[768,128]{1,0:T(8,128)(2,1)S(1)} %get-tuple-element.204.refs_4_.refs_10_), channel_id=1, source_target_pairs={{0,24},{4,28},{8,16},{12,20},{16,8},{20,12},{24,0},{28,4},{1,25},{... | collective-permute-start | bytes 589832 | tf_op jit(solution)/shard_map/ppermute | solution.py:1096
  154.6 19.4 %collective-permute-start.31 = (bf16[768,128]{1,0:T(8,128)(2,1)S(1)}, bf16[768,128]{1,0:T(8,128)(2,1)S(1)}, u32[]{:S(2)}, u32[]{:S(2)}) collective-permute-start(bf16[768,128]{1,0:T(8,128)(2,1)S(1)} %get-tuple-element.204.refs_4_.refs_10_), channel_id=1, source_target_pairs={{0,16},{4,20},{8,24},{12,28},{16,0},{20,4},{24,8},{28,12},{1,17},{... | collective-permute-start | bytes 589832 | tf_op jit(solution)/shard_map/ppermute | solution.py:1096
  156.3 17.7 %collective-permute-start.30 = (bf16[768,128]{1,0:T(8,128)(2,1)S(1)}, bf16[768,128]{1,0:T(8,128)(2,1)S(1)}, u32[]{:S(2)}, u32[]{:S(2)}) collective-permute-start(bf16[768,128]{1,0:T(8,128)(2,1)S(1)} %get-tuple-element.204.refs_4_.refs_10_), channel_id=1, source_target_pairs={{0,8},{4,12},{8,0},{12,4},{16,24},{20,28},{24,16},{28,20},{1,9},{5... | collective-permute-start | bytes 589832 | tf_op jit(solution)/shard_map/ppermute | solution.py:1096
  174.1 9.6 %collective-permute-start.42 = (bf16[1152,128]{1,0:T(8,128)(2,1)}, bf16[1152,128]{1,0:T(8,128)(2,1)S(1)}, u32[]{:S(2)}, u32[]{:S(2)}) collective-permute-start(bf16[1152,128]{1,0:T(8,128)(2,1)} %get-tuple-element.202), channel_id=1, source_target_pairs={{0,8},{4,12},{8,0},{12,4},{16,24},{20,28},{24,16},{28,20},{1,9},{5... | collective-permute-start | bytes 884744 | tf_op jit(solution)/shard_map/ppermute | solution.py:1096
  174.9 9.3 %collective-permute-start.43 = (bf16[1152,128]{1,0:T(8,128)(2,1)}, bf16[1152,128]{1,0:T(8,128)(2,1)S(1)}, u32[]{:S(2)}, u32[]{:S(2)}) collective-permute-start(bf16[1152,128]{1,0:T(8,128)(2,1)} %get-tuple-element.203), channel_id=1, source_target_pairs={{0,16},{4,20},{8,24},{12,28},{16,0},{20,4},{24,8},{28,12},{1,17},{... | collective-permute-start | bytes 884744 | tf_op jit(solution)/shard_map/ppermute | solution.py:1096
  184.2 8.5 %collective-permute-start.44 = (bf16[2304,128]{1,0:T(8,128)(2,1)S(1)}, bf16[2304,128]{1,0:T(8,128)(2,1)S(1)}, u32[]{:S(2)}, u32[]{:S(2)}) collective-permute-start(bf16[2304,128]{1,0:T(8,128)(2,1)S(1)} %get-tuple-element.213.refs_0_), channel_id=1, source_target_pairs={{0,4},{4,0},{8,12},{12,8},{16,20},{20,16},{24,28},{28,24},{1,5},{5... | collective-permute-start | bytes 1769480 | tf_op jit(solution)/shard_map/ppermute | solution.py:1096
  184.2 9.8 %collective-permute-start.45 = (bf16[2304,128]{1,0:T(8,128)(2,1)}, bf16[2304,128]{1,0:T(8,128)(2,1)S(1)}, u32[]{:S(2)}, u32[]{:S(2)}) collective-permute-start(bf16[2304,128]{1,0:T(8,128)(2,1)} %collective-permute-done.33.refs_0_.refs_1_), channel_id=1, source_target_pairs={{0,4},{4,0},{8,12},{12,8},{16,20},{20,16},{24,28},{28,24},{1,5},{5... | collective-permute-start | bytes 1769480 | tf_op jit(solution)/shard_map/ppermute | solution.py:1096
  184.8 9.3 %collective-permute-start.46 = (bf16[2304,128]{1,0:T(8,128)(2,1)}, bf16[2304,128]{1,0:T(8,128)(2,1)S(1)}, u32[]{:S(2)}, u32[]{:S(2)}) collective-permute-start(bf16[2304,128]{1,0:T(8,128)(2,1)} %collective-permute-done.34.refs_1_.refs_2_), channel_id=1, source_target_pairs={{0,4},{4,0},{8,12},{12,8},{16,20},{20,16},{24,28},{28,24},{1,5},{5... | collective-permute-start | bytes 1769480 | tf_op jit(solution)/shard_map/ppermute | solution.py:1096
  187.9 16.3 %collective-permute-start.39 = (bf16[624,128]{1,0:T(8,128)(2,1)}, bf16[624,128]{1,0:T(8,128)(2,1)S(1)}, u32[]{:S(2)}, u32[]{:S(2)}) collective-permute-start(bf16[624,128]{1,0:T(8,128)(2,1)} %get-tuple-element.209), channel_id=1, source_target_pairs={{0,1},{1,2},{2,3},{3,0},{4,5},{5,6},{6,7},{7,4},{8,9},{9,10},{10,1... | collective-permute-start | bytes 479240 | tf_op jit(solution)/shard_map/ppermute | solution.py:1077
  190.1 14.1 %collective-permute-start.40 = (bf16[624,128]{1,0:T(8,128)(2,1)}, bf16[624,128]{1,0:T(8,128)(2,1)S(1)}, u32[]{:S(2)}, u32[]{:S(2)}) collective-permute-start(bf16[624,128]{1,0:T(8,128)(2,1)} %get-tuple-element.210), channel_id=1, source_target_pairs={{0,2},{1,3},{2,0},{3,1},{4,6},{5,7},{6,4},{7,5},{8,10},{9,11},{10,... | collective-permute-start | bytes 479240 | tf_op jit(solution)/shard_map/ppermute | solution.py:1077
  192.7 11.5 %collective-permute-start.41 = (bf16[624,128]{1,0:T(8,128)(2,1)}, bf16[624,128]{1,0:T(8,128)(2,1)S(1)}, u32[]{:S(2)}, u32[]{:S(2)}) collective-permute-start(bf16[624,128]{1,0:T(8,128)(2,1)} %get-tuple-element.211), channel_id=1, source_target_pairs={{0,3},{1,0},{2,1},{3,2},{4,7},{5,4},{6,5},{7,6},{8,11},{9,8},{10,9... | collective-permute-start | bytes 479240 | tf_op jit(solution)/shard_map/ppermute | solution.py:1077
  (63 other events, 606.0 us)

commit v7 on v6

--- a/solution.py
+++ b/solution.py
@@ -262,10 +262,6 @@
         [(resets_in, resets), (routes_in, routes), (cotangent_in, cotangent)], early_arrivals
     )
     arriving = run_copies(copies, arrivals)
-    for copy in early:
-        copy.wait()
-    fill_choose(capacity, length, experts, routes, choose)
-    slots = dot_nn(choose[...], cotangent[...]).astype(BF16)
     started = []
     for index in range(experts):
         copies = []
@@ -274,6 +270,10 @@
             target = message.at[index, pl.ds(which * share, share)]
             copies.append((staged.at[index, which], target))
         started += run_copies(copies, semaphores.at[pl.ds(2 * index, 2)])
+    for copy in early:
+        copy.wait()
+    fill_choose(capacity, length, experts, routes, choose)
+    slots = dot_nn(choose[...], cotangent[...]).astype(BF16)
     copies = []
     for index in range(experts):
         put_folded(packed.at[index], slots[index * capacity : (index + 1) * capacity])

time: 208 us -> 207 us (level)
  no operation moved by 1% of the time
where the time goes in v7:
time: 207 us; the launch traced here: 206 us
  Pallas kernels  81.2 us (39%)
  starting transfers between devices  71.3 us (34%)
  waiting for transfers between devices  49.8 us (24%)
    pallas_call x19, Pallas kernels, run_kernel(): pl.pallas_call(body, out_shape=[held(index, shape, dtype) for index, (sha...  81.2 us
    ppermute x24, starting transfers between devices, send_chunks(): lax.ppermute(chunks[s], 'tensor', pairs[s])  36.4 us
    ppermute x24, waiting for transfers between devices, send_chunks(): lax.ppermute(chunks[s], 'tensor', pairs[s])  27.2 us
    all_to_all x4, starting transfers between devices, exchange(): return lax.all_to_all(values, 'dp', split_axis=0, concat_axis=0, tiled=True)  18.4 us
    ppermute x25, starting transfers between devices, swap(): lax.ppermute(values, 'dp', [(i, i ^ bits) for i in range(NEAR_GROUPS)])  16.5 us
    ppermute x25, waiting for transfers between devices, swap(): lax.ppermute(values, 'dp', [(i, i ^ bits) for i in range(NEAR_GROUPS)])  15.6 us
    all_to_all x4, waiting for transfers between devices, exchange(): return lax.all_to_all(values, 'dp', split_axis=0, concat_axis=0, tiled=True)  7.04 us
  transfers between devices with their start and end apart: 53, of which 30 were waited for; matrix products, arithmetic and copies ran while one was open for 0% of the time, Pallas kernels for 36%

profile of v7, /device:TPU:0, one launch (start us, length us, event | category | flops | bytes accessed | tf_op | source)
XLA Modules:
  0.0 205.8 jit_solution(7001813180768948862)
XLA Ops:
  0.6 5.0 %shard_map.280 = (f32[4,128,128]{2,1,0:T(8,128)}, bf16[256,128]{1,0:T(8,128)(2,1)}, bf16[8,336,768]{2,1,0:T(8,128)(2,1)}) custom-call(s32[1,128]{1,0:T(1,128)} %bitcast.25, s32[1,128]{1,0:T(1,128)} %bitcast.26, bf16[128,1152]{1,0:T(8,128)(2,1)} %refs_7_.8, bf16[8,144,768]{2,1,0:T(8,128)(2,1)} %refs_3_.1, bf16[8,144,768]{2,1,0:T(8,128)(2,1)} %refs_4_.1), custom_call_target="tpu_custom_call" | custom-call | tf_op jit(solution)/shard_map/pallas_call | solution.py:70
  5.8 5.4 %all-to-all-start.1 = ((bf16[8,336,768]{2,1,0:T(8,128)(2,1)}), bf16[8,336,768]{2,1,0:T(8,128)(2,1)}, u32[]{:S(2)}, u32[]{:S(2)}) async-start(bf16[8,336,768]{2,1,0:T(8,128)(2,1)} %get-tuple-element.140), calls=%async_computation.1 | async-start | bytes 8257536 | tf_op jit(solution)/shard_map/all_to_all | solution.py:1149
  11.3 4.5 %collective-permute-start.2 = (bf16[288,128]{1,0:T(8,128)(2,1)S(1)}, bf16[288,128]{1,0:T(8,128)(2,1)S(1)}, u32[]{:S(2)}, u32[]{:S(2)}) collective-permute-start(bf16[288,128]{1,0:T(8,128)(2,1)S(1)} %bitcast.22), channel_id=1, source_target_pairs={{0,3},{1,0},{2,1},{3,2},{4,7},{5,4},{6,5},{7,6},{8,11},{9,8},{10,9... | collective-permute-start | bytes 221192 | tf_op jit(solution)/shard_map/ppermute | solution.py:1077
  18.4 5.0 %collective-permute-done.1.refs_3_ = bf16[288,128]{1,0:T(8,128)(2,1)S(1)} collective-permute-done((bf16[288,128]{1,0:T(8,128)(2,1)S(1)}, bf16[288,128]{1,0:T(8,128)(2,1)S(1)}, u32[]{:S(2)}, u32[]{:S(2)}) %collective-permute-start.1) | collective-permute-done | bytes 73760 | tf_op jit(solution)/shard_map/ppermute | solution.py:1077
  24.1 3.7 %shard_map.281 = (bf16[128,1152]{1,0:T(8,128)(2,1)}, bf16[1152,128]{1,0:T(8,128)(2,1)}, bf16[128,576]{1,0:T(8,128)(2,1)}, f32[128,576]{1,0:T(8,128)}, f32[128,57...) custom-call(s32[1]{0:T(128)} %bitcast.refs_0_, ...), custom_call_target="tpu_custom_call" | custom-call | tf_op jit(solution)/shard_map/pallas_call | solution.py:70
  36.0 6.4 %shard_map.282 = (bf16[32,1152]{1,0:T(8,128)(2,1)S(1)}, bf16[32,1152]{1,0:T(8,128)(2,1)S(1)}, bf16[32,1152]{1,0:T(8,128)(2,1)S(1)}, bf16[32,1152]{1,0:T(8,128)(2...) custom-call(s32[1]{0:T(128)} %bitcast.refs_0_, bf16[104,128]{1,0:T(8,128)(2,1)} %copy-done.14, ...), custom_call_target="tpu_custom_call" | custom-call | tf_op jit(solution)/shard_map/pallas_call | solution.py:70
  49.9 2.9 %collective-permute-start.11 = (bf16[32,1152]{1,0:T(8,128)(2,1)S(1)}, bf16[32,1152]{1,0:T(8,128)(2,1)S(1)}, u32[]{:S(2)}, u32[]{:S(2)}) collective-permute-start(bf16[32,1152]{1,0:T(8,128)(2,1)S(1)} %add_convert_fusion.1.refs_1_), channel_id=1, source_target_pairs={{0,3},{1,0},{2,1},{3,2},{4,7},{5,4},{6,5},{7,6},{8,11},{9,8},{10,9... | collective-permute-start | bytes 221192 | tf_op jit(solution)/shard_map/ppermute | solution.py:1077
  61.6 4.2 %all-to-all-start = ((bf16[8,32,1152]{2,1,0:T(8,128)(2,1)}), bf16[8,32,1152]{2,1,0:T(8,128)(2,1)}, u32[]{:S(2)}, u32[]{:S(2)}) async-start(bf16[8,32,1152]{2,1,0:T(8,128)(2,1)} %bitcast.18), calls=%async_computation | async-start | bytes 1179648 | tf_op jit(solution)/shard_map/all_to_all | solution.py:1149
  65.8 5.6 %shard_map.284 = (bf16[1152,768]{1,0:T(8,128)(2,1)}, bf16[1152,768]{1,0:T(8,128)(2,1)}, bf16[256,1152]{1,0:T(8,128)(2,1)}, f32[256,768]{1,0:T(8,128)}) custom-call(bf16[8,336,768]{2,1,0:T(8,128)(2,1)} %all-to-all-done.1.refs_0_), custom_call_target="tpu_custom_call" | custom-call | tf_op jit(solution)/shard_map/pallas_call | solution.py:70
  79.5 4.2 %shard_map.285 = (bf16[256,768]{1,0:T(8,128)(2,1)}, bf16[256,768]{1,0:T(8,128)(2,1)}, bf16[256,1152]{1,0:T(8,128)(2,1)}) custom-call(bf16[256,1152]{1,0:T(8,128)(2,1)} %bitcast.7.refs_0_, bf16[1152,768]{1,0:T(8,128)(2,1)} %get-tuple-element.142.refs_1_, f32[256,768]{1,0:T(8,128)} %get-tuple-element.143.refs_2_), custom_call_target="tpu_custom_call" | custom-call | tf_op jit(solution)/shard_map/pallas_call | solution.py:70
  85.1 4.2 %all-to-all-start.2 = ((bf16[8,32,1152]{2,1,0:T(8,128)(2,1)}), bf16[8,32,1152]{2,1,0:T(8,128)(2,1)}, u32[]{:S(2)}, u32[]{:S(2)}) async-start(bf16[8,32,1152]{2,1,0:T(8,128)(2,1)} %bitcast.19), calls=%async_computation.2 | async-start | bytes 1179648 | tf_op jit(solution)/shard_map/all_to_all | solution.py:1149
  89.9 5.0 %shard_map.287 = bf16[8,336,768]{2,1,0:T(8,128)(2,1)} custom-call(bf16[256,1152]{1,0:T(8,128)(2,1)} %bitcast.7.refs_0_, bf16[256,1152]{1,0:T(8,128)(2,1)} %get-tuple-element.151.refs_1_, bf16[256,768]{1,0:T(8,128)(2,1)} %get-tuple-element.152.refs_2_, bf16[256,768]{1,0:T(8,128)(2,1)} %get-tuple-element.153.refs_3_, bf16[1152,768]{1,0:T(8,128)(2,1)} %get-tuple-element.154.refs_4_), custom_call_target="tpu_custom_call" | custom-call | tf_op jit(solution)/shard_map/pallas_call | solution.py:70
  95.0 4.8 %all-to-all-done.2 = bf16[8,32,1152]{2,1,0:T(8,128)(2,1)} async-done(((bf16[8,32,1152]{2,1,0:T(8,128)(2,1)}), bf16[8,32,1152]{2,1,0:T(8,128)(2,1)}, u32[]{:S(2)}, u32[]{:S(2)}) %all-to-all-start.2) | async-done | bytes 589856 | tf_op jit(solution)/shard_map/all_to_all | solution.py:1149
  99.8 4.6 %all-to-all-start.3 = ((bf16[8,336,768]{2,1,0:T(8,128)(2,1)}), bf16[8,336,768]{2,1,0:T(8,128)(2,1)}, u32[]{:S(2)}, u32[]{:S(2)}) async-start(bf16[8,336,768]{2,1,0:T(8,128)(2,1)} %shard_map.287), calls=%async_computation.3 | async-start | bytes 8257536 | tf_op jit(solution)/shard_map/all_to_all | solution.py:1149
  113.3 2.9 %collective-permute-done.22 = bf16[32,1152]{1,0:T(8,128)(2,1)S(1)} collective-permute-done((bf16[32,1152]{1,0:T(8,128)(2,1)S(1)}, bf16[32,1152]{1,0:T(8,128)(2,1)S(1)}, u32[]{:S(2)}, u32[]{:S(2)}) %collective-permute-start.22) | collective-permute-done | bytes 73760 | tf_op jit(solution)/shard_map/ppermute | solution.py:1077
  120.1 4.6 %shard_map.289 = (f32[2048,640]{1,0:T(8,128)S(1)}, f32[2064,640]{1,0:T(8,128)S(1)}, f32[128,640]{1,0:T(8,128)S(1)}, f32[128,640]{1,0:T(8,128)S(1)}, f32[128,576]...) custom-call(f32[128,576]{1,0:T(8,128)} %get-tuple-element.160.refs_0_, ...), custom_call_target="tpu_custom_call" | custom-call | tf_op jit(solution)/shard_map/pallas_call | solution.py:70
  126.9 3.0 %shard_map.290 = (f32[288,128]{1,0:T(8,128)}, bf16[1152,128]{1,0:T(8,128)(2,1)S(1)}, f32[128,576]{1,0:T(8,128)S(1)}, f32[1,1152]{1,0:T(1,128)S(1)}) custom-call(s32[1]{0:T(128)} %bitcast.refs_0_, bf16[32,1152]{1,0:T(8,128)(2,1)} %copy-done.26, bf16[32,1152]{1,0:T(8,128)(2,1)S(1)} %collective-permute-done.24.refs_2_, ...), custom_call_target="tpu_custom_call" | custom-call | tf_op jit(solution)/shard_map/pallas_call | solution.py:70
  129.9 9.2 %shard_map.291 = (bf16[104,128]{1,0:T(8,128)(2,1)S(1)}, f32[128,576]{1,0:T(8,128)S(1)}, bf16[128,576]{1,0:T(8,128)(2,1)S(1)}, bf16[2304,128]{1,0:T(8,128)(2,1)S(1)}) custom-call(f32[128,576]{1,0:T(8,128)S(1)} %get-tuple-element.169.refs_0_, f32[128,576]{1,0:T(8,128)S(1)} %get-tuple-element.170.refs_1_, f32[128,576]{1,0:T(8,128)S(1)} %get-tuple-element.171.refs_2_, ...), custom_call_target="tpu_custom_call" | custom-call | tf_op jit(solution)/shard_map/pallas_call | solution.py:70
  150.2 3.4 %shard_map.292 = (bf16[4,304,128]{2,1,0:T(8,128)(2,1)}, bf16[768,128]{1,0:T(8,128)(2,1)S(1)}) custom-call(s32[1]{0:T(128)} %bitcast.refs_0_, bf16[104,128]{1,0:T(8,128)(2,1)} %copy-done.13, bf16[104,128]{1,0:T(8,128)(2,1)S(1)} %collective-permute-done.27.refs_2_, bf16[104,128]{1,0:T(8,128)(2,1)S(1)} %collective-permute-done.28.refs_3_, ...), custom_call_target="tpu_custom_call" | custom-call | tf_op jit(solution)/shard_map/pallas_call | solution.py:70
  157.2 3.5 %shard_map.293 = (bf16[1024,1152]{1,0:T(8,128)(2,1)S(1)}, bf16[576,1024]{1,0:T(8,128)(2,1)S(1)}, bf16[576,1024]{1,0:T(8,128)(2,1)S(1)}) custom-call(bf16[2304,128]{1,0:T(8,128)(2,1)} %copy-done.4, bf16[2304,128]{1,0:T(8,128)(2,1)} %collective-permute-done.12.refs_0_.refs_1_, bf16[2304,128]{1,0:T(8,128)(2,1)} %collective-permute-done.13.refs_1_.refs_2_, ...), custom_call_target="tpu_custom_call" | custom-call | tf_op jit(solution)/shard_map/pallas_call | solution.py:70
  160.7 4.2 %shard_map.294 = (f32[8,144,768]{2,1,0:T(8,128)}, f32[8,144,768]{2,1,0:T(8,128)}) custom-call(bf16[8,336,768]{2,1,0:T(8,128)(2,1)} %all-to-all-done.3.refs_0_.refs_3_), custom_call_target="tpu_custom_call" | custom-call | tf_op jit(solution)/shard_map/pallas_call | solution.py:70
  170.1 3.4 %collective-permute-done.31.refs_6_.refs_12_ = bf16[768,128]{1,0:T(8,128)(2,1)S(1)} collective-permute-done((bf16[768,128]{1,0:T(8,128)(2,1)S(1)}, bf16[768,128]{1,0:T(8,128)(2,1)S(1)}, u32[]{:S(2)}, u32[]{:S(2)}) %collective-permute-start.31) | collective-permute-done | bytes 196640 | tf_op jit(solution)/shard_map/ppermute | solution.py:1096
  177.7 3.7 %shard_map.296 = (bf16[624,128]{1,0:T(8,128)(2,1)}, bf16[624,128]{1,0:T(8,128)(2,1)}, bf16[624,128]{1,0:T(8,128)(2,1)}, bf16[624,128]{1,0:T(8,128)(2,1)}, f32[4,576]{1,0:T(4,128)}, /*index=5*/f32[576]{0:T(1024)}) custom-call(s32[1]{0:T(128)} %bitcast.refs_0_, bf16[256,128]{1,0:T(8,128)(2,1)} %get-tuple-element.128.refs_7_.refs_1_, ...), custom_call_target="tpu_custom_call" | custom-call | tf_op jit(solution)/shard_map/pallas_call | solution.py:70
  193.5 10.1 %shard_map.297 = (f32[576,1152]{1,0:T(8,128)}, f32[2,576,1152]{2,1,0:T(8,128)}, f32[104,576]{1,0:T(8,128)}, f32[72,576]{1,0:T(8,128)}, f32[576]{0:T(1024)}, /*in...) custom-call(bf16[2304,128]{1,0:T(8,128)(2,1)} %copy-done.5, bf16[2304,128]{1,0:T(8,128)(2,1)} %collective-permute-done.33.refs_0_.refs_1_, ...), custom_call_target="tpu_custom_call" | custom-call | tf_op jit(solution)/shard_map/pallas_call | solution.py:70
  (171 shorter events, 90.8 us)
Async XLA Ops:
  5.8 55.8 %all-to-all-start.1 = ((bf16[8,336,768]{2,1,0:T(8,128)(2,1)}), bf16[8,336,768]{2,1,0:T(8,128)(2,1)}, u32[]{:S(2)}, u32[]{:S(2)}) async-start(bf16[8,336,768]{2,1,0:T(8,128)(2,1)} %get-tuple-element.140), calls=%async_computation.1 | async-start | bytes 8257536 | tf_op jit(solution)/shard_map/all_to_all | solution.py:1149
  46.6 25.9 %collective-permute-start.13 = (bf16[2304,128]{1,0:T(8,128)(2,1)S(1)}, bf16[2304,128]{1,0:T(8,128)(2,1)}, u32[]{:S(2)}, u32[]{:S(2)}) collective-permute-start(bf16[2304,128]{1,0:T(8,128)(2,1)S(1)} %get-tuple-element.187.refs_0_), channel_id=1, source_target_pairs={{0,16},{4,20},{8,24},{12,28},{16,0},{20,4},{24,8},{28,12},{1,17},{... | collective-permute-start | bytes 1769480 | tf_op jit(solution)/shard_map/ppermute | solution.py:1096
  48.3 24.2 %collective-permute-start.12 = (bf16[2304,128]{1,0:T(8,128)(2,1)S(1)}, bf16[2304,128]{1,0:T(8,128)(2,1)}, u32[]{:S(2)}, u32[]{:S(2)}) collective-permute-start(bf16[2304,128]{1,0:T(8,128)(2,1)S(1)} %get-tuple-element.187.refs_0_), channel_id=1, source_target_pairs={{0,8},{4,12},{8,0},{12,4},{16,24},{20,28},{24,16},{28,20},{1,9},{5... | collective-permute-start | bytes 1769480 | tf_op jit(solution)/shard_map/ppermute | solution.py:1096
  61.6 17.9 %all-to-all-start = ((bf16[8,32,1152]{2,1,0:T(8,128)(2,1)}), bf16[8,32,1152]{2,1,0:T(8,128)(2,1)}, u32[]{:S(2)}, u32[]{:S(2)}) async-start(bf16[8,32,1152]{2,1,0:T(8,128)(2,1)} %bitcast.18), calls=%async_computation | async-start | bytes 1179648 | tf_op jit(solution)/shard_map/all_to_all | solution.py:1149
  74.4 9.7 %collective-permute-start.14 = (bf16[1152,128]{1,0:T(8,128)(2,1)}, bf16[1152,128]{1,0:T(8,128)(2,1)}, u32[]{:S(2)}, u32[]{:S(2)}) collective-permute-start(bf16[1152,128]{1,0:T(8,128)(2,1)} %get-tuple-element.148), channel_id=1, source_target_pairs={{0,8},{4,12},{8,0},{12,4},{16,24},{20,28},{24,16},{28,20},{1,9},{5... | collective-permute-start | bytes 884744 | tf_op jit(solution)/shard_map/ppermute | solution.py:1096
  75.7 9.4 %collective-permute-start.15 = (bf16[1152,128]{1,0:T(8,128)(2,1)}, bf16[1152,128]{1,0:T(8,128)(2,1)}, u32[]{:S(2)}, u32[]{:S(2)}) collective-permute-start(bf16[1152,128]{1,0:T(8,128)(2,1)} %get-tuple-element.149), channel_id=1, source_target_pairs={{0,16},{4,20},{8,24},{12,28},{16,0},{20,4},{24,8},{28,12},{1,17},{... | collective-permute-start | bytes 884744 | tf_op jit(solution)/shard_map/ppermute | solution.py:1096
  76.8 18.2 %collective-permute-start.16 = (bf16[2304,128]{1,0:T(8,128)(2,1)S(1)}, bf16[2304,128]{1,0:T(8,128)(2,1)}, u32[]{:S(2)}, u32[]{:S(2)}) collective-permute-start(bf16[2304,128]{1,0:T(8,128)(2,1)S(1)} %get-tuple-element.187.refs_0_), channel_id=1, source_target_pairs={{0,4},{4,0},{8,12},{12,8},{16,20},{20,16},{24,28},{28,24},{1,5},{5... | collective-permute-start | bytes 1769480 | tf_op jit(solution)/shard_map/ppermute | solution.py:1096
  76.8 18.2 %collective-permute-start.17 = (bf16[2304,128]{1,0:T(8,128)(2,1)}, bf16[2304,128]{1,0:T(8,128)(2,1)}, u32[]{:S(2)}, u32[]{:S(2)}) collective-permute-start(bf16[2304,128]{1,0:T(8,128)(2,1)} %collective-permute-done.12.refs_0_.refs_1_), channel_id=1, source_target_pairs={{0,4},{4,0},{8,12},{12,8},{16,20},{20,16},{24,28},{28,24},{1,5},{5... | collective-permute-start | bytes 1769480 | tf_op jit(solution)/shard_map/ppermute | solution.py:1096
  77.3 17.7 %collective-permute-start.18 = (bf16[2304,128]{1,0:T(8,128)(2,1)}, bf16[2304,128]{1,0:T(8,128)(2,1)}, u32[]{:S(2)}, u32[]{:S(2)}) collective-permute-start(bf16[2304,128]{1,0:T(8,128)(2,1)} %collective-permute-done.13.refs_1_.refs_2_), channel_id=1, source_target_pairs={{0,4},{4,0},{8,12},{12,8},{16,20},{20,16},{24,28},{28,24},{1,5},{5... | collective-permute-start | bytes 1769480 | tf_op jit(solution)/shard_map/ppermute | solution.py:1096
  85.1 14.7 %all-to-all-start.2 = ((bf16[8,32,1152]{2,1,0:T(8,128)(2,1)}), bf16[8,32,1152]{2,1,0:T(8,128)(2,1)}, u32[]{:S(2)}, u32[]{:S(2)}) async-start(bf16[8,32,1152]{2,1,0:T(8,128)(2,1)} %bitcast.19), calls=%async_computation.2 | async-start | bytes 1179648 | tf_op jit(solution)/shard_map/all_to_all | solution.py:1149
  99.8 57.4 %all-to-all-start.3 = ((bf16[8,336,768]{2,1,0:T(8,128)(2,1)}), bf16[8,336,768]{2,1,0:T(8,128)(2,1)}, u32[]{:S(2)}, u32[]{:S(2)}) async-start(bf16[8,336,768]{2,1,0:T(8,128)(2,1)} %shard_map.287), calls=%async_computation.3 | async-start | bytes 8257536 | tf_op jit(solution)/shard_map/all_to_all | solution.py:1149
  139.1 26.9 %collective-permute-start.34 = (bf16[2304,128]{1,0:T(8,128)(2,1)S(1)}, bf16[2304,128]{1,0:T(8,128)(2,1)}, u32[]{:S(2)}, u32[]{:S(2)}) collective-permute-start(bf16[2304,128]{1,0:T(8,128)(2,1)S(1)} %get-tuple-element.213.refs_0_), channel_id=1, source_target_pairs={{0,16},{4,20},{8,24},{12,28},{16,0},{20,4},{24,8},{28,12},{1,17},{... | collective-permute-start | bytes 1769480 | tf_op jit(solution)/shard_map/ppermute | solution.py:1096
  140.9 25.1 %collective-permute-start.33 = (bf16[2304,128]{1,0:T(8,128)(2,1)S(1)}, bf16[2304,128]{1,0:T(8,128)(2,1)}, u32[]{:S(2)}, u32[]{:S(2)}) collective-permute-start(bf16[2304,128]{1,0:T(8,128)(2,1)S(1)} %get-tuple-element.213.refs_0_), channel_id=1, source_target_pairs={{0,8},{4,12},{8,0},{12,4},{16,24},{20,28},{24,16},{28,20},{1,9},{5... | collective-permute-start | bytes 1769480 | tf_op jit(solution)/shard_map/ppermute | solution.py:1096
  153.7 16.4 %collective-permute-start.32 = (bf16[768,128]{1,0:T(8,128)(2,1)S(1)}, bf16[768,128]{1,0:T(8,128)(2,1)S(1)}, u32[]{:S(2)}, u32[]{:S(2)}) collective-permute-start(bf16[768,128]{1,0:T(8,128)(2,1)S(1)} %get-tuple-element.204.refs_4_.refs_10_), channel_id=1, source_target_pairs={{0,24},{4,28},{8,16},{12,20},{16,8},{20,12},{24,0},{28,4},{1,25},{... | collective-permute-start | bytes 589832 | tf_op jit(solution)/shard_map/ppermute | solution.py:1096
  154.0 19.4 %collective-permute-start.31 = (bf16[768,128]{1,0:T(8,128)(2,1)S(1)}, bf16[768,128]{1,0:T(8,128)(2,1)S(1)}, u32[]{:S(2)}, u32[]{:S(2)}) collective-permute-start(bf16[768,128]{1,0:T(8,128)(2,1)S(1)} %get-tuple-element.204.refs_4_.refs_10_), channel_id=1, source_target_pairs={{0,16},{4,20},{8,24},{12,28},{16,0},{20,4},{24,8},{28,12},{1,17},{... | collective-permute-start | bytes 589832 | tf_op jit(solution)/shard_map/ppermute | solution.py:1096
  155.7 17.7 %collective-permute-start.30 = (bf16[768,128]{1,0:T(8,128)(2,1)S(1)}, bf16[768,128]{1,0:T(8,128)(2,1)S(1)}, u32[]{:S(2)}, u32[]{:S(2)}) collective-permute-start(bf16[768,128]{1,0:T(8,128)(2,1)S(1)} %get-tuple-element.204.refs_4_.refs_10_), channel_id=1, source_target_pairs={{0,8},{4,12},{8,0},{12,4},{16,24},{20,28},{24,16},{28,20},{1,9},{5... | collective-permute-start | bytes 589832 | tf_op jit(solution)/shard_map/ppermute | solution.py:1096
  173.5 9.6 %collective-permute-start.42 = (bf16[1152,128]{1,0:T(8,128)(2,1)}, bf16[1152,128]{1,0:T(8,128)(2,1)S(1)}, u32[]{:S(2)}, u32[]{:S(2)}) collective-permute-start(bf16[1152,128]{1,0:T(8,128)(2,1)} %get-tuple-element.202), channel_id=1, source_target_pairs={{0,8},{4,12},{8,0},{12,4},{16,24},{20,28},{24,16},{28,20},{1,9},{5... | collective-permute-start | bytes 884744 | tf_op jit(solution)/shard_map/ppermute | solution.py:1096
  174.4 9.3 %collective-permute-start.43 = (bf16[1152,128]{1,0:T(8,128)(2,1)}, bf16[1152,128]{1,0:T(8,128)(2,1)S(1)}, u32[]{:S(2)}, u32[]{:S(2)}) collective-permute-start(bf16[1152,128]{1,0:T(8,128)(2,1)} %get-tuple-element.203), channel_id=1, source_target_pairs={{0,16},{4,20},{8,24},{12,28},{16,0},{20,4},{24,8},{28,12},{1,17},{... | collective-permute-start | bytes 884744 | tf_op jit(solution)/shard_map/ppermute | solution.py:1096
  183.7 8.5 %collective-permute-start.44 = (bf16[2304,128]{1,0:T(8,128)(2,1)S(1)}, bf16[2304,128]{1,0:T(8,128)(2,1)S(1)}, u32[]{:S(2)}, u32[]{:S(2)}) collective-permute-start(bf16[2304,128]{1,0:T(8,128)(2,1)S(1)} %get-tuple-element.213.refs_0_), channel_id=1, source_target_pairs={{0,4},{4,0},{8,12},{12,8},{16,20},{20,16},{24,28},{28,24},{1,5},{5... | collective-permute-start | bytes 1769480 | tf_op jit(solution)/shard_map/ppermute | solution.py:1096
  183.7 9.8 %collective-permute-start.45 = (bf16[2304,128]{1,0:T(8,128)(2,1)}, bf16[2304,128]{1,0:T(8,128)(2,1)S(1)}, u32[]{:S(2)}, u32[]{:S(2)}) collective-permute-start(bf16[2304,128]{1,0:T(8,128)(2,1)} %collective-permute-done.33.refs_0_.refs_1_), channel_id=1, source_target_pairs={{0,4},{4,0},{8,12},{12,8},{16,20},{20,16},{24,28},{28,24},{1,5},{5... | collective-permute-start | bytes 1769480 | tf_op jit(solution)/shard_map/ppermute | solution.py:1096
  184.2 9.3 %collective-permute-start.46 = (bf16[2304,128]{1,0:T(8,128)(2,1)}, bf16[2304,128]{1,0:T(8,128)(2,1)S(1)}, u32[]{:S(2)}, u32[]{:S(2)}) collective-permute-start(bf16[2304,128]{1,0:T(8,128)(2,1)} %collective-permute-done.34.refs_1_.refs_2_), channel_id=1, source_target_pairs={{0,4},{4,0},{8,12},{12,8},{16,20},{20,16},{24,28},{28,24},{1,5},{5... | collective-permute-start | bytes 1769480 | tf_op jit(solution)/shard_map/ppermute | solution.py:1096
  187.3 16.3 %collective-permute-start.39 = (bf16[624,128]{1,0:T(8,128)(2,1)}, bf16[624,128]{1,0:T(8,128)(2,1)S(1)}, u32[]{:S(2)}, u32[]{:S(2)}) collective-permute-start(bf16[624,128]{1,0:T(8,128)(2,1)} %get-tuple-element.209), channel_id=1, source_target_pairs={{0,1},{1,2},{2,3},{3,0},{4,5},{5,6},{6,7},{7,4},{8,9},{9,10},{10,1... | collective-permute-start | bytes 479240 | tf_op jit(solution)/shard_map/ppermute | solution.py:1077
  189.6 14.1 %collective-permute-start.40 = (bf16[624,128]{1,0:T(8,128)(2,1)}, bf16[624,128]{1,0:T(8,128)(2,1)S(1)}, u32[]{:S(2)}, u32[]{:S(2)}) collective-permute-start(bf16[624,128]{1,0:T(8,128)(2,1)} %get-tuple-element.210), channel_id=1, source_target_pairs={{0,2},{1,3},{2,0},{3,1},{4,6},{5,7},{6,4},{7,5},{8,10},{9,11},{10,... | collective-permute-start | bytes 479240 | tf_op jit(solution)/shard_map/ppermute | solution.py:1077
  192.2 11.5 %collective-permute-start.41 = (bf16[624,128]{1,0:T(8,128)(2,1)}, bf16[624,128]{1,0:T(8,128)(2,1)S(1)}, u32[]{:S(2)}, u32[]{:S(2)}) collective-permute-start(bf16[624,128]{1,0:T(8,128)(2,1)} %get-tuple-element.211), channel_id=1, source_target_pairs={{0,3},{1,0},{2,1},{3,2},{4,7},{5,4},{6,5},{7,6},{8,11},{9,8},{10,9... | collective-permute-start | bytes 479240 | tf_op jit(solution)/shard_map/ppermute | solution.py:1077
  (63 other events, 605.6 us)
